TPU v7x, 128 devices: a whole 4x4x4 slice. The times are simulated.
128 devices in a mesh: gx: 8 (over y, core), gy: 16 (over x, z).
Axes of the slice: x: 4, y: 4, z: 4, core: 2. Of those that a mesh axis runs over, the one named last changes fastest.
Arguments:
- point_feats: bfloat16 [262144, 96], P(('gx', 'gy')), may hold values from -6 to 6
- point_owner: int32 [262144, 1], P(('gx', 'gy')), may hold values from 0 to 127, as said below
- point_cell: int32 [262144], P(('gx', 'gy')), may hold values from 0 to 2047
- occupancy: int32 [64, 256, 16], P('gx', 'gy'), may hold values from 0 to 1, as said below
- w_conv: bfloat16 [27, 96, 96], replicated, may hold values from -0.125 to 0.125
- w_down: bfloat16 [8, 96, 192], replicated, may hold values from -0.21875 to 0.21875
- cotangent: bfloat16 [32, 128, 8, 192], P('gx', 'gy'), may hold values from -6 to 6
Outputs:
- features_out: bfloat16 [32, 128, 8, 192], P('gx', 'gy')
- grad_points: bfloat16 [262144, 96], P(('gx', 'gy'))
- grad_conv: float32 [27, 96, 96], replicated
- grad_down: float32 [8, 96, 192], replicated
Inputs may be any that keep to these rules, and one draw needn't show every extreme that they name: `point_owner`: among the points of one device no owner is named more than 32 times, and in every draw some owner is named exactly 32 times among the points of each device. `occupancy`: every voxel that holds some point is active.
All inputs are finite; a program needn't handle non-finite values.
Results may differ from a plain program's by a relative error of at most 0.0067.
Values may be sent and summed in bfloat16 or wider, within the bound.
No kernel may reach another device: no remote copies, remote signals or barrier semaphores. Data moves between devices by JAX's collectives and lax.ppermute only.
A program may use at most 64 MiB of HBM per device.

v0:
```python
import functools
import math

import jax
import jax.numpy as jnp
from jax import lax
from jax.experimental import pallas as pl
from jax.experimental.pallas import tpu as pltpu
from jax.sharding import PartitionSpec as P

F32 = jnp.float32
BF16 = jnp.bfloat16
LANE = 128
WIDE = 256
PACK = 4
AXES = ("gx", "gy")
NT = (((1,), (1,)), ((), ()))
NN = (((1,), (0,)), ((), ()))
TN = (((0,), (0,)), ((), ()))


def iota(shape, dim):
    return lax.broadcasted_iota(jnp.int32, shape, dim)


def mm(a, b, dims=NN):
    return lax.dot_general(a, b, dims, preferred_element_type=F32)


def one_hot(mask):
    return jnp.where(mask, 1.0, 0.0).astype(BF16)


def call(kernel, outs, args, name, scratch=(), flops=0, megabytes=4):
    return pl.pallas_call(
        kernel,
        out_shape=outs,
        in_specs=[pl.BlockSpec(memory_space=pltpu.VMEM)] * len(args),
        out_specs=jax.tree.map(lambda _: pl.BlockSpec(memory_space=pltpu.VMEM), outs),
        scratch_shapes=list(scratch),
        compiler_params=pltpu.CompilerParams(vmem_limit_bytes=48 * 1024 * 1024),
        cost_estimate=pl.CostEstimate(
            flops=flops, bytes_accessed=megabytes * 1000000, transcendentals=0
        ),
        name=name,
    )(*args)


def struct(shape, dtype):
    return jax.ShapeDtypeStruct(shape, dtype)


def dispatch_kernel(feats_ref, owner_ref, cell_ref, send_ref, slot_ref, *, devices, cap):
    channels, points = feats_ref.shape
    owner = owner_ref[...]
    hot = iota((devices, points), 0) == owner
    block = min(256, points)
    upper = one_hot(iota((block, block), 0) < iota((block, block), 1))
    carry = jnp.zeros((devices, 1), F32)
    ranks = []
    for start in range(0, points, block):
        part = jnp.where(hot[:, start : start + block], 1.0, 0.0)
        before = mm(part.astype(BF16), upper) + carry
        ranks.append(jnp.sum(part * before, axis=0, keepdims=True))
        carry = carry + jnp.sum(part, axis=1, keepdims=True)
    rank = jnp.concatenate(ranks, axis=1).astype(jnp.int32)
    row = owner * (cap // PACK) + (rank >> 2)
    quarter = rank & 3
    slot_ref[0:1, :] = row
    slot_ref[1:2, :] = quarter
    cell = cell_ref[...]
    line = iota((LANE - channels, points), 0)
    extra = jnp.where(line == 0, cell >> 6, 0)
    extra = jnp.where(line == 1, (cell >> 1) & 31, extra)
    extra = jnp.where(line == 2, cell & 1, extra)
    whole = jnp.concatenate([feats_ref[...], extra.astype(F32).astype(BF16)], axis=0)
    spread = jnp.concatenate([whole * one_hot(quarter == q) for q in range(PACK)], axis=0)
    rows = send_ref.shape[0]
    step = min(256, rows)
    for start in range(0, rows, step):
        pick = one_hot(iota((step, points), 0) + start == row)
        send_ref[start : start + step, :] = mm(pick, spread, NT).astype(BF16)


def pool_kernel(got_ref, grid_ref, total_ref, *, channels):
    rows = got_ref.shape[0]
    pairs = grid_ref.shape[0]
    lane = iota((8, LANE), 1)
    weigh = jnp.where(lane == channels, 32.0, jnp.where(lane == channels + 1, 1.0, 0.0))
    weigh = weigh.astype(BF16)
    step = 256
    for q in range(PACK):
        block = got_ref[:, q * LANE : (q + 1) * LANE]
        place = mm(weigh, block, NT)[0:1].astype(jnp.int32)
        odd = block * block[:, channels + 2 : channels + 3]
        both = jnp.concatenate([block - odd, odd], axis=1)
        for start in range(0, pairs, step):
            pick = one_hot(iota((step, rows), 0) + start == place)
            part = mm(pick, both)
            if q == 0:
                total_ref[start : start + step, :] = part
            elif q < PACK - 1:
                total_ref[start : start + step, :] += part
            else:
                grid_ref[start : start + step, :] = (
                    total_ref[start : start + step, :] + part
                ).astype(BF16)


def weights_kernel(conv_ref, down_ref, conv_out, down_out):
    channels = conv_ref.shape[1]
    conv_out[...] = jnp.zeros(conv_out.shape, BF16)
    down_out[...] = jnp.zeros(down_out.shape, BF16)
    a, b = slice(0, channels), slice(LANE, LANE + channels)
    for j in range(9):
        low, mid, high = conv_ref[3 * j], conv_ref[3 * j + 1], conv_ref[3 * j + 2]
        conv_out[j, 0, a, a] = mid
        conv_out[j, 0, a, b] = low
        conv_out[j, 0, b, a] = high
        conv_out[j, 0, b, b] = mid
        conv_out[j, 1, a, b] = high
        conv_out[j, 1, b, a] = low
    for j in range(4):
        down_out[j, a, :] = down_ref[2 * j]
        down_out[j, b, :] = down_ref[2 * j + 1]


def fill(center_ref, x_low, x_high, y_low, y_high, pad_ref, side_ref):
    ext_x, ext_y, half, wide = pad_ref.shape
    pad_ref[1 : ext_x - 1, 1 : ext_y - 1] = (
        center_ref[...].astype(F32).reshape(ext_x - 2, ext_y - 2, half, wide)
    )
    pad_ref[0, 1 : ext_y - 1] = x_low[...].astype(F32).reshape(ext_y - 2, half, wide)
    pad_ref[ext_x - 1, 1 : ext_y - 1] = x_high[...].astype(F32).reshape(ext_y - 2, half, wide)
    pad_ref[:, 0] = y_low[...].astype(F32).reshape(ext_x, half, wide)
    pad_ref[:, ext_y - 1] = y_high[...].astype(F32).reshape(ext_x, half, wide)
    level = iota((ext_x * ext_y, half, LANE), 1)
    even = pad_ref[:, :, :, :LANE].reshape(ext_x * ext_y, half, LANE)
    odd = pad_ref[:, :, :, LANE:].reshape(ext_x * ext_y, half, LANE)
    even = jnp.where(level == half - 1, 0.0, pltpu.roll(even, half - 1, 1))
    odd = jnp.where(level == 0, 0.0, pltpu.roll(odd, 1, 1))
    side_ref[:, :, :, :LANE] = even.reshape(ext_x, ext_y, half, LANE)
    side_ref[:, :, :, LANE:] = odd.reshape(ext_x, ext_y, half, LANE)


def window(ref, j, first, count):
    dx, dy = j // 3, j % 3
    ext_y, half, wide = ref.shape[1] - 2, ref.shape[2], ref.shape[3]
    rows = ref[first + dx : first + dx + count, dy : dy + ext_y]
    return rows.reshape(count * ext_y * half, wide).astype(BF16)


def convolve(pad_ref, side_ref, weight_ref, first, count, back):
    total = None
    for j in range(9):
        for t, ref in enumerate((pad_ref, side_ref)):
            weight = weight_ref[8 - j if back else j, t]
            part = mm(window(ref, j, first, count), weight, NT if back else NN)
            total = part if total is None else total + part
    return total


def logistic(values):
    return 1.0 / (1.0 + jnp.exp(-values))


def level_kernel(
    center_ref, x_low, x_high, y_low, y_high, mask_ref, coarse_ref, conv_ref, down_ref, cot_ref,
    features_ref, fine_ref, delta_coarse_ref, delta_ref,
    pad_ref, side_ref, fine_s, slope_s,
):
    fill(center_ref, x_low, x_high, y_low, y_high, pad_ref, side_ref)
    ext_x, ext_y, half, wide = (
        pad_ref.shape[0] - 2, pad_ref.shape[1] - 2, pad_ref.shape[2], pad_ref.shape[3]
    )
    count = 4
    for first in range(0, ext_x, count):
        rows = slice(first * ext_y * half, (first + count) * ext_y * half)
        pre = convolve(pad_ref, side_ref, conv_ref, first, count, False)
        mask = mask_ref[rows, :].astype(F32)
        sigma = logistic(pre)
        fine = (pre * sigma * mask).astype(BF16)
        slope = sigma * (1.0 + pre * (1.0 - sigma)) * mask
        fine_ref[rows, :] = fine
        shape = (count // 2, 2, ext_y // 2, 2, half, wide)
        fine_s[first // 2 : (first + count) // 2] = fine.astype(F32).reshape(shape)
        slope_s[first // 2 : (first + count) // 2] = slope.reshape(shape)
    coarse_rows = ext_x // 2 * (ext_y // 2) * half
    pre = None
    for j in range(4):
        piece = fine_s[:, j // 2, :, j % 2].reshape(coarse_rows, wide).astype(BF16)
        part = mm(piece, down_ref[j])
        pre = part if pre is None else pre + part
    sigma = logistic(pre)
    mask = coarse_ref[...].astype(F32)
    features_ref[...] = (pre * sigma * mask).astype(BF16)
    slope = sigma * (1.0 + pre * (1.0 - sigma))
    delta = (cot_ref[...].astype(F32) * mask * slope).astype(BF16)
    delta_coarse_ref[...] = delta
    for j in range(4):
        back = mm(delta, down_ref[j], NT).reshape(ext_x // 2, ext_y // 2, half, wide)
        fine_s[:, j // 2, :, j % 2] = back * slope_s[:, j // 2, :, j % 2]
    delta_ref[...] = fine_s[...].reshape(ext_x * ext_y * half, wide).astype(BF16)


def weight_grad_kernel(
    center_ref, x_low, x_high, y_low, y_high, fine_ref, delta_coarse_ref, delta_ref, out_ref,
    pad_ref, side_ref, fine_s, *, channels, scale,
):
    fill(center_ref, x_low, x_high, y_low, y_high, pad_ref, side_ref)
    ext_x, ext_y, half, wide = (
        pad_ref.shape[0] - 2, pad_ref.shape[1] - 2, pad_ref.shape[2], pad_ref.shape[3]
    )
    turned = delta_ref[...].astype(F32).T.astype(BF16)
    lo, hi = slice(0, LANE), slice(LANE, WIDE)
    for j in range(9):
        main = mm(turned, window(pad_ref, j, 0, ext_x))
        side = mm(turned, window(side_ref, j, 0, ext_x))
        low = main[hi, lo] + side[lo, hi]
        mid = main[lo, lo] + main[hi, hi]
        high = main[lo, hi] + side[hi, lo]
        for t, part in enumerate((low, mid, high)):
            start = (3 * j + t) * channels
            out_ref[start : start + channels, :] = (part.T[:channels] * scale).astype(BF16)
    fine_s[...] = fine_ref[...].astype(F32).reshape(fine_s.shape)
    coarse_rows = ext_x // 2 * (ext_y // 2) * half
    base = 27 * channels
    for j in range(4):
        piece = fine_s[:, j // 2, :, j % 2].reshape(coarse_rows, wide).astype(BF16)
        grad = mm(piece, delta_coarse_ref[...], TN) * scale
        first, second = grad[:channels], grad[LANE : LANE + channels]
        start = base + 2 * j * channels
        out_ref[start : start + channels, :] = first[:, :LANE].astype(BF16)
        out_ref[start + channels : start + 2 * channels, :] = second[:, :LANE].astype(BF16)
        start = base + (8 + j) * channels
        tail = jnp.concatenate([first[:, LANE:], second[:, LANE:]], axis=1)
        out_ref[start : start + channels, :] = tail.astype(BF16)
    end = base + 12 * channels
    out_ref[end:, :] = jnp.zeros((out_ref.shape[0] - end, LANE), BF16)


def input_grad_kernel(
    center_ref, x_low, x_high, y_low, y_high, conv_ref, got_ref, back_ref,
    pad_ref, side_ref, grad_s, *, channels,
):
    fill(center_ref, x_low, x_high, y_low, y_high, pad_ref, side_ref)
    ext_x, ext_y, half = pad_ref.shape[0] - 2, pad_ref.shape[1] - 2, pad_ref.shape[2]
    count = 4
    for first in range(0, ext_x, count):
        rows = slice(first * ext_y * half, (first + count) * ext_y * half)
        grad_s[rows, :] = convolve(pad_ref, side_ref, conv_ref, first, count, True).astype(BF16)
    grad = grad_s[...]
    pairs = grad.shape[0]
    rows = got_ref.shape[0]
    step = min(256, rows)
    for q in range(PACK):
        for start in range(0, rows, step):
            info = got_ref[start : start + step, q * LANE : (q + 1) * LANE].astype(F32)
            place = info[:, channels : channels + 1] * 32.0 + info[:, channels + 1 : channels + 2]
            pick = one_hot(iota((step, pairs), 1) == place.astype(jnp.int32))
            both = mm(pick, grad)
            odd = info[:, channels + 2 : channels + 3] > 0.5
            row = jnp.where(odd, both[:, LANE:], both[:, :LANE])
            back_ref[start : start + step, q * LANE : (q + 1) * LANE] = row.astype(BF16)


def collect_kernel(back_ref, slot_ref, out_ref):
    channels, points = out_ref.shape
    rows = back_ref.shape[0]
    step = min(512, points)
    for start in range(0, points, step):
        row = slot_ref[0:1, start : start + step]
        quarter = slot_ref[1:2, start : start + step]
        pick = one_hot(iota((rows, step), 0) == row)
        found = mm(back_ref[...], pick, TN)
        total = jnp.zeros((channels, step), F32)
        for q in range(PACK):
            total = jnp.where(quarter == q, found[q * LANE : q * LANE + channels], total)
        out_ref[:, start : start + step] = total.astype(BF16)


def sum_kernel(parts_ref, out_ref):
    total = jnp.sum(parts_ref[...].astype(F32), axis=0).astype(BF16)
    out_ref[...] = jnp.broadcast_to(total[None], out_ref.shape)


def unpack_kernel(all_ref, conv_ref, down_ref):
    channels = conv_ref.shape[1]
    base = 27 * channels
    for j in range(27):
        conv_ref[j] = all_ref[j * channels : (j + 1) * channels, :channels].astype(F32)
    for j in range(8):
        start = base + j * channels
        down_ref[j, :, :LANE] = all_ref[start : start + channels, :].astype(F32)
        start = base + (8 + j // 2) * channels
        tail = all_ref[start : start + channels, :].astype(F32)
        rest = down_ref.shape[2] - LANE
        down_ref[j, :, LANE:] = tail[:, (j % 2) * rest : (j % 2 + 1) * rest]


def shift(block, axis, step):
    count = lax.axis_size(axis)
    pairs = [(i, i + step) for i in range(count) if 0 <= i + step < count]
    return lax.ppermute(block, axis, pairs)


def halo(center, ext_x, ext_y, half):
    wide = center.shape[1]
    slab = ext_y * half
    x_low = shift(center[-slab:], "gx", 1)
    x_high = shift(center[:slab], "gx", -1)
    whole = center.reshape(ext_x, ext_y, half, wide)
    low, high = x_low.reshape(1, ext_y, half, wide), x_high.reshape(1, ext_y, half, wide)

    def edge(y):
        parts = [low[:, y], whole[:, y], high[:, y]]
        return jnp.concatenate(parts, axis=0).reshape((ext_x + 2) * half, wide)

    y_low = shift(edge(ext_y - 1), "gy", 1)
    y_high = shift(edge(0), "gy", -1)
    return x_low, x_high, y_low, y_high


def exchange(blocks):
    return lax.all_to_all(blocks, AXES, split_axis=0, concat_axis=0, tiled=True)


def shards(point_feats, point_owner, point_cell, occupancy, w_conv, w_down, cotangent):
    points, channels = point_feats.shape
    devices = lax.axis_size("gx") * lax.axis_size("gy")
    cap = 32
    ext_x, ext_y, ext_z = occupancy.shape
    half = ext_z // 2
    pairs = ext_x * ext_y * half
    coarse = w_down.shape[2]
    coarse_rows = ext_x // 2 * (ext_y // 2) * half
    slot_rows = devices * cap // PACK
    scale = 1.0 / math.sqrt(float(ext_x * ext_y * ext_z * devices))
    padded = (ext_x + 2, ext_y + 2, half, WIDE)
    split = (ext_x // 2, 2, ext_y // 2, 2, half, WIDE)

    send, slot = call(
        functools.partial(dispatch_kernel, devices=devices, cap=cap),
        (struct((slot_rows, PACK * LANE), BF16), struct((2, points), jnp.int32)),
        (point_feats.T, point_owner.reshape(1, points), point_cell.reshape(1, points)),
        "dispatch",
        flops=2 * points * slot_rows * PACK * LANE,
    )
    got = exchange(send.reshape(devices, cap // PACK, PACK * LANE)).reshape(
        slot_rows, PACK * LANE
    )
    conv_blocks, down_blocks = call(
        weights_kernel,
        (struct((9, 2, WIDE, WIDE), BF16), struct((4, WIDE, coarse), BF16)),
        (w_conv, w_down),
        "weights",
    )
    mask = jnp.broadcast_to(
        occupancy.reshape(pairs, 2, 1).astype(BF16), (pairs, 2, LANE)
    ).reshape(pairs, WIDE)
    coarse_mask = jnp.max(occupancy.reshape(ext_x // 2, 2, ext_y // 2, 2, half, 2), axis=(1, 3, 5))
    coarse_mask = jnp.broadcast_to(
        coarse_mask.reshape(coarse_rows, 1).astype(BF16), (coarse_rows, coarse)
    )
    grid = call(
        functools.partial(pool_kernel, channels=channels),
        struct((pairs, WIDE), BF16),
        (got,),
        "pool",
        scratch=[pltpu.VMEM((pairs, WIDE), F32)],
        flops=2 * pairs * slot_rows * PACK * WIDE,
    )
    rim = halo(grid, ext_x, ext_y, half)
    conv_flops = 2 * pairs * 18 * WIDE * WIDE
    features, fine, delta_coarse, delta = call(
        level_kernel,
        (
            struct((coarse_rows, coarse), BF16),
            struct((pairs, WIDE), BF16),
            struct((coarse_rows, coarse), BF16),
            struct((pairs, WIDE), BF16),
        ),
        (grid, *rim, mask, coarse_mask, conv_blocks, down_blocks,
         cotangent.reshape(coarse_rows, coarse)),
        "level",
        scratch=[
            pltpu.VMEM(padded, F32),
            pltpu.VMEM(padded, F32),
            pltpu.VMEM(split, F32),
            pltpu.VMEM(split, F32),
        ],
        flops=conv_flops,
        megabytes=8,
    )
    delta_rim = halo(delta, ext_x, ext_y, half)
    used = 27 * channels + 12 * channels
    chunk = -(-used // (16 * devices)) * 16
    packed = call(
        functools.partial(weight_grad_kernel, channels=channels, scale=scale),
        struct((devices * chunk, LANE), BF16),
        (grid, *rim, fine, delta_coarse, delta),
        "weight_grad",
        scratch=[pltpu.VMEM(padded, F32), pltpu.VMEM(padded, F32), pltpu.VMEM(split, F32)],
        flops=conv_flops,
        megabytes=8,
    )
    terms = exchange(packed.reshape(devices, chunk, LANE))
    back = call(
        functools.partial(input_grad_kernel, channels=channels),
        struct((slot_rows, PACK * LANE), BF16),
        (delta, *delta_rim, conv_blocks, got),
        "input_grad",
        scratch=[
            pltpu.VMEM(padded, F32), pltpu.VMEM(padded, F32), pltpu.VMEM((pairs, WIDE), BF16)
        ],
        flops=conv_flops + 2 * pairs * slot_rows * PACK * WIDE,
        megabytes=8,
    )
    returned = exchange(back.reshape(devices, cap // PACK, PACK * LANE)).reshape(
        slot_rows, PACK * LANE
    )
    summed = call(
        sum_kernel, struct((devices, chunk, LANE), BF16), (terms,), "sum", flops=devices * chunk * LANE
    )
    gathered = exchange(summed).reshape(devices * chunk, LANE)
    grad_points = call(
        collect_kernel,
        struct((channels, points), BF16),
        (returned, slot),
        "collect",
        flops=2 * points * slot_rows * PACK * LANE,
    ).T
    grad_conv, grad_down = call(
        unpack_kernel,
        (struct(w_conv.shape, F32), struct(w_down.shape, F32)),
        (gathered,),
        "unpack",
    )
    return (
        features.reshape(ext_x // 2, ext_y // 2, half, coarse),
        grad_points,
        grad_conv,
        grad_down,
    )


def solution(mesh):
    placed = (
        P(("gx", "gy"), None),
        P(("gx", "gy"), None),
        P(("gx", "gy")),
        P("gx", "gy", None),
        P(),
        P(),
        P("gx", "gy", None, None),
    )
    return jax.shard_map(
        shards,
        mesh=mesh,
        in_specs=placed,
        out_specs=(P("gx", "gy", None, None), P(("gx", "gy"), None), P(), P()),
        check_vma=False,
    )
```

profile of v0, /device:TPU:1, one launch (start us, length us, event | category | flops | bytes accessed | tf_op | source)
XLA Modules:
  0.0 155.4 jit_solution(15375184941298685145)
XLA Ops:
  0.6 0.0 copy-start.6
  0.6 1.0 copy-done.6
  1.6 0.0 copy-start.8
  1.6 0.7 copy-done.8
  2.3 0.0 copy-start.9
  2.3 0.7 copy-done.9
  3.0 2.7 %dispatch.1 = (bf16[1024,512]{1,0:T(8,128)(2,1)S(1)}, s32[2,2048]{1,0:T(2,128)S(1)}) custom-call(bf16[96,2048]{1,0:T(8,128)(2,1)S(1)} %bitcast.74, s32[1,2048]{1,0:T(1,128)S(1)} %bitcast.76, s32[1,2048]{1,0:T(1,128)S(1)} %bitcast.77), custom_call_target="tpu_custom_call" | custom-call | flops 2147483648 | bytes 4000000 | tf_op jit(solution)/shard_map/dispatch/pallas_call | solution.py:35
  5.7 29.9 %all_to_all.20 = bf16[128,8,512]{2,1,0:T(8,128)(2,1)S(1)} all-to-all(bf16[128,8,512]{2,1,0:T(8,128)(2,1)S(1)} %bitcast.66), channel_id=1, replica_groups=mesh['gx'=8,'gy'=16] {'gx','gy'}, dimensions={0} | all-to-all | bytes 2097152 | tf_op jit(solution)/shard_map/all_to_all | solution.py:325
  35.7 0.0 copy-start.10
  35.7 2.9 %pool.1.center_ref = bf16[1024,256]{1,0:T(8,128)(2,1)S(1)} custom-call(bf16[1024,512]{1,0:T(8,128)(2,1)S(1)} %bitcast.63), custom_call_target="tpu_custom_call" | custom-call | flops 2147483648 | bytes 4000000 | tf_op jit(solution)/shard_map/pool/pallas_call | solution.py:35
  38.6 0.0 copy-start
  38.6 0.0 copy-start.1
  38.6 3.5 %collective-permute-start.1 = (bf16[128,256]{1,0:T(8,128)(2,1)S(1)}, bf16[128,256]{1,0:T(8,128)(2,1)S(1)}, u32[]{:S(2)}, u32[]{:S(2)}) collective-permute-start(bf16[128,256]{1,0:T(8,128)(2,1)S(1)} %get-tuple-element.30), channel_id=1, source_target_pairs={{16,0},{32,16},{48,32},{64,48},{80,64},{96,80},{112,96},{17,1},{33... | collective-permute-start | bytes 196616 | tf_op jit(solution)/shard_map/ppermute | solution.py:304
  42.2 2.2 %collective-permute-start = (bf16[128,256]{1,0:T(8,128)(2,1)S(1)}, bf16[128,256]{1,0:T(8,128)(2,1)S(1)}, u32[]{:S(2)}, u32[]{:S(2)}) collective-permute-start(bf16[128,256]{1,0:T(8,128)(2,1)S(1)} %get-tuple-element.31), channel_id=1, source_target_pairs={{0,16},{16,32},{32,48},{48,64},{64,80},{80,96},{96,112},{1,17},{17... | collective-permute-start | bytes 196616 | tf_op jit(solution)/shard_map/ppermute | solution.py:304
  44.3 0.0 collective-permute-done.1.x_high
  44.4 1.3 collective-permute-done.x_low
  45.7 0.6 maximum_bitcast_fusion
  46.3 0.0 copy-start.7
  46.3 2.7 %collective-permute-start.2 = (bf16[80,256]{1,0:T(8,128)(2,1)}, bf16[80,256]{1,0:T(8,128)(2,1)S(1)}, u32[]{:S(2)}, u32[]{:S(2)}) collective-permute-start(bf16[80,256]{1,0:T(8,128)(2,1)} %maximum_bitcast_fusion), channel_id=1, source_target_pairs={{0,1},{1,2},{2,3},{3,4},{4,5},{5,6},{6,7},{7,8},{8,9},{9,10},{10,1... | collective-permute-start | bytes 122888 | tf_op jit(solution)/shard_map/ppermute | solution.py:304
  49.0 0.6 maximum_bitcast_fusion.1
  49.6 1.3 collective-permute-start.3
  50.9 0.0 copy-done.10
  51.0 1.0 reshape.102
  51.9 0.2 convert_element_type.23
  52.2 2.9 %broadcast_in_dim.4 = bf16[1024,2,128]{2,1,0:T(2,128)(2,1)S(1)} broadcast(bf16[1024,2]{1,0:T(8,128)(2,1)S(1)} %convert_element_type.23), dimensions={0,1} | broadcast | bytes 528384 | tf_op jit(solution)/shard_map/broadcast_in_dim | solution.py:358
  55.1 0.1 copy.25
  55.2 1.7 %reduce_max.9 = s32[4,8,8]{2,1,0:T(8,128)S(1)} reduce(s32[4,2,8,2,8,2]{5,4,3,2,1,0:T(8,128)} %reshape.102, s32[]{:T(128)} %constant.0.clone.1), dimensions={1,3,5}, to_apply=%region_0.0 | reduce | flops 1792 | bytes 9220 | tf_op jit(solution)/shard_map/reduce_max | solution.py:361
  56.9 0.1 convert_element_type.25
  57.0 0.0 copy-done
  57.0 0.0 copy-done.1
  57.0 0.4 weights.1
  57.4 0.0 copy-start.4
  57.4 0.0 collective-permute-done.2.y_low
  57.4 0.0 collective-permute-done.3.y_high
  57.4 0.1 broadcast_in_dim.5.coarse_ref
  57.5 0.0 copy-done.7
  57.5 3.8 %level.1 = (bf16[256,192]{1,0:T(8,128)(2,1)}, bf16[1024,256]{1,0:T(8,128)(2,1)S(1)}, bf16[256,192]{1,0:T(8,128)(2,1)S(1)}, bf16[1024,256]{1,0:T(8,128)(2,1)S(1)}) custom-call(bf16[1024,256]{1,0:T(8,128)(2,1)S(1)} %pool.1.center_ref, bf16[128,256]{1,0:T(8,128)(2,1)S(1)} %collective-permute-done.x_low, bf16[128,256]{1,0:T(8,128)(2,1)S(1)} %collective-permute-done.1.x_high, ...), custom_call_target="tpu_custom_call" | custom-call | flops 2415919104 | bytes 8000000 | tf_op jit(solution)/shard_map/level/pallas_call | solution.py:35
  61.4 0.0 copy-done.4
  61.4 0.0 copy-start.2
  61.4 2.0 %collective-permute-start.5 = (bf16[128,256]{1,0:T(8,128)(2,1)S(1)}, bf16[128,256]{1,0:T(8,128)(2,1)S(1)}, u32[]{:S(2)}, u32[]{:S(2)}) collective-permute-start(bf16[128,256]{1,0:T(8,128)(2,1)S(1)} %get-tuple-element.26), channel_id=1, source_target_pairs={{16,0},{32,16},{48,32},{64,48},{80,64},{96,80},{112,96},{17,1},{33... | collective-permute-start | bytes 196616 | tf_op jit(solution)/shard_map/ppermute | solution.py:304
  63.4 4.7 %collective-permute-start.4 = (bf16[128,256]{1,0:T(8,128)(2,1)S(1)}, bf16[128,256]{1,0:T(8,128)(2,1)S(1)}, u32[]{:S(2)}, u32[]{:S(2)}) collective-permute-start(bf16[128,256]{1,0:T(8,128)(2,1)S(1)} %get-tuple-element.27), channel_id=1, source_target_pairs={{0,16},{16,32},{32,48},{48,64},{64,80},{80,96},{96,112},{1,17},{17... | collective-permute-start | bytes 196616 | tf_op jit(solution)/shard_map/ppermute | solution.py:304
  68.1 3.8 %weight_grad.1 = bf16[4096,128]{1,0:T(8,128)(2,1)} custom-call(bf16[1024,256]{1,0:T(8,128)(2,1)S(1)} %pool.1.center_ref, bf16[128,256]{1,0:T(8,128)(2,1)S(1)} %collective-permute-done.x_low, bf16[128,256]{1,0:T(8,128)(2,1)S(1)} %collective-permute-done.1.x_high, bf16[80,256]{1,0:T(8,128)(2,1)S(1)} %collective-permute-done.2.y_low, ...), custom_call_target="tpu_custom_call" | custom-call | flops 2415919104 | bytes 8000000 | tf_op jit(solution)/shard_map/weight_grad/pallas_call | solution.py:35
  71.9 0.0 copy-done.2
  71.9 7.6 %all-to-all-start.2 = ((bf16[128,32,128]{2,1,0:T(8,128)(2,1)}), bf16[128,32,128]{2,1,0:T(8,128)(2,1)S(1)}, u32[]{:S(2)}, u32[]{:S(2)}) async-start(bf16[128,32,128]{2,1,0:T(8,128)(2,1)} %bitcast.32), calls=%async_computation.2 | async-start | bytes 2097152 | tf_op jit(solution)/shard_map/all_to_all | solution.py:325
  79.6 0.0 collective-permute-done.5.x_high
  79.6 0.0 collective-permute-done.4.x_low
  79.6 3.4 %collective-permute-start.6 = (bf16[80,256]{1,0:T(8,128)(2,1)S(1)}, bf16[80,256]{1,0:T(8,128)(2,1)S(1)}, u32[]{:S(2)}, u32[]{:S(2)}) collective-permute-start(bf16[80,256]{1,0:T(8,128)(2,1)S(1)} %maximum_bitcast_fusion.2), channel_id=1, source_target_pairs={{0,1},{1,2},{2,3},{3,4},{4,5},{5,6},{6,7},{7,8},{8,9},{9,10},{10,1... | collective-permute-start | bytes 122888 | tf_op jit(solution)/shard_map/ppermute | solution.py:304
  83.0 1.3 collective-permute-start.7
  84.3 2.1 %collective-permute-done.6.y_low = bf16[80,256]{1,0:T(8,128)(2,1)S(1)} collective-permute-done((bf16[80,256]{1,0:T(8,128)(2,1)S(1)}, bf16[80,256]{1,0:T(8,128)(2,1)S(1)}, u32[]{:S(2)}, u32[]{:S(2)}) %collective-permute-start.6) | collective-permute-done | bytes 40992 | tf_op jit(solution)/shard_map/ppermute | solution.py:304
  86.4 5.3 %collective-permute-done.7.y_high = bf16[80,256]{1,0:T(8,128)(2,1)S(1)} collective-permute-done((bf16[80,256]{1,0:T(8,128)(2,1)S(1)}, bf16[80,256]{1,0:T(8,128)(2,1)S(1)}, u32[]{:S(2)}, u32[]{:S(2)}) %collective-permute-start.7) | collective-permute-done | bytes 40992 | tf_op jit(solution)/shard_map/ppermute | solution.py:304
  91.7 0.0 copy-start.3
  91.7 1.0 copy-done.3
  92.7 0.0 copy-start.5
  92.7 1.7 %copy-done.5 = bf16[9,2,256,256]{3,2,1,0:T(8,128)(2,1)S(1)} copy-done((bf16[9,2,256,256]{3,2,1,0:T(8,128)(2,1)S(1)}, bf16[9,2,256,256]{3,2,1,0:T(8,128)(2,1)}, u32[]{:S(2)}) %copy-start.5) | copy-done | bytes 2359320
  94.4 5.9 %input_grad.1 = bf16[1024,512]{1,0:T(8,128)(2,1)} custom-call(bf16[1024,256]{1,0:T(8,128)(2,1)S(1)} %copy-done.3, bf16[128,256]{1,0:T(8,128)(2,1)S(1)} %collective-permute-done.4.x_low, bf16[128,256]{1,0:T(8,128)(2,1)S(1)} %collective-permute-done.5.x_high, bf16[80,256]{1,0:T(8,128)(2,1)S(1)} %collective-permute-done.6.y_low, ...), custom_call_target="tpu_custom_call" | custom-call | flops 4563402752 | bytes 8000000 | tf_op jit(solution)/shard_map/input_grad/pallas_call | solution.py:35
  100.3 0.0 all-to-all-done.2.parts_ref
  100.3 11.4 %all-to-all-start.1 = ((bf16[128,8,512]{2,1,0:T(8,128)(2,1)}), bf16[128,8,512]{2,1,0:T(8,128)(2,1)S(1)}, u32[]{:S(2)}, u32[]{:S(2)}) async-start(bf16[128,8,512]{2,1,0:T(8,128)(2,1)} %bitcast.29), calls=%async_computation.1 | async-start | bytes 2097152 | tf_op jit(solution)/shard_map/all_to_all | solution.py:325
  111.7 1.2 sum.1
  112.9 17.4 %all-to-all-done.1 = bf16[128,8,512]{2,1,0:T(8,128)(2,1)S(1)} async-done(((bf16[128,8,512]{2,1,0:T(8,128)(2,1)}), bf16[128,8,512]{2,1,0:T(8,128)(2,1)S(1)}, u32[]{:S(2)}, u32[]{:S(2)}) %all-to-all-start.1) | async-done | bytes 1048608 | tf_op jit(solution)/shard_map/all_to_all | solution.py:325
  130.3 4.9 %all-to-all-start.3 = ((bf16[128,32,128]{2,1,0:T(8,128)(2,1)}), bf16[128,32,128]{2,1,0:T(8,128)(2,1)S(1)}, u32[]{:S(2)}, u32[]{:S(2)}) async-start(bf16[128,32,128]{2,1,0:T(8,128)(2,1)} %sum.1), calls=%async_computation.3 | async-start | bytes 2097152 | tf_op jit(solution)/shard_map/all_to_all | solution.py:325
  135.2 3.2 %collect.1 = bf16[96,2048]{1,0:T(8,128)(2,1)} custom-call(bf16[1024,512]{1,0:T(8,128)(2,1)S(1)} %bitcast.65, s32[2,2048]{1,0:T(2,128)S(1)} %get-tuple-element.19.slot_ref), custom_call_target="tpu_custom_call" | custom-call | flops 2147483648 | bytes 4000000 | tf_op jit(solution)/shard_map/collect/pallas_call | solution.py:35
  138.5 15.5 %all-to-all-done.3 = bf16[128,32,128]{2,1,0:T(8,128)(2,1)S(1)} async-done(((bf16[128,32,128]{2,1,0:T(8,128)(2,1)}), bf16[128,32,128]{2,1,0:T(8,128)(2,1)S(1)}, u32[]{:S(2)}, u32[]{:S(2)}) %all-to-all-start.3) | async-done | bytes 1048608 | tf_op jit(solution)/shard_map/all_to_all | solution.py:325
  154.0 1.4 unpack.1
  (12 shorter events, 0.1 us)
Async XLA Ops:
  0.6 1.0 copy-start.6
  1.6 0.7 copy-start.8
  2.3 0.7 copy-start.9
  35.7 15.3 %copy-start.10 = (s32[8,16,16]{2,1,0:T(8,128)S(1)}, s32[8,16,16]{2,1,0:T(8,128)}, u32[]{:S(2)}) copy-start(s32[8,16,16]{2,1,0:T(8,128)} %param.10) | copy-start | bytes 24580
  38.6 18.4 %copy-start = (bf16[27,96,96]{2,1,0:T(8,128)(2,1)S(1)}, bf16[27,96,96]{2,1,0:T(8,128)(2,1)}, u32[]{:S(2)}) copy-start(bf16[27,96,96]{2,1,0:T(8,128)(2,1)} %conv_ref.1) | copy-start | bytes 1492996
  38.6 18.4 %copy-start.1 = (bf16[8,96,192]{2,1,0:T(8,128)(2,1)S(1)}, bf16[8,96,192]{2,1,0:T(8,128)(2,1)}, u32[]{:S(2)}) copy-start(bf16[8,96,192]{2,1,0:T(8,128)(2,1)} %down_ref.1) | copy-start | bytes 884740
  38.6 5.7 %collective-permute-start.1 = (bf16[128,256]{1,0:T(8,128)(2,1)S(1)}, bf16[128,256]{1,0:T(8,128)(2,1)S(1)}, u32[]{:S(2)}, u32[]{:S(2)}) collective-permute-start(bf16[128,256]{1,0:T(8,128)(2,1)S(1)} %get-tuple-element.30), channel_id=1, source_target_pairs={{16,0},{32,16},{48,32},{64,48},{80,64},{96,80},{112,96},{17,1},{33... | collective-permute-start | bytes 196616 | tf_op jit(solution)/shard_map/ppermute | solution.py:304
  42.2 3.5 %collective-permute-start = (bf16[128,256]{1,0:T(8,128)(2,1)S(1)}, bf16[128,256]{1,0:T(8,128)(2,1)S(1)}, u32[]{:S(2)}, u32[]{:S(2)}) collective-permute-start(bf16[128,256]{1,0:T(8,128)(2,1)S(1)} %get-tuple-element.31), channel_id=1, source_target_pairs={{0,16},{16,32},{32,48},{48,64},{64,80},{80,96},{96,112},{1,17},{17... | collective-permute-start | bytes 196616 | tf_op jit(solution)/shard_map/ppermute | solution.py:304
  46.3 11.2 %copy-start.7 = (bf16[4,8,8,192]{3,2,1,0:T(8,128)(2,1)S(1)}, bf16[4,8,8,192]{3,2,1,0:T(8,128)(2,1)}, u32[]{:S(2)}) copy-start(bf16[4,8,8,192]{3,2,1,0:T(8,128)(2,1)} %param.13) | copy-start | bytes 294916
  46.3 11.1 %collective-permute-start.2 = (bf16[80,256]{1,0:T(8,128)(2,1)}, bf16[80,256]{1,0:T(8,128)(2,1)S(1)}, u32[]{:S(2)}, u32[]{:S(2)}) collective-permute-start(bf16[80,256]{1,0:T(8,128)(2,1)} %maximum_bitcast_fusion), channel_id=1, source_target_pairs={{0,1},{1,2},{2,3},{3,4},{4,5},{5,6},{6,7},{7,8},{8,9},{9,10},{10,1... | collective-permute-start | bytes 122888 | tf_op jit(solution)/shard_map/ppermute | solution.py:304
  49.6 7.8 %collective-permute-start.3 = (bf16[80,256]{1,0:T(8,128)(2,1)}, bf16[80,256]{1,0:T(8,128)(2,1)S(1)}, u32[]{:S(2)}, u32[]{:S(2)}) collective-permute-start(bf16[80,256]{1,0:T(8,128)(2,1)} %maximum_bitcast_fusion.1), channel_id=1, source_target_pairs={{1,0},{2,1},{3,2},{4,3},{5,4},{6,5},{7,6},{8,7},{9,8},{10,9},{11,1... | collective-permute-start | bytes 122888 | tf_op jit(solution)/shard_map/ppermute | solution.py:304
  57.4 4.0 %copy-start.4 = (bf16[9,2,256,256]{3,2,1,0:T(8,128)(2,1)}, bf16[9,2,256,256]{3,2,1,0:T(8,128)(2,1)S(1)}, u32[]{:S(2)}) copy-start(bf16[9,2,256,256]{3,2,1,0:T(8,128)(2,1)S(1)} %get-tuple-element.15.conv_ref) | copy-start | bytes 7077892
  61.4 10.5 %copy-start.2 = (bf16[1024,256]{1,0:T(8,128)(2,1)}, bf16[1024,256]{1,0:T(8,128)(2,1)S(1)}, u32[]{:S(2)}) copy-start(bf16[1024,256]{1,0:T(8,128)(2,1)S(1)} %get-tuple-element.18.center_ref.delta_ref) | copy-start | bytes 1572868
  61.4 18.1 %collective-permute-start.5 = (bf16[128,256]{1,0:T(8,128)(2,1)S(1)}, bf16[128,256]{1,0:T(8,128)(2,1)S(1)}, u32[]{:S(2)}, u32[]{:S(2)}) collective-permute-start(bf16[128,256]{1,0:T(8,128)(2,1)S(1)} %get-tuple-element.26), channel_id=1, source_target_pairs={{16,0},{32,16},{48,32},{64,48},{80,64},{96,80},{112,96},{17,1},{33... | collective-permute-start | bytes 196616 | tf_op jit(solution)/shard_map/ppermute | solution.py:304
  63.4 16.2 %collective-permute-start.4 = (bf16[128,256]{1,0:T(8,128)(2,1)S(1)}, bf16[128,256]{1,0:T(8,128)(2,1)S(1)}, u32[]{:S(2)}, u32[]{:S(2)}) collective-permute-start(bf16[128,256]{1,0:T(8,128)(2,1)S(1)} %get-tuple-element.27), channel_id=1, source_target_pairs={{0,16},{16,32},{32,48},{48,64},{64,80},{80,96},{96,112},{1,17},{17... | collective-permute-start | bytes 196616 | tf_op jit(solution)/shard_map/ppermute | solution.py:304
  71.9 28.4 %all-to-all-start.2 = ((bf16[128,32,128]{2,1,0:T(8,128)(2,1)}), bf16[128,32,128]{2,1,0:T(8,128)(2,1)S(1)}, u32[]{:S(2)}, u32[]{:S(2)}) async-start(bf16[128,32,128]{2,1,0:T(8,128)(2,1)} %bitcast.32), calls=%async_computation.2 | async-start | bytes 2097152 | tf_op jit(solution)/shard_map/all_to_all | solution.py:325
  79.6 6.8 %collective-permute-start.6 = (bf16[80,256]{1,0:T(8,128)(2,1)S(1)}, bf16[80,256]{1,0:T(8,128)(2,1)S(1)}, u32[]{:S(2)}, u32[]{:S(2)}) collective-permute-start(bf16[80,256]{1,0:T(8,128)(2,1)S(1)} %maximum_bitcast_fusion.2), channel_id=1, source_target_pairs={{0,1},{1,2},{2,3},{3,4},{4,5},{5,6},{6,7},{7,8},{8,9},{9,10},{10,1... | collective-permute-start | bytes 122888 | tf_op jit(solution)/shard_map/ppermute | solution.py:304
  83.0 8.6 %collective-permute-start.7 = (bf16[80,256]{1,0:T(8,128)(2,1)S(1)}, bf16[80,256]{1,0:T(8,128)(2,1)S(1)}, u32[]{:S(2)}, u32[]{:S(2)}) collective-permute-start(bf16[80,256]{1,0:T(8,128)(2,1)S(1)} %maximum_bitcast_fusion.3), channel_id=1, source_target_pairs={{1,0},{2,1},{3,2},{4,3},{5,4},{6,5},{7,6},{8,7},{9,8},{10,9},{11,1... | collective-permute-start | bytes 122888 | tf_op jit(solution)/shard_map/ppermute | solution.py:304
  91.7 1.0 copy-start.3
  92.7 1.7 %copy-start.5 = (bf16[9,2,256,256]{3,2,1,0:T(8,128)(2,1)S(1)}, bf16[9,2,256,256]{3,2,1,0:T(8,128)(2,1)}, u32[]{:S(2)}) copy-start(bf16[9,2,256,256]{3,2,1,0:T(8,128)(2,1)} %copy-done.4) | copy-start | bytes 7077892
  100.3 30.0 %all-to-all-start.1 = ((bf16[128,8,512]{2,1,0:T(8,128)(2,1)}), bf16[128,8,512]{2,1,0:T(8,128)(2,1)S(1)}, u32[]{:S(2)}, u32[]{:S(2)}) async-start(bf16[128,8,512]{2,1,0:T(8,128)(2,1)} %bitcast.29), calls=%async_computation.1 | async-start | bytes 2097152 | tf_op jit(solution)/shard_map/all_to_all | solution.py:325
  130.3 23.7 %all-to-all-start.3 = ((bf16[128,32,128]{2,1,0:T(8,128)(2,1)}), bf16[128,32,128]{2,1,0:T(8,128)(2,1)S(1)}, u32[]{:S(2)}, u32[]{:S(2)}) async-start(bf16[128,32,128]{2,1,0:T(8,128)(2,1)} %sum.1), calls=%async_computation.3 | async-start | bytes 2097152 | tf_op jit(solution)/shard_map/all_to_all | solution.py:325
where the time goes:
time: 156 us; the launch traced here: 155 us
  starting transfers between devices  45 us (29%)
  waiting for transfers between devices  41.6 us (27%)
  blocking collectives  29.9 us (19%)
  Pallas kernels  25.4 us (16%)
  local copies, waits for them, and re-layouts  9.56 us (6%)
  other arithmetic  2.94 us (2%)
    all_to_all x3, waiting for transfers between devices, exchange(): return lax.all_to_all(blocks, AXES, split_axis=0, concat_axis=0, tiled=True)  32.9 us
    all_to_all x1, blocking collectives, exchange(): return lax.all_to_all(blocks, AXES, split_axis=0, concat_axis=0, tiled=True)  29.9 us
    pallas_call x9, Pallas kernels, call(): pl.pallas_call(kernel, out_shape=outs, in_specs=[pl.BlockSpec(memory_spac...  25.4 us
    all_to_all x3, starting transfers between devices, exchange(): return lax.all_to_all(blocks, AXES, split_axis=0, concat_axis=0, tiled=True)  23.9 us
    ppermute x8, starting transfers between devices, shift(): return lax.ppermute(block, axis, pairs)  21.1 us
    ppermute x8, waiting for transfers between devices, shift(): return lax.ppermute(block, axis, pairs)  8.65 us
    unnamed x23, local copies, waits for them, and re-layouts  5.2 us
  transfers between devices with their start and end apart: 11, of which 5 were waited for; matrix products, arithmetic and copies ran while one was open for 4% of the time, Pallas kernels for 9%

commit v1 on v0

v1 whole, which is shorter than its diff:
```python
import functools
import math

import jax
import jax.numpy as jnp
from jax import lax
from jax.experimental import pallas as pl
from jax.experimental.pallas import tpu as pltpu
from jax.sharding import PartitionSpec as P

F32 = jnp.float32
BF16 = jnp.bfloat16
LANE = 128
WIDE = 256
PACK = 4
AXES = ("gx", "gy")
NT = (((1,), (1,)), ((), ()))
NN = (((1,), (0,)), ((), ()))
TN = (((0,), (0,)), ((), ()))


def iota(shape, dim):
    return lax.broadcasted_iota(jnp.int32, shape, dim)


def mm(a, b, dims=NN):
    return lax.dot_general(a, b, dims, preferred_element_type=F32)


def one_hot(mask):
    return jnp.where(mask, 1.0, 0.0).astype(BF16)


def call(kernel, outs, args, name, scratch=(), flops=0, megabytes=4):
    return pl.pallas_call(
        kernel,
        out_shape=outs,
        in_specs=[pl.BlockSpec(memory_space=pltpu.VMEM)] * len(args),
        out_specs=jax.tree.map(lambda _: pl.BlockSpec(memory_space=pltpu.VMEM), outs),
        scratch_shapes=list(scratch),
        compiler_params=pltpu.CompilerParams(vmem_limit_bytes=48 * 1024 * 1024),
        cost_estimate=pl.CostEstimate(
            flops=flops, bytes_accessed=megabytes * 1000000, transcendentals=0
        ),
        name=name,
    )(*args)


def struct(shape, dtype):
    return jax.ShapeDtypeStruct(shape, dtype)


def dispatch_kernel(feats_ref, owner_ref, cell_ref, send_ref, slot_ref, *, devices, cap):
    channels, points = feats_ref.shape
    owner = owner_ref[...]
    hot = iota((devices, points), 0) == owner
    block = min(256, points)
    upper = one_hot(iota((block, block), 0) < iota((block, block), 1))
    carry = jnp.zeros((devices, 1), F32)
    ranks = []
    for start in range(0, points, block):
        part = jnp.where(hot[:, start : start + block], 1.0, 0.0)
        before = mm(part.astype(BF16), upper) + carry
        ranks.append(jnp.sum(part * before, axis=0, keepdims=True))
        carry = carry + jnp.sum(part, axis=1, keepdims=True)
    rank = jnp.concatenate(ranks, axis=1).astype(jnp.int32)
    row = owner * (cap // PACK) + (rank >> 2)
    quarter = rank & 3
    slot_ref[0:1, :] = row
    slot_ref[1:2, :] = quarter
    cell = cell_ref[...]
    line = iota((LANE - channels, points), 0)
    extra = jnp.where(line == 0, cell >> 6, 0)
    extra = jnp.where(line == 1, (cell >> 1) & 31, extra)
    extra = jnp.where(line == 2, cell & 1, extra)
    whole = jnp.concatenate([feats_ref[...], extra.astype(F32).astype(BF16)], axis=0)
    spread = jnp.concatenate([whole * one_hot(quarter == q) for q in range(PACK)], axis=0)
    rows = send_ref.shape[0]
    step = min(256, rows)
    for start in range(0, rows, step):
        pick = one_hot(iota((step, points), 0) + start == row)
        send_ref[start : start + step, :] = mm(pick, spread, NT).astype(BF16)


def pool_kernel(
    got_ref, coarse_ref, grid_ref, first_ref, last_ref, total_ref, *, channels, rim, slab, coarse_slab
):
    rows = got_ref.shape[0]
    pairs = grid_ref.shape[0]
    lane = iota((8, LANE), 1)
    weigh = jnp.where(lane == channels, 32.0, jnp.where(lane == channels + 1, 1.0, 0.0))
    weigh = weigh.astype(BF16)
    step = 256
    for q in range(PACK):
        block = got_ref[:, q * LANE : (q + 1) * LANE]
        place = mm(weigh, block, NT)[0:1].astype(jnp.int32)
        odd = block * block[:, channels + 2 : channels + 3]
        both = jnp.concatenate([block - odd, odd], axis=1)
        for start in range(0, pairs, step):
            pick = one_hot(iota((step, rows), 0) + start == place)
            part = mm(pick, both)
            if q == 0:
                total_ref[start : start + step, :] = part
            elif q < PACK - 1:
                total_ref[start : start + step, :] += part
            else:
                grid_ref[start : start + step, :] = (
                    total_ref[start : start + step, :] + part
                ).astype(BF16)
    edge = rim * slab
    first_ref[:edge, :] = grid_ref[:edge, :]
    first_ref[edge:, :] = coarse_ref[:coarse_slab, :]
    last_ref[:edge, :] = grid_ref[pairs - edge :, :]
    last_ref[edge:, :] = coarse_ref[coarse_ref.shape[0] - coarse_slab :, :]


def prepare_kernel(conv_ref, down_ref, cot_ref, occ_ref, conv_out, down_out, coarse_out, *, ext_y):
    channels = conv_ref.shape[1]
    conv_out[...] = jnp.zeros(conv_out.shape, BF16)
    down_out[...] = jnp.zeros(down_out.shape, BF16)
    a, b = slice(0, channels), slice(LANE, LANE + channels)
    for j in range(9):
        low, mid, high = conv_ref[3 * j], conv_ref[3 * j + 1], conv_ref[3 * j + 2]
        conv_out[j, 0, a, a] = mid
        conv_out[j, 0, a, b] = low
        conv_out[j, 0, b, a] = high
        conv_out[j, 0, b, b] = mid
        conv_out[j, 1, a, b] = high
        conv_out[j, 1, b, a] = low
    for j in range(4):
        down_out[j, a, :] = down_ref[2 * j]
        down_out[j, b, :] = down_ref[2 * j + 1]
    columns, depth = occ_ref.shape
    rows, coarse = cot_ref.shape
    half = depth // 2
    rest = WIDE - coarse
    occ = occ_ref[...].astype(F32).astype(BF16)
    row = iota((rows, columns), 0)
    place, column = row // half, iota((rows, columns), 1)
    base = place // (ext_y // 2) * 2 * ext_y + place % (ext_y // 2) * 2
    level = iota((rows, depth), 1) // 2 == iota((rows, depth), 0) % half
    total = jnp.zeros((rows, rest), F32)
    for j in range(4):
        pick = one_hot(base + j // 2 * ext_y + j % 2 == column)
        found = jnp.where(level, mm(pick, occ), 0.0).astype(BF16)
        spot = iota((depth, rest), 1) == 2 * j + iota((depth, rest), 0) % 2
        total = total + mm(found, one_hot(spot))
    coarse_out[:, :coarse] = cot_ref[...]
    coarse_out[:, coarse:] = total.astype(BF16)


def as_field(rows, ext_x, ext_y, half):
    return rows.astype(F32).reshape(ext_x, ext_y, half, rows.shape[1])


def edge_kernel(grid_ref, coarse_ref, low_ref, high_ref, first_ref, last_ref, *, fields):
    start_in, start_out = 0, 0
    for ref, (ext_x, ext_y, half, rim) in zip((grid_ref, coarse_ref), fields):
        size_in = rim * ext_y * half
        parts = [
            as_field(low_ref[start_in : start_in + size_in, :], rim, ext_y, half),
            as_field(ref[...], ext_x, ext_y, half),
            as_field(high_ref[start_in : start_in + size_in, :], rim, ext_y, half),
        ]
        at = start_out
        for part in parts:
            size = part.shape[0] * rim * half
            for out, y in ((first_ref, 0), (last_ref, ext_y - rim)):
                out[at : at + size, :] = part[:, y : y + rim].reshape(size, WIDE).astype(BF16)
            at += size
        start_in += size_in
        start_out = at


def fill_field(pad_ref, center, low, high, first, last, rim):
    ext_x, ext_y = pad_ref.shape[0] - 2 * rim, pad_ref.shape[1] - 2 * rim
    half = pad_ref.shape[2]
    pad_ref[rim : rim + ext_x, rim : rim + ext_y] = as_field(center, ext_x, ext_y, half)
    pad_ref[:rim, rim : rim + ext_y] = as_field(low, rim, ext_y, half)
    pad_ref[rim + ext_x :, rim : rim + ext_y] = as_field(high, rim, ext_y, half)
    pad_ref[:, :rim] = as_field(first, ext_x + 2 * rim, rim, half)
    pad_ref[:, rim + ext_y :] = as_field(last, ext_x + 2 * rim, rim, half)


def fill_side(pad_ref, side_ref):
    ext_x, ext_y, half, wide = pad_ref.shape
    level = iota((ext_x * ext_y, half, LANE), 1)
    even = pad_ref[:, :, :, :LANE].reshape(ext_x * ext_y, half, LANE)
    odd = pad_ref[:, :, :, LANE:].reshape(ext_x * ext_y, half, LANE)
    even = jnp.where(level == half - 1, 0.0, pltpu.roll(even, half - 1, 1))
    odd = jnp.where(level == 0, 0.0, pltpu.roll(odd, 1, 1))
    side_ref[:, :, :, :LANE] = even.reshape(ext_x, ext_y, half, LANE)
    side_ref[:, :, :, LANE:] = odd.reshape(ext_x, ext_y, half, LANE)


def window(ref, j, first, count):
    dx, dy = j // 3, j % 3
    ext_y, half, wide = ref.shape[1] - 2, ref.shape[2], ref.shape[3]
    rows = ref[first + dx : first + dx + count, dy : dy + ext_y]
    return rows.reshape(count * ext_y * half, wide).astype(BF16)


def convolve(pad_ref, side_ref, weight_ref, first, count, back):
    total = None
    for j in range(9):
        for t, ref in enumerate((pad_ref, side_ref)):
            weight = weight_ref[8 - j if back else j, t]
            part = mm(window(ref, j, first, count), weight, NT if back else NN)
            total = part if total is None else total + part
    return total


def logistic(values):
    return 1.0 / (1.0 + jnp.exp(-values))


def inner(field, rim):
    part = field[rim : field.shape[0] - rim, rim : field.shape[1] - rim]
    return part.reshape(part.shape[0] * part.shape[1] * part.shape[2], part.shape[3])


def level_kernel(
    grid_ref, coarse_ref, x_low, x_high, y_low, y_high, conv_ref, down_ref,
    features_ref, fine_ref, delta_coarse_ref, delta_ref, near_ref,
    pad_ref, side_ref, coarse_s, mask_s, fine_s, slope_s,
):
    ext_x, ext_y, half, wide = (
        pad_ref.shape[0] - 2, pad_ref.shape[1] - 2, pad_ref.shape[2], pad_ref.shape[3]
    )
    cut_x, cut_y = 3 * (ext_y - 4) * half, 3 * (ext_x + 2) * half
    fill_field(
        pad_ref, grid_ref[...], x_low[:cut_x, :], x_high[:cut_x, :],
        y_low[:cut_y, :], y_high[:cut_y, :], 3,
    )
    fill_field(
        coarse_s, coarse_ref[...], x_low[cut_x:, :], x_high[cut_x:, :],
        y_low[cut_y:, :], y_high[cut_y:, :], 1,
    )
    fill_side(pad_ref, side_ref)
    near_ref[...] = inner(pad_ref[...], 2).astype(BF16)
    coarse_x, coarse_y = ext_x // 2, ext_y // 2
    coarse_rows = coarse_x * coarse_y * half
    coarse = down_ref.shape[2]
    given = coarse_s[...].reshape(coarse_rows, wide).astype(BF16)
    largest = None
    for j in range(4):
        spot = iota((wide, wide), 0) == coarse + 2 * j + iota((wide, wide), 1) // LANE
        mask = mm(given, one_hot(spot))
        mask_s[:, j // 2, :, j % 2] = mask.reshape(coarse_x, coarse_y, half, wide)
        largest = mask if largest is None else jnp.maximum(largest, mask)
    largest = jnp.maximum(largest[:, :LANE], largest[:, LANE:])
    coarse_mask = jnp.concatenate([largest, largest[:, : coarse - LANE]], axis=1)
    count = 4
    for first in range(0, ext_x, count):
        pre = convolve(pad_ref, side_ref, conv_ref, first, count, False)
        part = slice(first // 2, (first + count) // 2)
        mask = mask_s[part].reshape(count * ext_y * half, wide)
        sigma = logistic(pre)
        shape = (count // 2, 2, coarse_y, 2, half, wide)
        fine_s[part] = (pre * sigma * mask).astype(BF16).astype(F32).reshape(shape)
        slope_s[part] = (sigma * (1.0 + pre * (1.0 - sigma)) * mask).reshape(shape)
    field = (ext_x, ext_y, half, wide)
    fine_ref[...] = inner(fine_s[...].reshape(field), 2).astype(BF16)
    pre = None
    for j in range(4):
        piece = fine_s[:, j // 2, :, j % 2].reshape(coarse_rows, wide).astype(BF16)
        part = mm(piece, down_ref[j])
        pre = part if pre is None else pre + part
    sigma = logistic(pre)
    coarse_field = (coarse_x, coarse_y, half, coarse)
    features = pre * sigma * coarse_mask
    features_ref[...] = inner(features.reshape(coarse_field), 1).astype(BF16)
    slope = sigma * (1.0 + pre * (1.0 - sigma))
    cot = coarse_s[:, :, :, :coarse].reshape(coarse_rows, coarse)
    delta = cot * coarse_mask * slope
    delta_coarse_ref[...] = inner(delta.reshape(coarse_field), 1).astype(BF16)
    delta = delta.astype(BF16)
    for j in range(4):
        back = mm(delta, down_ref[j], NT).reshape(coarse_x, coarse_y, half, wide)
        fine_s[:, j // 2, :, j % 2] = back * slope_s[:, j // 2, :, j % 2]
    delta_ref[...] = inner(fine_s[...].reshape(field), 1).astype(BF16)


def weight_grad_kernel(
    near_ref, fine_ref, delta_coarse_ref, delta_ref, out_ref,
    pad_ref, side_ref, delta_s, fine_s, *, channels, scale,
):
    ext_x, ext_y, half, wide = (
        pad_ref.shape[0] - 2, pad_ref.shape[1] - 2, pad_ref.shape[2], pad_ref.shape[3]
    )
    pad_ref[...] = as_field(near_ref[...], ext_x + 2, ext_y + 2, half)
    fill_side(pad_ref, side_ref)
    delta_s[...] = as_field(delta_ref[...], ext_x + 2, ext_y + 2, half)
    turned = inner(delta_s[...], 1).T.astype(BF16)
    lo, hi = slice(0, LANE), slice(LANE, WIDE)
    for j in range(9):
        main = mm(turned, window(pad_ref, j, 0, ext_x))
        side = mm(turned, window(side_ref, j, 0, ext_x))
        low = main[hi, lo] + side[lo, hi]
        mid = main[lo, lo] + main[hi, hi]
        high = main[lo, hi] + side[hi, lo]
        for t, part in enumerate((low, mid, high)):
            start = (3 * j + t) * channels
            out_ref[start : start + channels, :] = (part.T[:channels] * scale).astype(BF16)
    fine_s[...] = fine_ref[...].astype(F32).reshape(fine_s.shape)
    coarse_rows = ext_x // 2 * (ext_y // 2) * half
    base = 27 * channels
    for j in range(4):
        piece = fine_s[:, j // 2, :, j % 2].reshape(coarse_rows, wide).astype(BF16)
        grad = mm(piece, delta_coarse_ref[...], TN) * scale
        first, second = grad[:channels], grad[LANE : LANE + channels]
        start = base + 2 * j * channels
        out_ref[start : start + channels, :] = first[:, :LANE].astype(BF16)
        out_ref[start + channels : start + 2 * channels, :] = second[:, :LANE].astype(BF16)
        start = base + (8 + j) * channels
        tail = jnp.concatenate([first[:, LANE:], second[:, LANE:]], axis=1)
        out_ref[start : start + channels, :] = tail.astype(BF16)
    end = base + 12 * channels
    out_ref[end:, :] = jnp.zeros((out_ref.shape[0] - end, LANE), BF16)


def input_grad_kernel(delta_ref, conv_ref, got_ref, back_ref, pad_ref, side_ref, grad_s, *, channels):
    ext_x, ext_y, half = pad_ref.shape[0] - 2, pad_ref.shape[1] - 2, pad_ref.shape[2]
    pad_ref[...] = as_field(delta_ref[...], ext_x + 2, ext_y + 2, half)
    fill_side(pad_ref, side_ref)
    count = 4
    for first in range(0, ext_x, count):
        rows = slice(first * ext_y * half, (first + count) * ext_y * half)
        grad_s[rows, :] = convolve(pad_ref, side_ref, conv_ref, first, count, True).astype(BF16)
    grad = grad_s[...]
    pairs = grad.shape[0]
    rows = got_ref.shape[0]
    step = min(256, rows)
    for start in range(0, rows, step):
        found = []
        for q in range(PACK):
            info = got_ref[start : start + step, q * LANE : (q + 1) * LANE].astype(F32)
            place = info[:, channels : channels + 1] * 32.0 + info[:, channels + 1 : channels + 2]
            pick = one_hot(iota((step, pairs), 1) == place.astype(jnp.int32))
            both = mm(pick, grad)
            odd = info[:, channels + 2 : channels + 3] > 0.5
            found.append(jnp.where(odd, both[:, LANE:], both[:, :LANE])[:, :channels])
        back_ref[start : start + step, :] = jnp.concatenate(found, axis=1).astype(BF16)


def join_kernel(terms_ref, back_ref, out_ref, *, block, per_axis):
    total = jnp.sum(terms_ref[...].astype(F32), axis=0)
    rows, wide = back_ref.shape
    out_ref[:, :wide] = back_ref[...]
    lines = total.shape[0] // 2
    halves = []
    for h in range(2):
        parts = [total[h * lines + k : h * lines + k + block] for k in range(0, lines, block)]
        half = jnp.concatenate(parts, axis=1)
        halves.append(jnp.concatenate([half] * per_axis, axis=0).astype(BF16))
    step = block * per_axis
    for g in range(rows // step):
        out_ref[g * step : (g + 1) * step, wide:] = halves[g % 2]


def collect_kernel(back_ref, slot_ref, out_ref):
    channels, points = out_ref.shape
    rows = back_ref.shape[0]
    back = back_ref[:, : PACK * channels]
    step = min(512, points)
    for start in range(0, points, step):
        row = slot_ref[0:1, start : start + step]
        quarter = slot_ref[1:2, start : start + step]
        pick = one_hot(iota((rows, step), 0) == row)
        found = mm(back, pick, TN)
        total = jnp.zeros((channels, step), F32)
        for q in range(PACK):
            total = jnp.where(quarter == q, found[q * channels : (q + 1) * channels], total)
        out_ref[:, start : start + step] = total.astype(BF16)


def unpack_kernel(core_ref, mine_ref, theirs_ref, conv_ref, down_ref, all_s, *, block):
    channels = conv_ref.shape[1]
    devices, count = all_s.shape[0], all_s.shape[1] // 2
    skip = mine_ref.shape[1] - theirs_ref.shape[1]
    swap = jnp.broadcast_to(core_ref[...], (block * devices, LANE)) > 0
    for k in range(count):
        mine = mine_ref[:, skip + k * LANE : skip + (k + 1) * LANE].astype(F32)
        theirs = theirs_ref[:, k * LANE : (k + 1) * LANE].astype(F32)
        shape = (devices, block, LANE)
        all_s[:, k] = jnp.where(swap, theirs, mine).reshape(shape)
        all_s[:, count + k] = jnp.where(swap, mine, theirs).reshape(shape)
    whole = all_s[...].reshape(devices * 2 * count * block, LANE)
    base = 27 * channels
    for j in range(27):
        conv_ref[j] = whole[j * channels : (j + 1) * channels, :channels]
    rest = down_ref.shape[2] - LANE
    for j in range(8):
        start = base + j * channels
        down_ref[j, :, :LANE] = whole[start : start + channels]
        start = base + (8 + j // 2) * channels
        tail = whole[start : start + channels]
        down_ref[j, :, LANE:] = tail[:, (j % 2) * rest : (j % 2 + 1) * rest]


def shift(block, axis, step):
    count = lax.axis_size(axis)
    pairs = [(i, i + step) for i in range(count) if 0 <= i + step < count]
    return lax.ppermute(block, axis, pairs)


def exchange(blocks):
    return lax.all_to_all(blocks, AXES, split_axis=0, concat_axis=0, tiled=True)


def shards(point_feats, point_owner, point_cell, occupancy, w_conv, w_down, cotangent):
    points, channels = point_feats.shape
    count_x, count_y = lax.axis_size("gx"), lax.axis_size("gy")
    devices = count_x * count_y
    cap = 32
    block = cap // PACK
    ext_x, ext_y, ext_z = occupancy.shape
    half = ext_z // 2
    pairs = ext_x * ext_y * half
    coarse = w_down.shape[2]
    coarse_x, coarse_y = ext_x // 2, ext_y // 2
    coarse_rows = coarse_x * coarse_y * half
    slot_rows = devices * block
    scale = 1.0 / math.sqrt(float(ext_x * ext_y * ext_z * devices))
    conv_flops = 2 * pairs * 18 * WIDE * WIDE
    pick_flops = 2 * pairs * slot_rows * PACK * WIDE

    send, slot = call(
        functools.partial(dispatch_kernel, devices=devices, cap=cap),
        (struct((slot_rows, PACK * LANE), BF16), struct((2, points), jnp.int32)),
        (point_feats.T, point_owner.reshape(1, points), point_cell.reshape(1, points)),
        "dispatch",
        flops=2 * points * slot_rows * PACK * LANE,
    )
    got = exchange(send.reshape(devices, block, PACK * LANE)).reshape(slot_rows, PACK * LANE)
    conv_blocks, down_blocks, given = call(
        functools.partial(prepare_kernel, ext_y=ext_y),
        (
            struct((9, 2, WIDE, WIDE), BF16),
            struct((4, WIDE, coarse), BF16),
            struct((coarse_rows, WIDE), BF16),
        ),
        (w_conv, w_down, cotangent.reshape(coarse_rows, coarse),
         occupancy.reshape(ext_x * ext_y, ext_z)),
        "prepare",
    )
    x_rows = 3 * ext_y * half + coarse_y * half
    grid, x_first, x_last = call(
        functools.partial(
            pool_kernel, channels=channels, rim=3, slab=ext_y * half, coarse_slab=coarse_y * half
        ),
        (struct((pairs, WIDE), BF16), struct((x_rows, WIDE), BF16), struct((x_rows, WIDE), BF16)),
        (got, given),
        "pool",
        scratch=[pltpu.VMEM((pairs, WIDE), F32)],
        flops=pick_flops,
    )
    x_low, x_high = shift(x_last, "gx", 1), shift(x_first, "gx", -1)
    y_rows = 3 * (ext_x + 6) * half + (coarse_x + 2) * half
    y_first, y_last = call(
        functools.partial(
            edge_kernel, fields=((ext_x, ext_y, half, 3), (coarse_x, coarse_y, half, 1))
        ),
        (struct((y_rows, WIDE), BF16), struct((y_rows, WIDE), BF16)),
        (grid, given, x_low, x_high),
        "edge",
    )
    y_low, y_high = shift(y_last, "gy", 1), shift(y_first, "gy", -1)
    near = (ext_x + 2, ext_y + 2, half, WIDE)
    near_rows = near[0] * near[1] * half
    far = (ext_x + 6, ext_y + 6, half, WIDE)
    split = (coarse_x + 2, 2, coarse_y + 2, 2, half, WIDE)
    features, fine, delta_coarse, delta, grid_near = call(
        level_kernel,
        (
            struct((coarse_rows, coarse), BF16),
            struct((pairs, WIDE), BF16),
            struct((coarse_rows, coarse), BF16),
            struct((near_rows, WIDE), BF16),
            struct((near_rows, WIDE), BF16),
        ),
        (grid, given, x_low, x_high, y_low, y_high, conv_blocks, down_blocks),
        "level",
        scratch=[
            pltpu.VMEM(far, F32),
            pltpu.VMEM(far, F32),
            pltpu.VMEM((coarse_x + 2, coarse_y + 2, half, WIDE), F32),
            pltpu.VMEM(split, F32),
            pltpu.VMEM(split, F32),
            pltpu.VMEM(split, F32),
        ],
        flops=2 * conv_flops,
        megabytes=8,
    )
    used = 39 * channels
    chunk = -(-used // (32 * devices)) * 32
    packed = call(
        functools.partial(weight_grad_kernel, channels=channels, scale=scale),
        struct((devices * chunk, LANE), BF16),
        (grid_near, fine, delta_coarse, delta),
        "weight_grad",
        scratch=[
            pltpu.VMEM(near, F32),
            pltpu.VMEM(near, F32),
            pltpu.VMEM(near, F32),
            pltpu.VMEM((coarse_x, 2, coarse_y, 2, half, WIDE), F32),
        ],
        flops=conv_flops,
        megabytes=8,
    )
    terms = exchange(packed.reshape(devices, chunk, LANE))
    back = call(
        functools.partial(input_grad_kernel, channels=channels),
        struct((slot_rows, PACK * channels), BF16),
        (delta, conv_blocks, got),
        "input_grad",
        scratch=[pltpu.VMEM(near, F32), pltpu.VMEM(near, F32), pltpu.VMEM((pairs, WIDE), BF16)],
        flops=conv_flops + pick_flops,
        megabytes=8,
    )
    half_lanes = chunk // 2 // block * LANE
    joined_lanes = PACK * channels + half_lanes
    joined = call(
        functools.partial(join_kernel, block=block, per_axis=count_y),
        struct((slot_rows, joined_lanes), BF16),
        (terms, back),
        "join",
        flops=devices * chunk * LANE,
    )
    returned = exchange(joined.reshape(devices, block, joined_lanes)).reshape(
        slot_rows, joined_lanes
    )
    theirs = lax.ppermute(
        returned[:, PACK * channels :], "gx", [(i, i ^ 1) for i in range(count_x)]
    )
    grad_points = call(
        collect_kernel,
        struct((channels, points), BF16),
        (returned, slot),
        "collect",
        flops=2 * points * slot_rows * PACK * LANE,
    ).T
    core = jnp.broadcast_to(lax.axis_index("gx") & 1, (1, LANE)).astype(jnp.int32)
    grad_conv, grad_down = call(
        functools.partial(unpack_kernel, block=block),
        (struct(w_conv.shape, F32), struct(w_down.shape, F32)),
        (core, returned, theirs),
        "unpack",
        scratch=[pltpu.VMEM((devices, chunk // block, block, LANE), F32)],
    )
    return (
        features.reshape(coarse_x, coarse_y, half, coarse),
        grad_points,
        grad_conv,
        grad_down,
    )


def solution(mesh):
    placed = (
        P(("gx", "gy"), None),
        P(("gx", "gy"), None),
        P(("gx", "gy")),
        P("gx", "gy", None),
        P(),
        P(),
        P("gx", "gy", None, None),
    )
    return jax.shard_map(
        shards,
        mesh=mesh,
        in_specs=placed,
        out_specs=(P("gx", "gy", None, None), P(("gx", "gy"), None), P(), P()),
        check_vma=False,
    )
```

time: 156 us -> 133 us (0.85)
  starting transfers between devices: 45 us -> 31.9 us
  waiting for transfers between devices: 41.6 us -> 37.3 us
  Pallas kernels: 25.4 us -> 29.6 us
  blocking collectives: 29.9 us -> 25.8 us
  other arithmetic: 2.94 us -> 0 us
  local copies, waits for them, and re-layouts: 9.56 us -> 6.63 us
    ppermute x8 -> x4, starting transfers between devices: 21.1 us -> 9.58 us  [shift(): return lax.ppermute(block, axis, pairs)]
    all_to_all x3 -> x2, waiting for transfers between devices: 32.9 us -> 27 us  [exchange(): return lax.all_to_all(blocks, AXES, split_axis=0, concat_axis=0, tiled=True)]
    all_to_all x1, blocking collectives: 29.9 us -> 25.8 us  [exchange(): return lax.all_to_all(blocks, AXES, split_axis=0, concat_axis=0, tiled=True)]
    pallas_call x9 -> x10, Pallas kernels: 25.4 us -> 29.6 us  [call(): pl.pallas_call(kernel, out_shape=outs, in_specs=[pl.BlockSpec(memory_spac...]
    all_to_all x3 -> x2, starting transfers between devices: 23.9 us -> 20.8 us  [exchange(): return lax.all_to_all(blocks, AXES, split_axis=0, concat_axis=0, tiled=True)]
    broadcast_in_dim x2 -> x1, local copies, waits for them, and re-layouts: 3.04 us -> 0.01 us  [shards(): jnp.broadcast_to(lax.axis_index('gx') & 1, (1, LANE)).astype(jnp.int32)]
    ppermute x8 -> x4, waiting for transfers between devices: 8.65 us -> 10.3 us  [shift(): return lax.ppermute(block, axis, pairs)]
    reduce_max x1 -> x0, other arithmetic: 1.66 us -> none  [shards(): jnp.max(occupancy.reshape(ext_x // 2, 2, ext_y // 2, 2, half, 2), axis=(1...]
  transfers between devices with their start and end apart: 11 -> 7, of which waited for: 5 -> 6; matrix products, arithmetic and copies ran while one was open for 4% -> 0% of each run, Pallas kernels for 9% -> 7%
where the time goes in v1:
time: 133 us; the launch traced here: 132 us
  waiting for transfers between devices  37.3 us (28%)
  starting transfers between devices  31.9 us (24%)
  Pallas kernels  29.6 us (22%)
  blocking collectives  25.8 us (19%)
  local copies, waits for them, and re-layouts  6.63 us (5%)
    pallas_call x10, Pallas kernels, call(): pl.pallas_call(kernel, out_shape=outs, in_specs=[pl.BlockSpec(memory_spac...  29.6 us
    all_to_all x2, waiting for transfers between devices, exchange(): return lax.all_to_all(blocks, AXES, split_axis=0, concat_axis=0, tiled=True)  27 us
    all_to_all x1, blocking collectives, exchange(): return lax.all_to_all(blocks, AXES, split_axis=0, concat_axis=0, tiled=True)  25.8 us
    all_to_all x2, starting transfers between devices, exchange(): return lax.all_to_all(blocks, AXES, split_axis=0, concat_axis=0, tiled=True)  20.8 us
    ppermute x4, waiting for transfers between devices, shift(): return lax.ppermute(block, axis, pairs)  10.3 us
    ppermute x4, starting transfers between devices, shift(): return lax.ppermute(block, axis, pairs)  9.58 us
    unnamed x22, local copies, waits for them, and re-layouts  6.6 us
  transfers between devices with their start and end apart: 7, of which 6 were waited for; matrix products, arithmetic and copies ran while one was open for 0% of the time, Pallas kernels for 7%

profile of v1, /device:TPU:1, one launch (start us, length us, event | category | flops | bytes accessed | tf_op | source)
XLA Modules:
  0.0 132.0 jit_solution(2109186843423620597)
XLA Ops:
  0.6 0.0 copy-start.6
  0.6 1.0 copy-done.6
  1.6 0.0 copy-start.7
  1.6 0.7 copy-done.7
  2.3 0.0 copy-start.8
  2.3 0.7 copy-done.8
  3.0 3.7 %dispatch.1 = (bf16[1024,512]{1,0:T(8,128)(2,1)}, s32[2,2048]{1,0:T(2,128)S(1)}) custom-call(bf16[96,2048]{1,0:T(8,128)(2,1)S(1)} %bitcast.20, s32[1,2048]{1,0:T(1,128)S(1)} %bitcast.21, s32[1,2048]{1,0:T(1,128)S(1)} %bitcast.22), custom_call_target="tpu_custom_call" | custom-call | flops 2147483648 | bytes 4000000 | tf_op jit(solution)/shard_map/dispatch/pallas_call | solution.py:35
  6.7 0.0 copy-start
  6.7 0.0 copy-start.1
  6.7 0.0 copy-start.2
  6.7 0.0 copy-start.3
  6.7 11.5 %all-to-all-start = ((bf16[128,8,512]{2,1,0:T(8,128)(2,1)}), bf16[128,8,512]{2,1,0:T(8,128)(2,1)S(1)}, u32[]{:S(2)}, u32[]{:S(2)}) async-start(bf16[128,8,512]{2,1,0:T(8,128)(2,1)} %bitcast.3), calls=%async_computation | async-start | bytes 2097152 | tf_op jit(solution)/shard_map/all_to_all | solution.py:408
  18.2 0.0 copy-done
  18.2 0.0 copy-done.1
  18.2 0.0 copy-done.2
  18.3 0.0 copy-done.3
  18.3 1.0 prepare.1
  19.3 0.0 copy-start.4
  19.3 1.4 %copy-done.4 = bf16[9,2,256,256]{3,2,1,0:T(8,128)(2,1)} copy-done((bf16[9,2,256,256]{3,2,1,0:T(8,128)(2,1)}, bf16[9,2,256,256]{3,2,1,0:T(8,128)(2,1)S(1)}, u32[]{:S(2)}) %copy-start.4) | copy-done | bytes 2359320
  20.7 16.1 %all-to-all-done = bf16[128,8,512]{2,1,0:T(8,128)(2,1)S(1)} async-done(((bf16[128,8,512]{2,1,0:T(8,128)(2,1)}), bf16[128,8,512]{2,1,0:T(8,128)(2,1)S(1)}, u32[]{:S(2)}, u32[]{:S(2)}) %all-to-all-start) | async-done | bytes 1048608 | tf_op jit(solution)/shard_map/all_to_all | solution.py:408
  36.9 2.9 %pool.1 = (bf16[1024,256]{1,0:T(8,128)(2,1)S(1)}, bf16[448,256]{1,0:T(8,128)(2,1)S(1)}, bf16[448,256]{1,0:T(8,128)(2,1)S(1)}) custom-call(bf16[1024,512]{1,0:T(8,128)(2,1)S(1)} %bitcast.16, bf16[256,256]{1,0:T(8,128)(2,1)S(1)} %get-tuple-element.22.coarse_ref), custom_call_target="tpu_custom_call" | custom-call | flops 2147483648 | bytes 4000000 | tf_op jit(solution)/shard_map/pool/pallas_call | solution.py:35
  39.8 3.6 %collective-permute-start = (bf16[448,256]{1,0:T(8,128)(2,1)S(1)}, bf16[448,256]{1,0:T(8,128)(2,1)S(1)}, u32[]{:S(2)}, u32[]{:S(2)}) collective-permute-start(bf16[448,256]{1,0:T(8,128)(2,1)S(1)} %get-tuple-element.24), channel_id=1, source_target_pairs={{0,16},{16,32},{32,48},{48,64},{64,80},{80,96},{96,112},{1,17},{17... | collective-permute-start | bytes 688136 | tf_op jit(solution)/shard_map/ppermute | solution.py:404
  43.4 1.9 %collective-permute-start.1 = (bf16[448,256]{1,0:T(8,128)(2,1)S(1)}, bf16[448,256]{1,0:T(8,128)(2,1)S(1)}, u32[]{:S(2)}, u32[]{:S(2)}) collective-permute-start(bf16[448,256]{1,0:T(8,128)(2,1)S(1)} %get-tuple-element.25), channel_id=1, source_target_pairs={{16,0},{32,16},{48,32},{64,48},{80,64},{96,80},{112,96},{17,1},{33... | collective-permute-start | bytes 688136 | tf_op jit(solution)/shard_map/ppermute | solution.py:404
  45.3 1.0 collective-permute-done.low_ref.x_low
  46.4 4.4 %collective-permute-done.1.high_ref.x_high = bf16[448,256]{1,0:T(8,128)(2,1)S(1)} collective-permute-done((bf16[448,256]{1,0:T(8,128)(2,1)S(1)}, bf16[448,256]{1,0:T(8,128)(2,1)S(1)}, u32[]{:S(2)}, u32[]{:S(2)}) %collective-permute-start.1) | collective-permute-done | bytes 229408 | tf_op jit(solution)/shard_map/ppermute | solution.py:404
  50.8 2.6 %collective-permute-start.2 = (bf16[384,256]{1,0:T(8,128)(2,1)S(1)}, bf16[384,256]{1,0:T(8,128)(2,1)S(1)}, u32[]{:S(2)}, u32[]{:S(2)}) collective-permute-start(bf16[384,256]{1,0:T(8,128)(2,1)S(1)} %get-tuple-element.26), channel_id=1, source_target_pairs={{0,1},{1,2},{2,3},{3,4},{4,5},{5,6},{6,7},{7,8},{8,9},{9,10},{10,1... | collective-permute-start | bytes 589832 | tf_op jit(solution)/shard_map/ppermute | solution.py:404
  53.4 1.5 %collective-permute-start.3 = (bf16[384,256]{1,0:T(8,128)(2,1)S(1)}, bf16[384,256]{1,0:T(8,128)(2,1)S(1)}, u32[]{:S(2)}, u32[]{:S(2)}) collective-permute-start(bf16[384,256]{1,0:T(8,128)(2,1)S(1)} %get-tuple-element.27), channel_id=1, source_target_pairs={{1,0},{2,1},{3,2},{4,3},{5,4},{6,5},{7,6},{8,7},{9,8},{10,9},{11,1... | collective-permute-start | bytes 589832 | tf_op jit(solution)/shard_map/ppermute | solution.py:404
  54.8 1.1 collective-permute-done.2.y_low
  55.9 3.8 %collective-permute-done.3.y_high = bf16[384,256]{1,0:T(8,128)(2,1)S(1)} collective-permute-done((bf16[384,256]{1,0:T(8,128)(2,1)S(1)}, bf16[384,256]{1,0:T(8,128)(2,1)S(1)}, u32[]{:S(2)}, u32[]{:S(2)}) %collective-permute-start.3) | collective-permute-done | bytes 196640 | tf_op jit(solution)/shard_map/ppermute | solution.py:404
  59.8 8.5 %level.1 = (bf16[256,192]{1,0:T(8,128)(2,1)}, bf16[1024,256]{1,0:T(8,128)(2,1)S(1)}, bf16[256,192]{1,0:T(8,128)(2,1)S(1)}, bf16[1440,256]{1,0:T(8,128)(2,1)S(1)}, bf16[1440,256]{1,0:T(8,128)(2,1)S(1)}) custom-call(bf16[1024,256]{1,0:T(8,128)(2,1)S(1)} %get-tuple-element.23.grid_ref, bf16[256,256]{1,0:T(8,128)(2,1)S(1)} %get-tuple-element.22.coarse_ref, ...), custom_call_target="tpu_custom_call" | custom-call | flops 4831838208 | bytes 8000000 | tf_op jit(solution)/shard_map/level/pallas_call | solution.py:35
  68.3 0.0 copy-start.9
  68.3 3.8 %weight_grad.1 = bf16[4096,128]{1,0:T(8,128)(2,1)} custom-call(bf16[1440,256]{1,0:T(8,128)(2,1)S(1)} %get-tuple-element.31.near_ref, bf16[1024,256]{1,0:T(8,128)(2,1)S(1)} %get-tuple-element.32.fine_ref, bf16[256,192]{1,0:T(8,128)(2,1)S(1)} %get-tuple-element.33.delta_coarse_ref, bf16[1440,256]{1,0:T(8,128)(2,1)S(1)} %get-tuple-element.34.delta_ref), custom_call_target="tpu_custom_call" | custom-call | flops 2415919104 | bytes 8000000 | tf_op jit(solution)/shard_map/weight_grad/pallas_call | solution.py:35
  72.1 0.0 copy-done.9
  72.1 9.3 %all-to-all-start.1 = ((bf16[128,32,128]{2,1,0:T(8,128)(2,1)}), bf16[128,32,128]{2,1,0:T(8,128)(2,1)S(1)}, u32[]{:S(2)}, u32[]{:S(2)}) async-start(bf16[128,32,128]{2,1,0:T(8,128)(2,1)} %bitcast.8), calls=%async_computation.1 | async-start | bytes 2097152 | tf_op jit(solution)/shard_map/all_to_all | solution.py:408
  81.4 0.0 copy-start.5
  81.4 1.7 %copy-done.5 = bf16[9,2,256,256]{3,2,1,0:T(8,128)(2,1)S(1)} copy-done((bf16[9,2,256,256]{3,2,1,0:T(8,128)(2,1)S(1)}, bf16[9,2,256,256]{3,2,1,0:T(8,128)(2,1)}, u32[]{:S(2)}) %copy-start.5) | copy-done | bytes 2359320
  83.1 0.0 copy-start.10
  83.1 1.1 copy-done.10
  84.2 5.0 %input_grad.1.back_ref = bf16[1024,384]{1,0:T(8,128)(2,1)S(1)} custom-call(bf16[1440,256]{1,0:T(8,128)(2,1)S(1)} %copy-done.10, bf16[9,2,256,256]{3,2,1,0:T(8,128)(2,1)S(1)} %copy-done.5, bf16[1024,512]{1,0:T(8,128)(2,1)S(1)} %bitcast.17), custom_call_target="tpu_custom_call" | custom-call | flops 4563402752 | bytes 8000000 | tf_op jit(solution)/shard_map/input_grad/pallas_call | solution.py:35
  89.2 10.8 %all-to-all-done.1.terms_ref = bf16[128,32,128]{2,1,0:T(8,128)(2,1)S(1)} async-done(((bf16[128,32,128]{2,1,0:T(8,128)(2,1)}), bf16[128,32,128]{2,1,0:T(8,128)(2,1)S(1)}, u32[]{:S(2)}, u32[]{:S(2)}) %all-to-all-start.1) | async-done | bytes 1048608 | tf_op jit(solution)/shard_map/all_to_all | solution.py:408
  100.0 0.3 join.1
  100.3 25.8 %all_to_all.15 = bf16[128,8,640]{2,1,0:T(8,128)(2,1)S(1)} all-to-all(bf16[128,8,640]{2,1,0:T(8,128)(2,1)S(1)} %bitcast.15), channel_id=1, replica_groups=mesh['gx'=8,'gy'=16] {'gx','gy'}, dimensions={0} | all-to-all | bytes 2621440 | tf_op jit(solution)/shard_map/all_to_all | solution.py:408
  126.1 1.6 %collective-permute-start.4 = (bf16[1024,256]{1,0:T(8,128)(2,1)S(1)}, bf16[1024,256]{1,0:T(8,128)(2,1)S(1)}, u32[]{:S(2)}, u32[]{:S(2)}) collective-permute-start(bf16[1024,256]{1,0:T(8,128)(2,1)S(1)} %slice.4), channel_id=1, source_target_pairs={{0,16},{16,0},{32,48},{48,32},{64,80},{80,64},{96,112},{112,96},{1... | collective-permute-start | bytes 1572872 | tf_op jit(solution)/shard_map/ppermute | solution.py:533
  127.7 2.7 %collect.1 = bf16[96,2048]{1,0:T(8,128)(2,1)} custom-call(bf16[1024,640]{1,0:T(8,128)(2,1)S(1)} %bitcast.13, s32[2,2048]{1,0:T(2,128)S(1)} %get-tuple-element.35.slot_ref), custom_call_target="tpu_custom_call" | custom-call | flops 2147483648 | bytes 4000000 | tf_op jit(solution)/shard_map/collect/pallas_call | solution.py:35
  130.4 0.0 collective-permute-done.4.theirs_ref
  130.4 1.6 %unpack.1 = (f32[27,96,96]{2,1,0:T(8,128)}, f32[8,96,192]{2,1,0:T(8,128)}) custom-call(s32[1,128]{1,0:T(1,128)S(1)} %broadcast_in_dim.3.core_ref, bf16[1024,640]{1,0:T(8,128)(2,1)S(1)} %bitcast.14, bf16[1024,256]{1,0:T(8,128)(2,1)S(1)} %collective-permute-done.4.theirs_ref), custom_call_target="tpu_custom_call" | custom-call | bytes 4000000 | tf_op jit(solution)/shard_map/unpack/pallas_call | solution.py:35
  (3 shorter events, 0.1 us)
Async XLA Ops:
  0.6 1.0 copy-start.6
  1.6 0.7 copy-start.7
  2.3 0.7 copy-start.8
  6.7 11.5 %copy-start = (bf16[27,96,96]{2,1,0:T(8,128)(2,1)S(1)}, bf16[27,96,96]{2,1,0:T(8,128)(2,1)}, u32[]{:S(2)}) copy-start(bf16[27,96,96]{2,1,0:T(8,128)(2,1)} %conv_ref.1) | copy-start | bytes 1492996
  6.7 11.5 %copy-start.1 = (bf16[8,96,192]{2,1,0:T(8,128)(2,1)S(1)}, bf16[8,96,192]{2,1,0:T(8,128)(2,1)}, u32[]{:S(2)}) copy-start(bf16[8,96,192]{2,1,0:T(8,128)(2,1)} %down_ref.1) | copy-start | bytes 884740
  6.7 11.5 %copy-start.2 = (bf16[4,8,8,192]{3,2,1,0:T(8,128)(2,1)S(1)}, bf16[4,8,8,192]{3,2,1,0:T(8,128)(2,1)}, u32[]{:S(2)}) copy-start(bf16[4,8,8,192]{3,2,1,0:T(8,128)(2,1)} %param.13) | copy-start | bytes 294916
  6.7 11.5 %copy-start.3 = (s32[8,16,16]{2,1,0:T(8,128)S(1)}, s32[8,16,16]{2,1,0:T(8,128)}, u32[]{:S(2)}) copy-start(s32[8,16,16]{2,1,0:T(8,128)} %param.10) | copy-start | bytes 24580
  6.7 30.1 %all-to-all-start = ((bf16[128,8,512]{2,1,0:T(8,128)(2,1)}), bf16[128,8,512]{2,1,0:T(8,128)(2,1)S(1)}, u32[]{:S(2)}, u32[]{:S(2)}) async-start(bf16[128,8,512]{2,1,0:T(8,128)(2,1)} %bitcast.3), calls=%async_computation | async-start | bytes 2097152 | tf_op jit(solution)/shard_map/all_to_all | solution.py:408
  19.3 1.4 %copy-start.4 = (bf16[9,2,256,256]{3,2,1,0:T(8,128)(2,1)}, bf16[9,2,256,256]{3,2,1,0:T(8,128)(2,1)S(1)}, u32[]{:S(2)}) copy-start(bf16[9,2,256,256]{3,2,1,0:T(8,128)(2,1)S(1)} %get-tuple-element.28.conv_ref) | copy-start | bytes 7077892
  39.8 6.6 %collective-permute-start = (bf16[448,256]{1,0:T(8,128)(2,1)S(1)}, bf16[448,256]{1,0:T(8,128)(2,1)S(1)}, u32[]{:S(2)}, u32[]{:S(2)}) collective-permute-start(bf16[448,256]{1,0:T(8,128)(2,1)S(1)} %get-tuple-element.24), channel_id=1, source_target_pairs={{0,16},{16,32},{32,48},{48,64},{64,80},{80,96},{96,112},{1,17},{17... | collective-permute-start | bytes 688136 | tf_op jit(solution)/shard_map/ppermute | solution.py:404
  43.4 7.3 %collective-permute-start.1 = (bf16[448,256]{1,0:T(8,128)(2,1)S(1)}, bf16[448,256]{1,0:T(8,128)(2,1)S(1)}, u32[]{:S(2)}, u32[]{:S(2)}) collective-permute-start(bf16[448,256]{1,0:T(8,128)(2,1)S(1)} %get-tuple-element.25), channel_id=1, source_target_pairs={{16,0},{32,16},{48,32},{64,48},{80,64},{96,80},{112,96},{17,1},{33... | collective-permute-start | bytes 688136 | tf_op jit(solution)/shard_map/ppermute | solution.py:404
  50.8 5.1 %collective-permute-start.2 = (bf16[384,256]{1,0:T(8,128)(2,1)S(1)}, bf16[384,256]{1,0:T(8,128)(2,1)S(1)}, u32[]{:S(2)}, u32[]{:S(2)}) collective-permute-start(bf16[384,256]{1,0:T(8,128)(2,1)S(1)} %get-tuple-element.26), channel_id=1, source_target_pairs={{0,1},{1,2},{2,3},{3,4},{4,5},{5,6},{6,7},{7,8},{8,9},{9,10},{10,1... | collective-permute-start | bytes 589832 | tf_op jit(solution)/shard_map/ppermute | solution.py:404
  53.4 6.4 %collective-permute-start.3 = (bf16[384,256]{1,0:T(8,128)(2,1)S(1)}, bf16[384,256]{1,0:T(8,128)(2,1)S(1)}, u32[]{:S(2)}, u32[]{:S(2)}) collective-permute-start(bf16[384,256]{1,0:T(8,128)(2,1)S(1)} %get-tuple-element.27), channel_id=1, source_target_pairs={{1,0},{2,1},{3,2},{4,3},{5,4},{6,5},{7,6},{8,7},{9,8},{10,9},{11,1... | collective-permute-start | bytes 589832 | tf_op jit(solution)/shard_map/ppermute | solution.py:404
  68.3 3.8 %copy-start.9 = (bf16[1440,256]{1,0:T(8,128)(2,1)}, bf16[1440,256]{1,0:T(8,128)(2,1)S(1)}, u32[]{:S(2)}) copy-start(bf16[1440,256]{1,0:T(8,128)(2,1)S(1)} %get-tuple-element.34.delta_ref) | copy-start | bytes 2211844
  72.1 27.9 %all-to-all-start.1 = ((bf16[128,32,128]{2,1,0:T(8,128)(2,1)}), bf16[128,32,128]{2,1,0:T(8,128)(2,1)S(1)}, u32[]{:S(2)}, u32[]{:S(2)}) async-start(bf16[128,32,128]{2,1,0:T(8,128)(2,1)} %bitcast.8), calls=%async_computation.1 | async-start | bytes 2097152 | tf_op jit(solution)/shard_map/all_to_all | solution.py:408
  81.4 1.7 %copy-start.5 = (bf16[9,2,256,256]{3,2,1,0:T(8,128)(2,1)S(1)}, bf16[9,2,256,256]{3,2,1,0:T(8,128)(2,1)}, u32[]{:S(2)}) copy-start(bf16[9,2,256,256]{3,2,1,0:T(8,128)(2,1)} %copy-done.4) | copy-start | bytes 7077892
  83.1 1.1 copy-start.10
  126.1 4.3 %collective-permute-start.4 = (bf16[1024,256]{1,0:T(8,128)(2,1)S(1)}, bf16[1024,256]{1,0:T(8,128)(2,1)S(1)}, u32[]{:S(2)}, u32[]{:S(2)}) collective-permute-start(bf16[1024,256]{1,0:T(8,128)(2,1)S(1)} %slice.4), channel_id=1, source_target_pairs={{0,16},{16,0},{32,48},{48,32},{64,80},{80,64},{96,112},{112,96},{1... | collective-permute-start | bytes 1572872 | tf_op jit(solution)/shard_map/ppermute | solution.py:533

commit v2 on v1

--- a/solution.py
+++ b/solution.py
@@ -83,7 +83,7 @@
 
 
 def pool_kernel(
-    got_ref, coarse_ref, grid_ref, first_ref, last_ref, total_ref, *, channels, rim, slab, coarse_slab
+    got_ref, coarse_ref, grid_ref, x_first, x_last, y_first, y_last, total_ref, *, channels, fields
 ):
     rows = got_ref.shape[0]
     pairs = grid_ref.shape[0]
@@ -99,34 +99,58 @@
         for start in range(0, pairs, step):
             pick = one_hot(iota((step, rows), 0) + start == place)
             part = mm(pick, both)
-            if q == 0:
-                total_ref[start : start + step, :] = part
-            elif q < PACK - 1:
-                total_ref[start : start + step, :] += part
-            else:
-                grid_ref[start : start + step, :] = (
-                    total_ref[start : start + step, :] + part
-                ).astype(BF16)
-    edge = rim * slab
-    first_ref[:edge, :] = grid_ref[:edge, :]
-    first_ref[edge:, :] = coarse_ref[:coarse_slab, :]
-    last_ref[:edge, :] = grid_ref[pairs - edge :, :]
-    last_ref[edge:, :] = coarse_ref[coarse_ref.shape[0] - coarse_slab :, :]
-
-
-def prepare_kernel(conv_ref, down_ref, cot_ref, occ_ref, conv_out, down_out, coarse_out, *, ext_y):
+            if q:
+                part = total_ref[start : start + step, :] + part
+            total_ref[start : start + step, :] = part
+    x_at, y_at = 0, 0
+    for ref, (ext_x, ext_y, half, rim) in zip((total_ref, coarse_ref), fields):
+        field = as_field(ref[...], ext_x, ext_y, half)
+        x_at = put_rows(x_first, x_at, field[:rim])
+        put_rows(x_last, x_at - rim * ext_y * half, field[ext_x - rim :])
+        y_at = put_rows(y_first, y_at, field[:, :rim])
+        put_rows(y_last, y_at - rim * ext_x * half, field[:, ext_y - rim :])
+    grid_ref[...] = total_ref[...].astype(BF16)
+
+
+def as_field(rows, ext_x, ext_y, half):
+    return rows.astype(F32).reshape(ext_x, ext_y, half, rows.shape[1])
+
+
+def put_rows(ref, at, field):
+    size = field.shape[0] * field.shape[1] * field.shape[2]
+    ref[at : at + size, :] = field.reshape(size, field.shape[3]).astype(BF16)
+    return at + size
+
+
+def corner_kernel(low_ref, high_ref, first_ref, last_ref, *, fields):
+    start, at = 0, 0
+    for _, ext_y, half, rim in fields:
+        size = rim * ext_y * half
+        for ref in (low_ref, high_ref):
+            field = as_field(ref[start : start + size, :], rim, ext_y, half)
+            put_rows(first_ref, at, field[:, :rim])
+            at = put_rows(last_ref, at, field[:, ext_y - rim :])
+        start += size
+
+
+def prepare_kernel(
+    conv_ref, down_ref, cot_ref, occ_ref, conv_out, back_out, down_out, coarse_out, *, ext_y
+):
     channels = conv_ref.shape[1]
     conv_out[...] = jnp.zeros(conv_out.shape, BF16)
+    back_out[...] = jnp.zeros(back_out.shape, BF16)
     down_out[...] = jnp.zeros(down_out.shape, BF16)
+    four = 4 * channels
     a, b = slice(0, channels), slice(LANE, LANE + channels)
     for j in range(9):
-        low, mid, high = conv_ref[3 * j], conv_ref[3 * j + 1], conv_ref[3 * j + 2]
-        conv_out[j, 0, a, a] = mid
-        conv_out[j, 0, a, b] = low
-        conv_out[j, 0, b, a] = high
-        conv_out[j, 0, b, b] = mid
-        conv_out[j, 1, a, b] = high
-        conv_out[j, 1, b, a] = low
+        for k in range(3):
+            weight = conv_ref[3 * j + k]
+            turned = weight.astype(F32).T.astype(BF16)
+            for z in range(2):
+                at, side = j * four + (k + z) * channels, (a, b)[z]
+                conv_out[at : at + channels, side] = weight
+                at = (8 - j) * four + (2 - k + z) * channels
+                back_out[at : at + channels, side] = turned
     for j in range(4):
         down_out[j, a, :] = down_ref[2 * j]
         down_out[j, b, :] = down_ref[2 * j + 1]
@@ -149,69 +173,40 @@
     coarse_out[:, coarse:] = total.astype(BF16)
 
 
-def as_field(rows, ext_x, ext_y, half):
-    return rows.astype(F32).reshape(ext_x, ext_y, half, rows.shape[1])
-
-
-def edge_kernel(grid_ref, coarse_ref, low_ref, high_ref, first_ref, last_ref, *, fields):
-    start_in, start_out = 0, 0
-    for ref, (ext_x, ext_y, half, rim) in zip((grid_ref, coarse_ref), fields):
-        size_in = rim * ext_y * half
-        parts = [
-            as_field(low_ref[start_in : start_in + size_in, :], rim, ext_y, half),
-            as_field(ref[...], ext_x, ext_y, half),
-            as_field(high_ref[start_in : start_in + size_in, :], rim, ext_y, half),
-        ]
-        at = start_out
-        for part in parts:
-            size = part.shape[0] * rim * half
-            for out, y in ((first_ref, 0), (last_ref, ext_y - rim)):
-                out[at : at + size, :] = part[:, y : y + rim].reshape(size, WIDE).astype(BF16)
-            at += size
-        start_in += size_in
-        start_out = at
-
-
-def fill_field(pad_ref, center, low, high, first, last, rim):
-    ext_x, ext_y = pad_ref.shape[0] - 2 * rim, pad_ref.shape[1] - 2 * rim
-    half = pad_ref.shape[2]
-    pad_ref[rim : rim + ext_x, rim : rim + ext_y] = as_field(center, ext_x, ext_y, half)
-    pad_ref[:rim, rim : rim + ext_y] = as_field(low, rim, ext_y, half)
-    pad_ref[rim + ext_x :, rim : rim + ext_y] = as_field(high, rim, ext_y, half)
-    pad_ref[:, :rim] = as_field(first, ext_x + 2 * rim, rim, half)
-    pad_ref[:, rim + ext_y :] = as_field(last, ext_x + 2 * rim, rim, half)
-
-
-def fill_side(pad_ref, side_ref):
+def fill_four(pad_ref, four_ref, channels):
     ext_x, ext_y, half, wide = pad_ref.shape
-    level = iota((ext_x * ext_y, half, LANE), 1)
-    even = pad_ref[:, :, :, :LANE].reshape(ext_x * ext_y, half, LANE)
-    odd = pad_ref[:, :, :, LANE:].reshape(ext_x * ext_y, half, LANE)
-    even = jnp.where(level == half - 1, 0.0, pltpu.roll(even, half - 1, 1))
-    odd = jnp.where(level == 0, 0.0, pltpu.roll(odd, 1, 1))
-    side_ref[:, :, :, :LANE] = even.reshape(ext_x, ext_y, half, LANE)
-    side_ref[:, :, :, LANE:] = odd.reshape(ext_x, ext_y, half, LANE)
-
-
-def window(ref, j, first, count):
-    dx, dy = j // 3, j % 3
-    ext_y, half, wide = ref.shape[1] - 2, ref.shape[2], ref.shape[3]
-    rows = ref[first + dx : first + dx + count, dy : dy + ext_y]
-    return rows.reshape(count * ext_y * half, wide).astype(BF16)
-
-
-def convolve(pad_ref, side_ref, weight_ref, first, count, back):
-    total = None
+    columns = ext_x * ext_y
+    level = iota((columns, half, LANE), 1)
+    even = pad_ref[:, :, :, :LANE].reshape(columns, half, LANE)
+    odd = pad_ref[:, :, :, LANE:].reshape(columns, half, LANE)
+    after = jnp.where(level == half - 1, 0.0, pltpu.roll(even, half - 1, 1))
+    before = jnp.where(level == 0, 0.0, pltpu.roll(odd, 1, 1))
+    parts = [part[:, :, :channels] for part in (before, even, odd, after)]
+    four = jnp.concatenate(parts, axis=2)
+    four_ref[...] = four.reshape(ext_x, ext_y, half, 4 * channels)
+
+
+def windows(ref, first_x, count_x, first_y, count_y):
+    parts = []
     for j in range(9):
-        for t, ref in enumerate((pad_ref, side_ref)):
-            weight = weight_ref[8 - j if back else j, t]
-            part = mm(window(ref, j, first, count), weight, NT if back else NN)
-            total = part if total is None else total + part
-    return total
+        x, y = first_x + j // 3, first_y + j % 3
+        part = ref[x : x + count_x, y : y + count_y]
+        parts.append(part.reshape(count_x * count_y * part.shape[2], part.shape[3]).astype(BF16))
+    return parts
+
+
+def convolve(four_ref, weight_ref, boxes):
+    rows = [jnp.concatenate(windows(four_ref, *box), axis=1) for box in boxes]
+    return mm(rows[0] if len(rows) == 1 else jnp.concatenate(rows, axis=0), weight_ref[...])
 
 
 def logistic(values):
     return 1.0 / (1.0 + jnp.exp(-values))
+
+
+def silu_and_slope(pre):
+    sigma = logistic(pre)
+    return (pre * sigma).astype(BF16), sigma * (1.0 + pre * (1.0 - sigma))
 
 
 def inner(field, rim):
@@ -219,55 +214,106 @@
     return part.reshape(part.shape[0] * part.shape[1] * part.shape[2], part.shape[3])
 
 
+def column_kernel(
+    grid_ref, x_low, x_high, conv_ref, silu_ref, slope_ref, pad_ref, four_ref, *, channels
+):
+    ext_x, ext_y, half = pad_ref.shape[0], pad_ref.shape[1], pad_ref.shape[2]
+    rim = 3
+    size = rim * ext_y * half
+    pad_ref[:rim] = as_field(x_low[:size, :], rim, ext_y, half)
+    pad_ref[rim : ext_x - rim] = as_field(grid_ref[...], ext_x - 2 * rim, ext_y, half)
+    pad_ref[ext_x - rim :] = as_field(x_high[:size, :], rim, ext_y, half)
+    fill_four(pad_ref, four_ref, channels)
+    count = 4
+    step = count * (ext_y - 2) * half
+    for first in range(0, ext_x - 2, count):
+        pre = convolve(four_ref, conv_ref, [(first, count, 0, ext_y - 2)])
+        rows = slice(first // count * step, (first // count + 1) * step)
+        silu_ref[rows, :], slope_ref[rows, :] = silu_and_slope(pre)
+
+
 def level_kernel(
-    grid_ref, coarse_ref, x_low, x_high, y_low, y_high, conv_ref, down_ref,
-    features_ref, fine_ref, delta_coarse_ref, delta_ref, near_ref,
-    pad_ref, side_ref, coarse_s, mask_s, fine_s, slope_s,
+    grid_ref, coarse_ref, x_low, x_high, y_low, y_high, c_low, c_high, silu_ref, slope_ref,
+    conv_ref, down_ref,
+    features_ref, fine_ref, delta_coarse_ref, delta_ref,
+    pad_ref, four_ref, coarse_s, mask_s, fine_s, slope_s, *, channels, fields,
 ):
-    ext_x, ext_y, half, wide = (
-        pad_ref.shape[0] - 2, pad_ref.shape[1] - 2, pad_ref.shape[2], pad_ref.shape[3]
-    )
-    cut_x, cut_y = 3 * (ext_y - 4) * half, 3 * (ext_x + 2) * half
-    fill_field(
-        pad_ref, grid_ref[...], x_low[:cut_x, :], x_high[:cut_x, :],
-        y_low[:cut_y, :], y_high[:cut_y, :], 3,
-    )
-    fill_field(
-        coarse_s, coarse_ref[...], x_low[cut_x:, :], x_high[cut_x:, :],
-        y_low[cut_y:, :], y_high[cut_y:, :], 1,
-    )
-    fill_side(pad_ref, side_ref)
-    near_ref[...] = inner(pad_ref[...], 2).astype(BF16)
-    coarse_x, coarse_y = ext_x // 2, ext_y // 2
-    coarse_rows = coarse_x * coarse_y * half
+    (ext_x, ext_y, half, rim), (coarse_x, coarse_y, _, _) = fields
+    wide = WIDE
+    slab, face, corner = rim * ext_y * half, ext_x * rim * half, rim * rim * half
+    long = ext_x + 2 * rim
+    grid = as_field(grid_ref[...], ext_x, ext_y, half)
+    low = as_field(x_low[:slab, :], rim, ext_y, half)
+    high = as_field(x_high[:slab, :], rim, ext_y, half)
+    for s, (y_ref, c_ref) in enumerate(((y_low, c_low), (y_high, c_high))):
+        ours, here, there = ((0, 3, 0), (ext_y - 2, 0, 2))[s]
+        base = s * long
+        parts = (
+            (low, as_field(c_ref[:corner, :], rim, rim, half)),
+            (grid, as_field(y_ref[:face, :], ext_x, rim, half)),
+            (high, as_field(c_ref[corner : 2 * corner, :], rim, rim, half)),
+        )
+        at = base
+        for mine, theirs in parts:
+            count = mine.shape[0]
+            pad_ref[at : at + count, here : here + 2] = mine[:, ours : ours + 2]
+            pad_ref[at : at + count, there : there + rim] = theirs
+            at += count
+    fill_four(pad_ref, four_ref, channels)
+    coarse_s[1 : 1 + coarse_x, 1 : 1 + coarse_y] = as_field(
+        coarse_ref[...], coarse_x, coarse_y, half
+    )
+    coarse_s[:1, 1 : 1 + coarse_y] = as_field(x_low[slab:, :], 1, coarse_y, half)
+    coarse_s[1 + coarse_x :, 1 : 1 + coarse_y] = as_field(x_high[slab:, :], 1, coarse_y, half)
+    for y, y_ref, c_ref in ((0, y_low, c_low), (1 + coarse_y, y_high, c_high)):
+        coarse_s[1 : 1 + coarse_x, y : y + 1] = as_field(y_ref[face:, :], coarse_x, 1, half)
+        corners = as_field(c_ref[2 * corner :, :], 2, 1, half)
+        coarse_s[:1, y : y + 1] = corners[:1]
+        coarse_s[1 + coarse_x :, y : y + 1] = corners[1:]
+    wide_x, wide_y = coarse_x + 2, coarse_y + 2
+    coarse_rows = wide_x * wide_y * half
     coarse = down_ref.shape[2]
     given = coarse_s[...].reshape(coarse_rows, wide).astype(BF16)
     largest = None
     for j in range(4):
         spot = iota((wide, wide), 0) == coarse + 2 * j + iota((wide, wide), 1) // LANE
         mask = mm(given, one_hot(spot))
-        mask_s[:, j // 2, :, j % 2] = mask.reshape(coarse_x, coarse_y, half, wide)
+        mask_s[:, j // 2, :, j % 2] = mask.reshape(wide_x, wide_y, half, wide)
         largest = mask if largest is None else jnp.maximum(largest, mask)
     largest = jnp.maximum(largest[:, :LANE], largest[:, LANE:])
     coarse_mask = jnp.concatenate([largest, largest[:, : coarse - LANE]], axis=1)
-    count = 4
-    for first in range(0, ext_x, count):
-        pre = convolve(pad_ref, side_ref, conv_ref, first, count, False)
-        part = slice(first // 2, (first + count) // 2)
-        mask = mask_s[part].reshape(count * ext_y * half, wide)
-        sigma = logistic(pre)
-        shape = (count // 2, 2, coarse_y, 2, half, wide)
-        fine_s[part] = (pre * sigma * mask).astype(BF16).astype(F32).reshape(shape)
-        slope_s[part] = (sigma * (1.0 + pre * (1.0 - sigma)) * mask).reshape(shape)
-    field = (ext_x, ext_y, half, wide)
+
+    out_x, out_y = 2 * wide_x, 2 * wide_y
+    strip = 3
+    boxes = [(0, out_x, 0, strip), (long, out_x, 0, strip)]
+    silu, slope = silu_and_slope(convolve(four_ref, conv_ref, boxes))
+    shape = (2, out_x, strip, half, wide)
+    edge_silu, edge_slope = silu.astype(F32).reshape(shape), slope.reshape(shape)
+    columns = out_y - 2 * strip
+    mid_silu = as_field(silu_ref[...], out_x, columns, half)
+    mid_slope = slope_ref[...].reshape(out_x, columns, half, wide)
+    shape = (wide_x, 2, half, wide)
+    for y in range(out_y):
+        if y < strip:
+            silu, slope = edge_silu[0, :, y], edge_slope[0, :, y]
+        elif y >= out_y - strip:
+            at = y - (out_y - strip)
+            silu, slope = edge_silu[1, :, at], edge_slope[1, :, at]
+        else:
+            silu, slope = mid_silu[:, y - strip], mid_slope[:, y - strip]
+        mask = mask_s[:, :, y // 2, y % 2]
+        fine_s[:, :, y // 2, y % 2] = silu.reshape(shape) * mask
+        slope_s[:, :, y // 2, y % 2] = slope.reshape(shape) * mask
+    field = (out_x, out_y, half, wide)
     fine_ref[...] = inner(fine_s[...].reshape(field), 2).astype(BF16)
+
     pre = None
     for j in range(4):
         piece = fine_s[:, j // 2, :, j % 2].reshape(coarse_rows, wide).astype(BF16)
         part = mm(piece, down_ref[j])
         pre = part if pre is None else pre + part
     sigma = logistic(pre)
-    coarse_field = (coarse_x, coarse_y, half, coarse)
+    coarse_field = (wide_x, wide_y, half, coarse)
     features = pre * sigma * coarse_mask
     features_ref[...] = inner(features.reshape(coarse_field), 1).astype(BF16)
     slope = sigma * (1.0 + pre * (1.0 - sigma))
@@ -276,37 +322,41 @@
     delta_coarse_ref[...] = inner(delta.reshape(coarse_field), 1).astype(BF16)
     delta = delta.astype(BF16)
     for j in range(4):
-        back = mm(delta, down_ref[j], NT).reshape(coarse_x, coarse_y, half, wide)
+        back = mm(delta, down_ref[j], NT).reshape(wide_x, wide_y, half, wide)
         fine_s[:, j // 2, :, j % 2] = back * slope_s[:, j // 2, :, j % 2]
     delta_ref[...] = inner(fine_s[...].reshape(field), 1).astype(BF16)
 
 
 def weight_grad_kernel(
-    near_ref, fine_ref, delta_coarse_ref, delta_ref, out_ref,
-    pad_ref, side_ref, delta_s, fine_s, *, channels, scale,
+    grid_ref, x_low, x_high, y_low, y_high, c_low, c_high, fine_ref, delta_coarse_ref, delta_ref,
+    out_ref, pad_ref, four_ref, delta_s, fine_s, *, channels, fields, scale,
 ):
-    ext_x, ext_y, half, wide = (
-        pad_ref.shape[0] - 2, pad_ref.shape[1] - 2, pad_ref.shape[2], pad_ref.shape[3]
-    )
-    pad_ref[...] = as_field(near_ref[...], ext_x + 2, ext_y + 2, half)
-    fill_side(pad_ref, side_ref)
+    (ext_x, ext_y, half, rim), _ = fields
+    slab, face, corner = rim * ext_y * half, ext_x * rim * half, rim * rim * half
+    pad_ref[1 : 1 + ext_x, 1 : 1 + ext_y] = as_field(grid_ref[...], ext_x, ext_y, half)
+    near = (rim - 1, 0)
+    for x, x_ref, at in ((0, x_low, near[0]), (1 + ext_x, x_high, near[1])):
+        field = as_field(x_ref[:slab, :], rim, ext_y, half)
+        pad_ref[x : x + 1, 1 : 1 + ext_y] = field[at : at + 1]
+    for y, y_ref, c_ref, at in ((0, y_low, c_low, near[0]), (1 + ext_y, y_high, c_high, near[1])):
+        field = as_field(y_ref[:face, :], ext_x, rim, half)
+        pad_ref[1 : 1 + ext_x, y : y + 1] = field[:, at : at + 1]
+        field = as_field(c_ref[: 2 * corner, :], 2 * rim, rim, half)[:, at : at + 1]
+        pad_ref[:1, y : y + 1] = field[rim - 1 : rim]
+        pad_ref[1 + ext_x :, y : y + 1] = field[rim : rim + 1]
+    fill_four(pad_ref, four_ref, channels)
     delta_s[...] = as_field(delta_ref[...], ext_x + 2, ext_y + 2, half)
     turned = inner(delta_s[...], 1).T.astype(BF16)
-    lo, hi = slice(0, LANE), slice(LANE, WIDE)
-    for j in range(9):
-        main = mm(turned, window(pad_ref, j, 0, ext_x))
-        side = mm(turned, window(side_ref, j, 0, ext_x))
-        low = main[hi, lo] + side[lo, hi]
-        mid = main[lo, lo] + main[hi, hi]
-        high = main[lo, hi] + side[hi, lo]
-        for t, part in enumerate((low, mid, high)):
-            start = (3 * j + t) * channels
-            out_ref[start : start + channels, :] = (part.T[:channels] * scale).astype(BF16)
+    three = 3 * channels
+    for j, part in enumerate(windows(four_ref, 0, ext_x, 0, ext_y)):
+        grad = mm(turned, part)
+        grad = grad[:LANE, :three] + grad[LANE:, channels:]
+        out_ref[j * three : (j + 1) * three, :] = (grad.T * scale).astype(BF16)
     fine_s[...] = fine_ref[...].astype(F32).reshape(fine_s.shape)
     coarse_rows = ext_x // 2 * (ext_y // 2) * half
     base = 27 * channels
     for j in range(4):
-        piece = fine_s[:, j // 2, :, j % 2].reshape(coarse_rows, wide).astype(BF16)
+        piece = fine_s[:, j // 2, :, j % 2].reshape(coarse_rows, WIDE).astype(BF16)
         grad = mm(piece, delta_coarse_ref[...], TN) * scale
         first, second = grad[:channels], grad[LANE : LANE + channels]
         start = base + 2 * j * channels
@@ -319,14 +369,14 @@
     out_ref[end:, :] = jnp.zeros((out_ref.shape[0] - end, LANE), BF16)
 
 
-def input_grad_kernel(delta_ref, conv_ref, got_ref, back_ref, pad_ref, side_ref, grad_s, *, channels):
+def input_grad_kernel(delta_ref, conv_ref, got_ref, back_ref, pad_ref, four_ref, grad_s, *, channels):
     ext_x, ext_y, half = pad_ref.shape[0] - 2, pad_ref.shape[1] - 2, pad_ref.shape[2]
     pad_ref[...] = as_field(delta_ref[...], ext_x + 2, ext_y + 2, half)
-    fill_side(pad_ref, side_ref)
+    fill_four(pad_ref, four_ref, channels)
     count = 4
     for first in range(0, ext_x, count):
         rows = slice(first * ext_y * half, (first + count) * ext_y * half)
-        grad_s[rows, :] = convolve(pad_ref, side_ref, conv_ref, first, count, True).astype(BF16)
+        grad_s[rows, :] = convolve(four_ref, conv_ref, [(first, count, 0, ext_y)]).astype(BF16)
     grad = grad_s[...]
     pairs = grad.shape[0]
     rows = got_ref.shape[0]
@@ -422,8 +472,11 @@
     coarse_rows = coarse_x * coarse_y * half
     slot_rows = devices * block
     scale = 1.0 / math.sqrt(float(ext_x * ext_y * ext_z * devices))
-    conv_flops = 2 * pairs * 18 * WIDE * WIDE
+    four = 4 * channels
+    conv_flops = 2 * pairs * 9 * four * WIDE
     pick_flops = 2 * pairs * slot_rows * PACK * WIDE
+    rim = 3
+    fields = ((ext_x, ext_y, half, rim), (coarse_x, coarse_y, half, 1))
 
     send, slot = call(
         functools.partial(dispatch_kernel, devices=devices, cap=cap),
@@ -433,76 +486,88 @@
         flops=2 * points * slot_rows * PACK * LANE,
     )
     got = exchange(send.reshape(devices, block, PACK * LANE)).reshape(slot_rows, PACK * LANE)
-    conv_blocks, down_blocks, given = call(
+    conv_blocks, back_blocks, down_blocks, given = call(
         functools.partial(prepare_kernel, ext_y=ext_y),
         (
-            struct((9, 2, WIDE, WIDE), BF16),
+            struct((9 * four, WIDE), BF16),
+            struct((9 * four, WIDE), BF16),
             struct((4, WIDE, coarse), BF16),
             struct((coarse_rows, WIDE), BF16),
         ),
         (w_conv, w_down, cotangent.reshape(coarse_rows, coarse),
          occupancy.reshape(ext_x * ext_y, ext_z)),
         "prepare",
-    )
-    x_rows = 3 * ext_y * half + coarse_y * half
-    grid, x_first, x_last = call(
-        functools.partial(
-            pool_kernel, channels=channels, rim=3, slab=ext_y * half, coarse_slab=coarse_y * half
-        ),
-        (struct((pairs, WIDE), BF16), struct((x_rows, WIDE), BF16), struct((x_rows, WIDE), BF16)),
+        flops=1000000000,
+    )
+    x_rows = sum(e[3] * e[1] * e[2] for e in fields)
+    y_rows = sum(e[3] * e[0] * e[2] for e in fields)
+    c_rows = sum(2 * e[3] * e[3] * e[2] for e in fields)
+    grid, x_first, x_last, y_first, y_last = call(
+        functools.partial(pool_kernel, channels=channels, fields=fields),
+        tuple(struct((n, WIDE), BF16) for n in (pairs, x_rows, x_rows, y_rows, y_rows)),
         (got, given),
         "pool",
         scratch=[pltpu.VMEM((pairs, WIDE), F32)],
         flops=pick_flops,
     )
     x_low, x_high = shift(x_last, "gx", 1), shift(x_first, "gx", -1)
-    y_rows = 3 * (ext_x + 6) * half + (coarse_x + 2) * half
-    y_first, y_last = call(
-        functools.partial(
-            edge_kernel, fields=((ext_x, ext_y, half, 3), (coarse_x, coarse_y, half, 1))
-        ),
-        (struct((y_rows, WIDE), BF16), struct((y_rows, WIDE), BF16)),
-        (grid, given, x_low, x_high),
-        "edge",
-    )
     y_low, y_high = shift(y_last, "gy", 1), shift(y_first, "gy", -1)
-    near = (ext_x + 2, ext_y + 2, half, WIDE)
+    c_first, c_last = call(
+        functools.partial(corner_kernel, fields=fields),
+        tuple(struct((n, WIDE), BF16) for n in (c_rows, c_rows)),
+        (x_low, x_high),
+        "corner",
+    )
+    c_low, c_high = shift(c_last, "gy", 1), shift(c_first, "gy", -1)
+    long = ext_x + 2 * rim
+    mid_rows = (ext_x + 4) * (ext_y - 2) * half
+    silu, slope = call(
+        functools.partial(column_kernel, channels=channels),
+        (struct((mid_rows, WIDE), BF16), struct((mid_rows, WIDE), F32)),
+        (grid, x_low, x_high, conv_blocks),
+        "column",
+        scratch=[
+            pltpu.VMEM((long, ext_y, half, WIDE), F32),
+            pltpu.VMEM((long, ext_y, half, four), F32),
+        ],
+        flops=2 * conv_flops,
+    )
+    near = (ext_x + 2, ext_y + 2, half)
     near_rows = near[0] * near[1] * half
-    far = (ext_x + 6, ext_y + 6, half, WIDE)
     split = (coarse_x + 2, 2, coarse_y + 2, 2, half, WIDE)
-    features, fine, delta_coarse, delta, grid_near = call(
-        level_kernel,
+    faces = (x_low, x_high, y_low, y_high, c_low, c_high)
+    features, fine, delta_coarse, delta = call(
+        functools.partial(level_kernel, channels=channels, fields=fields),
         (
             struct((coarse_rows, coarse), BF16),
             struct((pairs, WIDE), BF16),
             struct((coarse_rows, coarse), BF16),
             struct((near_rows, WIDE), BF16),
-            struct((near_rows, WIDE), BF16),
         ),
-        (grid, given, x_low, x_high, y_low, y_high, conv_blocks, down_blocks),
+        (grid, given, *faces, silu, slope, conv_blocks, down_blocks),
         "level",
         scratch=[
-            pltpu.VMEM(far, F32),
-            pltpu.VMEM(far, F32),
+            pltpu.VMEM((2 * long, 5, half, WIDE), F32),
+            pltpu.VMEM((2 * long, 5, half, four), F32),
             pltpu.VMEM((coarse_x + 2, coarse_y + 2, half, WIDE), F32),
             pltpu.VMEM(split, F32),
             pltpu.VMEM(split, F32),
             pltpu.VMEM(split, F32),
         ],
-        flops=2 * conv_flops,
+        flops=conv_flops,
         megabytes=8,
     )
     used = 39 * channels
     chunk = -(-used // (32 * devices)) * 32
     packed = call(
-        functools.partial(weight_grad_kernel, channels=channels, scale=scale),
+        functools.partial(weight_grad_kernel, channels=channels, fields=fields, scale=scale),
         struct((devices * chunk, LANE), BF16),
-        (grid_near, fine, delta_coarse, delta),
+        (grid, *faces, fine, delta_coarse, delta),
         "weight_grad",
         scratch=[
-            pltpu.VMEM(near, F32),
-            pltpu.VMEM(near, F32),
-            pltpu.VMEM(near, F32),
+            pltpu.VMEM((*near, WIDE), F32),
+            pltpu.VMEM((*near, four), F32),
+            pltpu.VMEM((*near, WIDE), F32),
             pltpu.VMEM((coarse_x, 2, coarse_y, 2, half, WIDE), F32),
         ],
         flops=conv_flops,
@@ -512,9 +577,13 @@
     back = call(
         functools.partial(input_grad_kernel, channels=channels),
         struct((slot_rows, PACK * channels), BF16),
-        (delta, conv_blocks, got),
+        (delta, back_blocks, got),
         "input_grad",
-        scratch=[pltpu.VMEM(near, F32), pltpu.VMEM(near, F32), pltpu.VMEM((pairs, WIDE), BF16)],
+        scratch=[
+            pltpu.VMEM((*near, WIDE), F32),
+            pltpu.VMEM((*near, four), F32),
+            pltpu.VMEM((pairs, WIDE), BF16),
+        ],
         flops=conv_flops + pick_flops,
         megabytes=8,
     )

time: 133 us -> 131 us (0.985)
  waiting for transfers between devices: 37.3 us -> 29.4 us
  starting transfers between devices: 31.9 us -> 37.9 us
    ppermute x4 -> x6, waiting for transfers between devices: 10.3 us -> 2.81 us  [shift(): return lax.ppermute(block, axis, pairs)]
    ppermute x4 -> x6, starting transfers between devices: 9.58 us -> 13.4 us  [shift(): return lax.ppermute(block, axis, pairs)]
    all_to_all x2, starting transfers between devices: 20.8 us -> 22.9 us  [exchange(): return lax.all_to_all(blocks, AXES, split_axis=0, concat_axis=0, tiled=True)]
    unnamed x22 -> x26, local copies, waits for them, and re-layouts: 6.6 us -> 7.42 us
    pallas_call x10 -> x11, Pallas kernels: 29.6 us -> 28.8 us  [call(): pl.pallas_call(kernel, out_shape=outs, in_specs=[pl.BlockSpec(memory_spac...]
  transfers between devices with their start and end apart: 7 -> 9, of which waited for: 6 -> 4; matrix products, arithmetic and copies ran while one was open for 0% -> 0% of each run, Pallas kernels for 7% -> 9%
where the time goes in v2:
time: 131 us; the launch traced here: 130 us
  starting transfers between devices  37.9 us (29%)
  waiting for transfers between devices  29.4 us (22%)
  Pallas kernels  28.8 us (22%)
  blocking collectives  25.8 us (20%)
  local copies, waits for them, and re-layouts  7.46 us (6%)
    pallas_call x11, Pallas kernels, call(): pl.pallas_call(kernel, out_shape=outs, in_specs=[pl.BlockSpec(memory_spac...  28.8 us
    all_to_all x2, waiting for transfers between devices, exchange(): return lax.all_to_all(blocks, AXES, split_axis=0, concat_axis=0, tiled=True)  26.6 us
    all_to_all x1, blocking collectives, exchange(): return lax.all_to_all(blocks, AXES, split_axis=0, concat_axis=0, tiled=True)  25.8 us
    all_to_all x2, starting transfers between devices, exchange(): return lax.all_to_all(blocks, AXES, split_axis=0, concat_axis=0, tiled=True)  22.9 us
    ppermute x6, starting transfers between devices, shift(): return lax.ppermute(block, axis, pairs)  13.4 us
    unnamed x26, local copies, waits for them, and re-layouts  7.42 us
    ppermute x6, waiting for transfers between devices, shift(): return lax.ppermute(block, axis, pairs)  2.81 us
  transfers between devices with their start and end apart: 9, of which 4 were waited for; matrix products, arithmetic and copies ran while one was open for 0% of the time, Pallas kernels for 9%

profile of v2, /device:TPU:1, one launch (start us, length us, event | category | flops | bytes accessed | tf_op | source)
XLA Modules:
  0.0 130.2 jit_solution(8411605411232651074)
XLA Ops:
  0.6 0.0 copy-start.1
  0.6 1.0 copy-done.1
  1.6 0.0 copy-start.5
  1.6 0.7 copy-done.5
  2.3 0.0 copy-start.6
  2.3 0.7 copy-done.6
  3.0 3.7 %dispatch.1 = (bf16[1024,512]{1,0:T(8,128)(2,1)}, s32[2,2048]{1,0:T(2,128)S(1)}) custom-call(bf16[96,2048]{1,0:T(8,128)(2,1)S(1)} %bitcast.18, s32[1,2048]{1,0:T(1,128)S(1)} %bitcast.21, s32[1,2048]{1,0:T(1,128)S(1)} %bitcast.22), custom_call_target="tpu_custom_call" | custom-call | flops 2147483648 | bytes 4000000 | tf_op jit(solution)/shard_map/dispatch/pallas_call | solution.py:35
  6.7 0.0 copy-start
  6.7 0.0 copy-start.2
  6.7 0.0 copy-start.3
  6.7 0.0 copy-start.4
  6.7 11.5 %all-to-all-start = ((bf16[128,8,512]{2,1,0:T(8,128)(2,1)}), bf16[128,8,512]{2,1,0:T(8,128)(2,1)S(1)}, u32[]{:S(2)}, u32[]{:S(2)}) async-start(bf16[128,8,512]{2,1,0:T(8,128)(2,1)} %bitcast.3), calls=%async_computation | async-start | bytes 2097152 | tf_op jit(solution)/shard_map/all_to_all | solution.py:458
  18.2 0.0 copy-done
  18.2 0.0 copy-done.2
  18.2 0.0 copy-done.3
  18.3 0.0 copy-done.4
  18.3 1.0 prepare.1
  19.3 0.0 copy-start.7
  19.3 1.2 copy-done.7
  20.5 0.0 copy-start.11
  20.5 1.2 copy-done.11
  21.7 15.1 %all-to-all-done = bf16[128,8,512]{2,1,0:T(8,128)(2,1)S(1)} async-done(((bf16[128,8,512]{2,1,0:T(8,128)(2,1)}), bf16[128,8,512]{2,1,0:T(8,128)(2,1)S(1)}, u32[]{:S(2)}, u32[]{:S(2)}) %all-to-all-start) | async-done | bytes 1048608 | tf_op jit(solution)/shard_map/all_to_all | solution.py:458
  36.9 0.0 copy-start.8
  36.9 2.9 %pool.1 = (bf16[1024,256]{1,0:T(8,128)(2,1)S(1)}, bf16[448,256]{1,0:T(8,128)(2,1)S(1)}, bf16[448,256]{1,0:T(8,128)(2,1)S(1)}, bf16[224,256]{1,0:T(8,128)(2,1)S(1)}, bf16[224,256]{1,0:T(8,128)(2,1)S(1)}) custom-call(bf16[1024,512]{1,0:T(8,128)(2,1)S(1)} %bitcast.16, bf16[256,256]{1,0:T(8,128)(2,1)S(1)} %get-tuple-element.26.coarse_ref), custom_call_target="tpu_custom_call" | custom-call | flops 2147483648 | bytes 4000000 | tf_op jit(solution)/shard_map/pool/pallas_call | solution.py:35
  39.8 3.6 %collective-permute-start = (bf16[448,256]{1,0:T(8,128)(2,1)S(1)}, bf16[448,256]{1,0:T(8,128)(2,1)S(1)}, u32[]{:S(2)}, u32[]{:S(2)}) collective-permute-start(bf16[448,256]{1,0:T(8,128)(2,1)S(1)} %get-tuple-element.28), channel_id=1, source_target_pairs={{0,16},{16,32},{32,48},{48,64},{64,80},{80,96},{96,112},{1,17},{17... | collective-permute-start | bytes 688136 | tf_op jit(solution)/shard_map/ppermute | solution.py:454
  43.4 1.9 %collective-permute-start.1 = (bf16[448,256]{1,0:T(8,128)(2,1)S(1)}, bf16[448,256]{1,0:T(8,128)(2,1)S(1)}, u32[]{:S(2)}, u32[]{:S(2)}) collective-permute-start(bf16[448,256]{1,0:T(8,128)(2,1)S(1)} %get-tuple-element.29), channel_id=1, source_target_pairs={{16,0},{32,16},{48,32},{64,48},{80,64},{96,80},{112,96},{17,1},{33... | collective-permute-start | bytes 688136 | tf_op jit(solution)/shard_map/ppermute | solution.py:454
  45.4 2.6 %collective-permute-start.2 = (bf16[224,256]{1,0:T(8,128)(2,1)S(1)}, bf16[224,256]{1,0:T(8,128)(2,1)S(1)}, u32[]{:S(2)}, u32[]{:S(2)}) collective-permute-start(bf16[224,256]{1,0:T(8,128)(2,1)S(1)} %get-tuple-element.30), channel_id=1, source_target_pairs={{0,1},{1,2},{2,3},{3,4},{4,5},{5,6},{6,7},{7,8},{8,9},{9,10},{10,1... | collective-permute-start | bytes 344072 | tf_op jit(solution)/shard_map/ppermute | solution.py:454
  47.9 1.3 collective-permute-start.3
  49.2 0.0 collective-permute-done.low_ref.x_low
  49.2 1.5 %collective-permute-done.1.high_ref.x_high = bf16[448,256]{1,0:T(8,128)(2,1)S(1)} collective-permute-done((bf16[448,256]{1,0:T(8,128)(2,1)S(1)}, bf16[448,256]{1,0:T(8,128)(2,1)S(1)}, u32[]{:S(2)}, u32[]{:S(2)}) %collective-permute-start.1) | collective-permute-done | bytes 229408 | tf_op jit(solution)/shard_map/ppermute | solution.py:454
  50.8 2.5 %collective-permute-start.4 = (bf16[160,256]{1,0:T(8,128)(2,1)S(1)}, bf16[160,256]{1,0:T(8,128)(2,1)S(1)}, u32[]{:S(2)}, u32[]{:S(2)}) collective-permute-start(bf16[160,256]{1,0:T(8,128)(2,1)S(1)} %get-tuple-element.32), channel_id=1, source_target_pairs={{0,1},{1,2},{2,3},{3,4},{4,5},{5,6},{6,7},{7,8},{8,9},{9,10},{10,1... | collective-permute-start | bytes 245768 | tf_op jit(solution)/shard_map/ppermute | solution.py:454
  53.3 1.5 %collective-permute-start.5 = (bf16[160,256]{1,0:T(8,128)(2,1)S(1)}, bf16[160,256]{1,0:T(8,128)(2,1)S(1)}, u32[]{:S(2)}, u32[]{:S(2)}) collective-permute-start(bf16[160,256]{1,0:T(8,128)(2,1)S(1)} %get-tuple-element.33), channel_id=1, source_target_pairs={{1,0},{2,1},{3,2},{4,3},{5,4},{6,5},{7,6},{8,7},{9,8},{10,9},{11,1... | collective-permute-start | bytes 245768 | tf_op jit(solution)/shard_map/ppermute | solution.py:454
  54.8 0.0 copy-done.8
  54.8 3.1 %column.1 = (bf16[1344,256]{1,0:T(8,128)(2,1)S(1)}, f32[1344,256]{1,0:T(8,128)S(1)}) custom-call(bf16[1024,256]{1,0:T(8,128)(2,1)S(1)} %get-tuple-element.27.grid_ref, bf16[448,256]{1,0:T(8,128)(2,1)S(1)} %collective-permute-done.low_ref.x_low, bf16[448,256]{1,0:T(8,128)(2,1)S(1)} %collective-permute-done.1.high_ref.x_high, bf16[3456,256]{1,0:T(8,128)(2,1)S(1)} %copy-done.8), custom_call_target="tpu_custom_call" | custom-call | flops 3623878656 | bytes 4000000 | tf_op jit(solution)/shard_map/column/pallas_call | solution.py:35
  57.9 0.0 collective-permute-done.2.y_low
  57.9 0.0 collective-permute-done.3.y_high
  57.9 0.0 collective-permute-done.4.c_low
  57.9 1.3 collective-permute-done.5.c_high
  59.2 4.9 %level.1 = (bf16[256,192]{1,0:T(8,128)(2,1)}, bf16[1024,256]{1,0:T(8,128)(2,1)S(1)}, bf16[256,192]{1,0:T(8,128)(2,1)S(1)}, bf16[1440,256]{1,0:T(8,128)(2,1)S(1)}) custom-call(bf16[1024,256]{1,0:T(8,128)(2,1)S(1)} %get-tuple-element.27.grid_ref, bf16[256,256]{1,0:T(8,128)(2,1)S(1)} %get-tuple-element.26.coarse_ref, ...), custom_call_target="tpu_custom_call" | custom-call | flops 1811939328 | bytes 8000000 | tf_op jit(solution)/shard_map/level/pallas_call | solution.py:35
  64.1 0.0 copy-start.9
  64.1 4.1 %weight_grad.1 = bf16[4096,128]{1,0:T(8,128)(2,1)} custom-call(bf16[1024,256]{1,0:T(8,128)(2,1)S(1)} %get-tuple-element.27.grid_ref, bf16[448,256]{1,0:T(8,128)(2,1)S(1)} %collective-permute-done.low_ref.x_low, bf16[448,256]{1,0:T(8,128)(2,1)S(1)} %collective-permute-done.1.high_ref.x_high, bf16[224,256]{1,0:T(8,128)(2,1)S(1)} %collective-permute-done.2.y_low, ...), custom_call_target="tpu_custom_call" | custom-call | flops 1811939328 | bytes 8000000 | tf_op jit(solution)/shard_map/weight_grad/pallas_call | solution.py:35
  68.2 0.0 copy-done.9
  68.2 11.4 %all-to-all-start.1 = ((bf16[128,32,128]{2,1,0:T(8,128)(2,1)}), bf16[128,32,128]{2,1,0:T(8,128)(2,1)S(1)}, u32[]{:S(2)}, u32[]{:S(2)}) async-start(bf16[128,32,128]{2,1,0:T(8,128)(2,1)} %bitcast.8), calls=%async_computation.1 | async-start | bytes 2097152 | tf_op jit(solution)/shard_map/all_to_all | solution.py:458
  79.6 0.0 copy-start.10
  79.6 1.1 copy-done.10
  80.8 0.0 copy-start.12
  80.8 1.5 %copy-done.12 = bf16[3456,256]{1,0:T(8,128)(2,1)S(1)} copy-done((bf16[3456,256]{1,0:T(8,128)(2,1)S(1)}, bf16[3456,256]{1,0:T(8,128)(2,1)}, u32[]{:S(2)}) %copy-start.12) | copy-done | bytes 1769496
  82.2 4.5 %input_grad.1.back_ref = bf16[1024,384]{1,0:T(8,128)(2,1)S(1)} custom-call(bf16[1440,256]{1,0:T(8,128)(2,1)S(1)} %copy-done.10, bf16[3456,256]{1,0:T(8,128)(2,1)S(1)} %copy-done.12, bf16[1024,512]{1,0:T(8,128)(2,1)S(1)} %bitcast.17), custom_call_target="tpu_custom_call" | custom-call | flops 3959422976 | bytes 8000000 | tf_op jit(solution)/shard_map/input_grad/pallas_call | solution.py:35
  86.7 11.5 %all-to-all-done.1.terms_ref = bf16[128,32,128]{2,1,0:T(8,128)(2,1)S(1)} async-done(((bf16[128,32,128]{2,1,0:T(8,128)(2,1)}), bf16[128,32,128]{2,1,0:T(8,128)(2,1)S(1)}, u32[]{:S(2)}, u32[]{:S(2)}) %all-to-all-start.1) | async-done | bytes 1048608 | tf_op jit(solution)/shard_map/all_to_all | solution.py:458
  98.3 0.3 join.1
  98.5 25.8 %all_to_all.15 = bf16[128,8,640]{2,1,0:T(8,128)(2,1)S(1)} all-to-all(bf16[128,8,640]{2,1,0:T(8,128)(2,1)S(1)} %bitcast.15), channel_id=1, replica_groups=mesh['gx'=8,'gy'=16] {'gx','gy'}, dimensions={0} | all-to-all | bytes 2621440 | tf_op jit(solution)/shard_map/all_to_all | solution.py:458
  124.3 1.6 %collective-permute-start.6 = (bf16[1024,256]{1,0:T(8,128)(2,1)S(1)}, bf16[1024,256]{1,0:T(8,128)(2,1)S(1)}, u32[]{:S(2)}, u32[]{:S(2)}) collective-permute-start(bf16[1024,256]{1,0:T(8,128)(2,1)S(1)} %slice.4), channel_id=1, source_target_pairs={{0,16},{16,0},{32,48},{48,32},{64,80},{80,64},{96,112},{112,96},{1... | collective-permute-start | bytes 1572872 | tf_op jit(solution)/shard_map/ppermute | solution.py:602
  125.9 2.7 %collect.1 = bf16[96,2048]{1,0:T(8,128)(2,1)} custom-call(bf16[1024,640]{1,0:T(8,128)(2,1)S(1)} %bitcast.13, s32[2,2048]{1,0:T(2,128)S(1)} %get-tuple-element.43.slot_ref), custom_call_target="tpu_custom_call" | custom-call | flops 2147483648 | bytes 4000000 | tf_op jit(solution)/shard_map/collect/pallas_call | solution.py:35
  128.6 0.0 collective-permute-done.6.theirs_ref
  128.6 1.6 %unpack.1 = (f32[27,96,96]{2,1,0:T(8,128)}, f32[8,96,192]{2,1,0:T(8,128)}) custom-call(s32[1,128]{1,0:T(1,128)S(1)} %broadcast_in_dim.3.core_ref, bf16[1024,640]{1,0:T(8,128)(2,1)S(1)} %bitcast.14, bf16[1024,256]{1,0:T(8,128)(2,1)S(1)} %collective-permute-done.6.theirs_ref), custom_call_target="tpu_custom_call" | custom-call | bytes 4000000 | tf_op jit(solution)/shard_map/unpack/pallas_call | solution.py:35
  (3 shorter events, 0.0 us)
Async XLA Ops:
  0.6 1.0 copy-start.1
  1.6 0.7 copy-start.5
  2.3 0.7 copy-start.6
  6.7 11.5 %copy-start = (bf16[27,96,96]{2,1,0:T(8,128)(2,1)S(1)}, bf16[27,96,96]{2,1,0:T(8,128)(2,1)}, u32[]{:S(2)}) copy-start(bf16[27,96,96]{2,1,0:T(8,128)(2,1)} %conv_ref.1) | copy-start | bytes 1492996
  6.7 11.5 %copy-start.2 = (bf16[8,96,192]{2,1,0:T(8,128)(2,1)S(1)}, bf16[8,96,192]{2,1,0:T(8,128)(2,1)}, u32[]{:S(2)}) copy-start(bf16[8,96,192]{2,1,0:T(8,128)(2,1)} %down_ref.1) | copy-start | bytes 884740
  6.7 11.5 %copy-start.3 = (bf16[4,8,8,192]{3,2,1,0:T(8,128)(2,1)S(1)}, bf16[4,8,8,192]{3,2,1,0:T(8,128)(2,1)}, u32[]{:S(2)}) copy-start(bf16[4,8,8,192]{3,2,1,0:T(8,128)(2,1)} %param.13) | copy-start | bytes 294916
  6.7 11.5 %copy-start.4 = (s32[8,16,16]{2,1,0:T(8,128)S(1)}, s32[8,16,16]{2,1,0:T(8,128)}, u32[]{:S(2)}) copy-start(s32[8,16,16]{2,1,0:T(8,128)} %param.10) | copy-start | bytes 24580
  6.7 30.1 %all-to-all-start = ((bf16[128,8,512]{2,1,0:T(8,128)(2,1)}), bf16[128,8,512]{2,1,0:T(8,128)(2,1)S(1)}, u32[]{:S(2)}, u32[]{:S(2)}) async-start(bf16[128,8,512]{2,1,0:T(8,128)(2,1)} %bitcast.3), calls=%async_computation | async-start | bytes 2097152 | tf_op jit(solution)/shard_map/all_to_all | solution.py:458
  19.3 1.2 copy-start.7
  20.5 1.2 copy-start.11
  36.9 18.0 %copy-start.8 = (bf16[3456,256]{1,0:T(8,128)(2,1)S(1)}, bf16[3456,256]{1,0:T(8,128)(2,1)}, u32[]{:S(2)}) copy-start(bf16[3456,256]{1,0:T(8,128)(2,1)} %copy-done.7) | copy-start | bytes 5308420
  39.8 9.4 %collective-permute-start = (bf16[448,256]{1,0:T(8,128)(2,1)S(1)}, bf16[448,256]{1,0:T(8,128)(2,1)S(1)}, u32[]{:S(2)}, u32[]{:S(2)}) collective-permute-start(bf16[448,256]{1,0:T(8,128)(2,1)S(1)} %get-tuple-element.28), channel_id=1, source_target_pairs={{0,16},{16,32},{32,48},{48,64},{64,80},{80,96},{96,112},{1,17},{17... | collective-permute-start | bytes 688136 | tf_op jit(solution)/shard_map/ppermute | solution.py:454
  43.4 7.3 %collective-permute-start.1 = (bf16[448,256]{1,0:T(8,128)(2,1)S(1)}, bf16[448,256]{1,0:T(8,128)(2,1)S(1)}, u32[]{:S(2)}, u32[]{:S(2)}) collective-permute-start(bf16[448,256]{1,0:T(8,128)(2,1)S(1)} %get-tuple-element.29), channel_id=1, source_target_pairs={{16,0},{32,16},{48,32},{64,48},{80,64},{96,80},{112,96},{17,1},{33... | collective-permute-start | bytes 688136 | tf_op jit(solution)/shard_map/ppermute | solution.py:454
  45.4 12.5 %collective-permute-start.2 = (bf16[224,256]{1,0:T(8,128)(2,1)S(1)}, bf16[224,256]{1,0:T(8,128)(2,1)S(1)}, u32[]{:S(2)}, u32[]{:S(2)}) collective-permute-start(bf16[224,256]{1,0:T(8,128)(2,1)S(1)} %get-tuple-element.30), channel_id=1, source_target_pairs={{0,1},{1,2},{2,3},{3,4},{4,5},{5,6},{6,7},{7,8},{8,9},{9,10},{10,1... | collective-permute-start | bytes 344072 | tf_op jit(solution)/shard_map/ppermute | solution.py:454
  47.9 10.0 %collective-permute-start.3 = (bf16[224,256]{1,0:T(8,128)(2,1)S(1)}, bf16[224,256]{1,0:T(8,128)(2,1)S(1)}, u32[]{:S(2)}, u32[]{:S(2)}) collective-permute-start(bf16[224,256]{1,0:T(8,128)(2,1)S(1)} %get-tuple-element.31), channel_id=1, source_target_pairs={{1,0},{2,1},{3,2},{4,3},{5,4},{6,5},{7,6},{8,7},{9,8},{10,9},{11,1... | collective-permute-start | bytes 344072 | tf_op jit(solution)/shard_map/ppermute | solution.py:454
  50.8 7.1 %collective-permute-start.4 = (bf16[160,256]{1,0:T(8,128)(2,1)S(1)}, bf16[160,256]{1,0:T(8,128)(2,1)S(1)}, u32[]{:S(2)}, u32[]{:S(2)}) collective-permute-start(bf16[160,256]{1,0:T(8,128)(2,1)S(1)} %get-tuple-element.32), channel_id=1, source_target_pairs={{0,1},{1,2},{2,3},{3,4},{4,5},{5,6},{6,7},{7,8},{8,9},{9,10},{10,1... | collective-permute-start | bytes 245768 | tf_op jit(solution)/shard_map/ppermute | solution.py:454
  53.3 5.8 %collective-permute-start.5 = (bf16[160,256]{1,0:T(8,128)(2,1)S(1)}, bf16[160,256]{1,0:T(8,128)(2,1)S(1)}, u32[]{:S(2)}, u32[]{:S(2)}) collective-permute-start(bf16[160,256]{1,0:T(8,128)(2,1)S(1)} %get-tuple-element.33), channel_id=1, source_target_pairs={{1,0},{2,1},{3,2},{4,3},{5,4},{6,5},{7,6},{8,7},{9,8},{10,9},{11,1... | collective-permute-start | bytes 245768 | tf_op jit(solution)/shard_map/ppermute | solution.py:454
  64.1 4.1 %copy-start.9 = (bf16[1440,256]{1,0:T(8,128)(2,1)}, bf16[1440,256]{1,0:T(8,128)(2,1)S(1)}, u32[]{:S(2)}) copy-start(bf16[1440,256]{1,0:T(8,128)(2,1)S(1)} %get-tuple-element.41.delta_ref) | copy-start | bytes 2211844
  68.2 30.0 %all-to-all-start.1 = ((bf16[128,32,128]{2,1,0:T(8,128)(2,1)}), bf16[128,32,128]{2,1,0:T(8,128)(2,1)S(1)}, u32[]{:S(2)}, u32[]{:S(2)}) async-start(bf16[128,32,128]{2,1,0:T(8,128)(2,1)} %bitcast.8), calls=%async_computation.1 | async-start | bytes 2097152 | tf_op jit(solution)/shard_map/all_to_all | solution.py:458
  79.6 1.1 copy-start.10
  80.8 1.5 %copy-start.12 = (bf16[3456,256]{1,0:T(8,128)(2,1)S(1)}, bf16[3456,256]{1,0:T(8,128)(2,1)}, u32[]{:S(2)}) copy-start(bf16[3456,256]{1,0:T(8,128)(2,1)} %copy-done.11) | copy-start | bytes 5308420
  124.3 4.3 %collective-permute-start.6 = (bf16[1024,256]{1,0:T(8,128)(2,1)S(1)}, bf16[1024,256]{1,0:T(8,128)(2,1)S(1)}, u32[]{:S(2)}, u32[]{:S(2)}) collective-permute-start(bf16[1024,256]{1,0:T(8,128)(2,1)S(1)} %slice.4), channel_id=1, source_target_pairs={{0,16},{16,0},{32,48},{48,32},{64,80},{80,64},{96,112},{112,96},{1... | collective-permute-start | bytes 1572872 | tf_op jit(solution)/shard_map/ppermute | solution.py:602

commit v3 on v2

--- a/solution.py
+++ b/solution.py
@@ -35,7 +35,9 @@
     return pl.pallas_call(
         kernel,
         out_shape=outs,
-        in_specs=[pl.BlockSpec(memory_space=pltpu.VMEM)] * len(args),
+        in_specs=[
+            pl.BlockSpec(memory_space=pltpu.SMEM if arg.ndim == 1 else pltpu.VMEM) for arg in args
+        ],
         out_specs=jax.tree.map(lambda _: pl.BlockSpec(memory_space=pltpu.VMEM), outs),
         scratch_shapes=list(scratch),
         compiler_params=pltpu.CompilerParams(vmem_limit_bytes=48 * 1024 * 1024),
@@ -83,7 +85,8 @@
 
 
 def pool_kernel(
-    got_ref, coarse_ref, grid_ref, x_first, x_last, y_first, y_last, total_ref, *, channels, fields
+    place_ref, got_ref, coarse_ref, grid_ref, x_first, x_last, y_first, y_last,
+    c_first_first, c_first_last, c_last_first, c_last_last, total_ref, *, channels, fields, counts,
 ):
     rows = got_ref.shape[0]
     pairs = grid_ref.shape[0]
@@ -102,13 +105,23 @@
             if q:
                 part = total_ref[start : start + step, :] + part
             total_ref[start : start + step, :] = part
-    x_at, y_at = 0, 0
+    x_inner = [jnp.where(place_ref[0] == end, 0.0, 1.0) for end in (0, counts[0] - 1)]
+    y_inner = [jnp.where(place_ref[1] == end, 0.0, 1.0) for end in (0, counts[1] - 1)]
+    corners = ((c_first_first, c_first_last), (c_last_first, c_last_last))
+    x_at, y_at, c_at = 0, 0, 0
     for ref, (ext_x, ext_y, half, rim) in zip((total_ref, coarse_ref), fields):
         field = as_field(ref[...], ext_x, ext_y, half)
-        x_at = put_rows(x_first, x_at, field[:rim])
-        put_rows(x_last, x_at - rim * ext_y * half, field[ext_x - rim :])
-        y_at = put_rows(y_first, y_at, field[:, :rim])
-        put_rows(y_last, y_at - rim * ext_x * half, field[:, ext_y - rim :])
+        x_cuts = [slice(0, rim), slice(ext_x - rim, ext_x)]
+        y_cuts = [slice(0, rim), slice(ext_y - rim, ext_y)]
+        for i, x_ref in enumerate((x_first, x_last)):
+            put_rows(x_ref, x_at, field[x_cuts[i]] * x_inner[i])
+            put_rows((y_first, y_last)[i], y_at, field[:, y_cuts[i]] * y_inner[i])
+            for k in range(2):
+                part = field[x_cuts[i], y_cuts[k]] * (x_inner[i] * y_inner[k])
+                put_rows(corners[i][k], c_at, part)
+        x_at += rim * ext_y * half
+        y_at += rim * ext_x * half
+        c_at += rim * rim * half
     grid_ref[...] = total_ref[...].astype(BF16)
 
 
@@ -119,18 +132,6 @@
 def put_rows(ref, at, field):
     size = field.shape[0] * field.shape[1] * field.shape[2]
     ref[at : at + size, :] = field.reshape(size, field.shape[3]).astype(BF16)
-    return at + size
-
-
-def corner_kernel(low_ref, high_ref, first_ref, last_ref, *, fields):
-    start, at = 0, 0
-    for _, ext_y, half, rim in fields:
-        size = rim * ext_y * half
-        for ref in (low_ref, high_ref):
-            field = as_field(ref[start : start + size, :], rim, ext_y, half)
-            put_rows(first_ref, at, field[:, :rim])
-            at = put_rows(last_ref, at, field[:, ext_y - rim :])
-        start += size
 
 
 def prepare_kernel(
@@ -233,7 +234,7 @@
 
 
 def level_kernel(
-    grid_ref, coarse_ref, x_low, x_high, y_low, y_high, c_low, c_high, silu_ref, slope_ref,
+    grid_ref, coarse_ref, x_low, x_high, y_low, y_high, c_ll, c_lh, c_hl, c_hh, silu_ref, slope_ref,
     conv_ref, down_ref,
     features_ref, fine_ref, delta_coarse_ref, delta_ref,
     pad_ref, four_ref, coarse_s, mask_s, fine_s, slope_s, *, channels, fields,
@@ -245,13 +246,13 @@
     grid = as_field(grid_ref[...], ext_x, ext_y, half)
     low = as_field(x_low[:slab, :], rim, ext_y, half)
     high = as_field(x_high[:slab, :], rim, ext_y, half)
-    for s, (y_ref, c_ref) in enumerate(((y_low, c_low), (y_high, c_high))):
+    for s, (y_ref, c_low, c_high) in enumerate(((y_low, c_ll, c_hl), (y_high, c_lh, c_hh))):
         ours, here, there = ((0, 3, 0), (ext_y - 2, 0, 2))[s]
         base = s * long
         parts = (
-            (low, as_field(c_ref[:corner, :], rim, rim, half)),
+            (low, as_field(c_low[:corner, :], rim, rim, half)),
             (grid, as_field(y_ref[:face, :], ext_x, rim, half)),
-            (high, as_field(c_ref[corner : 2 * corner, :], rim, rim, half)),
+            (high, as_field(c_high[:corner, :], rim, rim, half)),
         )
         at = base
         for mine, theirs in parts:
@@ -265,11 +266,10 @@
     )
     coarse_s[:1, 1 : 1 + coarse_y] = as_field(x_low[slab:, :], 1, coarse_y, half)
     coarse_s[1 + coarse_x :, 1 : 1 + coarse_y] = as_field(x_high[slab:, :], 1, coarse_y, half)
-    for y, y_ref, c_ref in ((0, y_low, c_low), (1 + coarse_y, y_high, c_high)):
+    for y, y_ref, c_low, c_high in ((0, y_low, c_ll, c_hl), (1 + coarse_y, y_high, c_lh, c_hh)):
         coarse_s[1 : 1 + coarse_x, y : y + 1] = as_field(y_ref[face:, :], coarse_x, 1, half)
-        corners = as_field(c_ref[2 * corner :, :], 2, 1, half)
-        coarse_s[:1, y : y + 1] = corners[:1]
-        coarse_s[1 + coarse_x :, y : y + 1] = corners[1:]
+        coarse_s[:1, y : y + 1] = as_field(c_low[corner:, :], 1, 1, half)
+        coarse_s[1 + coarse_x :, y : y + 1] = as_field(c_high[corner:, :], 1, 1, half)
     wide_x, wide_y = coarse_x + 2, coarse_y + 2
     coarse_rows = wide_x * wide_y * half
     coarse = down_ref.shape[2]
@@ -328,7 +328,8 @@
 
 
 def weight_grad_kernel(
-    grid_ref, x_low, x_high, y_low, y_high, c_low, c_high, fine_ref, delta_coarse_ref, delta_ref,
+    grid_ref, x_low, x_high, y_low, y_high, c_ll, c_lh, c_hl, c_hh, fine_ref, delta_coarse_ref,
+    delta_ref,
     out_ref, pad_ref, four_ref, delta_s, fine_s, *, channels, fields, scale,
 ):
     (ext_x, ext_y, half, rim), _ = fields
@@ -338,12 +339,14 @@
     for x, x_ref, at in ((0, x_low, near[0]), (1 + ext_x, x_high, near[1])):
         field = as_field(x_ref[:slab, :], rim, ext_y, half)
         pad_ref[x : x + 1, 1 : 1 + ext_y] = field[at : at + 1]
-    for y, y_ref, c_ref, at in ((0, y_low, c_low, near[0]), (1 + ext_y, y_high, c_high, near[1])):
+    ends = ((0, y_low, c_ll, c_hl, near[0]), (1 + ext_y, y_high, c_lh, c_hh, near[1]))
+    for y, y_ref, c_low, c_high, at in ends:
         field = as_field(y_ref[:face, :], ext_x, rim, half)
         pad_ref[1 : 1 + ext_x, y : y + 1] = field[:, at : at + 1]
-        field = as_field(c_ref[: 2 * corner, :], 2 * rim, rim, half)[:, at : at + 1]
-        pad_ref[:1, y : y + 1] = field[rim - 1 : rim]
-        pad_ref[1 + ext_x :, y : y + 1] = field[rim : rim + 1]
+        field = as_field(c_low[:corner, :], rim, rim, half)
+        pad_ref[:1, y : y + 1] = field[near[0] : near[0] + 1, at : at + 1]
+        field = as_field(c_high[:corner, :], rim, rim, half)
+        pad_ref[1 + ext_x :, y : y + 1] = field[near[1] : near[1] + 1, at : at + 1]
     fill_four(pad_ref, four_ref, channels)
     delta_s[...] = as_field(delta_ref[...], ext_x + 2, ext_y + 2, half)
     turned = inner(delta_s[...], 1).T.astype(BF16)
@@ -424,11 +427,11 @@
         out_ref[:, start : start + step] = total.astype(BF16)
 
 
-def unpack_kernel(core_ref, mine_ref, theirs_ref, conv_ref, down_ref, all_s, *, block):
+def unpack_kernel(place_ref, mine_ref, theirs_ref, conv_ref, down_ref, all_s, *, block):
     channels = conv_ref.shape[1]
     devices, count = all_s.shape[0], all_s.shape[1] // 2
     skip = mine_ref.shape[1] - theirs_ref.shape[1]
-    swap = jnp.broadcast_to(core_ref[...], (block * devices, LANE)) > 0
+    swap = place_ref[0] % 2 == 1
     for k in range(count):
         mine = mine_ref[:, skip + k * LANE : skip + (k + 1) * LANE].astype(F32)
         theirs = theirs_ref[:, k * LANE : (k + 1) * LANE].astype(F32)
@@ -448,10 +451,14 @@
         down_ref[j, :, LANE:] = tail[:, (j % 2) * rest : (j % 2 + 1) * rest]
 
 
-def shift(block, axis, step):
-    count = lax.axis_size(axis)
-    pairs = [(i, i + step) for i in range(count) if 0 <= i + step < count]
-    return lax.ppermute(block, axis, pairs)
+def shift(block, step_x, step_y):
+    count_x, count_y = lax.axis_size("gx"), lax.axis_size("gy")
+    pairs = []
+    for x in range(count_x):
+        for y in range(count_y):
+            to = (x + step_x) % count_x * count_y + (y + step_y) % count_y
+            pairs.append((x * count_y + y, to))
+    return lax.ppermute(block, AXES, pairs)
 
 
 def exchange(blocks):
@@ -501,24 +508,23 @@
     )
     x_rows = sum(e[3] * e[1] * e[2] for e in fields)
     y_rows = sum(e[3] * e[0] * e[2] for e in fields)
-    c_rows = sum(2 * e[3] * e[3] * e[2] for e in fields)
-    grid, x_first, x_last, y_first, y_last = call(
-        functools.partial(pool_kernel, channels=channels, fields=fields),
-        tuple(struct((n, WIDE), BF16) for n in (pairs, x_rows, x_rows, y_rows, y_rows)),
-        (got, given),
+    c_rows = sum(e[3] * e[3] * e[2] for e in fields)
+    place = jnp.stack([lax.axis_index("gx"), lax.axis_index("gy")]).astype(jnp.int32)
+    sizes = (pairs, x_rows, x_rows, y_rows, y_rows, c_rows, c_rows, c_rows, c_rows)
+    grid, x_first, x_last, y_first, y_last, *corners = call(
+        functools.partial(
+            pool_kernel, channels=channels, fields=fields, counts=(count_x, count_y)
+        ),
+        tuple(struct((n, WIDE), BF16) for n in sizes),
+        (place, got, given),
         "pool",
         scratch=[pltpu.VMEM((pairs, WIDE), F32)],
         flops=pick_flops,
     )
-    x_low, x_high = shift(x_last, "gx", 1), shift(x_first, "gx", -1)
-    y_low, y_high = shift(y_last, "gy", 1), shift(y_first, "gy", -1)
-    c_first, c_last = call(
-        functools.partial(corner_kernel, fields=fields),
-        tuple(struct((n, WIDE), BF16) for n in (c_rows, c_rows)),
-        (x_low, x_high),
-        "corner",
-    )
-    c_low, c_high = shift(c_last, "gy", 1), shift(c_first, "gy", -1)
+    x_low, x_high = shift(x_last, 1, 0), shift(x_first, -1, 0)
+    y_low, y_high = shift(y_last, 0, 1), shift(y_first, 0, -1)
+    steps = ((-1, -1), (-1, 1), (1, -1), (1, 1))
+    c_hh, c_hl, c_lh, c_ll = [shift(part, *step) for part, step in zip(corners, steps)]
     long = ext_x + 2 * rim
     mid_rows = (ext_x + 4) * (ext_y - 2) * half
     silu, slope = call(
@@ -535,7 +541,7 @@
     near = (ext_x + 2, ext_y + 2, half)
     near_rows = near[0] * near[1] * half
     split = (coarse_x + 2, 2, coarse_y + 2, 2, half, WIDE)
-    faces = (x_low, x_high, y_low, y_high, c_low, c_high)
+    faces = (x_low, x_high, y_low, y_high, c_ll, c_lh, c_hl, c_hh)
     features, fine, delta_coarse, delta = call(
         functools.partial(level_kernel, channels=channels, fields=fields),
         (
@@ -609,11 +615,10 @@
         "collect",
         flops=2 * points * slot_rows * PACK * LANE,
     ).T
-    core = jnp.broadcast_to(lax.axis_index("gx") & 1, (1, LANE)).astype(jnp.int32)
     grad_conv, grad_down = call(
         functools.partial(unpack_kernel, block=block),
         (struct(w_conv.shape, F32), struct(w_down.shape, F32)),
-        (core, returned, theirs),
+        (place, returned, theirs),
         "unpack",
         scratch=[pltpu.VMEM((devices, chunk // block, block, LANE), F32)],
     )

time: 131 us -> 132 us (level)
    ppermute x6 -> x8, starting transfers between devices: 13.4 us -> 16.9 us  [shift(): return lax.ppermute(block, AXES, pairs)]
    all_to_all x2, starting transfers between devices: 22.9 us -> 20.6 us  [exchange(): return lax.all_to_all(blocks, AXES, split_axis=0, concat_axis=0, tiled=True)]
    pallas_call x11 -> x10, Pallas kernels: 28.8 us -> 29.9 us  [call(): pl.pallas_call(kernel, out_shape=outs, in_specs=[pl.BlockSpec(memory_spac...]
    ppermute x6 -> x8, waiting for transfers between devices: 2.81 us -> 1.84 us  [shift(): return lax.ppermute(block, AXES, pairs)]
  transfers between devices with their start and end apart: 9 -> 11, of which waited for: 4 -> 3; matrix products, arithmetic and copies ran while one was open for 0% -> 0% of each run, Pallas kernels for 9% -> 9%
where the time goes in v3:
time: 132 us
  starting transfers between devices  39.1 us (30%)
  Pallas kernels  29.9 us (23%)
  waiting for transfers between devices  28.4 us (22%)
  blocking collectives  25.8 us (20%)
  local copies, waits for them, and re-layouts  7.45 us (6%)
    pallas_call x10, Pallas kernels, call(): pl.pallas_call(kernel, out_shape=outs, in_specs=[pl.BlockSpec(memory_spac...  29.9 us
    all_to_all x2, waiting for transfers between devices, exchange(): return lax.all_to_all(blocks, AXES, split_axis=0, concat_axis=0, tiled=True)  26.6 us
    all_to_all x1, blocking collectives, exchange(): return lax.all_to_all(blocks, AXES, split_axis=0, concat_axis=0, tiled=True)  25.8 us
    all_to_all x2, starting transfers between devices, exchange(): return lax.all_to_all(blocks, AXES, split_axis=0, concat_axis=0, tiled=True)  20.6 us
    ppermute x8, starting transfers between devices, shift(): return lax.ppermute(block, AXES, pairs)  16.9 us
    unnamed x26, local copies, waits for them, and re-layouts  7.42 us
  transfers between devices with their start and end apart: 11, of which 3 were waited for; matrix products, arithmetic and copies ran while one was open for 0% of the time, Pallas kernels for 9%

profile of v3, /device:TPU:1, one launch (start us, length us, event | category | flops | bytes accessed | tf_op | source)
XLA Modules:
  0.0 131.5 jit_solution(2072428843738929084)
XLA Ops:
  0.6 0.0 copy-start.1
  0.6 1.0 copy-done.1
  1.6 0.0 copy-start.5
  1.6 0.7 copy-done.5
  2.3 0.0 copy-start.6
  2.3 0.7 copy-done.6
  3.0 3.7 %dispatch.1 = (bf16[1024,512]{1,0:T(8,128)(2,1)}, s32[2,2048]{1,0:T(2,128)S(1)}) custom-call(bf16[96,2048]{1,0:T(8,128)(2,1)S(1)} %bitcast.20, s32[1,2048]{1,0:T(1,128)S(1)} %bitcast.23, s32[1,2048]{1,0:T(1,128)S(1)} %bitcast.24), custom_call_target="tpu_custom_call" | custom-call | flops 2147483648 | bytes 4000000 | tf_op jit(solution)/shard_map/dispatch/pallas_call | solution.py:35
  6.7 0.0 copy-start
  6.7 0.0 copy-start.2
  6.7 0.0 copy-start.3
  6.7 0.0 copy-start.4
  6.7 11.5 %all-to-all-start = ((bf16[128,8,512]{2,1,0:T(8,128)(2,1)}), bf16[128,8,512]{2,1,0:T(8,128)(2,1)S(1)}, u32[]{:S(2)}, u32[]{:S(2)}) async-start(bf16[128,8,512]{2,1,0:T(8,128)(2,1)} %bitcast.5), calls=%async_computation | async-start | bytes 2097152 | tf_op jit(solution)/shard_map/all_to_all | solution.py:465
  18.2 0.0 copy-done
  18.2 0.0 copy-done.2
  18.3 0.0 copy-done.3
  18.3 0.0 copy-done.4
  18.3 1.0 prepare.1
  19.3 0.0 copy-start.7
  19.3 1.2 copy-done.7
  20.5 0.0 copy-start.11
  20.5 1.2 copy-done.11
  21.7 0.1 pad_add_fusion.place_ref
  21.8 15.0 %all-to-all-done = bf16[128,8,512]{2,1,0:T(8,128)(2,1)S(1)} async-done(((bf16[128,8,512]{2,1,0:T(8,128)(2,1)}), bf16[128,8,512]{2,1,0:T(8,128)(2,1)S(1)}, u32[]{:S(2)}, u32[]{:S(2)}) %all-to-all-start) | async-done | bytes 1048608 | tf_op jit(solution)/shard_map/all_to_all | solution.py:465
  36.9 0.0 copy-start.8
  36.9 3.5 %pool.1 = (bf16[1024,256]{1,0:T(8,128)(2,1)S(1)}, bf16[448,256]{1,0:T(8,128)(2,1)S(1)}, bf16[448,256]{1,0:T(8,128)(2,1)S(1)}, bf16[224,256]{1,0:T(8,128)(2,1)S(1...) custom-call(s32[2]{0:T(128)S(1)} %pad_add_fusion.place_ref, ...), custom_call_target="tpu_custom_call" | custom-call | flops 2147483648 | bytes 4000000 | tf_op jit(solution)/shard_map/pool/pallas_call | solution.py:35
  40.3 1.7 %collective-permute-start = (bf16[448,256]{1,0:T(8,128)(2,1)S(1)}, bf16[448,256]{1,0:T(8,128)(2,1)S(1)}, u32[]{:S(2)}, u32[]{:S(2)}) collective-permute-start(bf16[448,256]{1,0:T(8,128)(2,1)S(1)} %get-tuple-element.30), channel_id=1, source_target_pairs={{0,16},{1,17},{2,18},{3,19},{4,20},{5,21},{6,22},{7,23},{8,24},{9,... | collective-permute-start | bytes 688136 | tf_op jit(solution)/shard_map/ppermute | solution.py:461
  42.1 0.0 collective-permute-start.1
  42.1 2.1 %collective-permute-start.4 = (bf16[80,256]{1,0:T(8,128)(2,1)S(1)}, bf16[80,256]{1,0:T(8,128)(2,1)S(1)}, u32[]{:S(2)}, u32[]{:S(2)}) collective-permute-start(bf16[80,256]{1,0:T(8,128)(2,1)S(1)} %get-tuple-element.34), channel_id=1, source_target_pairs={{0,17},{1,18},{2,19},{3,20},{4,21},{5,22},{6,23},{7,24},{8,25},{9,... | collective-permute-start | bytes 122888 | tf_op jit(solution)/shard_map/ppermute | solution.py:461
  44.2 2.8 %collective-permute-start.5 = (bf16[80,256]{1,0:T(8,128)(2,1)S(1)}, bf16[80,256]{1,0:T(8,128)(2,1)S(1)}, u32[]{:S(2)}, u32[]{:S(2)}) collective-permute-start(bf16[80,256]{1,0:T(8,128)(2,1)S(1)} %get-tuple-element.35), channel_id=1, source_target_pairs={{0,31},{1,16},{2,17},{3,18},{4,19},{5,20},{6,21},{7,22},{8,23},{9,... | collective-permute-start | bytes 122888 | tf_op jit(solution)/shard_map/ppermute | solution.py:461
  47.0 0.0 collective-permute-start.6
  47.0 1.8 %collective-permute-done.4.c_ll = bf16[80,256]{1,0:T(8,128)(2,1)S(1)} collective-permute-done((bf16[80,256]{1,0:T(8,128)(2,1)S(1)}, bf16[80,256]{1,0:T(8,128)(2,1)S(1)}, u32[]{:S(2)}, u32[]{:S(2)}) %collective-permute-start.4) | collective-permute-done | bytes 40992 | tf_op jit(solution)/shard_map/ppermute | solution.py:461
  48.8 5.5 %collective-permute-start.7 = (bf16[80,256]{1,0:T(8,128)(2,1)S(1)}, bf16[80,256]{1,0:T(8,128)(2,1)S(1)}, u32[]{:S(2)}, u32[]{:S(2)}) collective-permute-start(bf16[80,256]{1,0:T(8,128)(2,1)S(1)} %get-tuple-element.37), channel_id=1, source_target_pairs={{0,127},{1,112},{2,113},{3,114},{4,115},{5,116},{6,117},{7,118},{8... | collective-permute-start | bytes 122888 | tf_op jit(solution)/shard_map/ppermute | solution.py:461
  54.3 0.0 collective-permute-done.x_low
  54.3 0.7 collective-permute-start.2
  55.0 0.0 collective-permute-done.1.x_high
  55.0 4.1 %collective-permute-start.3 = (bf16[224,256]{1,0:T(8,128)(2,1)S(1)}, bf16[224,256]{1,0:T(8,128)(2,1)S(1)}, u32[]{:S(2)}, u32[]{:S(2)}) collective-permute-start(bf16[224,256]{1,0:T(8,128)(2,1)S(1)} %get-tuple-element.33), channel_id=1, source_target_pairs={{0,15},{1,0},{2,1},{3,2},{4,3},{5,4},{6,5},{7,6},{8,7},{9,8},{10,9... | collective-permute-start | bytes 344072 | tf_op jit(solution)/shard_map/ppermute | solution.py:461
  59.1 0.0 copy-done.8
  59.1 3.1 %column.1 = (bf16[1344,256]{1,0:T(8,128)(2,1)S(1)}, f32[1344,256]{1,0:T(8,128)S(1)}) custom-call(bf16[1024,256]{1,0:T(8,128)(2,1)S(1)} %get-tuple-element.29.grid_ref, bf16[448,256]{1,0:T(8,128)(2,1)S(1)} %collective-permute-done.x_low, bf16[448,256]{1,0:T(8,128)(2,1)S(1)} %collective-permute-done.1.x_high, bf16[3456,256]{1,0:T(8,128)(2,1)S(1)} %copy-done.8), custom_call_target="tpu_custom_call" | custom-call | flops 3623878656 | bytes 4000000 | tf_op jit(solution)/shard_map/column/pallas_call | solution.py:35
  62.2 0.0 collective-permute-done.5.c_lh
  62.2 0.0 collective-permute-done.6.c_hl
  62.2 0.0 collective-permute-done.7.c_hh
  62.2 0.0 collective-permute-done.2.y_low
  62.2 0.0 collective-permute-done.3.y_high
  62.2 5.0 %level.1 = (bf16[256,192]{1,0:T(8,128)(2,1)}, bf16[1024,256]{1,0:T(8,128)(2,1)S(1)}, bf16[256,192]{1,0:T(8,128)(2,1)S(1)}, bf16[1440,256]{1,0:T(8,128)(2,1)S(1)}) custom-call(bf16[1024,256]{1,0:T(8,128)(2,1)S(1)} %get-tuple-element.29.grid_ref, bf16[256,256]{1,0:T(8,128)(2,1)S(1)} %get-tuple-element.28.coarse_ref, ...), custom_call_target="tpu_custom_call" | custom-call | flops 1811939328 | bytes 8000000 | tf_op jit(solution)/shard_map/level/pallas_call | solution.py:35
  67.2 0.0 copy-start.9
  67.2 4.1 %weight_grad.1 = bf16[4096,128]{1,0:T(8,128)(2,1)} custom-call(bf16[1024,256]{1,0:T(8,128)(2,1)S(1)} %get-tuple-element.29.grid_ref, bf16[448,256]{1,0:T(8,128)(2,1)S(1)} %collective-permute-done.x_low, bf16[448,256]{1,0:T(8,128)(2,1)S(1)} %collective-permute-done.1.x_high, bf16[224,256]{1,0:T(8,128)(2,1)S(1)} %collective-permute-done.2.y_low, ...), custom_call_target="tpu_custom_call" | custom-call | flops 1811939328 | bytes 8000000 | tf_op jit(solution)/shard_map/weight_grad/pallas_call | solution.py:35
  71.3 0.0 copy-done.9
  71.3 9.1 %all-to-all-start.1 = ((bf16[128,32,128]{2,1,0:T(8,128)(2,1)}), bf16[128,32,128]{2,1,0:T(8,128)(2,1)S(1)}, u32[]{:S(2)}, u32[]{:S(2)}) async-start(bf16[128,32,128]{2,1,0:T(8,128)(2,1)} %bitcast.10), calls=%async_computation.1 | async-start | bytes 2097152 | tf_op jit(solution)/shard_map/all_to_all | solution.py:465
  80.4 0.0 copy-start.10
  80.5 1.1 copy-done.10
  81.6 0.0 copy-start.12
  81.6 1.5 %copy-done.12 = bf16[3456,256]{1,0:T(8,128)(2,1)S(1)} copy-done((bf16[3456,256]{1,0:T(8,128)(2,1)S(1)}, bf16[3456,256]{1,0:T(8,128)(2,1)}, u32[]{:S(2)}) %copy-start.12) | copy-done | bytes 1769496
  83.0 4.5 %input_grad.1.back_ref = bf16[1024,384]{1,0:T(8,128)(2,1)S(1)} custom-call(bf16[1440,256]{1,0:T(8,128)(2,1)S(1)} %copy-done.10, bf16[3456,256]{1,0:T(8,128)(2,1)S(1)} %copy-done.12, bf16[1024,512]{1,0:T(8,128)(2,1)S(1)} %bitcast.19), custom_call_target="tpu_custom_call" | custom-call | flops 3959422976 | bytes 8000000 | tf_op jit(solution)/shard_map/input_grad/pallas_call | solution.py:35
  87.5 11.5 %all-to-all-done.1.terms_ref = bf16[128,32,128]{2,1,0:T(8,128)(2,1)S(1)} async-done(((bf16[128,32,128]{2,1,0:T(8,128)(2,1)}), bf16[128,32,128]{2,1,0:T(8,128)(2,1)S(1)}, u32[]{:S(2)}, u32[]{:S(2)}) %all-to-all-start.1) | async-done | bytes 1048608 | tf_op jit(solution)/shard_map/all_to_all | solution.py:465
  99.1 0.3 join.1
  99.3 25.8 %all_to_all.15 = bf16[128,8,640]{2,1,0:T(8,128)(2,1)S(1)} all-to-all(bf16[128,8,640]{2,1,0:T(8,128)(2,1)S(1)} %bitcast.17), channel_id=1, replica_groups=mesh['gx'=8,'gy'=16] {'gx','gy'}, dimensions={0} | all-to-all | bytes 2621440 | tf_op jit(solution)/shard_map/all_to_all | solution.py:465
  125.1 1.6 %collective-permute-start.8 = (bf16[1024,256]{1,0:T(8,128)(2,1)S(1)}, bf16[1024,256]{1,0:T(8,128)(2,1)S(1)}, u32[]{:S(2)}, u32[]{:S(2)}) collective-permute-start(bf16[1024,256]{1,0:T(8,128)(2,1)S(1)} %slice.4), channel_id=1, source_target_pairs={{0,16},{16,0},{32,48},{48,32},{64,80},{80,64},{96,112},{112,96},{1... | collective-permute-start | bytes 1572872 | tf_op jit(solution)/shard_map/ppermute | solution.py:608
  126.7 2.7 %collect.1 = bf16[96,2048]{1,0:T(8,128)(2,1)} custom-call(bf16[1024,640]{1,0:T(8,128)(2,1)S(1)} %bitcast.15, s32[2,2048]{1,0:T(2,128)S(1)} %get-tuple-element.47.slot_ref), custom_call_target="tpu_custom_call" | custom-call | flops 2147483648 | bytes 4000000 | tf_op jit(solution)/shard_map/collect/pallas_call | solution.py:35
  129.4 0.0 collective-permute-done.8.theirs_ref
  129.4 2.1 %unpack.1 = (f32[27,96,96]{2,1,0:T(8,128)}, f32[8,96,192]{2,1,0:T(8,128)}) custom-call(s32[2]{0:T(128)S(1)} %pad_add_fusion.place_ref, bf16[1024,640]{1,0:T(8,128)(2,1)S(1)} %bitcast.16, bf16[1024,256]{1,0:T(8,128)(2,1)S(1)} %collective-permute-done.8.theirs_ref), custom_call_target="tpu_custom_call" | custom-call | bytes 4000000 | tf_op jit(solution)/shard_map/unpack/pallas_call | solution.py:35
  (1 shorter events, 0.0 us)
Async XLA Ops:
  0.6 1.0 copy-start.1
  1.6 0.7 copy-start.5
  2.3 0.7 copy-start.6
  6.7 11.5 %copy-start = (bf16[27,96,96]{2,1,0:T(8,128)(2,1)S(1)}, bf16[27,96,96]{2,1,0:T(8,128)(2,1)}, u32[]{:S(2)}) copy-start(bf16[27,96,96]{2,1,0:T(8,128)(2,1)} %conv_ref.1) | copy-start | bytes 1492996
  6.7 11.5 %copy-start.2 = (bf16[8,96,192]{2,1,0:T(8,128)(2,1)S(1)}, bf16[8,96,192]{2,1,0:T(8,128)(2,1)}, u32[]{:S(2)}) copy-start(bf16[8,96,192]{2,1,0:T(8,128)(2,1)} %down_ref.1) | copy-start | bytes 884740
  6.7 11.5 %copy-start.3 = (bf16[4,8,8,192]{3,2,1,0:T(8,128)(2,1)S(1)}, bf16[4,8,8,192]{3,2,1,0:T(8,128)(2,1)}, u32[]{:S(2)}) copy-start(bf16[4,8,8,192]{3,2,1,0:T(8,128)(2,1)} %param.13) | copy-start | bytes 294916
  6.7 11.5 %copy-start.4 = (s32[8,16,16]{2,1,0:T(8,128)S(1)}, s32[8,16,16]{2,1,0:T(8,128)}, u32[]{:S(2)}) copy-start(s32[8,16,16]{2,1,0:T(8,128)} %param.10) | copy-start | bytes 24580
  6.7 30.1 %all-to-all-start = ((bf16[128,8,512]{2,1,0:T(8,128)(2,1)}), bf16[128,8,512]{2,1,0:T(8,128)(2,1)S(1)}, u32[]{:S(2)}, u32[]{:S(2)}) async-start(bf16[128,8,512]{2,1,0:T(8,128)(2,1)} %bitcast.5), calls=%async_computation | async-start | bytes 2097152 | tf_op jit(solution)/shard_map/all_to_all | solution.py:465
  19.3 1.2 copy-start.7
  20.5 1.2 copy-start.11
  36.9 22.3 %copy-start.8 = (bf16[3456,256]{1,0:T(8,128)(2,1)S(1)}, bf16[3456,256]{1,0:T(8,128)(2,1)}, u32[]{:S(2)}) copy-start(bf16[3456,256]{1,0:T(8,128)(2,1)} %copy-done.7) | copy-start | bytes 5308420
  40.3 14.0 %collective-permute-start = (bf16[448,256]{1,0:T(8,128)(2,1)S(1)}, bf16[448,256]{1,0:T(8,128)(2,1)S(1)}, u32[]{:S(2)}, u32[]{:S(2)}) collective-permute-start(bf16[448,256]{1,0:T(8,128)(2,1)S(1)} %get-tuple-element.30), channel_id=1, source_target_pairs={{0,16},{1,17},{2,18},{3,19},{4,20},{5,21},{6,22},{7,23},{8,24},{9,... | collective-permute-start | bytes 688136 | tf_op jit(solution)/shard_map/ppermute | solution.py:461
  42.1 12.9 %collective-permute-start.1 = (bf16[448,256]{1,0:T(8,128)(2,1)S(1)}, bf16[448,256]{1,0:T(8,128)(2,1)S(1)}, u32[]{:S(2)}, u32[]{:S(2)}) collective-permute-start(bf16[448,256]{1,0:T(8,128)(2,1)S(1)} %get-tuple-element.31), channel_id=1, source_target_pairs={{0,112},{1,113},{2,114},{3,115},{4,116},{5,117},{6,118},{7,119},{8... | collective-permute-start | bytes 688136 | tf_op jit(solution)/shard_map/ppermute | solution.py:461
  42.1 6.7 %collective-permute-start.4 = (bf16[80,256]{1,0:T(8,128)(2,1)S(1)}, bf16[80,256]{1,0:T(8,128)(2,1)S(1)}, u32[]{:S(2)}, u32[]{:S(2)}) collective-permute-start(bf16[80,256]{1,0:T(8,128)(2,1)S(1)} %get-tuple-element.34), channel_id=1, source_target_pairs={{0,17},{1,18},{2,19},{3,20},{4,21},{5,22},{6,23},{7,24},{8,25},{9,... | collective-permute-start | bytes 122888 | tf_op jit(solution)/shard_map/ppermute | solution.py:461
  44.2 18.0 %collective-permute-start.5 = (bf16[80,256]{1,0:T(8,128)(2,1)S(1)}, bf16[80,256]{1,0:T(8,128)(2,1)S(1)}, u32[]{:S(2)}, u32[]{:S(2)}) collective-permute-start(bf16[80,256]{1,0:T(8,128)(2,1)S(1)} %get-tuple-element.35), channel_id=1, source_target_pairs={{0,31},{1,16},{2,17},{3,18},{4,19},{5,20},{6,21},{7,22},{8,23},{9,... | collective-permute-start | bytes 122888 | tf_op jit(solution)/shard_map/ppermute | solution.py:461
  47.0 15.2 %collective-permute-start.6 = (bf16[80,256]{1,0:T(8,128)(2,1)S(1)}, bf16[80,256]{1,0:T(8,128)(2,1)S(1)}, u32[]{:S(2)}, u32[]{:S(2)}) collective-permute-start(bf16[80,256]{1,0:T(8,128)(2,1)S(1)} %get-tuple-element.36), channel_id=1, source_target_pairs={{0,113},{1,114},{2,115},{3,116},{4,117},{5,118},{6,119},{7,120},{8... | collective-permute-start | bytes 122888 | tf_op jit(solution)/shard_map/ppermute | solution.py:461
  48.8 13.4 %collective-permute-start.7 = (bf16[80,256]{1,0:T(8,128)(2,1)S(1)}, bf16[80,256]{1,0:T(8,128)(2,1)S(1)}, u32[]{:S(2)}, u32[]{:S(2)}) collective-permute-start(bf16[80,256]{1,0:T(8,128)(2,1)S(1)} %get-tuple-element.37), channel_id=1, source_target_pairs={{0,127},{1,112},{2,113},{3,114},{4,115},{5,116},{6,117},{7,118},{8... | collective-permute-start | bytes 122888 | tf_op jit(solution)/shard_map/ppermute | solution.py:461
  54.3 7.9 %collective-permute-start.2 = (bf16[224,256]{1,0:T(8,128)(2,1)S(1)}, bf16[224,256]{1,0:T(8,128)(2,1)S(1)}, u32[]{:S(2)}, u32[]{:S(2)}) collective-permute-start(bf16[224,256]{1,0:T(8,128)(2,1)S(1)} %get-tuple-element.32), channel_id=1, source_target_pairs={{0,1},{1,2},{2,3},{3,4},{4,5},{5,6},{6,7},{7,8},{8,9},{9,10},{10,1... | collective-permute-start | bytes 344072 | tf_op jit(solution)/shard_map/ppermute | solution.py:461
  55.0 7.2 %collective-permute-start.3 = (bf16[224,256]{1,0:T(8,128)(2,1)S(1)}, bf16[224,256]{1,0:T(8,128)(2,1)S(1)}, u32[]{:S(2)}, u32[]{:S(2)}) collective-permute-start(bf16[224,256]{1,0:T(8,128)(2,1)S(1)} %get-tuple-element.33), channel_id=1, source_target_pairs={{0,15},{1,0},{2,1},{3,2},{4,3},{5,4},{6,5},{7,6},{8,7},{9,8},{10,9... | collective-permute-start | bytes 344072 | tf_op jit(solution)/shard_map/ppermute | solution.py:461
  67.2 4.1 %copy-start.9 = (bf16[1440,256]{1,0:T(8,128)(2,1)}, bf16[1440,256]{1,0:T(8,128)(2,1)S(1)}, u32[]{:S(2)}) copy-start(bf16[1440,256]{1,0:T(8,128)(2,1)S(1)} %get-tuple-element.45.delta_ref) | copy-start | bytes 2211844
  71.3 27.8 %all-to-all-start.1 = ((bf16[128,32,128]{2,1,0:T(8,128)(2,1)}), bf16[128,32,128]{2,1,0:T(8,128)(2,1)S(1)}, u32[]{:S(2)}, u32[]{:S(2)}) async-start(bf16[128,32,128]{2,1,0:T(8,128)(2,1)} %bitcast.10), calls=%async_computation.1 | async-start | bytes 2097152 | tf_op jit(solution)/shard_map/all_to_all | solution.py:465
  80.4 1.1 copy-start.10
  81.6 1.5 %copy-start.12 = (bf16[3456,256]{1,0:T(8,128)(2,1)S(1)}, bf16[3456,256]{1,0:T(8,128)(2,1)}, u32[]{:S(2)}) copy-start(bf16[3456,256]{1,0:T(8,128)(2,1)} %copy-done.11) | copy-start | bytes 5308420
  125.1 4.3 %collective-permute-start.8 = (bf16[1024,256]{1,0:T(8,128)(2,1)S(1)}, bf16[1024,256]{1,0:T(8,128)(2,1)S(1)}, u32[]{:S(2)}, u32[]{:S(2)}) collective-permute-start(bf16[1024,256]{1,0:T(8,128)(2,1)S(1)} %slice.4), channel_id=1, source_target_pairs={{0,16},{16,0},{32,48},{48,32},{64,80},{80,64},{96,112},{112,96},{1... | collective-permute-start | bytes 1572872 | tf_op jit(solution)/shard_map/ppermute | solution.py:608

commit v4 on v2

--- a/solution.py
+++ b/solution.py
@@ -35,7 +35,9 @@
     return pl.pallas_call(
         kernel,
         out_shape=outs,
-        in_specs=[pl.BlockSpec(memory_space=pltpu.VMEM)] * len(args),
+        in_specs=[
+            pl.BlockSpec(memory_space=pltpu.SMEM if arg.ndim == 1 else pltpu.VMEM) for arg in args
+        ],
         out_specs=jax.tree.map(lambda _: pl.BlockSpec(memory_space=pltpu.VMEM), outs),
         scratch_shapes=list(scratch),
         compiler_params=pltpu.CompilerParams(vmem_limit_bytes=48 * 1024 * 1024),
@@ -83,7 +85,8 @@
 
 
 def pool_kernel(
-    got_ref, coarse_ref, grid_ref, x_first, x_last, y_first, y_last, total_ref, *, channels, fields
+    place_ref, got_ref, coarse_ref, grid_ref, first_ref, last_ref, total_ref,
+    *, channels, fields, count,
 ):
     rows = got_ref.shape[0]
     pairs = grid_ref.shape[0]
@@ -102,13 +105,12 @@
             if q:
                 part = total_ref[start : start + step, :] + part
             total_ref[start : start + step, :] = part
-    x_at, y_at = 0, 0
+    at = 0
     for ref, (ext_x, ext_y, half, rim) in zip((total_ref, coarse_ref), fields):
         field = as_field(ref[...], ext_x, ext_y, half)
-        x_at = put_rows(x_first, x_at, field[:rim])
-        put_rows(x_last, x_at - rim * ext_y * half, field[ext_x - rim :])
-        y_at = put_rows(y_first, y_at, field[:, :rim])
-        put_rows(y_last, y_at - rim * ext_x * half, field[:, ext_y - rim :])
+        put_rows(first_ref, at, field[:rim] * inside(place_ref[0], 0))
+        put_rows(last_ref, at, field[ext_x - rim :] * inside(place_ref[0], count - 1))
+        at += rim * ext_y * half
     grid_ref[...] = total_ref[...].astype(BF16)
 
 
@@ -119,17 +121,27 @@
 def put_rows(ref, at, field):
     size = field.shape[0] * field.shape[1] * field.shape[2]
     ref[at : at + size, :] = field.reshape(size, field.shape[3]).astype(BF16)
-    return at + size
-
-
-def corner_kernel(low_ref, high_ref, first_ref, last_ref, *, fields):
+
+
+def inside(place, end):
+    return jnp.where(place == end, 0.0, 1.0)
+
+
+def edge_kernel(
+    place_ref, grid_ref, coarse_ref, low_ref, high_ref, first_ref, last_ref, *, fields, count
+):
     start, at = 0, 0
-    for _, ext_y, half, rim in fields:
+    for ref, (ext_x, ext_y, half, rim) in zip((grid_ref, coarse_ref), fields):
         size = rim * ext_y * half
-        for ref in (low_ref, high_ref):
-            field = as_field(ref[start : start + size, :], rim, ext_y, half)
-            put_rows(first_ref, at, field[:, :rim])
-            at = put_rows(last_ref, at, field[:, ext_y - rim :])
+        parts = (
+            as_field(low_ref[start : start + size, :], rim, ext_y, half),
+            as_field(ref[...], ext_x, ext_y, half),
+            as_field(high_ref[start : start + size, :], rim, ext_y, half),
+        )
+        for part in parts:
+            put_rows(first_ref, at, part[:, :rim] * inside(place_ref[1], 0))
+            put_rows(last_ref, at, part[:, ext_y - rim :] * inside(place_ref[1], count - 1))
+            at += part.shape[0] * rim * half
         start += size
 
 
@@ -233,31 +245,27 @@
 
 
 def level_kernel(
-    grid_ref, coarse_ref, x_low, x_high, y_low, y_high, c_low, c_high, silu_ref, slope_ref,
+    grid_ref, coarse_ref, x_low, x_high, y_low, y_high, silu_ref, slope_ref,
     conv_ref, down_ref,
     features_ref, fine_ref, delta_coarse_ref, delta_ref,
     pad_ref, four_ref, coarse_s, mask_s, fine_s, slope_s, *, channels, fields,
 ):
     (ext_x, ext_y, half, rim), (coarse_x, coarse_y, _, _) = fields
     wide = WIDE
-    slab, face, corner = rim * ext_y * half, ext_x * rim * half, rim * rim * half
     long = ext_x + 2 * rim
-    grid = as_field(grid_ref[...], ext_x, ext_y, half)
-    low = as_field(x_low[:slab, :], rim, ext_y, half)
-    high = as_field(x_high[:slab, :], rim, ext_y, half)
-    for s, (y_ref, c_ref) in enumerate(((y_low, c_low), (y_high, c_high))):
-        ours, here, there = ((0, 3, 0), (ext_y - 2, 0, 2))[s]
-        base = s * long
-        parts = (
-            (low, as_field(c_ref[:corner, :], rim, rim, half)),
-            (grid, as_field(y_ref[:face, :], ext_x, rim, half)),
-            (high, as_field(c_ref[corner : 2 * corner, :], rim, rim, half)),
-        )
-        at = base
-        for mine, theirs in parts:
-            count = mine.shape[0]
-            pad_ref[at : at + count, here : here + 2] = mine[:, ours : ours + 2]
-            pad_ref[at : at + count, there : there + rim] = theirs
+    slab, face = rim * ext_y * half, long * rim * half
+    parts = (
+        as_field(x_low[:slab, :], rim, ext_y, half),
+        as_field(grid_ref[...], ext_x, ext_y, half),
+        as_field(x_high[:slab, :], rim, ext_y, half),
+    )
+    for side, y_ref in enumerate((y_low, y_high)):
+        ours, here, there = ((0, rim, 0), (ext_y - 2, 0, 2))[side]
+        at = side * long
+        pad_ref[at : at + long, there : there + rim] = as_field(y_ref[:face, :], long, rim, half)
+        for part in parts:
+            count = part.shape[0]
+            pad_ref[at : at + count, here : here + 2] = part[:, ours : ours + 2]
             at += count
     fill_four(pad_ref, four_ref, channels)
     coarse_s[1 : 1 + coarse_x, 1 : 1 + coarse_y] = as_field(
@@ -265,11 +273,8 @@
     )
     coarse_s[:1, 1 : 1 + coarse_y] = as_field(x_low[slab:, :], 1, coarse_y, half)
     coarse_s[1 + coarse_x :, 1 : 1 + coarse_y] = as_field(x_high[slab:, :], 1, coarse_y, half)
-    for y, y_ref, c_ref in ((0, y_low, c_low), (1 + coarse_y, y_high, c_high)):
-        coarse_s[1 : 1 + coarse_x, y : y + 1] = as_field(y_ref[face:, :], coarse_x, 1, half)
-        corners = as_field(c_ref[2 * corner :, :], 2, 1, half)
-        coarse_s[:1, y : y + 1] = corners[:1]
-        coarse_s[1 + coarse_x :, y : y + 1] = corners[1:]
+    for y, y_ref in ((0, y_low), (1 + coarse_y, y_high)):
+        coarse_s[:, y : y + 1] = as_field(y_ref[face:, :], coarse_x + 2, 1, half)
     wide_x, wide_y = coarse_x + 2, coarse_y + 2
     coarse_rows = wide_x * wide_y * half
     coarse = down_ref.shape[2]
@@ -328,22 +333,19 @@
 
 
 def weight_grad_kernel(
-    grid_ref, x_low, x_high, y_low, y_high, c_low, c_high, fine_ref, delta_coarse_ref, delta_ref,
+    grid_ref, x_low, x_high, y_low, y_high, fine_ref, delta_coarse_ref, delta_ref,
     out_ref, pad_ref, four_ref, delta_s, fine_s, *, channels, fields, scale,
 ):
     (ext_x, ext_y, half, rim), _ = fields
-    slab, face, corner = rim * ext_y * half, ext_x * rim * half, rim * rim * half
+    long = ext_x + 2 * rim
+    slab, face = rim * ext_y * half, long * rim * half
     pad_ref[1 : 1 + ext_x, 1 : 1 + ext_y] = as_field(grid_ref[...], ext_x, ext_y, half)
-    near = (rim - 1, 0)
-    for x, x_ref, at in ((0, x_low, near[0]), (1 + ext_x, x_high, near[1])):
+    for x, x_ref, at in ((0, x_low, rim - 1), (1 + ext_x, x_high, 0)):
         field = as_field(x_ref[:slab, :], rim, ext_y, half)
         pad_ref[x : x + 1, 1 : 1 + ext_y] = field[at : at + 1]
-    for y, y_ref, c_ref, at in ((0, y_low, c_low, near[0]), (1 + ext_y, y_high, c_high, near[1])):
-        field = as_field(y_ref[:face, :], ext_x, rim, half)
-        pad_ref[1 : 1 + ext_x, y : y + 1] = field[:, at : at + 1]
-        field = as_field(c_ref[: 2 * corner, :], 2 * rim, rim, half)[:, at : at + 1]
-        pad_ref[:1, y : y + 1] = field[rim - 1 : rim]
-        pad_ref[1 + ext_x :, y : y + 1] = field[rim : rim + 1]
+    for y, y_ref, at in ((0, y_low, rim - 1), (1 + ext_y, y_high, 0)):
+        field = as_field(y_ref[:face, :], long, rim, half)
+        pad_ref[:, y : y + 1] = field[rim - 1 : long - rim + 1, at : at + 1]
     fill_four(pad_ref, four_ref, channels)
     delta_s[...] = as_field(delta_ref[...], ext_x + 2, ext_y + 2, half)
     turned = inner(delta_s[...], 1).T.astype(BF16)
@@ -424,11 +426,11 @@
         out_ref[:, start : start + step] = total.astype(BF16)
 
 
-def unpack_kernel(core_ref, mine_ref, theirs_ref, conv_ref, down_ref, all_s, *, block):
+def unpack_kernel(place_ref, mine_ref, theirs_ref, conv_ref, down_ref, all_s, *, block):
     channels = conv_ref.shape[1]
     devices, count = all_s.shape[0], all_s.shape[1] // 2
     skip = mine_ref.shape[1] - theirs_ref.shape[1]
-    swap = jnp.broadcast_to(core_ref[...], (block * devices, LANE)) > 0
+    swap = place_ref[0] % 2 == 1
     for k in range(count):
         mine = mine_ref[:, skip + k * LANE : skip + (k + 1) * LANE].astype(F32)
         theirs = theirs_ref[:, k * LANE : (k + 1) * LANE].astype(F32)
@@ -450,8 +452,7 @@
 
 def shift(block, axis, step):
     count = lax.axis_size(axis)
-    pairs = [(i, i + step) for i in range(count) if 0 <= i + step < count]
-    return lax.ppermute(block, axis, pairs)
+    return lax.ppermute(block, axis, [(i, (i + step) % count) for i in range(count)])
 
 
 def exchange(blocks):
@@ -500,25 +501,24 @@
         flops=1000000000,
     )
     x_rows = sum(e[3] * e[1] * e[2] for e in fields)
-    y_rows = sum(e[3] * e[0] * e[2] for e in fields)
-    c_rows = sum(2 * e[3] * e[3] * e[2] for e in fields)
-    grid, x_first, x_last, y_first, y_last = call(
-        functools.partial(pool_kernel, channels=channels, fields=fields),
-        tuple(struct((n, WIDE), BF16) for n in (pairs, x_rows, x_rows, y_rows, y_rows)),
-        (got, given),
+    y_rows = sum(e[3] * (e[0] + 2 * e[3]) * e[2] for e in fields)
+    place = jnp.stack([lax.axis_index("gx"), lax.axis_index("gy")]).astype(jnp.int32)
+    grid, x_first, x_last = call(
+        functools.partial(pool_kernel, channels=channels, fields=fields, count=count_x),
+        tuple(struct((n, WIDE), BF16) for n in (pairs, x_rows, x_rows)),
+        (place, got, given),
         "pool",
         scratch=[pltpu.VMEM((pairs, WIDE), F32)],
         flops=pick_flops,
     )
     x_low, x_high = shift(x_last, "gx", 1), shift(x_first, "gx", -1)
+    y_first, y_last = call(
+        functools.partial(edge_kernel, fields=fields, count=count_y),
+        tuple(struct((n, WIDE), BF16) for n in (y_rows, y_rows)),
+        (place, grid, given, x_low, x_high),
+        "edge",
+    )
     y_low, y_high = shift(y_last, "gy", 1), shift(y_first, "gy", -1)
-    c_first, c_last = call(
-        functools.partial(corner_kernel, fields=fields),
-        tuple(struct((n, WIDE), BF16) for n in (c_rows, c_rows)),
-        (x_low, x_high),
-        "corner",
-    )
-    c_low, c_high = shift(c_last, "gy", 1), shift(c_first, "gy", -1)
     long = ext_x + 2 * rim
     mid_rows = (ext_x + 4) * (ext_y - 2) * half
     silu, slope = call(
@@ -535,7 +535,7 @@
     near = (ext_x + 2, ext_y + 2, half)
     near_rows = near[0] * near[1] * half
     split = (coarse_x + 2, 2, coarse_y + 2, 2, half, WIDE)
-    faces = (x_low, x_high, y_low, y_high, c_low, c_high)
+    faces = (x_low, x_high, y_low, y_high)
     features, fine, delta_coarse, delta = call(
         functools.partial(level_kernel, channels=channels, fields=fields),
         (
@@ -609,11 +609,10 @@
         "collect",
         flops=2 * points * slot_rows * PACK * LANE,
     ).T
-    core = jnp.broadcast_to(lax.axis_index("gx") & 1, (1, LANE)).astype(jnp.int32)
     grad_conv, grad_down = call(
         functools.partial(unpack_kernel, block=block),
         (struct(w_conv.shape, F32), struct(w_down.shape, F32)),
-        (core, returned, theirs),
+        (place, returned, theirs),
         "unpack",
         scratch=[pltpu.VMEM((devices, chunk // block, block, LANE), F32)],
     )

time: 131 us -> 126 us (0.962)
  starting transfers between devices: 37.9 us -> 27.4 us
  waiting for transfers between devices: 29.4 us -> 33.5 us
  Pallas kernels: 28.8 us -> 30.5 us
    ppermute x6 -> x4, starting transfers between devices: 13.4 us -> 6.59 us  [shift(): lax.ppermute(block, axis, [(i, (i + step) % count) for i in range(count)])]
    ppermute x6 -> x4, waiting for transfers between devices: 2.81 us -> 6.97 us  [shift(): lax.ppermute(block, axis, [(i, (i + step) % count) for i in range(count)])]
    all_to_all x2, starting transfers between devices: 22.9 us -> 19.3 us  [exchange(): return lax.all_to_all(blocks, AXES, split_axis=0, concat_axis=0, tiled=True)]
    pallas_call x11, Pallas kernels: 28.8 us -> 30.5 us  [call(): pl.pallas_call(kernel, out_shape=outs, in_specs=[pl.BlockSpec(memory_spac...]
  transfers between devices with their start and end apart: 9 -> 7, of which waited for: 4 -> 5; matrix products, arithmetic and copies ran while one was open for 0% -> 0% of each run, Pallas kernels for 9% -> 9%
where the time goes in v4:
time: 126 us
  waiting for transfers between devices  33.5 us (27%)
  Pallas kernels  30.5 us (24%)
  starting transfers between devices  27.4 us (22%)
  blocking collectives  25.8 us (20%)
  local copies, waits for them, and re-layouts  7.46 us (6%)
    pallas_call x11, Pallas kernels, call(): pl.pallas_call(kernel, out_shape=outs, in_specs=[pl.BlockSpec(memory_spac...  30.5 us
    all_to_all x2, waiting for transfers between devices, exchange(): return lax.all_to_all(blocks, AXES, split_axis=0, concat_axis=0, tiled=True)  26.5 us
    all_to_all x1, blocking collectives, exchange(): return lax.all_to_all(blocks, AXES, split_axis=0, concat_axis=0, tiled=True)  25.8 us
    all_to_all x2, starting transfers between devices, exchange(): return lax.all_to_all(blocks, AXES, split_axis=0, concat_axis=0, tiled=True)  19.3 us
    unnamed x26, local copies, waits for them, and re-layouts  7.43 us
    ppermute x4, waiting for transfers between devices, shift(): lax.ppermute(block, axis, [(i, (i + step) % count) for i in range(count)])  6.97 us
    ppermute x4, starting transfers between devices, shift(): lax.ppermute(block, axis, [(i, (i + step) % count) for i in range(count)])  6.59 us
  transfers between devices with their start and end apart: 7, of which 5 were waited for; matrix products, arithmetic and copies ran while one was open for 0% of the time, Pallas kernels for 9%

profile of v4, /device:TPU:1, one launch (start us, length us, event | category | flops | bytes accessed | tf_op | source)
XLA Modules:
  0.0 125.5 jit_solution(7354935469848762221)
XLA Ops:
  0.6 0.0 copy-start.1
  0.6 1.0 copy-done.1
  1.6 0.0 copy-start.5
  1.6 0.7 copy-done.5
  2.3 0.0 copy-start.6
  2.3 0.7 copy-done.6
  3.0 3.7 %dispatch.1 = (bf16[1024,512]{1,0:T(8,128)(2,1)}, s32[2,2048]{1,0:T(2,128)S(1)}) custom-call(bf16[96,2048]{1,0:T(8,128)(2,1)S(1)} %bitcast.20, s32[1,2048]{1,0:T(1,128)S(1)} %bitcast.23, s32[1,2048]{1,0:T(1,128)S(1)} %bitcast.24), custom_call_target="tpu_custom_call" | custom-call | flops 2147483648 | bytes 4000000 | tf_op jit(solution)/shard_map/dispatch/pallas_call | solution.py:35
  6.7 0.0 copy-start
  6.7 0.0 copy-start.2
  6.7 0.0 copy-start.3
  6.7 0.0 copy-start.4
  6.7 11.5 %all-to-all-start = ((bf16[128,8,512]{2,1,0:T(8,128)(2,1)}), bf16[128,8,512]{2,1,0:T(8,128)(2,1)S(1)}, u32[]{:S(2)}, u32[]{:S(2)}) async-start(bf16[128,8,512]{2,1,0:T(8,128)(2,1)} %bitcast.5), calls=%async_computation | async-start | bytes 2097152 | tf_op jit(solution)/shard_map/all_to_all | solution.py:459
  18.2 0.0 copy-done
  18.2 0.0 copy-done.2
  18.3 0.0 copy-done.3
  18.3 0.0 copy-done.4
  18.3 1.0 prepare.1
  19.3 0.0 copy-start.7
  19.3 1.2 copy-done.7
  20.6 0.0 copy-start.11
  20.6 1.2 copy-done.11
  21.8 0.1 pad_add_fusion.place_ref
  21.8 15.0 %all-to-all-done = bf16[128,8,512]{2,1,0:T(8,128)(2,1)S(1)} async-done(((bf16[128,8,512]{2,1,0:T(8,128)(2,1)}), bf16[128,8,512]{2,1,0:T(8,128)(2,1)S(1)}, u32[]{:S(2)}, u32[]{:S(2)}) %all-to-all-start) | async-done | bytes 1048608 | tf_op jit(solution)/shard_map/all_to_all | solution.py:459
  36.9 0.0 copy-start.8
  36.9 3.5 %pool.1 = (bf16[1024,256]{1,0:T(8,128)(2,1)S(1)}, bf16[448,256]{1,0:T(8,128)(2,1)S(1)}, bf16[448,256]{1,0:T(8,128)(2,1)S(1)}) custom-call(s32[2]{0:T(128)S(1)} %pad_add_fusion.place_ref, bf16[1024,512]{1,0:T(8,128)(2,1)S(1)} %bitcast.18, bf16[256,256]{1,0:T(8,128)(2,1)S(1)} %get-tuple-element.24.coarse_ref), custom_call_target="tpu_custom_call" | custom-call | flops 2147483648 | bytes 4000000 | tf_op jit(solution)/shard_map/pool/pallas_call | solution.py:35
  40.3 1.7 %collective-permute-start = (bf16[448,256]{1,0:T(8,128)(2,1)S(1)}, bf16[448,256]{1,0:T(8,128)(2,1)S(1)}, u32[]{:S(2)}, u32[]{:S(2)}) collective-permute-start(bf16[448,256]{1,0:T(8,128)(2,1)S(1)} %get-tuple-element.26), channel_id=1, source_target_pairs={{0,16},{16,32},{32,48},{48,64},{64,80},{80,96},{96,112},{112,0},{1... | collective-permute-start | bytes 688136 | tf_op jit(solution)/shard_map/ppermute | solution.py:455
  42.1 0.0 collective-permute-start.1
  42.1 3.0 %collective-permute-done.low_ref.x_low = bf16[448,256]{1,0:T(8,128)(2,1)S(1)} collective-permute-done((bf16[448,256]{1,0:T(8,128)(2,1)S(1)}, bf16[448,256]{1,0:T(8,128)(2,1)S(1)}, u32[]{:S(2)}, u32[]{:S(2)}) %collective-permute-start) | collective-permute-done | bytes 229408 | tf_op jit(solution)/shard_map/ppermute | solution.py:455
  45.0 2.8 %collective-permute-done.1.high_ref.x_high = bf16[448,256]{1,0:T(8,128)(2,1)S(1)} collective-permute-done((bf16[448,256]{1,0:T(8,128)(2,1)S(1)}, bf16[448,256]{1,0:T(8,128)(2,1)S(1)}, u32[]{:S(2)}, u32[]{:S(2)}) %collective-permute-start.1) | collective-permute-done | bytes 229408 | tf_op jit(solution)/shard_map/ppermute | solution.py:455
  47.8 0.6 edge.1
  48.4 0.7 collective-permute-start.2
  49.1 4.1 %collective-permute-start.3 = (bf16[384,256]{1,0:T(8,128)(2,1)S(1)}, bf16[384,256]{1,0:T(8,128)(2,1)S(1)}, u32[]{:S(2)}, u32[]{:S(2)}) collective-permute-start(bf16[384,256]{1,0:T(8,128)(2,1)S(1)} %get-tuple-element.29), channel_id=1, source_target_pairs={{0,15},{1,0},{2,1},{3,2},{4,3},{5,4},{6,5},{7,6},{8,7},{9,8},{10,9... | collective-permute-start | bytes 589832 | tf_op jit(solution)/shard_map/ppermute | solution.py:455
  53.3 0.0 copy-done.8
  53.3 3.1 %column.1 = (bf16[1344,256]{1,0:T(8,128)(2,1)S(1)}, f32[1344,256]{1,0:T(8,128)S(1)}) custom-call(bf16[1024,256]{1,0:T(8,128)(2,1)S(1)} %get-tuple-element.25.grid_ref, bf16[448,256]{1,0:T(8,128)(2,1)S(1)} %collective-permute-done.low_ref.x_low, bf16[448,256]{1,0:T(8,128)(2,1)S(1)} %collective-permute-done.1.high_ref.x_high, bf16[3456,256]{1,0:T(8,128)(2,1)S(1)} %copy-done.8), custom_call_target="tpu_custom_call" | custom-call | flops 3623878656 | bytes 4000000 | tf_op jit(solution)/shard_map/column/pallas_call | solution.py:35
  56.3 1.2 collective-permute-done.2.y_low
  57.6 0.0 collective-permute-done.3.y_high
  57.6 4.9 %level.1 = (bf16[256,192]{1,0:T(8,128)(2,1)}, bf16[1024,256]{1,0:T(8,128)(2,1)S(1)}, bf16[256,192]{1,0:T(8,128)(2,1)S(1)}, bf16[1440,256]{1,0:T(8,128)(2,1)S(1)}) custom-call(bf16[1024,256]{1,0:T(8,128)(2,1)S(1)} %get-tuple-element.25.grid_ref, bf16[256,256]{1,0:T(8,128)(2,1)S(1)} %get-tuple-element.24.coarse_ref, ...), custom_call_target="tpu_custom_call" | custom-call | flops 1811939328 | bytes 8000000 | tf_op jit(solution)/shard_map/level/pallas_call | solution.py:35
  62.5 0.0 copy-start.9
  62.5 4.1 %weight_grad.1 = bf16[4096,128]{1,0:T(8,128)(2,1)} custom-call(bf16[1024,256]{1,0:T(8,128)(2,1)S(1)} %get-tuple-element.25.grid_ref, bf16[448,256]{1,0:T(8,128)(2,1)S(1)} %collective-permute-done.low_ref.x_low, bf16[448,256]{1,0:T(8,128)(2,1)S(1)} %collective-permute-done.1.high_ref.x_high, bf16[384,256]{1,0:T(8,128)(2,1)S(1)} %collective-permute-done.2.y_low, ...), custom_call_target="tpu_custom_call" | custom-call | flops 1811939328 | bytes 8000000 | tf_op jit(solution)/shard_map/weight_grad/pallas_call | solution.py:35
  66.6 0.0 copy-done.9
  66.6 7.8 %all-to-all-start.1 = ((bf16[128,32,128]{2,1,0:T(8,128)(2,1)}), bf16[128,32,128]{2,1,0:T(8,128)(2,1)S(1)}, u32[]{:S(2)}, u32[]{:S(2)}) async-start(bf16[128,32,128]{2,1,0:T(8,128)(2,1)} %bitcast.10), calls=%async_computation.1 | async-start | bytes 2097152 | tf_op jit(solution)/shard_map/all_to_all | solution.py:459
  74.4 0.0 copy-start.10
  74.4 1.1 copy-done.10
  75.5 0.0 copy-start.12
  75.5 1.5 %copy-done.12 = bf16[3456,256]{1,0:T(8,128)(2,1)S(1)} copy-done((bf16[3456,256]{1,0:T(8,128)(2,1)S(1)}, bf16[3456,256]{1,0:T(8,128)(2,1)}, u32[]{:S(2)}) %copy-start.12) | copy-done | bytes 1769496
  77.0 4.5 %input_grad.1.back_ref = bf16[1024,384]{1,0:T(8,128)(2,1)S(1)} custom-call(bf16[1440,256]{1,0:T(8,128)(2,1)S(1)} %copy-done.10, bf16[3456,256]{1,0:T(8,128)(2,1)S(1)} %copy-done.12, bf16[1024,512]{1,0:T(8,128)(2,1)S(1)} %bitcast.19), custom_call_target="tpu_custom_call" | custom-call | flops 3959422976 | bytes 8000000 | tf_op jit(solution)/shard_map/input_grad/pallas_call | solution.py:35
  81.5 11.5 %all-to-all-done.1.terms_ref = bf16[128,32,128]{2,1,0:T(8,128)(2,1)S(1)} async-done(((bf16[128,32,128]{2,1,0:T(8,128)(2,1)}), bf16[128,32,128]{2,1,0:T(8,128)(2,1)S(1)}, u32[]{:S(2)}, u32[]{:S(2)}) %all-to-all-start.1) | async-done | bytes 1048608 | tf_op jit(solution)/shard_map/all_to_all | solution.py:459
  93.0 0.3 join.1
  93.3 25.8 %all_to_all.15 = bf16[128,8,640]{2,1,0:T(8,128)(2,1)S(1)} all-to-all(bf16[128,8,640]{2,1,0:T(8,128)(2,1)S(1)} %bitcast.17), channel_id=1, replica_groups=mesh['gx'=8,'gy'=16] {'gx','gy'}, dimensions={0} | all-to-all | bytes 2621440 | tf_op jit(solution)/shard_map/all_to_all | solution.py:459
  119.1 1.6 %collective-permute-start.4 = (bf16[1024,256]{1,0:T(8,128)(2,1)S(1)}, bf16[1024,256]{1,0:T(8,128)(2,1)S(1)}, u32[]{:S(2)}, u32[]{:S(2)}) collective-permute-start(bf16[1024,256]{1,0:T(8,128)(2,1)S(1)} %slice.4), channel_id=1, source_target_pairs={{0,16},{16,0},{32,48},{48,32},{64,80},{80,64},{96,112},{112,96},{1... | collective-permute-start | bytes 1572872 | tf_op jit(solution)/shard_map/ppermute | solution.py:602
  120.6 2.7 %collect.1 = bf16[96,2048]{1,0:T(8,128)(2,1)} custom-call(bf16[1024,640]{1,0:T(8,128)(2,1)S(1)} %bitcast.15, s32[2,2048]{1,0:T(2,128)S(1)} %get-tuple-element.39.slot_ref), custom_call_target="tpu_custom_call" | custom-call | flops 2147483648 | bytes 4000000 | tf_op jit(solution)/shard_map/collect/pallas_call | solution.py:35
  123.4 0.0 collective-permute-done.4.theirs_ref
  123.4 2.1 %unpack.1 = (f32[27,96,96]{2,1,0:T(8,128)}, f32[8,96,192]{2,1,0:T(8,128)}) custom-call(s32[2]{0:T(128)S(1)} %pad_add_fusion.place_ref, bf16[1024,640]{1,0:T(8,128)(2,1)S(1)} %bitcast.16, bf16[1024,256]{1,0:T(8,128)(2,1)S(1)} %collective-permute-done.4.theirs_ref), custom_call_target="tpu_custom_call" | custom-call | bytes 4000000 | tf_op jit(solution)/shard_map/unpack/pallas_call | solution.py:35
  (1 shorter events, 0.0 us)
Async XLA Ops:
  0.6 1.0 copy-start.1
  1.6 0.7 copy-start.5
  2.3 0.7 copy-start.6
  6.7 11.5 %copy-start = (bf16[27,96,96]{2,1,0:T(8,128)(2,1)S(1)}, bf16[27,96,96]{2,1,0:T(8,128)(2,1)}, u32[]{:S(2)}) copy-start(bf16[27,96,96]{2,1,0:T(8,128)(2,1)} %conv_ref.1) | copy-start | bytes 1492996
  6.7 11.5 %copy-start.2 = (bf16[8,96,192]{2,1,0:T(8,128)(2,1)S(1)}, bf16[8,96,192]{2,1,0:T(8,128)(2,1)}, u32[]{:S(2)}) copy-start(bf16[8,96,192]{2,1,0:T(8,128)(2,1)} %down_ref.1) | copy-start | bytes 884740
  6.7 11.5 %copy-start.3 = (bf16[4,8,8,192]{3,2,1,0:T(8,128)(2,1)S(1)}, bf16[4,8,8,192]{3,2,1,0:T(8,128)(2,1)}, u32[]{:S(2)}) copy-start(bf16[4,8,8,192]{3,2,1,0:T(8,128)(2,1)} %param.13) | copy-start | bytes 294916
  6.7 11.5 %copy-start.4 = (s32[8,16,16]{2,1,0:T(8,128)S(1)}, s32[8,16,16]{2,1,0:T(8,128)}, u32[]{:S(2)}) copy-start(s32[8,16,16]{2,1,0:T(8,128)} %param.10) | copy-start | bytes 24580
  6.7 30.1 %all-to-all-start = ((bf16[128,8,512]{2,1,0:T(8,128)(2,1)}), bf16[128,8,512]{2,1,0:T(8,128)(2,1)S(1)}, u32[]{:S(2)}, u32[]{:S(2)}) async-start(bf16[128,8,512]{2,1,0:T(8,128)(2,1)} %bitcast.5), calls=%async_computation | async-start | bytes 2097152 | tf_op jit(solution)/shard_map/all_to_all | solution.py:459
  19.3 1.2 copy-start.7
  20.6 1.2 copy-start.11
  36.9 16.4 %copy-start.8 = (bf16[3456,256]{1,0:T(8,128)(2,1)S(1)}, bf16[3456,256]{1,0:T(8,128)(2,1)}, u32[]{:S(2)}) copy-start(bf16[3456,256]{1,0:T(8,128)(2,1)} %copy-done.7) | copy-start | bytes 5308420
  40.3 4.7 %collective-permute-start = (bf16[448,256]{1,0:T(8,128)(2,1)S(1)}, bf16[448,256]{1,0:T(8,128)(2,1)S(1)}, u32[]{:S(2)}, u32[]{:S(2)}) collective-permute-start(bf16[448,256]{1,0:T(8,128)(2,1)S(1)} %get-tuple-element.26), channel_id=1, source_target_pairs={{0,16},{16,32},{32,48},{48,64},{64,80},{80,96},{96,112},{112,0},{1... | collective-permute-start | bytes 688136 | tf_op jit(solution)/shard_map/ppermute | solution.py:455
  42.1 5.7 %collective-permute-start.1 = (bf16[448,256]{1,0:T(8,128)(2,1)S(1)}, bf16[448,256]{1,0:T(8,128)(2,1)S(1)}, u32[]{:S(2)}, u32[]{:S(2)}) collective-permute-start(bf16[448,256]{1,0:T(8,128)(2,1)S(1)} %get-tuple-element.27), channel_id=1, source_target_pairs={{0,112},{16,0},{32,16},{48,32},{64,48},{80,64},{96,80},{112,96},{1... | collective-permute-start | bytes 688136 | tf_op jit(solution)/shard_map/ppermute | solution.py:455
  48.4 9.1 %collective-permute-start.2 = (bf16[384,256]{1,0:T(8,128)(2,1)S(1)}, bf16[384,256]{1,0:T(8,128)(2,1)S(1)}, u32[]{:S(2)}, u32[]{:S(2)}) collective-permute-start(bf16[384,256]{1,0:T(8,128)(2,1)S(1)} %get-tuple-element.28), channel_id=1, source_target_pairs={{0,1},{1,2},{2,3},{3,4},{4,5},{5,6},{6,7},{7,8},{8,9},{9,10},{10,1... | collective-permute-start | bytes 589832 | tf_op jit(solution)/shard_map/ppermute | solution.py:455
  49.1 8.4 %collective-permute-start.3 = (bf16[384,256]{1,0:T(8,128)(2,1)S(1)}, bf16[384,256]{1,0:T(8,128)(2,1)S(1)}, u32[]{:S(2)}, u32[]{:S(2)}) collective-permute-start(bf16[384,256]{1,0:T(8,128)(2,1)S(1)} %get-tuple-element.29), channel_id=1, source_target_pairs={{0,15},{1,0},{2,1},{3,2},{4,3},{5,4},{6,5},{7,6},{8,7},{9,8},{10,9... | collective-permute-start | bytes 589832 | tf_op jit(solution)/shard_map/ppermute | solution.py:455
  62.5 4.1 %copy-start.9 = (bf16[1440,256]{1,0:T(8,128)(2,1)}, bf16[1440,256]{1,0:T(8,128)(2,1)S(1)}, u32[]{:S(2)}) copy-start(bf16[1440,256]{1,0:T(8,128)(2,1)S(1)} %get-tuple-element.37.delta_ref) | copy-start | bytes 2211844
  66.6 26.4 %all-to-all-start.1 = ((bf16[128,32,128]{2,1,0:T(8,128)(2,1)}), bf16[128,32,128]{2,1,0:T(8,128)(2,1)S(1)}, u32[]{:S(2)}, u32[]{:S(2)}) async-start(bf16[128,32,128]{2,1,0:T(8,128)(2,1)} %bitcast.10), calls=%async_computation.1 | async-start | bytes 2097152 | tf_op jit(solution)/shard_map/all_to_all | solution.py:459
  74.4 1.1 copy-start.10
  75.5 1.5 %copy-start.12 = (bf16[3456,256]{1,0:T(8,128)(2,1)S(1)}, bf16[3456,256]{1,0:T(8,128)(2,1)}, u32[]{:S(2)}) copy-start(bf16[3456,256]{1,0:T(8,128)(2,1)} %copy-done.11) | copy-start | bytes 5308420
  119.1 4.3 %collective-permute-start.4 = (bf16[1024,256]{1,0:T(8,128)(2,1)S(1)}, bf16[1024,256]{1,0:T(8,128)(2,1)S(1)}, u32[]{:S(2)}, u32[]{:S(2)}) collective-permute-start(bf16[1024,256]{1,0:T(8,128)(2,1)S(1)} %slice.4), channel_id=1, source_target_pairs={{0,16},{16,0},{32,48},{48,32},{64,80},{80,64},{96,112},{112,96},{1... | collective-permute-start | bytes 1572872 | tf_op jit(solution)/shard_map/ppermute | solution.py:602

commit v5 on v4

--- a/solution.py
+++ b/solution.py
@@ -40,7 +40,7 @@
         ],
         out_specs=jax.tree.map(lambda _: pl.BlockSpec(memory_space=pltpu.VMEM), outs),
         scratch_shapes=list(scratch),
-        compiler_params=pltpu.CompilerParams(vmem_limit_bytes=48 * 1024 * 1024),
+        compiler_params=pltpu.CompilerParams(vmem_limit_bytes=24 * 1024 * 1024),
         cost_estimate=pl.CostEstimate(
             flops=flops, bytes_accessed=megabytes * 1000000, transcendentals=0
         ),
@@ -333,8 +333,8 @@
 
 
 def weight_grad_kernel(
-    grid_ref, x_low, x_high, y_low, y_high, fine_ref, delta_coarse_ref, delta_ref,
-    out_ref, pad_ref, four_ref, delta_s, fine_s, *, channels, fields, scale,
+    place_ref, grid_ref, x_low, x_high, y_low, y_high, fine_ref, delta_coarse_ref, delta_ref,
+    keep_ref, give_ref, pad_ref, four_ref, delta_s, fine_s, out_ref, *, channels, fields, scale,
 ):
     (ext_x, ext_y, half, rim), _ = fields
     long = ext_x + 2 * rim
@@ -353,7 +353,7 @@
     for j, part in enumerate(windows(four_ref, 0, ext_x, 0, ext_y)):
         grad = mm(turned, part)
         grad = grad[:LANE, :three] + grad[LANE:, channels:]
-        out_ref[j * three : (j + 1) * three, :] = (grad.T * scale).astype(BF16)
+        out_ref[j * three : (j + 1) * three, :] = grad.T * scale
     fine_s[...] = fine_ref[...].astype(F32).reshape(fine_s.shape)
     coarse_rows = ext_x // 2 * (ext_y // 2) * half
     base = 27 * channels
@@ -362,13 +362,22 @@
         grad = mm(piece, delta_coarse_ref[...], TN) * scale
         first, second = grad[:channels], grad[LANE : LANE + channels]
         start = base + 2 * j * channels
-        out_ref[start : start + channels, :] = first[:, :LANE].astype(BF16)
-        out_ref[start + channels : start + 2 * channels, :] = second[:, :LANE].astype(BF16)
+        out_ref[start : start + channels, :] = first[:, :LANE]
+        out_ref[start + channels : start + 2 * channels, :] = second[:, :LANE]
         start = base + (8 + j) * channels
         tail = jnp.concatenate([first[:, LANE:], second[:, LANE:]], axis=1)
-        out_ref[start : start + channels, :] = tail.astype(BF16)
+        out_ref[start : start + channels, :] = tail
     end = base + 12 * channels
-    out_ref[end:, :] = jnp.zeros((out_ref.shape[0] - end, LANE), BF16)
+    out_ref[end:, :] = jnp.zeros((out_ref.shape[0] - end, LANE), F32)
+    size = keep_ref.shape[0]
+    core = place_ref[0] % 2
+    keep_ref[...] = out_ref[pl.ds(pl.multiple_of(core * size, size), size), :]
+    give = out_ref[pl.ds(pl.multiple_of((1 - core) * size, size), size), :]
+    give_ref[...] = give.astype(BF16)
+
+
+def pair_kernel(keep_ref, other_ref, out_ref):
+    out_ref[...] = (keep_ref[...] + other_ref[...].astype(F32)).astype(BF16)
 
 
 def input_grad_kernel(delta_ref, conv_ref, got_ref, back_ref, pad_ref, four_ref, grad_s, *, channels):
@@ -426,18 +435,22 @@
         out_ref[:, start : start + step] = total.astype(BF16)
 
 
-def unpack_kernel(place_ref, mine_ref, theirs_ref, conv_ref, down_ref, all_s, *, block):
+def unpack_kernel(place_ref, mine_ref, theirs_ref, conv_ref, down_ref, all_s, *, block, per_axis):
     channels = conv_ref.shape[1]
-    devices, count = all_s.shape[0], all_s.shape[1] // 2
+    count = all_s.shape[2] // 2
     skip = mine_ref.shape[1] - theirs_ref.shape[1]
     swap = place_ref[0] % 2 == 1
-    for k in range(count):
-        mine = mine_ref[:, skip + k * LANE : skip + (k + 1) * LANE].astype(F32)
-        theirs = theirs_ref[:, k * LANE : (k + 1) * LANE].astype(F32)
-        shape = (devices, block, LANE)
-        all_s[:, k] = jnp.where(swap, theirs, mine).reshape(shape)
-        all_s[:, count + k] = jnp.where(swap, mine, theirs).reshape(shape)
-    whole = all_s[...].reshape(devices * 2 * count * block, LANE)
+    step = block * per_axis
+    for g in range(mine_ref.shape[0] // step):
+        rows = slice(g * step, (g + 1) * step)
+        chips = slice(g // 2 * per_axis, (g // 2 + 1) * per_axis)
+        for k in range(count):
+            mine = mine_ref[rows, skip + k * LANE : skip + (k + 1) * LANE].astype(F32)
+            theirs = theirs_ref[rows, k * LANE : (k + 1) * LANE].astype(F32)
+            shape = (per_axis, block, LANE)
+            all_s[g % 2, chips, k] = jnp.where(swap, theirs, mine).reshape(shape)
+            all_s[g % 2, chips, count + k] = jnp.where(swap, mine, theirs).reshape(shape)
+    whole = all_s[...].reshape(mine_ref.shape[0] // block * 2 * count * block, LANE)
     base = 27 * channels
     for j in range(27):
         conv_ref[j] = whole[j * channels : (j + 1) * channels, :channels]
@@ -455,8 +468,12 @@
     return lax.ppermute(block, axis, [(i, (i + step) % count) for i in range(count)])
 
 
-def exchange(blocks):
-    return lax.all_to_all(blocks, AXES, split_axis=0, concat_axis=0, tiled=True)
+def to_other_core(block):
+    return lax.ppermute(block, "gx", [(i, i ^ 1) for i in range(lax.axis_size("gx"))])
+
+
+def exchange(blocks, **groups):
+    return lax.all_to_all(blocks, AXES, split_axis=0, concat_axis=0, tiled=True, **groups)
 
 
 def shards(point_feats, point_owner, point_cell, occupancy, w_conv, w_down, cotangent):
@@ -559,21 +576,32 @@
     )
     used = 39 * channels
     chunk = -(-used // (32 * devices)) * 32
-    packed = call(
+    half_rows = devices // 2 * chunk
+    keep, give = call(
         functools.partial(weight_grad_kernel, channels=channels, fields=fields, scale=scale),
-        struct((devices * chunk, LANE), BF16),
-        (grid, *faces, fine, delta_coarse, delta),
+        (struct((half_rows, LANE), F32), struct((half_rows, LANE), BF16)),
+        (place, grid, *faces, fine, delta_coarse, delta),
         "weight_grad",
         scratch=[
             pltpu.VMEM((*near, WIDE), F32),
             pltpu.VMEM((*near, four), F32),
             pltpu.VMEM((*near, WIDE), F32),
             pltpu.VMEM((coarse_x, 2, coarse_y, 2, half, WIDE), F32),
+            pltpu.VMEM((2 * half_rows, LANE), F32),
         ],
         flops=conv_flops,
         megabytes=8,
     )
-    terms = exchange(packed.reshape(devices, chunk, LANE))
+    both = call(
+        pair_kernel, struct((half_rows, LANE), BF16), (keep, to_other_core(give)), "pair"
+    )
+    terms = exchange(
+        both.reshape(devices // 2, chunk, LANE),
+        axis_index_groups=[
+            [x * count_y + y for x in range(core, count_x, 2) for y in range(count_y)]
+            for core in range(2)
+        ],
+    )
     back = call(
         functools.partial(input_grad_kernel, channels=channels),
         struct((slot_rows, PACK * channels), BF16),
@@ -599,9 +627,7 @@
     returned = exchange(joined.reshape(devices, block, joined_lanes)).reshape(
         slot_rows, joined_lanes
     )
-    theirs = lax.ppermute(
-        returned[:, PACK * channels :], "gx", [(i, i ^ 1) for i in range(count_x)]
-    )
+    theirs = to_other_core(returned[:, PACK * channels :])
     grad_points = call(
         collect_kernel,
         struct((channels, points), BF16),
@@ -610,11 +636,11 @@
         flops=2 * points * slot_rows * PACK * LANE,
     ).T
     grad_conv, grad_down = call(
-        functools.partial(unpack_kernel, block=block),
+        functools.partial(unpack_kernel, block=block, per_axis=count_y),
         (struct(w_conv.shape, F32), struct(w_down.shape, F32)),
         (place, returned, theirs),
         "unpack",
-        scratch=[pltpu.VMEM((devices, chunk // block, block, LANE), F32)],
+        scratch=[pltpu.VMEM((2, devices // 2, chunk // block, block, LANE), F32)],
     )
     return (
         features.reshape(coarse_x, coarse_y, half, coarse),

time: 126 us -> 123 us (0.976)
  waiting for transfers between devices: 33.5 us -> 29 us
  starting transfers between devices: 27.4 us -> 29.1 us
    all_to_all x2, waiting for transfers between devices: 26.5 us -> 20.5 us  [exchange(): lax.all_to_all(blocks, AXES, split_axis=0, concat_axis=0, tiled=True, **g...]
    ppermute x1 -> x2, starting transfers between devices: 1.57 us -> 3.21 us  [to_other_core(): lax.ppermute(block, 'gx', [(i, i ^ 1) for i in range(lax.axis_size('gx'))])]
    ppermute x1 -> x2, waiting for transfers between devices: 0.01 us -> 1.54 us  [to_other_core(): lax.ppermute(block, 'gx', [(i, i ^ 1) for i in range(lax.axis_size('gx'))])]
    pallas_call x11 -> x12, Pallas kernels: 30.5 us -> 29.7 us  [call(): pl.pallas_call(kernel, out_shape=outs, in_specs=[pl.BlockSpec(memory_spac...]
  transfers between devices with their start and end apart: 7 -> 8, of which waited for: 5 -> 6; matrix products, arithmetic and copies ran while one was open for 0% -> 0% of each run, Pallas kernels for 9% -> 9%
where the time goes in v5:
time: 123 us; the launch traced here: 122 us
  Pallas kernels  29.7 us (24%)
  starting transfers between devices  29.1 us (24%)
  waiting for transfers between devices  29 us (24%)
  blocking collectives  26.3 us (21%)
  local copies, waits for them, and re-layouts  7.13 us (6%)
    pallas_call x12, Pallas kernels, call(): pl.pallas_call(kernel, out_shape=outs, in_specs=[pl.BlockSpec(memory_spac...  29.7 us
    all_to_all x1, blocking collectives, exchange(): lax.all_to_all(blocks, AXES, split_axis=0, concat_axis=0, tiled=True, **g...  26.3 us
    all_to_all x2, waiting for transfers between devices, exchange(): lax.all_to_all(blocks, AXES, split_axis=0, concat_axis=0, tiled=True, **g...  20.5 us
    all_to_all x2, starting transfers between devices, exchange(): lax.all_to_all(blocks, AXES, split_axis=0, concat_axis=0, tiled=True, **g...  19.3 us
    unnamed x26, local copies, waits for them, and re-layouts  7.1 us
    ppermute x4, waiting for transfers between devices, shift(): lax.ppermute(block, axis, [(i, (i + step) % count) for i in range(count)])  6.96 us
    ppermute x4, starting transfers between devices, shift(): lax.ppermute(block, axis, [(i, (i + step) % count) for i in range(count)])  6.59 us
    ppermute x2, starting transfers between devices, to_other_core(): lax.ppermute(block, 'gx', [(i, i ^ 1) for i in range(lax.axis_size('gx'))])  3.21 us
  transfers between devices with their start and end apart: 8, of which 6 were waited for; matrix products, arithmetic and copies ran while one was open for 0% of the time, Pallas kernels for 9%

profile of v5, /device:TPU:1, one launch (start us, length us, event | category | flops | bytes accessed | tf_op | source)
XLA Modules:
  0.0 122.1 jit_solution(16099342182147529540)
XLA Ops:
  0.6 0.0 copy-start.1
  0.6 1.0 copy-done.1
  1.6 0.0 copy-start.5
  1.6 0.7 copy-done.5
  2.3 0.0 copy-start.6
  2.3 0.7 copy-done.6
  3.0 3.7 %dispatch.1 = (bf16[1024,512]{1,0:T(8,128)(2,1)}, s32[2,2048]{1,0:T(2,128)S(1)}) custom-call(bf16[96,2048]{1,0:T(8,128)(2,1)S(1)} %bitcast.20, s32[1,2048]{1,0:T(1,128)S(1)} %bitcast.23, s32[1,2048]{1,0:T(1,128)S(1)} %bitcast.24), custom_call_target="tpu_custom_call" | custom-call | flops 2147483648 | bytes 4000000 | tf_op jit(solution)/shard_map/dispatch/pallas_call | solution.py:35
  6.7 0.0 copy-start
  6.7 0.0 copy-start.2
  6.7 0.0 copy-start.3
  6.7 0.0 copy-start.4
  6.7 11.5 %all-to-all-start = ((bf16[128,8,512]{2,1,0:T(8,128)(2,1)}), bf16[128,8,512]{2,1,0:T(8,128)(2,1)S(1)}, u32[]{:S(2)}, u32[]{:S(2)}) async-start(bf16[128,8,512]{2,1,0:T(8,128)(2,1)} %bitcast.5), calls=%async_computation | async-start | bytes 2097152 | tf_op jit(solution)/shard_map/all_to_all | solution.py:476
  18.2 0.0 copy-done
  18.2 0.0 copy-done.2
  18.3 0.0 copy-done.3
  18.3 0.0 copy-done.4
  18.3 1.0 prepare.1
  19.3 0.0 copy-start.7
  19.3 1.2 %copy-done.7 = bf16[3456,256]{1,0:T(8,128)(2,1)} copy-done((bf16[3456,256]{1,0:T(8,128)(2,1)}, bf16[3456,256]{1,0:T(8,128)(2,1)S(1)}, u32[]{:S(2)}) %copy-start.7) | copy-done | bytes 1769496
  20.5 0.0 copy-start.9
  20.5 0.8 copy-done.9
  21.3 0.0 copy-start.11
  21.3 1.2 copy-done.11
  22.5 0.1 pad_add_fusion.place_ref
  22.6 14.2 %all-to-all-done = bf16[128,8,512]{2,1,0:T(8,128)(2,1)S(1)} async-done(((bf16[128,8,512]{2,1,0:T(8,128)(2,1)}), bf16[128,8,512]{2,1,0:T(8,128)(2,1)S(1)}, u32[]{:S(2)}, u32[]{:S(2)}) %all-to-all-start) | async-done | bytes 1048608 | tf_op jit(solution)/shard_map/all_to_all | solution.py:476
  36.9 0.0 copy-start.8
  36.9 3.5 %pool.1 = (bf16[1024,256]{1,0:T(8,128)(2,1)S(1)}, bf16[448,256]{1,0:T(8,128)(2,1)S(1)}, bf16[448,256]{1,0:T(8,128)(2,1)S(1)}) custom-call(s32[2]{0:T(128)S(1)} %pad_add_fusion.place_ref, bf16[1024,512]{1,0:T(8,128)(2,1)S(1)} %bitcast.18, bf16[256,256]{1,0:T(8,128)(2,1)S(1)} %get-tuple-element.26.coarse_ref), custom_call_target="tpu_custom_call" | custom-call | flops 2147483648 | bytes 4000000 | tf_op jit(solution)/shard_map/pool/pallas_call | solution.py:35
  40.3 1.7 %collective-permute-start = (bf16[448,256]{1,0:T(8,128)(2,1)S(1)}, bf16[448,256]{1,0:T(8,128)(2,1)S(1)}, u32[]{:S(2)}, u32[]{:S(2)}) collective-permute-start(bf16[448,256]{1,0:T(8,128)(2,1)S(1)} %get-tuple-element.28), channel_id=1, source_target_pairs={{0,16},{16,32},{32,48},{48,64},{64,80},{80,96},{96,112},{112,0},{1... | collective-permute-start | bytes 688136 | tf_op jit(solution)/shard_map/ppermute | solution.py:468
  42.1 0.0 collective-permute-start.1
  42.1 3.0 %collective-permute-done.low_ref.x_low = bf16[448,256]{1,0:T(8,128)(2,1)S(1)} collective-permute-done((bf16[448,256]{1,0:T(8,128)(2,1)S(1)}, bf16[448,256]{1,0:T(8,128)(2,1)S(1)}, u32[]{:S(2)}, u32[]{:S(2)}) %collective-permute-start) | collective-permute-done | bytes 229408 | tf_op jit(solution)/shard_map/ppermute | solution.py:468
  45.0 2.8 %collective-permute-done.1.high_ref.x_high = bf16[448,256]{1,0:T(8,128)(2,1)S(1)} collective-permute-done((bf16[448,256]{1,0:T(8,128)(2,1)S(1)}, bf16[448,256]{1,0:T(8,128)(2,1)S(1)}, u32[]{:S(2)}, u32[]{:S(2)}) %collective-permute-start.1) | collective-permute-done | bytes 229408 | tf_op jit(solution)/shard_map/ppermute | solution.py:468
  47.8 0.6 edge.1
  48.4 0.7 collective-permute-start.2
  49.1 4.1 %collective-permute-start.3 = (bf16[384,256]{1,0:T(8,128)(2,1)S(1)}, bf16[384,256]{1,0:T(8,128)(2,1)S(1)}, u32[]{:S(2)}, u32[]{:S(2)}) collective-permute-start(bf16[384,256]{1,0:T(8,128)(2,1)S(1)} %get-tuple-element.31), channel_id=1, source_target_pairs={{0,15},{1,0},{2,1},{3,2},{4,3},{5,4},{6,5},{7,6},{8,7},{9,8},{10,9... | collective-permute-start | bytes 589832 | tf_op jit(solution)/shard_map/ppermute | solution.py:468
  53.3 0.0 copy-done.8
  53.3 0.0 copy-start.10
  53.3 3.1 %column.1 = (bf16[1344,256]{1,0:T(8,128)(2,1)S(1)}, f32[1344,256]{1,0:T(8,128)S(1)}) custom-call(bf16[1024,256]{1,0:T(8,128)(2,1)S(1)} %get-tuple-element.27.grid_ref, bf16[448,256]{1,0:T(8,128)(2,1)S(1)} %collective-permute-done.low_ref.x_low, bf16[448,256]{1,0:T(8,128)(2,1)S(1)} %collective-permute-done.1.high_ref.x_high, bf16[3456,256]{1,0:T(8,128)(2,1)S(1)} %copy-done.8), custom_call_target="tpu_custom_call" | custom-call | flops 3623878656 | bytes 4000000 | tf_op jit(solution)/shard_map/column/pallas_call | solution.py:35
  56.3 1.2 collective-permute-done.2.y_low
  57.6 0.0 collective-permute-done.3.y_high
  57.6 0.0 copy-done.10
  57.6 3.5 %level.1 = (bf16[256,192]{1,0:T(8,128)(2,1)}, bf16[1024,256]{1,0:T(8,128)(2,1)S(1)}, bf16[256,192]{1,0:T(8,128)(2,1)S(1)}, bf16[1440,256]{1,0:T(8,128)(2,1)S(1)}) custom-call(bf16[1024,256]{1,0:T(8,128)(2,1)S(1)} %get-tuple-element.27.grid_ref, bf16[256,256]{1,0:T(8,128)(2,1)S(1)} %get-tuple-element.26.coarse_ref, ...), custom_call_target="tpu_custom_call" | custom-call | flops 1811939328 | bytes 8000000 | tf_op jit(solution)/shard_map/level/pallas_call | solution.py:35
  61.0 4.0 %weight_grad.1 = (f32[2048,128]{1,0:T(8,128)S(1)}, bf16[2048,128]{1,0:T(8,128)(2,1)S(1)}) custom-call(s32[2]{0:T(128)S(1)} %pad_add_fusion.place_ref, bf16[1024,256]{1,0:T(8,128)(2,1)S(1)} %get-tuple-element.27.grid_ref, bf16[448,256]{1,0:T(8,128)(2,1)S(1)} %collective-permute-done.low_ref.x_low, ...), custom_call_target="tpu_custom_call" | custom-call | flops 1811939328 | bytes 8000000 | tf_op jit(solution)/shard_map/weight_grad/pallas_call | solution.py:35
  65.0 1.6 %collective-permute-start.4 = (bf16[2048,128]{1,0:T(8,128)(2,1)S(1)}, bf16[2048,128]{1,0:T(8,128)(2,1)S(1)}, u32[]{:S(2)}, u32[]{:S(2)}) collective-permute-start(bf16[2048,128]{1,0:T(8,128)(2,1)S(1)} %get-tuple-element.41), channel_id=1, source_target_pairs={{0,16},{16,0},{32,48},{48,32},{64,80},{80,64},{96,112},{112,96},{1... | collective-permute-start | bytes 1572872 | tf_op jit(solution)/shard_map/ppermute | solution.py:472
  66.7 1.5 %collective-permute-done.4.other_ref = bf16[2048,128]{1,0:T(8,128)(2,1)S(1)} collective-permute-done((bf16[2048,128]{1,0:T(8,128)(2,1)S(1)}, bf16[2048,128]{1,0:T(8,128)(2,1)S(1)}, u32[]{:S(2)}, u32[]{:S(2)}) %collective-permute-start.4) | collective-permute-done | bytes 524320 | tf_op jit(solution)/shard_map/ppermute | solution.py:472
  68.2 0.9 pair.1
  69.1 7.8 %all-to-all-start.1 = ((bf16[64,32,128]{2,1,0:T(8,128)(2,1)}), bf16[64,32,128]{2,1,0:T(8,128)(2,1)S(1)}, u32[]{:S(2)}, u32[]{:S(2)}) async-start(bf16[64,32,128]{2,1,0:T(8,128)(2,1)} %bitcast.10), calls=%async_computation.1 | async-start | bytes 1048576 | tf_op jit(solution)/shard_map/all_to_all | solution.py:476
  77.0 0.0 copy-start.12
  77.0 1.5 %copy-done.12 = bf16[3456,256]{1,0:T(8,128)(2,1)S(1)} copy-done((bf16[3456,256]{1,0:T(8,128)(2,1)S(1)}, bf16[3456,256]{1,0:T(8,128)(2,1)}, u32[]{:S(2)}) %copy-start.12) | copy-done | bytes 1769496
  78.5 4.5 %input_grad.1.back_ref = bf16[1024,384]{1,0:T(8,128)(2,1)S(1)} custom-call(bf16[1440,256]{1,0:T(8,128)(2,1)S(1)} %get-tuple-element.39.delta_ref, bf16[3456,256]{1,0:T(8,128)(2,1)S(1)} %copy-done.12, bf16[1024,512]{1,0:T(8,128)(2,1)S(1)} %bitcast.19), custom_call_target="tpu_custom_call" | custom-call | flops 3959422976 | bytes 8000000 | tf_op jit(solution)/shard_map/input_grad/pallas_call | solution.py:35
  83.0 6.3 %all-to-all-done.1.terms_ref = bf16[64,32,128]{2,1,0:T(8,128)(2,1)S(1)} async-done(((bf16[64,32,128]{2,1,0:T(8,128)(2,1)}), bf16[64,32,128]{2,1,0:T(8,128)(2,1)S(1)}, u32[]{:S(2)}, u32[]{:S(2)}) %all-to-all-start.1) | async-done | bytes 524320 | tf_op jit(solution)/shard_map/all_to_all | solution.py:476
  89.2 0.2 join.1
  89.4 26.3 %all_to_all.15 = bf16[128,8,640]{2,1,0:T(8,128)(2,1)S(1)} all-to-all(bf16[128,8,640]{2,1,0:T(8,128)(2,1)S(1)} %bitcast.17), channel_id=1, replica_groups=mesh['gx'=8,'gy'=16] {'gx','gy'}, dimensions={0} | all-to-all | bytes 2621440 | tf_op jit(solution)/shard_map/all_to_all | solution.py:476
  115.8 1.6 %collective-permute-start.5 = (bf16[1024,256]{1,0:T(8,128)(2,1)S(1)}, bf16[1024,256]{1,0:T(8,128)(2,1)S(1)}, u32[]{:S(2)}, u32[]{:S(2)}) collective-permute-start(bf16[1024,256]{1,0:T(8,128)(2,1)S(1)} %slice.4), channel_id=1, source_target_pairs={{0,16},{16,0},{32,48},{48,32},{64,80},{80,64},{96,112},{112,96},{1... | collective-permute-start | bytes 1572872 | tf_op jit(solution)/shard_map/ppermute | solution.py:472
  117.3 2.7 %collect.1 = bf16[96,2048]{1,0:T(8,128)(2,1)} custom-call(bf16[1024,640]{1,0:T(8,128)(2,1)S(1)} %bitcast.15, s32[2,2048]{1,0:T(2,128)S(1)} %get-tuple-element.43.slot_ref), custom_call_target="tpu_custom_call" | custom-call | flops 2147483648 | bytes 4000000 | tf_op jit(solution)/shard_map/collect/pallas_call | solution.py:35
  120.0 0.0 collective-permute-done.5.theirs_ref
  120.0 2.1 %unpack.1 = (f32[27,96,96]{2,1,0:T(8,128)}, f32[8,96,192]{2,1,0:T(8,128)}) custom-call(s32[2]{0:T(128)S(1)} %pad_add_fusion.place_ref, bf16[1024,640]{1,0:T(8,128)(2,1)S(1)} %bitcast.16, bf16[1024,256]{1,0:T(8,128)(2,1)S(1)} %collective-permute-done.5.theirs_ref), custom_call_target="tpu_custom_call" | custom-call | bytes 4000000 | tf_op jit(solution)/shard_map/unpack/pallas_call | solution.py:35
  (1 shorter events, 0.0 us)
Async XLA Ops:
  0.6 1.0 copy-start.1
  1.6 0.7 copy-start.5
  2.3 0.7 copy-start.6
  6.7 11.5 %copy-start = (bf16[27,96,96]{2,1,0:T(8,128)(2,1)S(1)}, bf16[27,96,96]{2,1,0:T(8,128)(2,1)}, u32[]{:S(2)}) copy-start(bf16[27,96,96]{2,1,0:T(8,128)(2,1)} %conv_ref.1) | copy-start | bytes 1492996
  6.7 11.5 %copy-start.2 = (bf16[8,96,192]{2,1,0:T(8,128)(2,1)S(1)}, bf16[8,96,192]{2,1,0:T(8,128)(2,1)}, u32[]{:S(2)}) copy-start(bf16[8,96,192]{2,1,0:T(8,128)(2,1)} %down_ref.1) | copy-start | bytes 884740
  6.7 11.5 %copy-start.3 = (bf16[4,8,8,192]{3,2,1,0:T(8,128)(2,1)S(1)}, bf16[4,8,8,192]{3,2,1,0:T(8,128)(2,1)}, u32[]{:S(2)}) copy-start(bf16[4,8,8,192]{3,2,1,0:T(8,128)(2,1)} %param.13) | copy-start | bytes 294916
  6.7 11.5 %copy-start.4 = (s32[8,16,16]{2,1,0:T(8,128)S(1)}, s32[8,16,16]{2,1,0:T(8,128)}, u32[]{:S(2)}) copy-start(s32[8,16,16]{2,1,0:T(8,128)} %param.10) | copy-start | bytes 24580
  6.7 30.1 %all-to-all-start = ((bf16[128,8,512]{2,1,0:T(8,128)(2,1)}), bf16[128,8,512]{2,1,0:T(8,128)(2,1)S(1)}, u32[]{:S(2)}, u32[]{:S(2)}) async-start(bf16[128,8,512]{2,1,0:T(8,128)(2,1)} %bitcast.5), calls=%async_computation | async-start | bytes 2097152 | tf_op jit(solution)/shard_map/all_to_all | solution.py:476
  19.3 1.2 %copy-start.7 = (bf16[3456,256]{1,0:T(8,128)(2,1)}, bf16[3456,256]{1,0:T(8,128)(2,1)S(1)}, u32[]{:S(2)}) copy-start(bf16[3456,256]{1,0:T(8,128)(2,1)S(1)} %get-tuple-element.32.conv_ref) | copy-start | bytes 5308420
  20.5 0.8 copy-start.9
  21.3 1.2 copy-start.11
  36.9 16.4 %copy-start.8 = (bf16[3456,256]{1,0:T(8,128)(2,1)S(1)}, bf16[3456,256]{1,0:T(8,128)(2,1)}, u32[]{:S(2)}) copy-start(bf16[3456,256]{1,0:T(8,128)(2,1)} %copy-done.7) | copy-start | bytes 5308420
  40.3 4.7 %collective-permute-start = (bf16[448,256]{1,0:T(8,128)(2,1)S(1)}, bf16[448,256]{1,0:T(8,128)(2,1)S(1)}, u32[]{:S(2)}, u32[]{:S(2)}) collective-permute-start(bf16[448,256]{1,0:T(8,128)(2,1)S(1)} %get-tuple-element.28), channel_id=1, source_target_pairs={{0,16},{16,32},{32,48},{48,64},{64,80},{80,96},{96,112},{112,0},{1... | collective-permute-start | bytes 688136 | tf_op jit(solution)/shard_map/ppermute | solution.py:468
  42.1 5.7 %collective-permute-start.1 = (bf16[448,256]{1,0:T(8,128)(2,1)S(1)}, bf16[448,256]{1,0:T(8,128)(2,1)S(1)}, u32[]{:S(2)}, u32[]{:S(2)}) collective-permute-start(bf16[448,256]{1,0:T(8,128)(2,1)S(1)} %get-tuple-element.29), channel_id=1, source_target_pairs={{0,112},{16,0},{32,16},{48,32},{64,48},{80,64},{96,80},{112,96},{1... | collective-permute-start | bytes 688136 | tf_op jit(solution)/shard_map/ppermute | solution.py:468
  48.4 9.1 %collective-permute-start.2 = (bf16[384,256]{1,0:T(8,128)(2,1)S(1)}, bf16[384,256]{1,0:T(8,128)(2,1)S(1)}, u32[]{:S(2)}, u32[]{:S(2)}) collective-permute-start(bf16[384,256]{1,0:T(8,128)(2,1)S(1)} %get-tuple-element.30), channel_id=1, source_target_pairs={{0,1},{1,2},{2,3},{3,4},{4,5},{5,6},{6,7},{7,8},{8,9},{9,10},{10,1... | collective-permute-start | bytes 589832 | tf_op jit(solution)/shard_map/ppermute | solution.py:468
  49.1 8.4 %collective-permute-start.3 = (bf16[384,256]{1,0:T(8,128)(2,1)S(1)}, bf16[384,256]{1,0:T(8,128)(2,1)S(1)}, u32[]{:S(2)}, u32[]{:S(2)}) collective-permute-start(bf16[384,256]{1,0:T(8,128)(2,1)S(1)} %get-tuple-element.31), channel_id=1, source_target_pairs={{0,15},{1,0},{2,1},{3,2},{4,3},{5,4},{6,5},{7,6},{8,7},{9,8},{10,9... | collective-permute-start | bytes 589832 | tf_op jit(solution)/shard_map/ppermute | solution.py:468
  53.3 4.3 %copy-start.10 = (bf16[4,256,192]{2,1,0:T(8,128)(2,1)S(1)}, bf16[4,256,192]{2,1,0:T(8,128)(2,1)}, u32[]{:S(2)}) copy-start(bf16[4,256,192]{2,1,0:T(8,128)(2,1)} %copy-done.9) | copy-start | bytes 1179652
  65.0 3.2 %collective-permute-start.4 = (bf16[2048,128]{1,0:T(8,128)(2,1)S(1)}, bf16[2048,128]{1,0:T(8,128)(2,1)S(1)}, u32[]{:S(2)}, u32[]{:S(2)}) collective-permute-start(bf16[2048,128]{1,0:T(8,128)(2,1)S(1)} %get-tuple-element.41), channel_id=1, source_target_pairs={{0,16},{16,0},{32,48},{48,32},{64,80},{80,64},{96,112},{112,96},{1... | collective-permute-start | bytes 1572872 | tf_op jit(solution)/shard_map/ppermute | solution.py:472
  69.1 20.1 %all-to-all-start.1 = ((bf16[64,32,128]{2,1,0:T(8,128)(2,1)}), bf16[64,32,128]{2,1,0:T(8,128)(2,1)S(1)}, u32[]{:S(2)}, u32[]{:S(2)}) async-start(bf16[64,32,128]{2,1,0:T(8,128)(2,1)} %bitcast.10), calls=%async_computation.1 | async-start | bytes 1048576 | tf_op jit(solution)/shard_map/all_to_all | solution.py:476
  77.0 1.5 %copy-start.12 = (bf16[3456,256]{1,0:T(8,128)(2,1)S(1)}, bf16[3456,256]{1,0:T(8,128)(2,1)}, u32[]{:S(2)}) copy-start(bf16[3456,256]{1,0:T(8,128)(2,1)} %copy-done.11) | copy-start | bytes 5308420
  115.8 4.3 %collective-permute-start.5 = (bf16[1024,256]{1,0:T(8,128)(2,1)S(1)}, bf16[1024,256]{1,0:T(8,128)(2,1)S(1)}, u32[]{:S(2)}, u32[]{:S(2)}) collective-permute-start(bf16[1024,256]{1,0:T(8,128)(2,1)S(1)} %slice.4), channel_id=1, source_target_pairs={{0,16},{16,0},{32,48},{48,32},{64,80},{80,64},{96,112},{112,96},{1... | collective-permute-start | bytes 1572872 | tf_op jit(solution)/shard_map/ppermute | solution.py:472

commit v6 on v5

--- a/solution.py
+++ b/solution.py
@@ -31,16 +31,24 @@
     return jnp.where(mask, 1.0, 0.0).astype(BF16)
 
 
-def call(kernel, outs, args, name, scratch=(), flops=0, megabytes=4):
+def call(
+    kernel, outs, args, name, scratch=(), flops=0, megabytes=4, far=(), far_outs=(), grant=24
+):
+    def spec(index, array, group):
+        if index in group:
+            return pl.BlockSpec(memory_space=pl.ANY)
+        scalars = array.ndim == 1
+        return pl.BlockSpec(memory_space=pltpu.SMEM if scalars else pltpu.VMEM)
+
+    single = not isinstance(outs, tuple)
+    out_specs = [spec(i, out, far_outs) for i, out in enumerate((outs,) if single else outs)]
     return pl.pallas_call(
         kernel,
         out_shape=outs,
-        in_specs=[
-            pl.BlockSpec(memory_space=pltpu.SMEM if arg.ndim == 1 else pltpu.VMEM) for arg in args
-        ],
-        out_specs=jax.tree.map(lambda _: pl.BlockSpec(memory_space=pltpu.VMEM), outs),
+        in_specs=[spec(i, arg, far) for i, arg in enumerate(args)],
+        out_specs=out_specs[0] if single else tuple(out_specs),
         scratch_shapes=list(scratch),
-        compiler_params=pltpu.CompilerParams(vmem_limit_bytes=24 * 1024 * 1024),
+        compiler_params=pltpu.CompilerParams(vmem_limit_bytes=grant * 1024 * 1024),
         cost_estimate=pl.CostEstimate(
             flops=flops, bytes_accessed=megabytes * 1000000, transcendentals=0
         ),
@@ -52,8 +60,20 @@
     return jax.ShapeDtypeStruct(shape, dtype)
 
 
-def dispatch_kernel(feats_ref, owner_ref, cell_ref, send_ref, slot_ref, *, devices, cap):
+def dispatch_kernel(
+    feats_in, owner_in, cell_in, send_out, slot_ref,
+    feats_ref, owner_ref, cell_ref, send_ref, in_sems, out_sems, *, devices, cap,
+):
+    loads = [
+        pltpu.make_async_copy(source, target, in_sems.at[i])
+        for i, (source, target) in enumerate(
+            ((owner_in, owner_ref), (cell_in, cell_ref), (feats_in, feats_ref))
+        )
+    ]
+    for load in loads:
+        load.start()
     channels, points = feats_ref.shape
+    loads[0].wait()
     owner = owner_ref[...]
     hot = iota((devices, points), 0) == owner
     block = min(256, points)
@@ -70,18 +90,29 @@
     quarter = rank & 3
     slot_ref[0:1, :] = row
     slot_ref[1:2, :] = quarter
+    loads[1].wait()
     cell = cell_ref[...]
     line = iota((LANE - channels, points), 0)
     extra = jnp.where(line == 0, cell >> 6, 0)
     extra = jnp.where(line == 1, (cell >> 1) & 31, extra)
     extra = jnp.where(line == 2, cell & 1, extra)
+    loads[2].wait()
     whole = jnp.concatenate([feats_ref[...], extra.astype(F32).astype(BF16)], axis=0)
     spread = jnp.concatenate([whole * one_hot(quarter == q) for q in range(PACK)], axis=0)
     rows = send_ref.shape[0]
     step = min(256, rows)
+    stores = []
     for start in range(0, rows, step):
         pick = one_hot(iota((step, points), 0) + start == row)
-        send_ref[start : start + step, :] = mm(pick, spread, NT).astype(BF16)
+        part = slice(start, start + step)
+        send_ref[part, :] = mm(pick, spread, NT).astype(BF16)
+        store = pltpu.make_async_copy(
+            send_ref.at[part], send_out.at[part], out_sems.at[start // step]
+        )
+        store.start()
+        stores.append(store)
+    for store in stores:
+        store.wait()
 
 
 def pool_kernel(
@@ -501,7 +532,18 @@
         (struct((slot_rows, PACK * LANE), BF16), struct((2, points), jnp.int32)),
         (point_feats.T, point_owner.reshape(1, points), point_cell.reshape(1, points)),
         "dispatch",
+        scratch=[
+            pltpu.VMEM((channels, points), BF16),
+            pltpu.VMEM((1, points), jnp.int32),
+            pltpu.VMEM((1, points), jnp.int32),
+            pltpu.VMEM((slot_rows, PACK * LANE), BF16),
+            pltpu.SemaphoreType.DMA((3,)),
+            pltpu.SemaphoreType.DMA((-(-slot_rows // 256),)),
+        ],
         flops=2 * points * slot_rows * PACK * LANE,
+        far=(0, 1, 2),
+        far_outs=(0,),
+        grant=56,
     )
     got = exchange(send.reshape(devices, block, PACK * LANE)).reshape(slot_rows, PACK * LANE)
     conv_blocks, back_blocks, down_blocks, given = call(

time: 123 us -> 121 us (0.984)
  local copies, waits for them, and re-layouts: 7.13 us -> 4.77 us
    unnamed x26 -> x22, local copies, waits for them, and re-layouts: 7.1 us -> 4.74 us
where the time goes in v6:
time: 121 us
  Pallas kernels  30.8 us (25%)
  starting transfers between devices  29.1 us (24%)
  waiting for transfers between devices  29 us (24%)
  blocking collectives  26.3 us (22%)
  local copies, waits for them, and re-layouts  4.77 us (4%)
    pallas_call x12, Pallas kernels, call(): pl.pallas_call(kernel, out_shape=outs, in_specs=[spec(i, arg, far) for i,...  30.8 us
    all_to_all x1, blocking collectives, exchange(): lax.all_to_all(blocks, AXES, split_axis=0, concat_axis=0, tiled=True, **g...  26.3 us
    all_to_all x2, waiting for transfers between devices, exchange(): lax.all_to_all(blocks, AXES, split_axis=0, concat_axis=0, tiled=True, **g...  20.5 us
    all_to_all x2, starting transfers between devices, exchange(): lax.all_to_all(blocks, AXES, split_axis=0, concat_axis=0, tiled=True, **g...  19.3 us
    ppermute x4, waiting for transfers between devices, shift(): lax.ppermute(block, axis, [(i, (i + step) % count) for i in range(count)])  6.98 us
    ppermute x4, starting transfers between devices, shift(): lax.ppermute(block, axis, [(i, (i + step) % count) for i in range(count)])  6.6 us
    unnamed x22, local copies, waits for them, and re-layouts  4.74 us
    ppermute x2, starting transfers between devices, to_other_core(): lax.ppermute(block, 'gx', [(i, i ^ 1) for i in range(lax.axis_size('gx'))])  3.2 us
  transfers between devices with their start and end apart: 8, of which 6 were waited for; matrix products, arithmetic and copies ran while one was open for 0% of the time, Pallas kernels for 9%

profile of v6, /device:TPU:1, one launch (start us, length us, event | category | flops | bytes accessed | tf_op | source)
XLA Modules:
  0.0 120.9 jit_solution(17394235927701060781)
XLA Ops:
  0.6 4.9 %dispatch.1 = (bf16[1024,512]{1,0:T(8,128)(2,1)}, s32[2,2048]{1,0:T(2,128)}) custom-call(bf16[96,2048]{1,0:T(8,128)(2,1)} %bitcast.23, s32[1,2048]{1,0:T(1,128)} %bitcast.24, s32[1,2048]{1,0:T(1,128)} %bitcast.25), custom_call_target="tpu_custom_call" | custom-call | flops 2147483648 | bytes 4000000 | tf_op jit(solution)/shard_map/dispatch/pallas_call | solution.py:45
  5.5 0.0 copy-start
  5.5 0.0 copy-start.1
  5.5 0.0 copy-start.2
  5.5 0.0 copy-start.3
  5.5 11.5 %all-to-all-start = ((bf16[128,8,512]{2,1,0:T(8,128)(2,1)}), bf16[128,8,512]{2,1,0:T(8,128)(2,1)S(1)}, u32[]{:S(2)}, u32[]{:S(2)}) async-start(bf16[128,8,512]{2,1,0:T(8,128)(2,1)} %bitcast.22), calls=%async_computation | async-start | bytes 2097152 | tf_op jit(solution)/shard_map/all_to_all | solution.py:507
  17.1 0.0 copy-done
  17.1 0.0 copy-done.1
  17.1 0.0 copy-done.2
  17.1 0.0 copy-done.3
  17.1 1.0 prepare.1
  18.1 0.0 copy-start.4
  18.1 1.2 %copy-done.4 = bf16[3456,256]{1,0:T(8,128)(2,1)} copy-done((bf16[3456,256]{1,0:T(8,128)(2,1)}, bf16[3456,256]{1,0:T(8,128)(2,1)S(1)}, u32[]{:S(2)}) %copy-start.4) | copy-done | bytes 1769496
  19.4 0.0 copy-start.6
  19.4 0.8 copy-done.6
  20.2 0.0 copy-start.8
  20.2 1.2 copy-done.8
  21.4 0.1 pad_add_fusion.place_ref
  21.5 14.2 %all-to-all-done = bf16[128,8,512]{2,1,0:T(8,128)(2,1)S(1)} async-done(((bf16[128,8,512]{2,1,0:T(8,128)(2,1)}), bf16[128,8,512]{2,1,0:T(8,128)(2,1)S(1)}, u32[]{:S(2)}, u32[]{:S(2)}) %all-to-all-start) | async-done | bytes 1048608 | tf_op jit(solution)/shard_map/all_to_all | solution.py:507
  35.7 0.0 copy-start.5
  35.7 3.5 %pool.1 = (bf16[1024,256]{1,0:T(8,128)(2,1)S(1)}, bf16[448,256]{1,0:T(8,128)(2,1)S(1)}, bf16[448,256]{1,0:T(8,128)(2,1)S(1)}) custom-call(s32[2]{0:T(128)S(1)} %pad_add_fusion.place_ref, bf16[1024,512]{1,0:T(8,128)(2,1)S(1)} %bitcast.18, bf16[256,256]{1,0:T(8,128)(2,1)S(1)} %get-tuple-element.26.coarse_ref), custom_call_target="tpu_custom_call" | custom-call | flops 2147483648 | bytes 4000000 | tf_op jit(solution)/shard_map/pool/pallas_call | solution.py:45
  39.2 1.7 %collective-permute-start = (bf16[448,256]{1,0:T(8,128)(2,1)S(1)}, bf16[448,256]{1,0:T(8,128)(2,1)S(1)}, u32[]{:S(2)}, u32[]{:S(2)}) collective-permute-start(bf16[448,256]{1,0:T(8,128)(2,1)S(1)} %get-tuple-element.28), channel_id=1, source_target_pairs={{0,16},{16,32},{32,48},{48,64},{64,80},{80,96},{96,112},{112,0},{1... | collective-permute-start | bytes 688136 | tf_op jit(solution)/shard_map/ppermute | solution.py:499
  40.9 0.0 collective-permute-start.1
  40.9 3.0 %collective-permute-done.low_ref.x_low = bf16[448,256]{1,0:T(8,128)(2,1)S(1)} collective-permute-done((bf16[448,256]{1,0:T(8,128)(2,1)S(1)}, bf16[448,256]{1,0:T(8,128)(2,1)S(1)}, u32[]{:S(2)}, u32[]{:S(2)}) %collective-permute-start) | collective-permute-done | bytes 229408 | tf_op jit(solution)/shard_map/ppermute | solution.py:499
  43.9 2.8 %collective-permute-done.1.high_ref.x_high = bf16[448,256]{1,0:T(8,128)(2,1)S(1)} collective-permute-done((bf16[448,256]{1,0:T(8,128)(2,1)S(1)}, bf16[448,256]{1,0:T(8,128)(2,1)S(1)}, u32[]{:S(2)}, u32[]{:S(2)}) %collective-permute-start.1) | collective-permute-done | bytes 229408 | tf_op jit(solution)/shard_map/ppermute | solution.py:499
  46.6 0.6 edge.1
  47.3 0.7 collective-permute-start.2
  48.0 4.1 %collective-permute-start.3 = (bf16[384,256]{1,0:T(8,128)(2,1)S(1)}, bf16[384,256]{1,0:T(8,128)(2,1)S(1)}, u32[]{:S(2)}, u32[]{:S(2)}) collective-permute-start(bf16[384,256]{1,0:T(8,128)(2,1)S(1)} %get-tuple-element.31), channel_id=1, source_target_pairs={{0,15},{1,0},{2,1},{3,2},{4,3},{5,4},{6,5},{7,6},{8,7},{9,8},{10,9... | collective-permute-start | bytes 589832 | tf_op jit(solution)/shard_map/ppermute | solution.py:499
  52.1 0.0 copy-done.5
  52.1 0.0 copy-start.7
  52.1 3.0 %column.1 = (bf16[1344,256]{1,0:T(8,128)(2,1)S(1)}, f32[1344,256]{1,0:T(8,128)S(1)}) custom-call(bf16[1024,256]{1,0:T(8,128)(2,1)S(1)} %get-tuple-element.27.grid_ref, bf16[448,256]{1,0:T(8,128)(2,1)S(1)} %collective-permute-done.low_ref.x_low, bf16[448,256]{1,0:T(8,128)(2,1)S(1)} %collective-permute-done.1.high_ref.x_high, bf16[3456,256]{1,0:T(8,128)(2,1)S(1)} %copy-done.5), custom_call_target="tpu_custom_call" | custom-call | flops 3623878656 | bytes 4000000 | tf_op jit(solution)/shard_map/column/pallas_call | solution.py:45
  55.2 1.2 %collective-permute-done.2.y_low = bf16[384,256]{1,0:T(8,128)(2,1)S(1)} collective-permute-done((bf16[384,256]{1,0:T(8,128)(2,1)S(1)}, bf16[384,256]{1,0:T(8,128)(2,1)S(1)}, u32[]{:S(2)}, u32[]{:S(2)}) %collective-permute-start.2) | collective-permute-done | bytes 196640 | tf_op jit(solution)/shard_map/ppermute | solution.py:499
  56.4 0.0 collective-permute-done.3.y_high
  56.4 0.0 copy-done.7
  56.4 3.5 %level.1 = (bf16[256,192]{1,0:T(8,128)(2,1)}, bf16[1024,256]{1,0:T(8,128)(2,1)S(1)}, bf16[256,192]{1,0:T(8,128)(2,1)S(1)}, bf16[1440,256]{1,0:T(8,128)(2,1)S(1)}) custom-call(bf16[1024,256]{1,0:T(8,128)(2,1)S(1)} %get-tuple-element.27.grid_ref, bf16[256,256]{1,0:T(8,128)(2,1)S(1)} %get-tuple-element.26.coarse_ref, ...), custom_call_target="tpu_custom_call" | custom-call | flops 1811939328 | bytes 8000000 | tf_op jit(solution)/shard_map/level/pallas_call | solution.py:45
  59.9 4.0 %weight_grad.1 = (f32[2048,128]{1,0:T(8,128)S(1)}, bf16[2048,128]{1,0:T(8,128)(2,1)S(1)}) custom-call(s32[2]{0:T(128)S(1)} %pad_add_fusion.place_ref, bf16[1024,256]{1,0:T(8,128)(2,1)S(1)} %get-tuple-element.27.grid_ref, bf16[448,256]{1,0:T(8,128)(2,1)S(1)} %collective-permute-done.low_ref.x_low, ...), custom_call_target="tpu_custom_call" | custom-call | flops 1811939328 | bytes 8000000 | tf_op jit(solution)/shard_map/weight_grad/pallas_call | solution.py:45
  63.9 1.6 %collective-permute-start.4 = (bf16[2048,128]{1,0:T(8,128)(2,1)S(1)}, bf16[2048,128]{1,0:T(8,128)(2,1)S(1)}, u32[]{:S(2)}, u32[]{:S(2)}) collective-permute-start(bf16[2048,128]{1,0:T(8,128)(2,1)S(1)} %get-tuple-element.41), channel_id=1, source_target_pairs={{0,16},{16,0},{32,48},{48,32},{64,80},{80,64},{96,112},{112,96},{1... | collective-permute-start | bytes 1572872 | tf_op jit(solution)/shard_map/ppermute | solution.py:503
  65.5 1.5 %collective-permute-done.4.other_ref = bf16[2048,128]{1,0:T(8,128)(2,1)S(1)} collective-permute-done((bf16[2048,128]{1,0:T(8,128)(2,1)S(1)}, bf16[2048,128]{1,0:T(8,128)(2,1)S(1)}, u32[]{:S(2)}, u32[]{:S(2)}) %collective-permute-start.4) | collective-permute-done | bytes 524320 | tf_op jit(solution)/shard_map/ppermute | solution.py:503
  67.1 0.9 pair.1
  67.9 7.8 %all-to-all-start.1 = ((bf16[64,32,128]{2,1,0:T(8,128)(2,1)}), bf16[64,32,128]{2,1,0:T(8,128)(2,1)S(1)}, u32[]{:S(2)}, u32[]{:S(2)}) async-start(bf16[64,32,128]{2,1,0:T(8,128)(2,1)} %bitcast.10), calls=%async_computation.1 | async-start | bytes 1048576 | tf_op jit(solution)/shard_map/all_to_all | solution.py:507
  75.8 0.0 copy-start.9
  75.8 1.5 %copy-done.9 = bf16[3456,256]{1,0:T(8,128)(2,1)S(1)} copy-done((bf16[3456,256]{1,0:T(8,128)(2,1)S(1)}, bf16[3456,256]{1,0:T(8,128)(2,1)}, u32[]{:S(2)}) %copy-start.9) | copy-done | bytes 1769496
  77.2 4.5 %input_grad.1.back_ref = bf16[1024,384]{1,0:T(8,128)(2,1)S(1)} custom-call(bf16[1440,256]{1,0:T(8,128)(2,1)S(1)} %get-tuple-element.39.delta_ref, bf16[3456,256]{1,0:T(8,128)(2,1)S(1)} %copy-done.9, bf16[1024,512]{1,0:T(8,128)(2,1)S(1)} %bitcast.19), custom_call_target="tpu_custom_call" | custom-call | flops 3959422976 | bytes 8000000 | tf_op jit(solution)/shard_map/input_grad/pallas_call | solution.py:45
  81.8 6.3 %all-to-all-done.1.terms_ref = bf16[64,32,128]{2,1,0:T(8,128)(2,1)S(1)} async-done(((bf16[64,32,128]{2,1,0:T(8,128)(2,1)}), bf16[64,32,128]{2,1,0:T(8,128)(2,1)S(1)}, u32[]{:S(2)}, u32[]{:S(2)}) %all-to-all-start.1) | async-done | bytes 524320 | tf_op jit(solution)/shard_map/all_to_all | solution.py:507
  88.0 0.2 join.1
  88.2 0.0 copy-start.10
  88.2 26.3 %all_to_all.15 = bf16[128,8,640]{2,1,0:T(8,128)(2,1)S(1)} all-to-all(bf16[128,8,640]{2,1,0:T(8,128)(2,1)S(1)} %bitcast.17), channel_id=1, replica_groups=mesh['gx'=8,'gy'=16] {'gx','gy'}, dimensions={0} | all-to-all | bytes 2621440 | tf_op jit(solution)/shard_map/all_to_all | solution.py:507
  114.6 1.6 %collective-permute-start.5 = (bf16[1024,256]{1,0:T(8,128)(2,1)S(1)}, bf16[1024,256]{1,0:T(8,128)(2,1)S(1)}, u32[]{:S(2)}, u32[]{:S(2)}) collective-permute-start(bf16[1024,256]{1,0:T(8,128)(2,1)S(1)} %slice.4), channel_id=1, source_target_pairs={{0,16},{16,0},{32,48},{48,32},{64,80},{80,64},{96,112},{112,96},{1... | collective-permute-start | bytes 1572872 | tf_op jit(solution)/shard_map/ppermute | solution.py:503
  116.1 0.0 copy-done.10
  116.1 2.7 %collect.1 = bf16[96,2048]{1,0:T(8,128)(2,1)} custom-call(bf16[1024,640]{1,0:T(8,128)(2,1)S(1)} %bitcast.15, s32[2,2048]{1,0:T(2,128)S(1)} %copy-done.10), custom_call_target="tpu_custom_call" | custom-call | flops 2147483648 | bytes 4000000 | tf_op jit(solution)/shard_map/collect/pallas_call | solution.py:45
  118.8 0.0 collective-permute-done.5.theirs_ref
  118.9 2.1 %unpack.1 = (f32[27,96,96]{2,1,0:T(8,128)}, f32[8,96,192]{2,1,0:T(8,128)}) custom-call(s32[2]{0:T(128)S(1)} %pad_add_fusion.place_ref, bf16[1024,640]{1,0:T(8,128)(2,1)S(1)} %bitcast.16, bf16[1024,256]{1,0:T(8,128)(2,1)S(1)} %collective-permute-done.5.theirs_ref), custom_call_target="tpu_custom_call" | custom-call | bytes 4000000 | tf_op jit(solution)/shard_map/unpack/pallas_call | solution.py:45
  (1 shorter events, 0.0 us)
Async XLA Ops:
  5.5 11.6 %copy-start = (bf16[27,96,96]{2,1,0:T(8,128)(2,1)S(1)}, bf16[27,96,96]{2,1,0:T(8,128)(2,1)}, u32[]{:S(2)}) copy-start(bf16[27,96,96]{2,1,0:T(8,128)(2,1)} %conv_ref.1) | copy-start | bytes 1492996
  5.5 11.6 %copy-start.1 = (bf16[8,96,192]{2,1,0:T(8,128)(2,1)S(1)}, bf16[8,96,192]{2,1,0:T(8,128)(2,1)}, u32[]{:S(2)}) copy-start(bf16[8,96,192]{2,1,0:T(8,128)(2,1)} %down_ref.1) | copy-start | bytes 884740
  5.5 11.6 %copy-start.2 = (bf16[4,8,8,192]{3,2,1,0:T(8,128)(2,1)S(1)}, bf16[4,8,8,192]{3,2,1,0:T(8,128)(2,1)}, u32[]{:S(2)}) copy-start(bf16[4,8,8,192]{3,2,1,0:T(8,128)(2,1)} %param.13) | copy-start | bytes 294916
  5.5 11.6 %copy-start.3 = (s32[8,16,16]{2,1,0:T(8,128)S(1)}, s32[8,16,16]{2,1,0:T(8,128)}, u32[]{:S(2)}) copy-start(s32[8,16,16]{2,1,0:T(8,128)} %param.10) | copy-start | bytes 24580
  5.5 30.1 %all-to-all-start = ((bf16[128,8,512]{2,1,0:T(8,128)(2,1)}), bf16[128,8,512]{2,1,0:T(8,128)(2,1)S(1)}, u32[]{:S(2)}, u32[]{:S(2)}) async-start(bf16[128,8,512]{2,1,0:T(8,128)(2,1)} %bitcast.22), calls=%async_computation | async-start | bytes 2097152 | tf_op jit(solution)/shard_map/all_to_all | solution.py:507
  18.1 1.2 %copy-start.4 = (bf16[3456,256]{1,0:T(8,128)(2,1)}, bf16[3456,256]{1,0:T(8,128)(2,1)S(1)}, u32[]{:S(2)}) copy-start(bf16[3456,256]{1,0:T(8,128)(2,1)S(1)} %get-tuple-element.32.conv_ref) | copy-start | bytes 5308420
  19.4 0.8 copy-start.6
  20.2 1.2 copy-start.8
  35.7 16.4 %copy-start.5 = (bf16[3456,256]{1,0:T(8,128)(2,1)S(1)}, bf16[3456,256]{1,0:T(8,128)(2,1)}, u32[]{:S(2)}) copy-start(bf16[3456,256]{1,0:T(8,128)(2,1)} %copy-done.4) | copy-start | bytes 5308420
  39.2 4.7 %collective-permute-start = (bf16[448,256]{1,0:T(8,128)(2,1)S(1)}, bf16[448,256]{1,0:T(8,128)(2,1)S(1)}, u32[]{:S(2)}, u32[]{:S(2)}) collective-permute-start(bf16[448,256]{1,0:T(8,128)(2,1)S(1)} %get-tuple-element.28), channel_id=1, source_target_pairs={{0,16},{16,32},{32,48},{48,64},{64,80},{80,96},{96,112},{112,0},{1... | collective-permute-start | bytes 688136 | tf_op jit(solution)/shard_map/ppermute | solution.py:499
  40.9 5.7 %collective-permute-start.1 = (bf16[448,256]{1,0:T(8,128)(2,1)S(1)}, bf16[448,256]{1,0:T(8,128)(2,1)S(1)}, u32[]{:S(2)}, u32[]{:S(2)}) collective-permute-start(bf16[448,256]{1,0:T(8,128)(2,1)S(1)} %get-tuple-element.29), channel_id=1, source_target_pairs={{0,112},{16,0},{32,16},{48,32},{64,48},{80,64},{96,80},{112,96},{1... | collective-permute-start | bytes 688136 | tf_op jit(solution)/shard_map/ppermute | solution.py:499
  47.3 9.2 %collective-permute-start.2 = (bf16[384,256]{1,0:T(8,128)(2,1)S(1)}, bf16[384,256]{1,0:T(8,128)(2,1)S(1)}, u32[]{:S(2)}, u32[]{:S(2)}) collective-permute-start(bf16[384,256]{1,0:T(8,128)(2,1)S(1)} %get-tuple-element.30), channel_id=1, source_target_pairs={{0,1},{1,2},{2,3},{3,4},{4,5},{5,6},{6,7},{7,8},{8,9},{9,10},{10,1... | collective-permute-start | bytes 589832 | tf_op jit(solution)/shard_map/ppermute | solution.py:499
  48.0 8.4 %collective-permute-start.3 = (bf16[384,256]{1,0:T(8,128)(2,1)S(1)}, bf16[384,256]{1,0:T(8,128)(2,1)S(1)}, u32[]{:S(2)}, u32[]{:S(2)}) collective-permute-start(bf16[384,256]{1,0:T(8,128)(2,1)S(1)} %get-tuple-element.31), channel_id=1, source_target_pairs={{0,15},{1,0},{2,1},{3,2},{4,3},{5,4},{6,5},{7,6},{8,7},{9,8},{10,9... | collective-permute-start | bytes 589832 | tf_op jit(solution)/shard_map/ppermute | solution.py:499
  52.1 4.3 %copy-start.7 = (bf16[4,256,192]{2,1,0:T(8,128)(2,1)S(1)}, bf16[4,256,192]{2,1,0:T(8,128)(2,1)}, u32[]{:S(2)}) copy-start(bf16[4,256,192]{2,1,0:T(8,128)(2,1)} %copy-done.6) | copy-start | bytes 1179652
  63.9 3.2 %collective-permute-start.4 = (bf16[2048,128]{1,0:T(8,128)(2,1)S(1)}, bf16[2048,128]{1,0:T(8,128)(2,1)S(1)}, u32[]{:S(2)}, u32[]{:S(2)}) collective-permute-start(bf16[2048,128]{1,0:T(8,128)(2,1)S(1)} %get-tuple-element.41), channel_id=1, source_target_pairs={{0,16},{16,0},{32,48},{48,32},{64,80},{80,64},{96,112},{112,96},{1... | collective-permute-start | bytes 1572872 | tf_op jit(solution)/shard_map/ppermute | solution.py:503
  67.9 20.1 %all-to-all-start.1 = ((bf16[64,32,128]{2,1,0:T(8,128)(2,1)}), bf16[64,32,128]{2,1,0:T(8,128)(2,1)S(1)}, u32[]{:S(2)}, u32[]{:S(2)}) async-start(bf16[64,32,128]{2,1,0:T(8,128)(2,1)} %bitcast.10), calls=%async_computation.1 | async-start | bytes 1048576 | tf_op jit(solution)/shard_map/all_to_all | solution.py:507
  75.8 1.5 %copy-start.9 = (bf16[3456,256]{1,0:T(8,128)(2,1)S(1)}, bf16[3456,256]{1,0:T(8,128)(2,1)}, u32[]{:S(2)}) copy-start(bf16[3456,256]{1,0:T(8,128)(2,1)} %copy-done.8) | copy-start | bytes 5308420
  88.2 27.9 %copy-start.10 = (s32[2,2048]{1,0:T(2,128)S(1)}, s32[2,2048]{1,0:T(2,128)}, u32[]{:S(2)}) copy-start(s32[2,2048]{1,0:T(2,128)} %get-tuple-element.43.slot_ref) | copy-start | bytes 49156
  114.6 4.3 %collective-permute-start.5 = (bf16[1024,256]{1,0:T(8,128)(2,1)S(1)}, bf16[1024,256]{1,0:T(8,128)(2,1)S(1)}, u32[]{:S(2)}, u32[]{:S(2)}) collective-permute-start(bf16[1024,256]{1,0:T(8,128)(2,1)S(1)} %slice.4), channel_id=1, source_target_pairs={{0,16},{16,0},{32,48},{48,32},{64,80},{80,64},{96,112},{112,96},{1... | collective-permute-start | bytes 1572872 | tf_op jit(solution)/shard_map/ppermute | solution.py:503

commit v7 on v6

--- a/solution.py
+++ b/solution.py
@@ -125,17 +125,17 @@
     weigh = jnp.where(lane == channels, 32.0, jnp.where(lane == channels + 1, 1.0, 0.0))
     weigh = weigh.astype(BF16)
     step = 256
+    places, parts = [], []
     for q in range(PACK):
         block = got_ref[:, q * LANE : (q + 1) * LANE]
-        place = mm(weigh, block, NT)[0:1].astype(jnp.int32)
+        places.append(mm(weigh, block, NT)[0:1].astype(jnp.int32))
         odd = block * block[:, channels + 2 : channels + 3]
-        both = jnp.concatenate([block - odd, odd], axis=1)
-        for start in range(0, pairs, step):
-            pick = one_hot(iota((step, rows), 0) + start == place)
-            part = mm(pick, both)
-            if q:
-                part = total_ref[start : start + step, :] + part
-            total_ref[start : start + step, :] = part
+        parts.append(jnp.concatenate([block - odd, odd], axis=1))
+    place = jnp.concatenate(places, axis=1)
+    both = jnp.concatenate(parts, axis=0)
+    for start in range(0, pairs, step):
+        pick = one_hot(iota((step, PACK * rows), 0) + start == place)
+        total_ref[start : start + step, :] = mm(pick, both)
     at = 0
     for ref, (ext_x, ext_y, half, rim) in zip((total_ref, coarse_ref), fields):
         field = as_field(ref[...], ext_x, ext_y, half)
@@ -177,12 +177,14 @@
 
 
 def prepare_kernel(
-    conv_ref, down_ref, cot_ref, occ_ref, conv_out, back_out, down_out, coarse_out, *, ext_y
+    conv_ref, down_ref, cot_ref, occ_ref,
+    conv_out, back_out, down_out, down_back_out, coarse_out, *, ext_y
 ):
     channels = conv_ref.shape[1]
     conv_out[...] = jnp.zeros(conv_out.shape, BF16)
     back_out[...] = jnp.zeros(back_out.shape, BF16)
     down_out[...] = jnp.zeros(down_out.shape, BF16)
+    down_back_out[...] = jnp.zeros(down_back_out.shape, BF16)
     four = 4 * channels
     a, b = slice(0, channels), slice(LANE, LANE + channels)
     for j in range(9):
@@ -194,9 +196,10 @@
                 conv_out[at : at + channels, side] = weight
                 at = (8 - j) * four + (2 - k + z) * channels
                 back_out[at : at + channels, side] = turned
-    for j in range(4):
-        down_out[j, a, :] = down_ref[2 * j]
-        down_out[j, b, :] = down_ref[2 * j + 1]
+    for j in range(8):
+        part = slice(j * LANE, j * LANE + channels)
+        down_out[part, :] = down_ref[j]
+        down_back_out[:, part] = down_ref[j].astype(F32).T.astype(BF16)
     columns, depth = occ_ref.shape
     rows, coarse = cot_ref.shape
     half = depth // 2
@@ -239,8 +242,8 @@
 
 
 def convolve(four_ref, weight_ref, boxes):
-    rows = [jnp.concatenate(windows(four_ref, *box), axis=1) for box in boxes]
-    return mm(rows[0] if len(rows) == 1 else jnp.concatenate(rows, axis=0), weight_ref[...])
+    weight = weight_ref[...]
+    return [mm(jnp.concatenate(windows(four_ref, *box), axis=1), weight) for box in boxes]
 
 
 def logistic(values):
@@ -252,37 +255,113 @@
     return (pre * sigma).astype(BF16), sigma * (1.0 + pre * (1.0 - sigma))
 
 
-def inner(field, rim):
-    part = field[rim : field.shape[0] - rim, rim : field.shape[1] - rim]
-    return part.reshape(part.shape[0] * part.shape[1] * part.shape[2], part.shape[3])
-
-
-def column_kernel(
-    grid_ref, x_low, x_high, conv_ref, silu_ref, slope_ref, pad_ref, four_ref, *, channels
+def rows_of(field):
+    return field.reshape(field.shape[0] * field.shape[1] * field.shape[2], field.shape[3])
+
+
+def child_masks(coarse_s, mask_s, coarse):
+    count_x, count_y, half, wide = coarse_s.shape
+    given = rows_of(coarse_s[:, :, :, LANE:]).astype(BF16)
+    spot = iota((LANE, 4 * wide), 0) == coarse - LANE + iota((LANE, 4 * wide), 1) // LANE
+    masks = mm(given, one_hot(spot))
+    largest = None
+    for j in range(4):
+        mask = masks[:, j * wide : (j + 1) * wide]
+        mask_s[:, j // 2, :, j % 2] = mask.reshape(count_x, count_y, half, wide)
+        largest = mask if largest is None else jnp.maximum(largest, mask)
+    largest = jnp.maximum(largest[:, :LANE], largest[:, LANE:])
+    largest = jnp.concatenate([largest, largest[:, : coarse - LANE]], axis=1)
+    return largest.reshape(count_x, count_y, half, coarse)
+
+
+def coarse_pass(
+    fine_s, slope_s, delta_s, coarse_s, coarse_mask, down_ref, down_back_ref, first, count
+):
+    coarse = down_ref.shape[1]
+    columns = slice(first, first + count)
+    pieces = [rows_of(fine_s[:, j // 2, columns, j % 2]).astype(BF16) for j in range(4)]
+    pre = mm(jnp.concatenate(pieces, axis=1), down_ref[...])
+    sigma = logistic(pre)
+    shape = (coarse_s.shape[0], count, coarse_s.shape[2], coarse)
+    mask = rows_of(coarse_mask[:, columns])
+    features = (pre * sigma * mask).reshape(shape)
+    slope = sigma * (1.0 + pre * (1.0 - sigma))
+    delta = (rows_of(coarse_s[:, columns, :, :coarse]) * mask * slope).astype(BF16)
+    back = mm(delta, down_back_ref[...])
+    for j in range(4):
+        part = back[:, j * WIDE : (j + 1) * WIDE].reshape(*shape[:3], WIDE)
+        delta_s[:, j // 2, :, j % 2] = part * slope_s[:, j // 2, columns, j % 2]
+    return features, delta.astype(F32).reshape(shape)
+
+
+def as_columns(ref):
+    count_x, _, count_y, _, half, wide = ref.shape
+    return ref[...].reshape(2 * count_x, 2 * count_y, half, wide)
+
+
+def middle_kernel(
+    grid_ref, coarse_ref, x_low, x_high, conv_ref, down_ref, down_back_ref,
+    fine_ref, slope_ref, features_ref, delta_ref, conv_grad_ref, down_grad_ref,
+    pad_ref, four_ref, coarse_s, mask_s, fine_s, slope_s, delta_s, *, channels, rim,
 ):
     ext_x, ext_y, half = pad_ref.shape[0], pad_ref.shape[1], pad_ref.shape[2]
-    rim = 3
     size = rim * ext_y * half
     pad_ref[:rim] = as_field(x_low[:size, :], rim, ext_y, half)
     pad_ref[rim : ext_x - rim] = as_field(grid_ref[...], ext_x - 2 * rim, ext_y, half)
     pad_ref[ext_x - rim :] = as_field(x_high[:size, :], rim, ext_y, half)
     fill_four(pad_ref, four_ref, channels)
-    count = 4
-    step = count * (ext_y - 2) * half
+    coarse_x, coarse_y = coarse_s.shape[0], coarse_s.shape[1]
+    coarse = down_ref.shape[1]
+    coarse_s[:1] = as_field(x_low[size:, :], 1, coarse_y, half)
+    coarse_s[1 : coarse_x - 1] = as_field(coarse_ref[...], coarse_x - 2, coarse_y, half)
+    coarse_s[coarse_x - 1 :] = as_field(x_high[size:, :], 1, coarse_y, half)
+    coarse_mask = child_masks(coarse_s, mask_s, coarse)
+    count, inside_y = 4, ext_y - 2
     for first in range(0, ext_x - 2, count):
-        pre = convolve(four_ref, conv_ref, [(first, count, 0, ext_y - 2)])
-        rows = slice(first // count * step, (first // count + 1) * step)
-        silu_ref[rows, :], slope_ref[rows, :] = silu_and_slope(pre)
-
-
-def level_kernel(
-    grid_ref, coarse_ref, x_low, x_high, y_low, y_high, silu_ref, slope_ref,
-    conv_ref, down_ref,
-    features_ref, fine_ref, delta_coarse_ref, delta_ref,
-    pad_ref, four_ref, coarse_s, mask_s, fine_s, slope_s, *, channels, fields,
+        (pre,) = convolve(four_ref, conv_ref, [(first, count, 0, inside_y)])
+        silu, slope = silu_and_slope(pre)
+        silu = as_field(silu, count, inside_y, half)
+        slope = slope.reshape(silu.shape)
+        part = slice(first // 2, (first + count) // 2)
+        shape = (count // 2, 2, half, WIDE)
+        for y in range(1, ext_y - 1):
+            mask = mask_s[part, :, y // 2, y % 2]
+            fine_s[part, :, y // 2, y % 2] = silu[:, y - 1].reshape(shape) * mask
+            slope_s[part, :, y // 2, y % 2] = slope[:, y - 1].reshape(shape) * mask
+    size = 2 * coarse_x * half
+    for at, y in enumerate((1, ext_y - 2)):
+        rows = slice(at * size, (at + 1) * size)
+        fine_ref[rows, :] = fine_s[:, :, y // 2, y % 2].reshape(size, WIDE).astype(BF16)
+        slope_ref[rows, :] = slope_s[:, :, y // 2, y % 2].reshape(size, WIDE)
+    middle = coarse_y - 2
+    features, delta_coarse = coarse_pass(
+        fine_s, slope_s, delta_s, coarse_s, coarse_mask, down_ref, down_back_ref, 1, middle
+    )
+    features_ref[...] = rows_of(features[1 : coarse_x - 1]).astype(BF16)
+    delta = as_columns(delta_s)
+    delta_ref[...] = rows_of(delta[1 : 2 * coarse_x - 1]).astype(BF16)
+    turned = rows_of(delta[2 : 2 * coarse_x - 2]).T.astype(BF16)
+    box = (rim - 1, 2 * (coarse_x - 2), 1, 2 * middle)
+    for j, part in enumerate(windows(four_ref, *box)):
+        conv_grad_ref[j * LANE : (j + 1) * LANE, :] = fold(mm(turned, part), channels)
+    ours = rows_of(delta_coarse[1 : coarse_x - 1]).astype(BF16)
+    for j in range(4):
+        piece = fine_s[1 : coarse_x - 1, j // 2, 1 : 1 + middle, j % 2]
+        down_grad_ref[j * WIDE : (j + 1) * WIDE, :] = mm(rows_of(piece).astype(BF16), ours, TN)
+
+
+def fold(grad, channels):
+    return grad[:LANE, : 3 * channels] + grad[LANE:, channels:]
+
+
+def strip_kernel(
+    place_ref, grid_ref, coarse_ref, x_low, x_high, y_low, y_high, fine_ref, slope_ref,
+    mid_features_ref, mid_delta_ref, conv_grad_ref, down_grad_ref, conv_ref, down_ref,
+    down_back_ref, features_ref, delta_ref, keep_ref, give_ref,
+    pad_ref, four_ref, coarse_s, mask_s, fine_s, slope_s, delta_s, sum_s,
+    *, channels, fields, scale,
 ):
     (ext_x, ext_y, half, rim), (coarse_x, coarse_y, _, _) = fields
-    wide = WIDE
     long = ext_x + 2 * rim
     slab, face = rim * ext_y * half, long * rim * half
     parts = (
@@ -291,119 +370,89 @@
         as_field(x_high[:slab, :], rim, ext_y, half),
     )
     for side, y_ref in enumerate((y_low, y_high)):
-        ours, here, there = ((0, rim, 0), (ext_y - 2, 0, 2))[side]
+        ours, here, there = ((0, rim, 0), (ext_y - rim, 0, rim))[side]
         at = side * long
         pad_ref[at : at + long, there : there + rim] = as_field(y_ref[:face, :], long, rim, half)
         for part in parts:
             count = part.shape[0]
-            pad_ref[at : at + count, here : here + 2] = part[:, ours : ours + 2]
+            pad_ref[at : at + count, here : here + rim] = part[:, ours : ours + rim]
             at += count
     fill_four(pad_ref, four_ref, channels)
-    coarse_s[1 : 1 + coarse_x, 1 : 1 + coarse_y] = as_field(
-        coarse_ref[...], coarse_x, coarse_y, half
-    )
-    coarse_s[:1, 1 : 1 + coarse_y] = as_field(x_low[slab:, :], 1, coarse_y, half)
-    coarse_s[1 + coarse_x :, 1 : 1 + coarse_y] = as_field(x_high[slab:, :], 1, coarse_y, half)
-    for y, y_ref in ((0, y_low), (1 + coarse_y, y_high)):
-        coarse_s[:, y : y + 1] = as_field(y_ref[face:, :], coarse_x + 2, 1, half)
-    wide_x, wide_y = coarse_x + 2, coarse_y + 2
-    coarse_rows = wide_x * wide_y * half
-    coarse = down_ref.shape[2]
-    given = coarse_s[...].reshape(coarse_rows, wide).astype(BF16)
-    largest = None
-    for j in range(4):
-        spot = iota((wide, wide), 0) == coarse + 2 * j + iota((wide, wide), 1) // LANE
-        mask = mm(given, one_hot(spot))
-        mask_s[:, j // 2, :, j % 2] = mask.reshape(wide_x, wide_y, half, wide)
-        largest = mask if largest is None else jnp.maximum(largest, mask)
-    largest = jnp.maximum(largest[:, :LANE], largest[:, LANE:])
-    coarse_mask = jnp.concatenate([largest, largest[:, : coarse - LANE]], axis=1)
-
-    out_x, out_y = 2 * wide_x, 2 * wide_y
-    strip = 3
-    boxes = [(0, out_x, 0, strip), (long, out_x, 0, strip)]
-    silu, slope = silu_and_slope(convolve(four_ref, conv_ref, boxes))
-    shape = (2, out_x, strip, half, wide)
-    edge_silu, edge_slope = silu.astype(F32).reshape(shape), slope.reshape(shape)
-    columns = out_y - 2 * strip
-    mid_silu = as_field(silu_ref[...], out_x, columns, half)
-    mid_slope = slope_ref[...].reshape(out_x, columns, half, wide)
-    shape = (wide_x, 2, half, wide)
-    for y in range(out_y):
-        if y < strip:
-            silu, slope = edge_silu[0, :, y], edge_slope[0, :, y]
-        elif y >= out_y - strip:
-            at = y - (out_y - strip)
-            silu, slope = edge_silu[1, :, at], edge_slope[1, :, at]
+    parts = (
+        as_field(x_low[slab:, :], 1, coarse_y, half),
+        as_field(coarse_ref[...], coarse_x, coarse_y, half),
+        as_field(x_high[slab:, :], 1, coarse_y, half),
+    )
+    for side, y_ref in enumerate((y_low, y_high)):
+        y = side * (coarse_y - 1)
+        theirs = 3 * side
+        coarse_s[:, theirs : theirs + 1] = as_field(y_ref[face:, :], coarse_x + 2, 1, half)
+        at = 0
+        for part in parts:
+            count = part.shape[0]
+            coarse_s[at : at + count, 1 + side : 2 + side] = part[:, y : y + 1]
+            at += count
+    coarse = down_ref.shape[1]
+    coarse_mask = child_masks(coarse_s, mask_s, coarse)
+    out_x, strip = ext_x + 4, 3
+    boxes = [(0, out_x, 0, strip), (long, out_x, 1, strip)]
+    shape = (out_x, strip, half, WIDE)
+    ends = [silu_and_slope(pre) for pre in convolve(four_ref, conv_ref, boxes)]
+    ends = [(silu.astype(F32).reshape(shape), slope.reshape(shape)) for silu, slope in ends]
+    shape = (coarse_x + 2, 2, half, WIDE)
+    size = out_x * half
+    for y in range(8):
+        if y in (3, 4):
+            rows = slice((y - 3) * size, (y - 2) * size)
+            fine_s[:, :, y // 2, y % 2] = fine_ref[rows, :].astype(F32).reshape(shape)
+            slope_s[:, :, y // 2, y % 2] = slope_ref[rows, :].reshape(shape)
         else:
-            silu, slope = mid_silu[:, y - strip], mid_slope[:, y - strip]
-        mask = mask_s[:, :, y // 2, y % 2]
-        fine_s[:, :, y // 2, y % 2] = silu.reshape(shape) * mask
-        slope_s[:, :, y // 2, y % 2] = slope.reshape(shape) * mask
-    field = (out_x, out_y, half, wide)
-    fine_ref[...] = inner(fine_s[...].reshape(field), 2).astype(BF16)
-
-    pre = None
-    for j in range(4):
-        piece = fine_s[:, j // 2, :, j % 2].reshape(coarse_rows, wide).astype(BF16)
-        part = mm(piece, down_ref[j])
-        pre = part if pre is None else pre + part
-    sigma = logistic(pre)
-    coarse_field = (wide_x, wide_y, half, coarse)
-    features = pre * sigma * coarse_mask
-    features_ref[...] = inner(features.reshape(coarse_field), 1).astype(BF16)
-    slope = sigma * (1.0 + pre * (1.0 - sigma))
-    cot = coarse_s[:, :, :, :coarse].reshape(coarse_rows, coarse)
-    delta = cot * coarse_mask * slope
-    delta_coarse_ref[...] = inner(delta.reshape(coarse_field), 1).astype(BF16)
-    delta = delta.astype(BF16)
-    for j in range(4):
-        back = mm(delta, down_ref[j], NT).reshape(wide_x, wide_y, half, wide)
-        fine_s[:, j // 2, :, j % 2] = back * slope_s[:, j // 2, :, j % 2]
-    delta_ref[...] = inner(fine_s[...].reshape(field), 1).astype(BF16)
-
-
-def weight_grad_kernel(
-    place_ref, grid_ref, x_low, x_high, y_low, y_high, fine_ref, delta_coarse_ref, delta_ref,
-    keep_ref, give_ref, pad_ref, four_ref, delta_s, fine_s, out_ref, *, channels, fields, scale,
-):
-    (ext_x, ext_y, half, rim), _ = fields
-    long = ext_x + 2 * rim
-    slab, face = rim * ext_y * half, long * rim * half
-    pad_ref[1 : 1 + ext_x, 1 : 1 + ext_y] = as_field(grid_ref[...], ext_x, ext_y, half)
-    for x, x_ref, at in ((0, x_low, rim - 1), (1 + ext_x, x_high, 0)):
-        field = as_field(x_ref[:slab, :], rim, ext_y, half)
-        pad_ref[x : x + 1, 1 : 1 + ext_y] = field[at : at + 1]
-    for y, y_ref, at in ((0, y_low, rim - 1), (1 + ext_y, y_high, 0)):
-        field = as_field(y_ref[:face, :], long, rim, half)
-        pad_ref[:, y : y + 1] = field[rim - 1 : long - rim + 1, at : at + 1]
-    fill_four(pad_ref, four_ref, channels)
-    delta_s[...] = as_field(delta_ref[...], ext_x + 2, ext_y + 2, half)
-    turned = inner(delta_s[...], 1).T.astype(BF16)
+            side, at = y // 5, y % 5
+            mask = mask_s[:, :, y // 2, y % 2]
+            silu, slope = ends[side]
+            fine_s[:, :, y // 2, y % 2] = silu[:, at].reshape(shape) * mask
+            slope_s[:, :, y // 2, y % 2] = slope[:, at].reshape(shape) * mask
+    features, delta_coarse = coarse_pass(
+        fine_s, slope_s, delta_s, coarse_s, coarse_mask, down_ref, down_back_ref, 0, 4
+    )
+    features = features[1 : 1 + coarse_x]
+    mid = as_field(mid_features_ref[...], coarse_x, coarse_y - 2, half)
+    features = jnp.concatenate([features[:, 1:2], mid, features[:, 2:3]], axis=1)
+    features_ref[...] = rows_of(features).astype(BF16)
+    delta = as_columns(delta_s)
+    mid = as_field(mid_delta_ref[...], ext_x + 2, ext_y - 4, half)
+    near = delta[1 : out_x - 1]
+    near = jnp.concatenate([near[:, 1:4], mid, near[:, 4:7]], axis=1)
+    delta_ref[...] = rows_of(near).astype(BF16)
+    ours = delta[2 : 2 + ext_x]
+    turned = jnp.concatenate([rows_of(ours[:, 2:4]), rows_of(ours[:, 4:6])], axis=0)
+    turned = turned.T.astype(BF16)
+    low = windows(four_ref, rim - 1, ext_x, rim - 1, 2)
+    high = windows(four_ref, long + rim - 1, ext_x, 0, 2)
     three = 3 * channels
-    for j, part in enumerate(windows(four_ref, 0, ext_x, 0, ext_y)):
-        grad = mm(turned, part)
-        grad = grad[:LANE, :three] + grad[LANE:, channels:]
-        out_ref[j * three : (j + 1) * three, :] = grad.T * scale
-    fine_s[...] = fine_ref[...].astype(F32).reshape(fine_s.shape)
-    coarse_rows = ext_x // 2 * (ext_y // 2) * half
+    for j in range(9):
+        grad = fold(mm(turned, jnp.concatenate([low[j], high[j]], axis=0)), channels)
+        grad = grad + conv_grad_ref[j * LANE : (j + 1) * LANE, :]
+        sum_s[j * three : (j + 1) * three, :] = grad.T * scale
+    ours = rows_of(delta_coarse[1 : 1 + coarse_x, 1:3]).astype(BF16)
     base = 27 * channels
     for j in range(4):
-        piece = fine_s[:, j // 2, :, j % 2].reshape(coarse_rows, WIDE).astype(BF16)
-        grad = mm(piece, delta_coarse_ref[...], TN) * scale
+        piece = rows_of(fine_s[1 : 1 + coarse_x, j // 2, 1:3, j % 2]).astype(BF16)
+        grad = (mm(piece, ours, TN) + down_grad_ref[j * WIDE : (j + 1) * WIDE, :]) * scale
         first, second = grad[:channels], grad[LANE : LANE + channels]
         start = base + 2 * j * channels
-        out_ref[start : start + channels, :] = first[:, :LANE]
-        out_ref[start + channels : start + 2 * channels, :] = second[:, :LANE]
+        sum_s[start : start + channels, :] = first[:, :LANE]
+        sum_s[start + channels : start + 2 * channels, :] = second[:, :LANE]
         start = base + (8 + j) * channels
-        tail = jnp.concatenate([first[:, LANE:], second[:, LANE:]], axis=1)
-        out_ref[start : start + channels, :] = tail
+        sum_s[start : start + channels, :] = jnp.concatenate(
+            [first[:, LANE:], second[:, LANE:]], axis=1
+        )
     end = base + 12 * channels
-    out_ref[end:, :] = jnp.zeros((out_ref.shape[0] - end, LANE), F32)
+    sum_s[end:, :] = jnp.zeros((sum_s.shape[0] - end, LANE), F32)
     size = keep_ref.shape[0]
     core = place_ref[0] % 2
-    keep_ref[...] = out_ref[pl.ds(pl.multiple_of(core * size, size), size), :]
-    give = out_ref[pl.ds(pl.multiple_of((1 - core) * size, size), size), :]
+    keep_ref[...] = sum_s[pl.ds(pl.multiple_of(core * size, size), size), :]
+    give = sum_s[pl.ds(pl.multiple_of((1 - core) * size, size), size), :]
     give_ref[...] = give.astype(BF16)
 
 
@@ -418,7 +467,8 @@
     count = 4
     for first in range(0, ext_x, count):
         rows = slice(first * ext_y * half, (first + count) * ext_y * half)
-        grad_s[rows, :] = convolve(four_ref, conv_ref, [(first, count, 0, ext_y)]).astype(BF16)
+        (grad,) = convolve(four_ref, conv_ref, [(first, count, 0, ext_y)])
+        grad_s[rows, :] = grad.astype(BF16)
     grad = grad_s[...]
     pairs = grad.shape[0]
     rows = got_ref.shape[0]
@@ -546,12 +596,13 @@
         grant=56,
     )
     got = exchange(send.reshape(devices, block, PACK * LANE)).reshape(slot_rows, PACK * LANE)
-    conv_blocks, back_blocks, down_blocks, given = call(
+    conv_blocks, back_blocks, down_blocks, down_back, given = call(
         functools.partial(prepare_kernel, ext_y=ext_y),
         (
             struct((9 * four, WIDE), BF16),
             struct((9 * four, WIDE), BF16),
-            struct((4, WIDE, coarse), BF16),
+            struct((4 * WIDE, coarse), BF16),
+            struct((coarse, 4 * WIDE), BF16),
             struct((coarse_rows, WIDE), BF16),
         ),
         (w_conv, w_down, cotangent.reshape(coarse_rows, coarse),
@@ -579,56 +630,58 @@
     )
     y_low, y_high = shift(y_last, "gy", 1), shift(y_first, "gy", -1)
     long = ext_x + 2 * rim
-    mid_rows = (ext_x + 4) * (ext_y - 2) * half
-    silu, slope = call(
-        functools.partial(column_kernel, channels=channels),
-        (struct((mid_rows, WIDE), BF16), struct((mid_rows, WIDE), F32)),
-        (grid, x_low, x_high, conv_blocks),
-        "column",
+    near = (ext_x + 2, ext_y + 2, half)
+    near_rows = near[0] * near[1] * half
+    edge_rows = 2 * (ext_x + 4) * half
+
+    def split(columns):
+        return pltpu.VMEM((coarse_x + 2, 2, columns, 2, half, WIDE), F32)
+
+    middle = call(
+        functools.partial(middle_kernel, channels=channels, rim=rim),
+        (
+            struct((edge_rows, WIDE), BF16),
+            struct((edge_rows, WIDE), F32),
+            struct((coarse_x * (coarse_y - 2) * half, coarse), BF16),
+            struct(((ext_x + 2) * (ext_y - 4) * half, WIDE), BF16),
+            struct((9 * LANE, 3 * channels), F32),
+            struct((4 * WIDE, coarse), F32),
+        ),
+        (grid, given, x_low, x_high, conv_blocks, down_blocks, down_back),
+        "middle",
         scratch=[
             pltpu.VMEM((long, ext_y, half, WIDE), F32),
             pltpu.VMEM((long, ext_y, half, four), F32),
+            pltpu.VMEM((coarse_x + 2, coarse_y, half, WIDE), F32),
+            split(coarse_y),
+            split(coarse_y),
+            split(coarse_y),
+            split(coarse_y - 2),
         ],
-        flops=2 * conv_flops,
-    )
-    near = (ext_x + 2, ext_y + 2, half)
-    near_rows = near[0] * near[1] * half
-    split = (coarse_x + 2, 2, coarse_y + 2, 2, half, WIDE)
-    faces = (x_low, x_high, y_low, y_high)
-    features, fine, delta_coarse, delta = call(
-        functools.partial(level_kernel, channels=channels, fields=fields),
-        (
-            struct((coarse_rows, coarse), BF16),
-            struct((pairs, WIDE), BF16),
-            struct((coarse_rows, coarse), BF16),
-            struct((near_rows, WIDE), BF16),
-        ),
-        (grid, given, *faces, silu, slope, conv_blocks, down_blocks),
-        "level",
-        scratch=[
-            pltpu.VMEM((2 * long, 5, half, WIDE), F32),
-            pltpu.VMEM((2 * long, 5, half, four), F32),
-            pltpu.VMEM((coarse_x + 2, coarse_y + 2, half, WIDE), F32),
-            pltpu.VMEM(split, F32),
-            pltpu.VMEM(split, F32),
-            pltpu.VMEM(split, F32),
-        ],
-        flops=conv_flops,
-        megabytes=8,
+        flops=3 * conv_flops,
     )
     used = 39 * channels
     chunk = -(-used // (32 * devices)) * 32
     half_rows = devices // 2 * chunk
-    keep, give = call(
-        functools.partial(weight_grad_kernel, channels=channels, fields=fields, scale=scale),
-        (struct((half_rows, LANE), F32), struct((half_rows, LANE), BF16)),
-        (place, grid, *faces, fine, delta_coarse, delta),
-        "weight_grad",
+    features, delta, keep, give = call(
+        functools.partial(strip_kernel, channels=channels, fields=fields, scale=scale),
+        (
+            struct((coarse_rows, coarse), BF16),
+            struct((near_rows, WIDE), BF16),
+            struct((half_rows, LANE), F32),
+            struct((half_rows, LANE), BF16),
+        ),
+        (place, grid, given, x_low, x_high, y_low, y_high, *middle, conv_blocks, down_blocks,
+         down_back),
+        "strip",
         scratch=[
-            pltpu.VMEM((*near, WIDE), F32),
-            pltpu.VMEM((*near, four), F32),
-            pltpu.VMEM((*near, WIDE), F32),
-            pltpu.VMEM((coarse_x, 2, coarse_y, 2, half, WIDE), F32),
+            pltpu.VMEM((2 * long, 2 * rim, half, WIDE), F32),
+            pltpu.VMEM((2 * long, 2 * rim, half, four), F32),
+            pltpu.VMEM((coarse_x + 2, 4, half, WIDE), F32),
+            split(4),
+            split(4),
+            split(4),
+            split(4),
             pltpu.VMEM((2 * half_rows, LANE), F32),
         ],
         flops=conv_flops,

time: 121 us -> 119 us (0.983)
  waiting for transfers between devices: 29 us -> 25 us
  starting transfers between devices: 29.1 us -> 25.8 us
  local copies, waits for them, and re-layouts: 4.77 us -> 7.61 us
  Pallas kernels: 30.8 us -> 32.7 us
    all_to_all x2, starting transfers between devices: 19.3 us -> 16.4 us  [exchange(): lax.all_to_all(blocks, AXES, split_axis=0, concat_axis=0, tiled=True, **g...]
    unnamed x22, local copies, waits for them, and re-layouts: 4.74 us -> 7.58 us
    all_to_all x2, waiting for transfers between devices: 20.5 us -> 17.7 us  [exchange(): lax.all_to_all(blocks, AXES, split_axis=0, concat_axis=0, tiled=True, **g...]
    pallas_call x12 -> x11, Pallas kernels: 30.8 us -> 32.7 us  [call(): pl.pallas_call(kernel, out_shape=outs, in_specs=[spec(i, arg, far) for i,...]
    ppermute x4, waiting for transfers between devices: 6.98 us -> 5.74 us  [shift(): lax.ppermute(block, axis, [(i, (i + step) % count) for i in range(count)])]
  transfers between devices with their start and end apart: 8 -> 8, of which waited for: 6 -> 5; matrix products, arithmetic and copies ran while one was open for 0% -> 0% of each run, Pallas kernels for 9% -> 13%
where the time goes in v7:
time: 119 us; the launch traced here: 118 us
  Pallas kernels  32.7 us (27%)
  blocking collectives  26.3 us (22%)
  starting transfers between devices  25.8 us (22%)
  waiting for transfers between devices  25 us (21%)
  local copies, waits for them, and re-layouts  7.61 us (6%)
    pallas_call x11, Pallas kernels, call(): pl.pallas_call(kernel, out_shape=outs, in_specs=[spec(i, arg, far) for i,...  32.7 us
    all_to_all x1, blocking collectives, exchange(): lax.all_to_all(blocks, AXES, split_axis=0, concat_axis=0, tiled=True, **g...  26.3 us
    all_to_all x2, waiting for transfers between devices, exchange(): lax.all_to_all(blocks, AXES, split_axis=0, concat_axis=0, tiled=True, **g...  17.7 us
    all_to_all x2, starting transfers between devices, exchange(): lax.all_to_all(blocks, AXES, split_axis=0, concat_axis=0, tiled=True, **g...  16.4 us
    unnamed x22, local copies, waits for them, and re-layouts  7.58 us
    ppermute x4, starting transfers between devices, shift(): lax.ppermute(block, axis, [(i, (i + step) % count) for i in range(count)])  6.6 us
    ppermute x4, waiting for transfers between devices, shift(): lax.ppermute(block, axis, [(i, (i + step) % count) for i in range(count)])  5.74 us
    ppermute x2, starting transfers between devices, to_other_core(): lax.ppermute(block, 'gx', [(i, i ^ 1) for i in range(lax.axis_size('gx'))])  2.8 us
  transfers between devices with their start and end apart: 8, of which 5 were waited for; matrix products, arithmetic and copies ran while one was open for 0% of the time, Pallas kernels for 13%

profile of v7, /device:TPU:1, one launch (start us, length us, event | category | flops | bytes accessed | tf_op | source)
XLA Modules:
  0.0 118.3 jit_solution(8003303350897819483)
XLA Ops:
  0.6 4.8 %dispatch.1 = (bf16[1024,512]{1,0:T(8,128)(2,1)}, s32[2,2048]{1,0:T(2,128)}) custom-call(bf16[96,2048]{1,0:T(8,128)(2,1)} %bitcast.23, s32[1,2048]{1,0:T(1,128)} %bitcast.25, s32[1,2048]{1,0:T(1,128)} %bitcast.26), custom_call_target="tpu_custom_call" | custom-call | flops 2147483648 | bytes 4000000 | tf_op jit(solution)/shard_map/dispatch/pallas_call | solution.py:45
  5.5 0.0 copy-start.7
  5.5 11.5 %all-to-all-start = ((bf16[128,8,512]{2,1,0:T(8,128)(2,1)}), bf16[128,8,512]{2,1,0:T(8,128)(2,1)S(1)}, u32[]{:S(2)}, u32[]{:S(2)}) async-start(bf16[128,8,512]{2,1,0:T(8,128)(2,1)} %bitcast.22), calls=%async_computation | async-start | bytes 2097152 | tf_op jit(solution)/shard_map/all_to_all | solution.py:557
  17.0 0.0 copy-done.7
  17.0 0.0 copy-start.4
  17.0 1.1 copy-done.4
  18.1 0.0 copy-start.5
  18.1 1.0 copy-done.5
  19.1 0.0 copy-start.6
  19.1 0.9 copy-done.6
  20.0 1.0 prepare.1
  21.0 0.0 copy-start
  21.0 0.7 copy-done
  21.7 0.0 copy-start.8
  21.7 1.2 %copy-done.8 = bf16[3456,256]{1,0:T(8,128)(2,1)} copy-done((bf16[3456,256]{1,0:T(8,128)(2,1)}, bf16[3456,256]{1,0:T(8,128)(2,1)S(1)}, u32[]{:S(2)}) %copy-start.8) | copy-done | bytes 1769496
  23.0 0.1 pad_add_fusion.place_ref
  23.1 12.6 %all-to-all-done = bf16[128,8,512]{2,1,0:T(8,128)(2,1)S(1)} async-done(((bf16[128,8,512]{2,1,0:T(8,128)(2,1)}), bf16[128,8,512]{2,1,0:T(8,128)(2,1)S(1)}, u32[]{:S(2)}, u32[]{:S(2)}) %all-to-all-start) | async-done | bytes 1048608 | tf_op jit(solution)/shard_map/all_to_all | solution.py:557
  35.6 0.0 copy-start.1
  35.6 3.2 %pool.1 = (bf16[1024,256]{1,0:T(8,128)(2,1)S(1)}, bf16[448,256]{1,0:T(8,128)(2,1)S(1)}, bf16[448,256]{1,0:T(8,128)(2,1)S(1)}) custom-call(s32[2]{0:T(128)S(1)} %pad_add_fusion.place_ref, bf16[1024,512]{1,0:T(8,128)(2,1)S(1)} %bitcast.18, bf16[256,256]{1,0:T(8,128)(2,1)S(1)} %get-tuple-element.29.coarse_ref), custom_call_target="tpu_custom_call" | custom-call | flops 2147483648 | bytes 4000000 | tf_op jit(solution)/shard_map/pool/pallas_call | solution.py:45
  38.8 1.7 %collective-permute-start = (bf16[448,256]{1,0:T(8,128)(2,1)S(1)}, bf16[448,256]{1,0:T(8,128)(2,1)S(1)}, u32[]{:S(2)}, u32[]{:S(2)}) collective-permute-start(bf16[448,256]{1,0:T(8,128)(2,1)S(1)} %get-tuple-element.31), channel_id=1, source_target_pairs={{0,16},{16,32},{32,48},{48,64},{64,80},{80,96},{96,112},{112,0},{1... | collective-permute-start | bytes 688136 | tf_op jit(solution)/shard_map/ppermute | solution.py:549
  40.6 0.0 collective-permute-start.1
  40.6 3.0 %collective-permute-done.low_ref.x_low = bf16[448,256]{1,0:T(8,128)(2,1)S(1)} collective-permute-done((bf16[448,256]{1,0:T(8,128)(2,1)S(1)}, bf16[448,256]{1,0:T(8,128)(2,1)S(1)}, u32[]{:S(2)}, u32[]{:S(2)}) %collective-permute-start) | collective-permute-done | bytes 229408 | tf_op jit(solution)/shard_map/ppermute | solution.py:549
  43.5 2.8 %collective-permute-done.1.high_ref.x_high = bf16[448,256]{1,0:T(8,128)(2,1)S(1)} collective-permute-done((bf16[448,256]{1,0:T(8,128)(2,1)S(1)}, bf16[448,256]{1,0:T(8,128)(2,1)S(1)}, u32[]{:S(2)}, u32[]{:S(2)}) %collective-permute-start.1) | collective-permute-done | bytes 229408 | tf_op jit(solution)/shard_map/ppermute | solution.py:549
  46.3 0.6 edge.1
  46.9 0.7 collective-permute-start.2
  47.6 4.1 %collective-permute-start.3 = (bf16[384,256]{1,0:T(8,128)(2,1)S(1)}, bf16[384,256]{1,0:T(8,128)(2,1)S(1)}, u32[]{:S(2)}, u32[]{:S(2)}) collective-permute-start(bf16[384,256]{1,0:T(8,128)(2,1)S(1)} %get-tuple-element.34), channel_id=1, source_target_pairs={{0,15},{1,0},{2,1},{3,2},{4,3},{5,4},{6,5},{7,6},{8,7},{9,8},{10,9... | collective-permute-start | bytes 589832 | tf_op jit(solution)/shard_map/ppermute | solution.py:549
  51.8 0.0 copy-done.1
  51.8 7.5 %middle.1 = (bf16[192,256]{1,0:T(8,128)(2,1)S(1)}, f32[192,256]{1,0:T(8,128)S(1)}, bf16[192,192]{1,0:T(8,128)(2,1)S(1)}, bf16[960,256]{1,0:T(8,128)(2,1)S(1)}, f...) custom-call(bf16[1024,256]{1,0:T(8,128)(2,1)S(1)} %get-tuple-element.30.grid_ref, ...), custom_call_target="tpu_custom_call" | custom-call | flops 5435817984 | bytes 4000000 | tf_op jit(solution)/shard_map/middle/pallas_call | solution.py:45
  59.3 0.0 collective-permute-done.2.y_low
  59.3 0.0 collective-permute-done.3.y_high
  59.3 5.3 %strip.1 = (bf16[256,192]{1,0:T(8,128)(2,1)}, bf16[1440,256]{1,0:T(8,128)(2,1)S(1)}, f32[2048,128]{1,0:T(8,128)S(1)}, bf16[2048,128]{1,0:T(8,128)(2,1)S(1)}) custom-call(s32[2]{0:T(128)S(1)} %pad_add_fusion.place_ref, bf16[1024,256]{1,0:T(8,128)(2,1)S(1)} %get-tuple-element.30.grid_ref, bf16[256,256]{1,0:T(8,128)(2,1)S(1)} %get-tuple-element.29.coarse_ref, ...), custom_call_target="tpu_custom_call" | custom-call | flops 1811939328 | bytes 8000000 | tf_op jit(solution)/shard_map/strip/pallas_call | solution.py:45
  64.6 0.0 copy-start.2
  64.6 1.2 %collective-permute-start.4 = (bf16[2048,128]{1,0:T(8,128)(2,1)S(1)}, bf16[2048,128]{1,0:T(8,128)(2,1)S(1)}, u32[]{:S(2)}, u32[]{:S(2)}) collective-permute-start(bf16[2048,128]{1,0:T(8,128)(2,1)S(1)} %get-tuple-element.46), channel_id=1, source_target_pairs={{0,16},{16,0},{32,48},{48,32},{64,80},{80,64},{96,112},{112,96},{1... | collective-permute-start | bytes 1572872 | tf_op jit(solution)/shard_map/ppermute | solution.py:553
  65.8 1.5 %collective-permute-done.4.other_ref = bf16[2048,128]{1,0:T(8,128)(2,1)S(1)} collective-permute-done((bf16[2048,128]{1,0:T(8,128)(2,1)S(1)}, bf16[2048,128]{1,0:T(8,128)(2,1)S(1)}, u32[]{:S(2)}, u32[]{:S(2)}) %collective-permute-start.4) | collective-permute-done | bytes 524320 | tf_op jit(solution)/shard_map/ppermute | solution.py:553
  67.4 0.9 pair.1
  68.2 0.0 copy-done.2
  68.2 4.9 %all-to-all-start.1 = ((bf16[64,32,128]{2,1,0:T(8,128)(2,1)}), bf16[64,32,128]{2,1,0:T(8,128)(2,1)S(1)}, u32[]{:S(2)}, u32[]{:S(2)}) async-start(bf16[64,32,128]{2,1,0:T(8,128)(2,1)} %bitcast.10), calls=%async_computation.1 | async-start | bytes 1048576 | tf_op jit(solution)/shard_map/all_to_all | solution.py:557
  73.1 0.0 copy-start.3
  73.2 1.1 copy-done.3
  74.3 0.0 copy-start.9
  74.3 1.5 %copy-done.9 = bf16[3456,256]{1,0:T(8,128)(2,1)S(1)} copy-done((bf16[3456,256]{1,0:T(8,128)(2,1)S(1)}, bf16[3456,256]{1,0:T(8,128)(2,1)}, u32[]{:S(2)}) %copy-start.9) | copy-done | bytes 1769496
  75.7 4.5 %input_grad.1.back_ref = bf16[1024,384]{1,0:T(8,128)(2,1)S(1)} custom-call(bf16[1440,256]{1,0:T(8,128)(2,1)S(1)} %copy-done.3, bf16[3456,256]{1,0:T(8,128)(2,1)S(1)} %copy-done.9, bf16[1024,512]{1,0:T(8,128)(2,1)S(1)} %bitcast.19), custom_call_target="tpu_custom_call" | custom-call | flops 3959422976 | bytes 8000000 | tf_op jit(solution)/shard_map/input_grad/pallas_call | solution.py:45
  80.3 5.1 %all-to-all-done.1.terms_ref = bf16[64,32,128]{2,1,0:T(8,128)(2,1)S(1)} async-done(((bf16[64,32,128]{2,1,0:T(8,128)(2,1)}), bf16[64,32,128]{2,1,0:T(8,128)(2,1)S(1)}, u32[]{:S(2)}, u32[]{:S(2)}) %all-to-all-start.1) | async-done | bytes 524320 | tf_op jit(solution)/shard_map/all_to_all | solution.py:557
  85.4 0.2 join.1
  85.6 0.0 copy-start.10
  85.6 26.3 %all_to_all.15 = bf16[128,8,640]{2,1,0:T(8,128)(2,1)S(1)} all-to-all(bf16[128,8,640]{2,1,0:T(8,128)(2,1)S(1)} %bitcast.17), channel_id=1, replica_groups=mesh['gx'=8,'gy'=16] {'gx','gy'}, dimensions={0} | all-to-all | bytes 2621440 | tf_op jit(solution)/shard_map/all_to_all | solution.py:557
  111.9 1.6 %collective-permute-start.5 = (bf16[1024,256]{1,0:T(8,128)(2,1)S(1)}, bf16[1024,256]{1,0:T(8,128)(2,1)S(1)}, u32[]{:S(2)}, u32[]{:S(2)}) collective-permute-start(bf16[1024,256]{1,0:T(8,128)(2,1)S(1)} %slice.4), channel_id=1, source_target_pairs={{0,16},{16,0},{32,48},{48,32},{64,80},{80,64},{96,112},{112,96},{1... | collective-permute-start | bytes 1572872 | tf_op jit(solution)/shard_map/ppermute | solution.py:553
  113.5 0.0 copy-done.10
  113.5 2.7 %collect.1 = bf16[96,2048]{1,0:T(8,128)(2,1)} custom-call(bf16[1024,640]{1,0:T(8,128)(2,1)S(1)} %bitcast.15, s32[2,2048]{1,0:T(2,128)S(1)} %copy-done.10), custom_call_target="tpu_custom_call" | custom-call | flops 2147483648 | bytes 4000000 | tf_op jit(solution)/shard_map/collect/pallas_call | solution.py:45
  116.2 0.0 collective-permute-done.5.theirs_ref
  116.2 2.1 %unpack.1 = (f32[27,96,96]{2,1,0:T(8,128)}, f32[8,96,192]{2,1,0:T(8,128)}) custom-call(s32[2]{0:T(128)S(1)} %pad_add_fusion.place_ref, bf16[1024,640]{1,0:T(8,128)(2,1)S(1)} %bitcast.16, bf16[1024,256]{1,0:T(8,128)(2,1)S(1)} %collective-permute-done.5.theirs_ref), custom_call_target="tpu_custom_call" | custom-call | bytes 4000000 | tf_op jit(solution)/shard_map/unpack/pallas_call | solution.py:45
  (1 shorter events, 0.0 us)
Async XLA Ops:
  5.5 11.5 %copy-start.7 = (s32[8,16,16]{2,1,0:T(8,128)S(1)}, s32[8,16,16]{2,1,0:T(8,128)}, u32[]{:S(2)}) copy-start(s32[8,16,16]{2,1,0:T(8,128)} %param.10) | copy-start | bytes 24580
  5.5 30.1 %all-to-all-start = ((bf16[128,8,512]{2,1,0:T(8,128)(2,1)}), bf16[128,8,512]{2,1,0:T(8,128)(2,1)S(1)}, u32[]{:S(2)}, u32[]{:S(2)}) async-start(bf16[128,8,512]{2,1,0:T(8,128)(2,1)} %bitcast.22), calls=%async_computation | async-start | bytes 2097152 | tf_op jit(solution)/shard_map/all_to_all | solution.py:557
  17.0 1.1 copy-start.4
  18.1 1.0 copy-start.5
  19.1 0.9 copy-start.6
  21.0 0.7 copy-start
  21.7 1.3 %copy-start.8 = (bf16[3456,256]{1,0:T(8,128)(2,1)}, bf16[3456,256]{1,0:T(8,128)(2,1)S(1)}, u32[]{:S(2)}) copy-start(bf16[3456,256]{1,0:T(8,128)(2,1)S(1)} %get-tuple-element.48.conv_ref) | copy-start | bytes 5308420
  35.6 16.1 %copy-start.1 = (bf16[192,1024]{1,0:T(8,128)(2,1)S(1)}, bf16[192,1024]{1,0:T(8,128)(2,1)}, u32[]{:S(2)}) copy-start(bf16[192,1024]{1,0:T(8,128)(2,1)} %copy-done) | copy-start | bytes 1179652
  38.8 4.7 %collective-permute-start = (bf16[448,256]{1,0:T(8,128)(2,1)S(1)}, bf16[448,256]{1,0:T(8,128)(2,1)S(1)}, u32[]{:S(2)}, u32[]{:S(2)}) collective-permute-start(bf16[448,256]{1,0:T(8,128)(2,1)S(1)} %get-tuple-element.31), channel_id=1, source_target_pairs={{0,16},{16,32},{32,48},{48,64},{64,80},{80,96},{96,112},{112,0},{1... | collective-permute-start | bytes 688136 | tf_op jit(solution)/shard_map/ppermute | solution.py:549
  40.6 5.7 %collective-permute-start.1 = (bf16[448,256]{1,0:T(8,128)(2,1)S(1)}, bf16[448,256]{1,0:T(8,128)(2,1)S(1)}, u32[]{:S(2)}, u32[]{:S(2)}) collective-permute-start(bf16[448,256]{1,0:T(8,128)(2,1)S(1)} %get-tuple-element.32), channel_id=1, source_target_pairs={{0,112},{16,0},{32,16},{48,32},{64,48},{80,64},{96,80},{112,96},{1... | collective-permute-start | bytes 688136 | tf_op jit(solution)/shard_map/ppermute | solution.py:549
  46.9 12.4 %collective-permute-start.2 = (bf16[384,256]{1,0:T(8,128)(2,1)S(1)}, bf16[384,256]{1,0:T(8,128)(2,1)S(1)}, u32[]{:S(2)}, u32[]{:S(2)}) collective-permute-start(bf16[384,256]{1,0:T(8,128)(2,1)S(1)} %get-tuple-element.33), channel_id=1, source_target_pairs={{0,1},{1,2},{2,3},{3,4},{4,5},{5,6},{6,7},{7,8},{8,9},{9,10},{10,1... | collective-permute-start | bytes 589832 | tf_op jit(solution)/shard_map/ppermute | solution.py:549
  47.6 11.7 %collective-permute-start.3 = (bf16[384,256]{1,0:T(8,128)(2,1)S(1)}, bf16[384,256]{1,0:T(8,128)(2,1)S(1)}, u32[]{:S(2)}, u32[]{:S(2)}) collective-permute-start(bf16[384,256]{1,0:T(8,128)(2,1)S(1)} %get-tuple-element.34), channel_id=1, source_target_pairs={{0,15},{1,0},{2,1},{3,2},{4,3},{5,4},{6,5},{7,6},{8,7},{9,8},{10,9... | collective-permute-start | bytes 589832 | tf_op jit(solution)/shard_map/ppermute | solution.py:549
  64.6 3.7 %copy-start.2 = (bf16[1440,256]{1,0:T(8,128)(2,1)}, bf16[1440,256]{1,0:T(8,128)(2,1)S(1)}, u32[]{:S(2)}) copy-start(bf16[1440,256]{1,0:T(8,128)(2,1)S(1)} %get-tuple-element.47.delta_ref) | copy-start | bytes 2211844
  64.6 2.8 %collective-permute-start.4 = (bf16[2048,128]{1,0:T(8,128)(2,1)S(1)}, bf16[2048,128]{1,0:T(8,128)(2,1)S(1)}, u32[]{:S(2)}, u32[]{:S(2)}) collective-permute-start(bf16[2048,128]{1,0:T(8,128)(2,1)S(1)} %get-tuple-element.46), channel_id=1, source_target_pairs={{0,16},{16,0},{32,48},{48,32},{64,80},{80,64},{96,112},{112,96},{1... | collective-permute-start | bytes 1572872 | tf_op jit(solution)/shard_map/ppermute | solution.py:553
  68.2 17.2 %all-to-all-start.1 = ((bf16[64,32,128]{2,1,0:T(8,128)(2,1)}), bf16[64,32,128]{2,1,0:T(8,128)(2,1)S(1)}, u32[]{:S(2)}, u32[]{:S(2)}) async-start(bf16[64,32,128]{2,1,0:T(8,128)(2,1)} %bitcast.10), calls=%async_computation.1 | async-start | bytes 1048576 | tf_op jit(solution)/shard_map/all_to_all | solution.py:557
  73.1 1.1 copy-start.3
  74.3 1.5 %copy-start.9 = (bf16[3456,256]{1,0:T(8,128)(2,1)S(1)}, bf16[3456,256]{1,0:T(8,128)(2,1)}, u32[]{:S(2)}) copy-start(bf16[3456,256]{1,0:T(8,128)(2,1)} %copy-done.8) | copy-start | bytes 5308420
  85.6 27.9 %copy-start.10 = (s32[2,2048]{1,0:T(2,128)S(1)}, s32[2,2048]{1,0:T(2,128)}, u32[]{:S(2)}) copy-start(s32[2,2048]{1,0:T(2,128)} %get-tuple-element.49.slot_ref) | copy-start | bytes 49156
  111.9 4.3 %collective-permute-start.5 = (bf16[1024,256]{1,0:T(8,128)(2,1)S(1)}, bf16[1024,256]{1,0:T(8,128)(2,1)S(1)}, u32[]{:S(2)}, u32[]{:S(2)}) collective-permute-start(bf16[1024,256]{1,0:T(8,128)(2,1)S(1)} %slice.4), channel_id=1, source_target_pairs={{0,16},{16,0},{32,48},{48,32},{64,80},{80,64},{96,112},{112,96},{1... | collective-permute-start | bytes 1572872 | tf_op jit(solution)/shard_map/ppermute | solution.py:553

commit v8 on v7

--- a/solution.py
+++ b/solution.py
@@ -116,7 +116,7 @@
 
 
 def pool_kernel(
-    place_ref, got_ref, coarse_ref, grid_ref, first_ref, last_ref, total_ref,
+    place_ref, got_ref, coarse_ref, grid_ref, even_ref, odd_ref, total_ref,
     *, channels, fields, count,
 ):
     rows = got_ref.shape[0]
@@ -139,8 +139,11 @@
     at = 0
     for ref, (ext_x, ext_y, half, rim) in zip((total_ref, coarse_ref), fields):
         field = as_field(ref[...], ext_x, ext_y, half)
-        put_rows(first_ref, at, field[:rim] * inside(place_ref[0], 0))
-        put_rows(last_ref, at, field[ext_x - rim :] * inside(place_ref[0], count - 1))
+        first = field[:rim] * inside(place_ref[0], 0)
+        last = field[ext_x - rim :] * inside(place_ref[0], count - 1)
+        even, odd = by_parity(place_ref[0], first, last)
+        put_rows(even_ref, at, even)
+        put_rows(odd_ref, at, odd)
         at += rim * ext_y * half
     grid_ref[...] = total_ref[...].astype(BF16)
 
@@ -158,20 +161,25 @@
     return jnp.where(place == end, 0.0, 1.0)
 
 
+def by_parity(place, one, other):
+    swap = place % 2 == 1
+    return jnp.where(swap, one, other), jnp.where(swap, other, one)
+
+
 def edge_kernel(
-    place_ref, grid_ref, coarse_ref, low_ref, high_ref, first_ref, last_ref, *, fields, count
+    place_ref, grid_ref, coarse_ref, x_even, x_odd, even_ref, odd_ref, *, fields, count
 ):
     start, at = 0, 0
     for ref, (ext_x, ext_y, half, rim) in zip((grid_ref, coarse_ref), fields):
         size = rim * ext_y * half
-        parts = (
-            as_field(low_ref[start : start + size, :], rim, ext_y, half),
-            as_field(ref[...], ext_x, ext_y, half),
-            as_field(high_ref[start : start + size, :], rim, ext_y, half),
-        )
-        for part in parts:
-            put_rows(first_ref, at, part[:, :rim] * inside(place_ref[1], 0))
-            put_rows(last_ref, at, part[:, ext_y - rim :] * inside(place_ref[1], count - 1))
+        x_faces = [as_field(ref_x[start : start + size, :], rim, ext_y, half) for ref_x in (x_even, x_odd)]
+        low, high = by_parity(place_ref[0], *x_faces)
+        for part in (low, as_field(ref[...], ext_x, ext_y, half), high):
+            first = part[:, :rim] * inside(place_ref[1], 0)
+            last = part[:, ext_y - rim :] * inside(place_ref[1], count - 1)
+            even, odd = by_parity(place_ref[1], first, last)
+            put_rows(even_ref, at, even)
+            put_rows(odd_ref, at, odd)
             at += part.shape[0] * rim * half
         start += size
 
@@ -300,21 +308,21 @@
 
 
 def middle_kernel(
-    grid_ref, coarse_ref, x_low, x_high, conv_ref, down_ref, down_back_ref,
+    place_ref, grid_ref, coarse_ref, x_even, x_odd, conv_ref, down_ref, down_back_ref,
     fine_ref, slope_ref, features_ref, delta_ref, conv_grad_ref, down_grad_ref,
     pad_ref, four_ref, coarse_s, mask_s, fine_s, slope_s, delta_s, *, channels, rim,
 ):
     ext_x, ext_y, half = pad_ref.shape[0], pad_ref.shape[1], pad_ref.shape[2]
     size = rim * ext_y * half
-    pad_ref[:rim] = as_field(x_low[:size, :], rim, ext_y, half)
+    x_faces = [as_field(ref[:size, :], rim, ext_y, half) for ref in (x_even, x_odd)]
+    pad_ref[:rim], pad_ref[ext_x - rim :] = by_parity(place_ref[0], *x_faces)
     pad_ref[rim : ext_x - rim] = as_field(grid_ref[...], ext_x - 2 * rim, ext_y, half)
-    pad_ref[ext_x - rim :] = as_field(x_high[:size, :], rim, ext_y, half)
     fill_four(pad_ref, four_ref, channels)
     coarse_x, coarse_y = coarse_s.shape[0], coarse_s.shape[1]
     coarse = down_ref.shape[1]
-    coarse_s[:1] = as_field(x_low[size:, :], 1, coarse_y, half)
+    x_faces = [as_field(ref[size:, :], 1, coarse_y, half) for ref in (x_even, x_odd)]
+    coarse_s[:1], coarse_s[coarse_x - 1 :] = by_parity(place_ref[0], *x_faces)
     coarse_s[1 : coarse_x - 1] = as_field(coarse_ref[...], coarse_x - 2, coarse_y, half)
-    coarse_s[coarse_x - 1 :] = as_field(x_high[size:, :], 1, coarse_y, half)
     coarse_mask = child_masks(coarse_s, mask_s, coarse)
     count, inside_y = 4, ext_y - 2
     for first in range(0, ext_x - 2, count):
@@ -355,7 +363,7 @@
 
 
 def strip_kernel(
-    place_ref, grid_ref, coarse_ref, x_low, x_high, y_low, y_high, fine_ref, slope_ref,
+    place_ref, grid_ref, coarse_ref, x_even, x_odd, y_even, y_odd, fine_ref, slope_ref,
     mid_features_ref, mid_delta_ref, conv_grad_ref, down_grad_ref, conv_ref, down_ref,
     down_back_ref, features_ref, delta_ref, keep_ref, give_ref,
     pad_ref, four_ref, coarse_s, mask_s, fine_s, slope_s, delta_s, sum_s,
@@ -364,29 +372,27 @@
     (ext_x, ext_y, half, rim), (coarse_x, coarse_y, _, _) = fields
     long = ext_x + 2 * rim
     slab, face = rim * ext_y * half, long * rim * half
-    parts = (
-        as_field(x_low[:slab, :], rim, ext_y, half),
-        as_field(grid_ref[...], ext_x, ext_y, half),
-        as_field(x_high[:slab, :], rim, ext_y, half),
-    )
-    for side, y_ref in enumerate((y_low, y_high)):
+    x_faces = [as_field(ref[:slab, :], rim, ext_y, half) for ref in (x_even, x_odd)]
+    low, high = by_parity(place_ref[0], *x_faces)
+    parts = (low, as_field(grid_ref[...], ext_x, ext_y, half), high)
+    y_faces = [as_field(ref[:face, :], long, rim, half) for ref in (y_even, y_odd)]
+    for side, y_face in enumerate(by_parity(place_ref[1], *y_faces)):
         ours, here, there = ((0, rim, 0), (ext_y - rim, 0, rim))[side]
         at = side * long
-        pad_ref[at : at + long, there : there + rim] = as_field(y_ref[:face, :], long, rim, half)
+        pad_ref[at : at + long, there : there + rim] = y_face
         for part in parts:
             count = part.shape[0]
             pad_ref[at : at + count, here : here + rim] = part[:, ours : ours + rim]
             at += count
     fill_four(pad_ref, four_ref, channels)
-    parts = (
-        as_field(x_low[slab:, :], 1, coarse_y, half),
-        as_field(coarse_ref[...], coarse_x, coarse_y, half),
-        as_field(x_high[slab:, :], 1, coarse_y, half),
-    )
-    for side, y_ref in enumerate((y_low, y_high)):
+    x_faces = [as_field(ref[slab:, :], 1, coarse_y, half) for ref in (x_even, x_odd)]
+    low, high = by_parity(place_ref[0], *x_faces)
+    parts = (low, as_field(coarse_ref[...], coarse_x, coarse_y, half), high)
+    y_faces = [as_field(ref[face:, :], coarse_x + 2, 1, half) for ref in (y_even, y_odd)]
+    for side, y_face in enumerate(by_parity(place_ref[1], *y_faces)):
         y = side * (coarse_y - 1)
         theirs = 3 * side
-        coarse_s[:, theirs : theirs + 1] = as_field(y_ref[face:, :], coarse_x + 2, 1, half)
+        coarse_s[:, theirs : theirs + 1] = y_face
         at = 0
         for part in parts:
             count = part.shape[0]
@@ -433,12 +439,13 @@
     for j in range(9):
         grad = fold(mm(turned, jnp.concatenate([low[j], high[j]], axis=0)), channels)
         grad = grad + conv_grad_ref[j * LANE : (j + 1) * LANE, :]
-        sum_s[j * three : (j + 1) * three, :] = grad.T * scale
+        sum_s[j * three : (j + 1) * three, :] = (grad * scale).astype(BF16).T
     ours = rows_of(delta_coarse[1 : 1 + coarse_x, 1:3]).astype(BF16)
     base = 27 * channels
     for j in range(4):
         piece = rows_of(fine_s[1 : 1 + coarse_x, j // 2, 1:3, j % 2]).astype(BF16)
         grad = (mm(piece, ours, TN) + down_grad_ref[j * WIDE : (j + 1) * WIDE, :]) * scale
+        grad = grad.astype(BF16)
         first, second = grad[:channels], grad[LANE : LANE + channels]
         start = base + 2 * j * channels
         sum_s[start : start + channels, :] = first[:, :LANE]
@@ -448,16 +455,15 @@
             [first[:, LANE:], second[:, LANE:]], axis=1
         )
     end = base + 12 * channels
-    sum_s[end:, :] = jnp.zeros((sum_s.shape[0] - end, LANE), F32)
+    sum_s[end:, :] = jnp.zeros((sum_s.shape[0] - end, LANE), BF16)
     size = keep_ref.shape[0]
     core = place_ref[0] % 2
     keep_ref[...] = sum_s[pl.ds(pl.multiple_of(core * size, size), size), :]
-    give = sum_s[pl.ds(pl.multiple_of((1 - core) * size, size), size), :]
-    give_ref[...] = give.astype(BF16)
+    give_ref[...] = sum_s[pl.ds(pl.multiple_of((1 - core) * size, size), size), :]
 
 
 def pair_kernel(keep_ref, other_ref, out_ref):
-    out_ref[...] = (keep_ref[...] + other_ref[...].astype(F32)).astype(BF16)
+    out_ref[...] = (keep_ref[...].astype(F32) + other_ref[...].astype(F32)).astype(BF16)
 
 
 def input_grad_kernel(delta_ref, conv_ref, got_ref, back_ref, pad_ref, four_ref, grad_s, *, channels):
@@ -544,9 +550,15 @@
         down_ref[j, :, LANE:] = tail[:, (j % 2) * rest : (j % 2 + 1) * rest]
 
 
-def shift(block, axis, step):
+def swap_faces(even, odd, axis):
     count = lax.axis_size(axis)
-    return lax.ppermute(block, axis, [(i, (i + step) % count) for i in range(count)])
+    pairs = [
+        [(i, (i + 1) % count) for i in range(start, count, 2)]
+        + [((i + 1) % count, i) for i in range(start, count, 2)]
+        for start in range(2)
+    ]
+    odd = lax.ppermute(odd, axis, pairs[1])
+    return lax.ppermute(even, axis, pairs[0]), odd
 
 
 def to_other_core(block):
@@ -613,7 +625,7 @@
     x_rows = sum(e[3] * e[1] * e[2] for e in fields)
     y_rows = sum(e[3] * (e[0] + 2 * e[3]) * e[2] for e in fields)
     place = jnp.stack([lax.axis_index("gx"), lax.axis_index("gy")]).astype(jnp.int32)
-    grid, x_first, x_last = call(
+    grid, x_even, x_odd = call(
         functools.partial(pool_kernel, channels=channels, fields=fields, count=count_x),
         tuple(struct((n, WIDE), BF16) for n in (pairs, x_rows, x_rows)),
         (place, got, given),
@@ -621,14 +633,14 @@
         scratch=[pltpu.VMEM((pairs, WIDE), F32)],
         flops=pick_flops,
     )
-    x_low, x_high = shift(x_last, "gx", 1), shift(x_first, "gx", -1)
-    y_first, y_last = call(
+    x_faces = swap_faces(x_even, x_odd, "gx")
+    y_even, y_odd = call(
         functools.partial(edge_kernel, fields=fields, count=count_y),
         tuple(struct((n, WIDE), BF16) for n in (y_rows, y_rows)),
-        (place, grid, given, x_low, x_high),
+        (place, grid, given, *x_faces),
         "edge",
     )
-    y_low, y_high = shift(y_last, "gy", 1), shift(y_first, "gy", -1)
+    y_faces = swap_faces(y_even, y_odd, "gy")
     long = ext_x + 2 * rim
     near = (ext_x + 2, ext_y + 2, half)
     near_rows = near[0] * near[1] * half
@@ -647,7 +659,7 @@
             struct((9 * LANE, 3 * channels), F32),
             struct((4 * WIDE, coarse), F32),
         ),
-        (grid, given, x_low, x_high, conv_blocks, down_blocks, down_back),
+        (place, grid, given, *x_faces, conv_blocks, down_blocks, down_back),
         "middle",
         scratch=[
             pltpu.VMEM((long, ext_y, half, WIDE), F32),
@@ -668,11 +680,10 @@
         (
             struct((coarse_rows, coarse), BF16),
             struct((near_rows, WIDE), BF16),
-            struct((half_rows, LANE), F32),
+            struct((half_rows, LANE), BF16),
             struct((half_rows, LANE), BF16),
         ),
-        (place, grid, given, x_low, x_high, y_low, y_high, *middle, conv_blocks, down_blocks,
-         down_back),
+        (place, grid, given, *x_faces, *y_faces, *middle, conv_blocks, down_blocks, down_back),
         "strip",
         scratch=[
             pltpu.VMEM((2 * long, 2 * rim, half, WIDE), F32),
@@ -682,7 +693,7 @@
             split(4),
             split(4),
             split(4),
-            pltpu.VMEM((2 * half_rows, LANE), F32),
+            pltpu.VMEM((2 * half_rows, LANE), BF16),
         ],
         flops=conv_flops,
         megabytes=8,

time: 119 us -> 118 us (level)
    ppermute x4, starting transfers between devices: 6.6 us -> 3.6 us  [the longest x2 2.29 us: swap_faces(): return (lax.ppermute(even, axis, pairs[0]), odd)]
    all_to_all x2, starting transfers between devices: 16.4 us -> 18.1 us  [exchange(): lax.all_to_all(blocks, AXES, split_axis=0, concat_axis=0, tiled=True, **g...]
  transfers between devices with their start and end apart: 8 -> 8, of which waited for: 5 -> 5; matrix products, arithmetic and copies ran while one was open for 0% -> 0% of each run, Pallas kernels for 13% -> 14%
where the time goes in v8:
time: 118 us; the launch traced here: 117 us
  Pallas kernels  32.9 us (28%)
  blocking collectives  26.3 us (22%)
  starting transfers between devices  24.8 us (21%)
  waiting for transfers between devices  24.7 us (21%)
  local copies, waits for them, and re-layouts  7.61 us (6%)
    pallas_call x11, Pallas kernels, call(): pl.pallas_call(kernel, out_shape=outs, in_specs=[spec(i, arg, far) for i,...  32.9 us
    all_to_all x1, blocking collectives, exchange(): lax.all_to_all(blocks, AXES, split_axis=0, concat_axis=0, tiled=True, **g...  26.3 us
    all_to_all x2, starting transfers between devices, exchange(): lax.all_to_all(blocks, AXES, split_axis=0, concat_axis=0, tiled=True, **g...  18.1 us
    all_to_all x2, waiting for transfers between devices, exchange(): lax.all_to_all(blocks, AXES, split_axis=0, concat_axis=0, tiled=True, **g...  17.7 us
    unnamed x22, local copies, waits for them, and re-layouts  7.58 us
    ppermute x2, waiting for transfers between devices, swap_faces(): odd = lax.ppermute(odd, axis, pairs[1])  4.63 us
    ppermute x2, starting transfers between devices, to_other_core(): lax.ppermute(block, 'gx', [(i, i ^ 1) for i in range(lax.axis_size('gx'))])  3.15 us
  transfers between devices with their start and end apart: 8, of which 5 were waited for; matrix products, arithmetic and copies ran while one was open for 0% of the time, Pallas kernels for 14%

profile of v8, /device:TPU:1, one launch (start us, length us, event | category | flops | bytes accessed | tf_op | source)
XLA Modules:
  0.0 117.1 jit_solution(4362813949390207606)
XLA Ops:
  0.6 4.8 %dispatch.1 = (bf16[1024,512]{1,0:T(8,128)(2,1)}, s32[2,2048]{1,0:T(2,128)}) custom-call(bf16[96,2048]{1,0:T(8,128)(2,1)} %bitcast.23, s32[1,2048]{1,0:T(1,128)} %bitcast.25, s32[1,2048]{1,0:T(1,128)} %bitcast.26), custom_call_target="tpu_custom_call" | custom-call | flops 2147483648 | bytes 4000000 | tf_op jit(solution)/shard_map/dispatch/pallas_call | solution.py:45
  5.5 0.0 copy-start.7
  5.5 11.5 %all-to-all-start = ((bf16[128,8,512]{2,1,0:T(8,128)(2,1)}), bf16[128,8,512]{2,1,0:T(8,128)(2,1)S(1)}, u32[]{:S(2)}, u32[]{:S(2)}) async-start(bf16[128,8,512]{2,1,0:T(8,128)(2,1)} %bitcast.22), calls=%async_computation | async-start | bytes 2097152 | tf_op jit(solution)/shard_map/all_to_all | solution.py:569
  17.0 0.0 copy-done.7
  17.0 0.0 copy-start.4
  17.0 1.1 copy-done.4
  18.1 0.0 copy-start.5
  18.1 1.0 copy-done.5
  19.1 0.0 copy-start.6
  19.1 0.9 copy-done.6
  20.0 1.0 prepare.1
  21.0 0.0 copy-start
  21.0 0.7 copy-done
  21.7 0.0 copy-start.8
  21.7 1.2 %copy-done.8 = bf16[3456,256]{1,0:T(8,128)(2,1)} copy-done((bf16[3456,256]{1,0:T(8,128)(2,1)}, bf16[3456,256]{1,0:T(8,128)(2,1)S(1)}, u32[]{:S(2)}) %copy-start.8) | copy-done | bytes 1769496
  23.0 0.1 pad_add_fusion.place_ref
  23.1 12.6 %all-to-all-done = bf16[128,8,512]{2,1,0:T(8,128)(2,1)S(1)} async-done(((bf16[128,8,512]{2,1,0:T(8,128)(2,1)}), bf16[128,8,512]{2,1,0:T(8,128)(2,1)S(1)}, u32[]{:S(2)}, u32[]{:S(2)}) %all-to-all-start) | async-done | bytes 1048608 | tf_op jit(solution)/shard_map/all_to_all | solution.py:569
  35.6 0.0 copy-start.1
  35.6 3.2 %pool.1 = (bf16[1024,256]{1,0:T(8,128)(2,1)S(1)}, bf16[448,256]{1,0:T(8,128)(2,1)S(1)}, bf16[448,256]{1,0:T(8,128)(2,1)S(1)}) custom-call(s32[2]{0:T(128)S(1)} %pad_add_fusion.place_ref, bf16[1024,512]{1,0:T(8,128)(2,1)S(1)} %bitcast.18, bf16[256,256]{1,0:T(8,128)(2,1)S(1)} %get-tuple-element.29.coarse_ref), custom_call_target="tpu_custom_call" | custom-call | flops 2147483648 | bytes 4000000 | tf_op jit(solution)/shard_map/pool/pallas_call | solution.py:45
  38.8 1.6 %collective-permute-start = (bf16[448,256]{1,0:T(8,128)(2,1)S(1)}, bf16[448,256]{1,0:T(8,128)(2,1)S(1)}, u32[]{:S(2)}, u32[]{:S(2)}) collective-permute-start(bf16[448,256]{1,0:T(8,128)(2,1)S(1)} %get-tuple-element.31), channel_id=1, source_target_pairs={{0,16},{32,48},{64,80},{96,112},{16,0},{48,32},{80,64},{112,96},{1... | collective-permute-start | bytes 688136 | tf_op jit(solution)/shard_map/ppermute | solution.py:561
  40.4 0.3 collective-permute-start.1
  40.7 0.8 collective-permute-done.x_even
  41.5 4.6 %collective-permute-done.1.x_odd = bf16[448,256]{1,0:T(8,128)(2,1)S(1)} collective-permute-done((bf16[448,256]{1,0:T(8,128)(2,1)S(1)}, bf16[448,256]{1,0:T(8,128)(2,1)S(1)}, u32[]{:S(2)}, u32[]{:S(2)}) %collective-permute-start.1) | collective-permute-done | bytes 229408 | tf_op jit(solution)/shard_map/ppermute | solution.py:560
  46.1 0.7 edge.1
  46.8 0.7 collective-permute-start.2
  47.5 1.0 collective-permute-start.3
  48.5 0.0 copy-done.1
  48.5 8.0 %middle.1 = (bf16[192,256]{1,0:T(8,128)(2,1)S(1)}, f32[192,256]{1,0:T(8,128)S(1)}, bf16[192,192]{1,0:T(8,128)(2,1)S(1)}, bf16[960,256]{1,0:T(8,128)(2,1)S(1)}, f...) custom-call(s32[2]{0:T(128)S(1)} %pad_add_fusion.place_ref, bf16[1024,256]{1,0:T(8,128)(2,1)S(1)} %get-tuple-element.30.grid_ref, ...), custom_call_target="tpu_custom_call" | custom-call | flops 5435817984 | bytes 4000000 | tf_op jit(solution)/shard_map/middle/pallas_call | solution.py:45
  56.5 0.0 collective-permute-done.2.y_even
  56.6 0.0 collective-permute-done.3.y_odd
  56.6 4.8 %strip.1 = (bf16[256,192]{1,0:T(8,128)(2,1)}, bf16[1440,256]{1,0:T(8,128)(2,1)S(1)}, bf16[2048,128]{1,0:T(8,128)(2,1)S(1)}, bf16[2048,128]{1,0:T(8,128)(2,1)S(1)}) custom-call(s32[2]{0:T(128)S(1)} %pad_add_fusion.place_ref, bf16[1024,256]{1,0:T(8,128)(2,1)S(1)} %get-tuple-element.30.grid_ref, bf16[256,256]{1,0:T(8,128)(2,1)S(1)} %get-tuple-element.29.coarse_ref, ...), custom_call_target="tpu_custom_call" | custom-call | flops 1811939328 | bytes 8000000 | tf_op jit(solution)/shard_map/strip/pallas_call | solution.py:45
  61.4 0.0 copy-start.2
  61.4 1.6 %collective-permute-start.4 = (bf16[2048,128]{1,0:T(8,128)(2,1)S(1)}, bf16[2048,128]{1,0:T(8,128)(2,1)S(1)}, u32[]{:S(2)}, u32[]{:S(2)}) collective-permute-start(bf16[2048,128]{1,0:T(8,128)(2,1)S(1)} %get-tuple-element.46), channel_id=1, source_target_pairs={{0,16},{16,0},{32,48},{48,32},{64,80},{80,64},{96,112},{112,96},{1... | collective-permute-start | bytes 1572872 | tf_op jit(solution)/shard_map/ppermute | solution.py:565
  62.9 1.5 %collective-permute-done.4.other_ref = bf16[2048,128]{1,0:T(8,128)(2,1)S(1)} collective-permute-done((bf16[2048,128]{1,0:T(8,128)(2,1)S(1)}, bf16[2048,128]{1,0:T(8,128)(2,1)S(1)}, u32[]{:S(2)}, u32[]{:S(2)}) %collective-permute-start.4) | collective-permute-done | bytes 524320 | tf_op jit(solution)/shard_map/ppermute | solution.py:565
  64.5 0.9 pair.1
  65.4 0.0 copy-done.2
  65.4 6.6 %all-to-all-start.1 = ((bf16[64,32,128]{2,1,0:T(8,128)(2,1)}), bf16[64,32,128]{2,1,0:T(8,128)(2,1)S(1)}, u32[]{:S(2)}, u32[]{:S(2)}) async-start(bf16[64,32,128]{2,1,0:T(8,128)(2,1)} %bitcast.10), calls=%async_computation.1 | async-start | bytes 1048576 | tf_op jit(solution)/shard_map/all_to_all | solution.py:569
  72.0 0.0 copy-start.3
  72.0 1.1 copy-done.3
  73.1 0.0 copy-start.9
  73.1 1.5 %copy-done.9 = bf16[3456,256]{1,0:T(8,128)(2,1)S(1)} copy-done((bf16[3456,256]{1,0:T(8,128)(2,1)S(1)}, bf16[3456,256]{1,0:T(8,128)(2,1)}, u32[]{:S(2)}) %copy-start.9) | copy-done | bytes 1769496
  74.6 4.5 %input_grad.1.back_ref = bf16[1024,384]{1,0:T(8,128)(2,1)S(1)} custom-call(bf16[1440,256]{1,0:T(8,128)(2,1)S(1)} %copy-done.3, bf16[3456,256]{1,0:T(8,128)(2,1)S(1)} %copy-done.9, bf16[1024,512]{1,0:T(8,128)(2,1)S(1)} %bitcast.19), custom_call_target="tpu_custom_call" | custom-call | flops 3959422976 | bytes 8000000 | tf_op jit(solution)/shard_map/input_grad/pallas_call | solution.py:45
  79.1 5.1 %all-to-all-done.1.terms_ref = bf16[64,32,128]{2,1,0:T(8,128)(2,1)S(1)} async-done(((bf16[64,32,128]{2,1,0:T(8,128)(2,1)}), bf16[64,32,128]{2,1,0:T(8,128)(2,1)S(1)}, u32[]{:S(2)}, u32[]{:S(2)}) %all-to-all-start.1) | async-done | bytes 524320 | tf_op jit(solution)/shard_map/all_to_all | solution.py:569
  84.2 0.2 join.1
  84.4 0.0 copy-start.10
  84.4 26.3 %all_to_all.15 = bf16[128,8,640]{2,1,0:T(8,128)(2,1)S(1)} all-to-all(bf16[128,8,640]{2,1,0:T(8,128)(2,1)S(1)} %bitcast.17), channel_id=1, replica_groups=mesh['gx'=8,'gy'=16] {'gx','gy'}, dimensions={0} | all-to-all | bytes 2621440 | tf_op jit(solution)/shard_map/all_to_all | solution.py:569
  110.8 1.6 %collective-permute-start.5 = (bf16[1024,256]{1,0:T(8,128)(2,1)S(1)}, bf16[1024,256]{1,0:T(8,128)(2,1)S(1)}, u32[]{:S(2)}, u32[]{:S(2)}) collective-permute-start(bf16[1024,256]{1,0:T(8,128)(2,1)S(1)} %slice.4), channel_id=1, source_target_pairs={{0,16},{16,0},{32,48},{48,32},{64,80},{80,64},{96,112},{112,96},{1... | collective-permute-start | bytes 1572872 | tf_op jit(solution)/shard_map/ppermute | solution.py:565
  112.3 0.0 copy-done.10
  112.3 2.7 %collect.1 = bf16[96,2048]{1,0:T(8,128)(2,1)} custom-call(bf16[1024,640]{1,0:T(8,128)(2,1)S(1)} %bitcast.15, s32[2,2048]{1,0:T(2,128)S(1)} %copy-done.10), custom_call_target="tpu_custom_call" | custom-call | flops 2147483648 | bytes 4000000 | tf_op jit(solution)/shard_map/collect/pallas_call | solution.py:45
  115.1 0.0 collective-permute-done.5.theirs_ref
  115.1 2.1 %unpack.1 = (f32[27,96,96]{2,1,0:T(8,128)}, f32[8,96,192]{2,1,0:T(8,128)}) custom-call(s32[2]{0:T(128)S(1)} %pad_add_fusion.place_ref, bf16[1024,640]{1,0:T(8,128)(2,1)S(1)} %bitcast.16, bf16[1024,256]{1,0:T(8,128)(2,1)S(1)} %collective-permute-done.5.theirs_ref), custom_call_target="tpu_custom_call" | custom-call | bytes 4000000 | tf_op jit(solution)/shard_map/unpack/pallas_call | solution.py:45
  (1 shorter events, 0.0 us)
Async XLA Ops:
  5.5 11.5 %copy-start.7 = (s32[8,16,16]{2,1,0:T(8,128)S(1)}, s32[8,16,16]{2,1,0:T(8,128)}, u32[]{:S(2)}) copy-start(s32[8,16,16]{2,1,0:T(8,128)} %param.10) | copy-start | bytes 24580
  5.5 30.1 %all-to-all-start = ((bf16[128,8,512]{2,1,0:T(8,128)(2,1)}), bf16[128,8,512]{2,1,0:T(8,128)(2,1)S(1)}, u32[]{:S(2)}, u32[]{:S(2)}) async-start(bf16[128,8,512]{2,1,0:T(8,128)(2,1)} %bitcast.22), calls=%async_computation | async-start | bytes 2097152 | tf_op jit(solution)/shard_map/all_to_all | solution.py:569
  17.0 1.1 copy-start.4
  18.1 1.0 copy-start.5
  19.1 0.9 copy-start.6
  21.0 0.7 copy-start
  21.7 1.3 %copy-start.8 = (bf16[3456,256]{1,0:T(8,128)(2,1)}, bf16[3456,256]{1,0:T(8,128)(2,1)S(1)}, u32[]{:S(2)}) copy-start(bf16[3456,256]{1,0:T(8,128)(2,1)S(1)} %get-tuple-element.48.conv_ref) | copy-start | bytes 5308420
  35.6 12.9 %copy-start.1 = (bf16[192,1024]{1,0:T(8,128)(2,1)S(1)}, bf16[192,1024]{1,0:T(8,128)(2,1)}, u32[]{:S(2)}) copy-start(bf16[192,1024]{1,0:T(8,128)(2,1)} %copy-done) | copy-start | bytes 1179652
  38.8 2.7 %collective-permute-start = (bf16[448,256]{1,0:T(8,128)(2,1)S(1)}, bf16[448,256]{1,0:T(8,128)(2,1)S(1)}, u32[]{:S(2)}, u32[]{:S(2)}) collective-permute-start(bf16[448,256]{1,0:T(8,128)(2,1)S(1)} %get-tuple-element.31), channel_id=1, source_target_pairs={{0,16},{32,48},{64,80},{96,112},{16,0},{48,32},{80,64},{112,96},{1... | collective-permute-start | bytes 688136 | tf_op jit(solution)/shard_map/ppermute | solution.py:561
  40.4 5.7 %collective-permute-start.1 = (bf16[448,256]{1,0:T(8,128)(2,1)S(1)}, bf16[448,256]{1,0:T(8,128)(2,1)S(1)}, u32[]{:S(2)}, u32[]{:S(2)}) collective-permute-start(bf16[448,256]{1,0:T(8,128)(2,1)S(1)} %get-tuple-element.32), channel_id=1, source_target_pairs={{16,32},{48,64},{80,96},{112,0},{32,16},{64,48},{96,80},{0,112},{1... | collective-permute-start | bytes 688136 | tf_op jit(solution)/shard_map/ppermute | solution.py:560
  46.8 9.7 %collective-permute-start.2 = (bf16[384,256]{1,0:T(8,128)(2,1)S(1)}, bf16[384,256]{1,0:T(8,128)(2,1)S(1)}, u32[]{:S(2)}, u32[]{:S(2)}) collective-permute-start(bf16[384,256]{1,0:T(8,128)(2,1)S(1)} %get-tuple-element.33), channel_id=1, source_target_pairs={{0,1},{2,3},{4,5},{6,7},{8,9},{10,11},{12,13},{14,15},{1,0},{3,2},... | collective-permute-start | bytes 589832 | tf_op jit(solution)/shard_map/ppermute | solution.py:561
  47.5 9.0 %collective-permute-start.3 = (bf16[384,256]{1,0:T(8,128)(2,1)S(1)}, bf16[384,256]{1,0:T(8,128)(2,1)S(1)}, u32[]{:S(2)}, u32[]{:S(2)}) collective-permute-start(bf16[384,256]{1,0:T(8,128)(2,1)S(1)} %get-tuple-element.34), channel_id=1, source_target_pairs={{1,2},{3,4},{5,6},{7,8},{9,10},{11,12},{13,14},{15,0},{2,1},{4,3},... | collective-permute-start | bytes 589832 | tf_op jit(solution)/shard_map/ppermute | solution.py:560
  61.4 4.0 %copy-start.2 = (bf16[1440,256]{1,0:T(8,128)(2,1)}, bf16[1440,256]{1,0:T(8,128)(2,1)S(1)}, u32[]{:S(2)}) copy-start(bf16[1440,256]{1,0:T(8,128)(2,1)S(1)} %get-tuple-element.47.delta_ref) | copy-start | bytes 2211844
  61.4 3.1 %collective-permute-start.4 = (bf16[2048,128]{1,0:T(8,128)(2,1)S(1)}, bf16[2048,128]{1,0:T(8,128)(2,1)S(1)}, u32[]{:S(2)}, u32[]{:S(2)}) collective-permute-start(bf16[2048,128]{1,0:T(8,128)(2,1)S(1)} %get-tuple-element.46), channel_id=1, source_target_pairs={{0,16},{16,0},{32,48},{48,32},{64,80},{80,64},{96,112},{112,96},{1... | collective-permute-start | bytes 1572872 | tf_op jit(solution)/shard_map/ppermute | solution.py:565
  65.4 18.8 %all-to-all-start.1 = ((bf16[64,32,128]{2,1,0:T(8,128)(2,1)}), bf16[64,32,128]{2,1,0:T(8,128)(2,1)S(1)}, u32[]{:S(2)}, u32[]{:S(2)}) async-start(bf16[64,32,128]{2,1,0:T(8,128)(2,1)} %bitcast.10), calls=%async_computation.1 | async-start | bytes 1048576 | tf_op jit(solution)/shard_map/all_to_all | solution.py:569
  72.0 1.1 copy-start.3
  73.1 1.5 %copy-start.9 = (bf16[3456,256]{1,0:T(8,128)(2,1)S(1)}, bf16[3456,256]{1,0:T(8,128)(2,1)}, u32[]{:S(2)}) copy-start(bf16[3456,256]{1,0:T(8,128)(2,1)} %copy-done.8) | copy-start | bytes 5308420
  84.4 27.9 %copy-start.10 = (s32[2,2048]{1,0:T(2,128)S(1)}, s32[2,2048]{1,0:T(2,128)}, u32[]{:S(2)}) copy-start(s32[2,2048]{1,0:T(2,128)} %get-tuple-element.49.slot_ref) | copy-start | bytes 49156
  110.8 4.3 %collective-permute-start.5 = (bf16[1024,256]{1,0:T(8,128)(2,1)S(1)}, bf16[1024,256]{1,0:T(8,128)(2,1)S(1)}, u32[]{:S(2)}, u32[]{:S(2)}) collective-permute-start(bf16[1024,256]{1,0:T(8,128)(2,1)S(1)} %slice.4), channel_id=1, source_target_pairs={{0,16},{16,0},{32,48},{48,32},{64,80},{80,64},{96,112},{112,96},{1... | collective-permute-start | bytes 1572872 | tf_op jit(solution)/shard_map/ppermute | solution.py:565

commit v9 on v8

--- a/solution.py
+++ b/solution.py
@@ -139,12 +139,10 @@
     at = 0
     for ref, (ext_x, ext_y, half, rim) in zip((total_ref, coarse_ref), fields):
         field = as_field(ref[...], ext_x, ext_y, half)
+        packed = ref is total_ref
         first = field[:rim] * inside(place_ref[0], 0)
         last = field[ext_x - rim :] * inside(place_ref[0], count - 1)
-        even, odd = by_parity(place_ref[0], first, last)
-        put_rows(even_ref, at, even)
-        put_rows(odd_ref, at, odd)
-        at += rim * ext_y * half
+        at = put_faces(place_ref[0], (even_ref, odd_ref), at, first, last, packed)
     grid_ref[...] = total_ref[...].astype(BF16)
 
 
@@ -152,9 +150,63 @@
     return rows.astype(F32).reshape(ext_x, ext_y, half, rows.shape[1])
 
 
-def put_rows(ref, at, field):
-    size = field.shape[0] * field.shape[1] * field.shape[2]
-    ref[at : at + size, :] = field.reshape(size, field.shape[3]).astype(BF16)
+def packed_size(size):
+    return size - size // 64 * 16
+
+
+def pack_rows(rows):
+    quarter = rows.shape[0] // 64 * 16
+    third = LANE // 4
+    spare = iota((quarter, LANE), 1) >= 3 * third
+    halves = []
+    for lanes in (slice(0, LANE), slice(LANE, WIDE)):
+        moved = rows[3 * quarter : 4 * quarter, lanes]
+        parts = [
+            jnp.where(
+                spare,
+                pltpu.roll(moved, (3 - k) * third, 1),
+                rows[k * quarter : (k + 1) * quarter, lanes],
+            )
+            for k in range(3)
+        ]
+        if rows.shape[0] > 4 * quarter:
+            parts.append(rows[4 * quarter :, lanes])
+        halves.append(jnp.concatenate(parts, axis=0))
+    return jnp.concatenate(halves, axis=1)
+
+
+def unpack_rows(rows, size):
+    quarter = size // 64 * 16
+    third = LANE // 4
+    lane = iota((quarter, LANE), 1)
+    halves = []
+    for lanes in (slice(0, LANE), slice(LANE, WIDE)):
+        parts = [rows[k * quarter : (k + 1) * quarter, lanes] for k in range(3)]
+        back = [pltpu.roll(part, (k + 1) * third, 1) for k, part in enumerate(parts)]
+        moved = jnp.where(lane < third, back[0], jnp.where(lane < 2 * third, back[1], back[2]))
+        parts.append(moved)
+        if size > 4 * quarter:
+            parts.append(rows[3 * quarter :, lanes])
+        halves.append(jnp.concatenate(parts, axis=0))
+    return jnp.concatenate(halves, axis=1)
+
+
+def faces_of(place, refs, start, shape, packed):
+    count_x, count_y, half = shape
+    size = count_x * count_y * half
+    length = packed_size(size) if packed else size
+    both = by_parity(place, *[ref[start : start + length, :].astype(F32) for ref in refs])
+    if packed:
+        both = [unpack_rows(rows, size) for rows in both]
+    return [as_field(rows, count_x, count_y, half) for rows in both], start + length
+
+
+def put_faces(place, refs, at, first, last, packed):
+    for ref, field in zip(refs, by_parity(place, first, last)):
+        rows = rows_of(field)
+        rows = pack_rows(rows) if packed else rows
+        ref[at : at + rows.shape[0], :] = rows.astype(BF16)
+    return at + rows.shape[0]
 
 
 def inside(place, end):
@@ -171,17 +223,14 @@
 ):
     start, at = 0, 0
     for ref, (ext_x, ext_y, half, rim) in zip((grid_ref, coarse_ref), fields):
-        size = rim * ext_y * half
-        x_faces = [as_field(ref_x[start : start + size, :], rim, ext_y, half) for ref_x in (x_even, x_odd)]
-        low, high = by_parity(place_ref[0], *x_faces)
-        for part in (low, as_field(ref[...], ext_x, ext_y, half), high):
-            first = part[:, :rim] * inside(place_ref[1], 0)
-            last = part[:, ext_y - rim :] * inside(place_ref[1], count - 1)
-            even, odd = by_parity(place_ref[1], first, last)
-            put_rows(even_ref, at, even)
-            put_rows(odd_ref, at, odd)
-            at += part.shape[0] * rim * half
-        start += size
+        packed = ref is grid_ref
+        (low, high), start = faces_of(
+            place_ref[0], (x_even, x_odd), start, (rim, ext_y, half), packed
+        )
+        field = jnp.concatenate([low, as_field(ref[...], ext_x, ext_y, half), high], axis=0)
+        first = field[:, :rim] * inside(place_ref[1], 0)
+        last = field[:, ext_y - rim :] * inside(place_ref[1], count - 1)
+        at = put_faces(place_ref[1], (even_ref, odd_ref), at, first, last, packed)
 
 
 def prepare_kernel(
@@ -313,15 +362,15 @@
     pad_ref, four_ref, coarse_s, mask_s, fine_s, slope_s, delta_s, *, channels, rim,
 ):
     ext_x, ext_y, half = pad_ref.shape[0], pad_ref.shape[1], pad_ref.shape[2]
-    size = rim * ext_y * half
-    x_faces = [as_field(ref[:size, :], rim, ext_y, half) for ref in (x_even, x_odd)]
-    pad_ref[:rim], pad_ref[ext_x - rim :] = by_parity(place_ref[0], *x_faces)
+    refs = (x_even, x_odd)
+    (low, high), start = faces_of(place_ref[0], refs, 0, (rim, ext_y, half), True)
+    pad_ref[:rim], pad_ref[ext_x - rim :] = low, high
     pad_ref[rim : ext_x - rim] = as_field(grid_ref[...], ext_x - 2 * rim, ext_y, half)
     fill_four(pad_ref, four_ref, channels)
     coarse_x, coarse_y = coarse_s.shape[0], coarse_s.shape[1]
     coarse = down_ref.shape[1]
-    x_faces = [as_field(ref[size:, :], 1, coarse_y, half) for ref in (x_even, x_odd)]
-    coarse_s[:1], coarse_s[coarse_x - 1 :] = by_parity(place_ref[0], *x_faces)
+    (low, high), _ = faces_of(place_ref[0], refs, start, (1, coarse_y, half), False)
+    coarse_s[:1], coarse_s[coarse_x - 1 :] = low, high
     coarse_s[1 : coarse_x - 1] = as_field(coarse_ref[...], coarse_x - 2, coarse_y, half)
     coarse_mask = child_masks(coarse_s, mask_s, coarse)
     count, inside_y = 4, ext_y - 2
@@ -371,12 +420,11 @@
 ):
     (ext_x, ext_y, half, rim), (coarse_x, coarse_y, _, _) = fields
     long = ext_x + 2 * rim
-    slab, face = rim * ext_y * half, long * rim * half
-    x_faces = [as_field(ref[:slab, :], rim, ext_y, half) for ref in (x_even, x_odd)]
-    low, high = by_parity(place_ref[0], *x_faces)
+    x_refs, y_refs = (x_even, x_odd), (y_even, y_odd)
+    (low, high), x_start = faces_of(place_ref[0], x_refs, 0, (rim, ext_y, half), True)
     parts = (low, as_field(grid_ref[...], ext_x, ext_y, half), high)
-    y_faces = [as_field(ref[:face, :], long, rim, half) for ref in (y_even, y_odd)]
-    for side, y_face in enumerate(by_parity(place_ref[1], *y_faces)):
+    y_faces, y_start = faces_of(place_ref[1], y_refs, 0, (long, rim, half), True)
+    for side, y_face in enumerate(y_faces):
         ours, here, there = ((0, rim, 0), (ext_y - rim, 0, rim))[side]
         at = side * long
         pad_ref[at : at + long, there : there + rim] = y_face
@@ -385,11 +433,11 @@
             pad_ref[at : at + count, here : here + rim] = part[:, ours : ours + rim]
             at += count
     fill_four(pad_ref, four_ref, channels)
-    x_faces = [as_field(ref[slab:, :], 1, coarse_y, half) for ref in (x_even, x_odd)]
-    low, high = by_parity(place_ref[0], *x_faces)
+    (low, high), _ = faces_of(place_ref[0], x_refs, x_start, (1, coarse_y, half), False)
     parts = (low, as_field(coarse_ref[...], coarse_x, coarse_y, half), high)
-    y_faces = [as_field(ref[face:, :], coarse_x + 2, 1, half) for ref in (y_even, y_odd)]
-    for side, y_face in enumerate(by_parity(place_ref[1], *y_faces)):
+    shape = (coarse_x + 2, 1, half)
+    y_faces, _ = faces_of(place_ref[1], y_refs, y_start, shape, False)
+    for side, y_face in enumerate(y_faces):
         y = side * (coarse_y - 1)
         theirs = 3 * side
         coarse_s[:, theirs : theirs + 1] = y_face
@@ -622,8 +670,8 @@
         "prepare",
         flops=1000000000,
     )
-    x_rows = sum(e[3] * e[1] * e[2] for e in fields)
-    y_rows = sum(e[3] * (e[0] + 2 * e[3]) * e[2] for e in fields)
+    x_rows = packed_size(rim * ext_y * half) + coarse_y * half
+    y_rows = packed_size(rim * (ext_x + 2 * rim) * half) + (coarse_x + 2) * half
     place = jnp.stack([lax.axis_index("gx"), lax.axis_index("gy")]).astype(jnp.int32)
     grid, x_even, x_odd = call(
         functools.partial(pool_kernel, channels=channels, fields=fields, count=count_x),

time: 118 us -> 117 us (level)
  no operation moved by 1% of the time
where the time goes in v9:
time: 117 us
  Pallas kernels  33 us (28%)
  blocking collectives  26.3 us (22%)
  starting transfers between devices  24.8 us (21%)
  waiting for transfers between devices  24.2 us (21%)
  local copies, waits for them, and re-layouts  7.61 us (7%)
    pallas_call x11, Pallas kernels, call(): pl.pallas_call(kernel, out_shape=outs, in_specs=[spec(i, arg, far) for i,...  33 us
    all_to_all x1, blocking collectives, exchange(): lax.all_to_all(blocks, AXES, split_axis=0, concat_axis=0, tiled=True, **g...  26.3 us
    all_to_all x2, starting transfers between devices, exchange(): lax.all_to_all(blocks, AXES, split_axis=0, concat_axis=0, tiled=True, **g...  18.1 us
    all_to_all x2, waiting for transfers between devices, exchange(): lax.all_to_all(blocks, AXES, split_axis=0, concat_axis=0, tiled=True, **g...  17.7 us
    unnamed x22, local copies, waits for them, and re-layouts  7.58 us
    ppermute x2, waiting for transfers between devices, swap_faces(): odd = lax.ppermute(odd, axis, pairs[1])  4.17 us
    ppermute x2, starting transfers between devices, to_other_core(): lax.ppermute(block, 'gx', [(i, i ^ 1) for i in range(lax.axis_size('gx'))])  3.13 us
  transfers between devices with their start and end apart: 8, of which 5 were waited for; matrix products, arithmetic and copies ran while one was open for 0% of the time, Pallas kernels for 14%

profile of v9, /device:TPU:1, one launch (start us, length us, event | category | flops | bytes accessed | tf_op | source)
XLA Modules:
  0.0 116.7 jit_solution(13931333561429523290)
XLA Ops:
  0.6 4.8 %dispatch.1 = (bf16[1024,512]{1,0:T(8,128)(2,1)}, s32[2,2048]{1,0:T(2,128)}) custom-call(bf16[96,2048]{1,0:T(8,128)(2,1)} %bitcast.23, s32[1,2048]{1,0:T(1,128)} %bitcast.25, s32[1,2048]{1,0:T(1,128)} %bitcast.26), custom_call_target="tpu_custom_call" | custom-call | flops 2147483648 | bytes 4000000 | tf_op jit(solution)/shard_map/dispatch/pallas_call | solution.py:45
  5.5 0.0 copy-start.7
  5.5 11.5 %all-to-all-start = ((bf16[128,8,512]{2,1,0:T(8,128)(2,1)}), bf16[128,8,512]{2,1,0:T(8,128)(2,1)S(1)}, u32[]{:S(2)}, u32[]{:S(2)}) async-start(bf16[128,8,512]{2,1,0:T(8,128)(2,1)} %bitcast.22), calls=%async_computation | async-start | bytes 2097152 | tf_op jit(solution)/shard_map/all_to_all | solution.py:617
  17.0 0.0 copy-done.7
  17.0 0.0 copy-start.4
  17.0 1.1 copy-done.4
  18.1 0.0 copy-start.5
  18.1 1.0 copy-done.5
  19.1 0.0 copy-start.6
  19.1 0.9 copy-done.6
  20.0 1.0 prepare.1
  21.0 0.0 copy-start
  21.0 0.7 copy-done
  21.7 0.0 copy-start.8
  21.7 1.2 %copy-done.8 = bf16[3456,256]{1,0:T(8,128)(2,1)} copy-done((bf16[3456,256]{1,0:T(8,128)(2,1)}, bf16[3456,256]{1,0:T(8,128)(2,1)S(1)}, u32[]{:S(2)}) %copy-start.8) | copy-done | bytes 1769496
  23.0 0.1 pad_add_fusion.place_ref
  23.1 12.6 %all-to-all-done = bf16[128,8,512]{2,1,0:T(8,128)(2,1)S(1)} async-done(((bf16[128,8,512]{2,1,0:T(8,128)(2,1)}), bf16[128,8,512]{2,1,0:T(8,128)(2,1)S(1)}, u32[]{:S(2)}, u32[]{:S(2)}) %all-to-all-start) | async-done | bytes 1048608 | tf_op jit(solution)/shard_map/all_to_all | solution.py:617
  35.6 0.0 copy-start.1
  35.6 3.3 %pool.1 = (bf16[1024,256]{1,0:T(8,128)(2,1)S(1)}, bf16[352,256]{1,0:T(8,128)(2,1)S(1)}, bf16[352,256]{1,0:T(8,128)(2,1)S(1)}) custom-call(s32[2]{0:T(128)S(1)} %pad_add_fusion.place_ref, bf16[1024,512]{1,0:T(8,128)(2,1)S(1)} %bitcast.18, bf16[256,256]{1,0:T(8,128)(2,1)S(1)} %get-tuple-element.29.coarse_ref), custom_call_target="tpu_custom_call" | custom-call | flops 2147483648 | bytes 4000000 | tf_op jit(solution)/shard_map/pool/pallas_call | solution.py:45
  39.0 1.6 %collective-permute-start = (bf16[352,256]{1,0:T(8,128)(2,1)S(1)}, bf16[352,256]{1,0:T(8,128)(2,1)S(1)}, u32[]{:S(2)}, u32[]{:S(2)}) collective-permute-start(bf16[352,256]{1,0:T(8,128)(2,1)S(1)} %get-tuple-element.31), channel_id=1, source_target_pairs={{0,16},{32,48},{64,80},{96,112},{16,0},{48,32},{80,64},{112,96},{1... | collective-permute-start | bytes 540680 | tf_op jit(solution)/shard_map/ppermute | solution.py:609
  40.5 0.3 collective-permute-start.1
  40.9 0.7 collective-permute-done.x_even
  41.6 4.2 %collective-permute-done.1.x_odd = bf16[352,256]{1,0:T(8,128)(2,1)S(1)} collective-permute-done((bf16[352,256]{1,0:T(8,128)(2,1)S(1)}, bf16[352,256]{1,0:T(8,128)(2,1)S(1)}, u32[]{:S(2)}, u32[]{:S(2)}) %collective-permute-start.1) | collective-permute-done | bytes 180256 | tf_op jit(solution)/shard_map/ppermute | solution.py:608
  45.7 0.7 edge.1
  46.5 0.7 collective-permute-start.2
  47.2 1.0 collective-permute-start.3
  48.2 0.0 copy-done.1
  48.2 7.8 %middle.1 = (bf16[192,256]{1,0:T(8,128)(2,1)S(1)}, f32[192,256]{1,0:T(8,128)S(1)}, bf16[192,192]{1,0:T(8,128)(2,1)S(1)}, bf16[960,256]{1,0:T(8,128)(2,1)S(1)}, f...) custom-call(s32[2]{0:T(128)S(1)} %pad_add_fusion.place_ref, bf16[1024,256]{1,0:T(8,128)(2,1)S(1)} %get-tuple-element.30.grid_ref, ...), custom_call_target="tpu_custom_call" | custom-call | flops 5435817984 | bytes 4000000 | tf_op jit(solution)/shard_map/middle/pallas_call | solution.py:45
  56.0 0.0 collective-permute-done.2.y_even
  56.0 0.0 collective-permute-done.3.y_odd
  56.0 4.9 %strip.1 = (bf16[256,192]{1,0:T(8,128)(2,1)}, bf16[1440,256]{1,0:T(8,128)(2,1)S(1)}, bf16[2048,128]{1,0:T(8,128)(2,1)S(1)}, bf16[2048,128]{1,0:T(8,128)(2,1)S(1)}) custom-call(s32[2]{0:T(128)S(1)} %pad_add_fusion.place_ref, bf16[1024,256]{1,0:T(8,128)(2,1)S(1)} %get-tuple-element.30.grid_ref, bf16[256,256]{1,0:T(8,128)(2,1)S(1)} %get-tuple-element.29.coarse_ref, ...), custom_call_target="tpu_custom_call" | custom-call | flops 1811939328 | bytes 8000000 | tf_op jit(solution)/shard_map/strip/pallas_call | solution.py:45
  60.9 0.0 copy-start.2
  60.9 1.6 %collective-permute-start.4 = (bf16[2048,128]{1,0:T(8,128)(2,1)S(1)}, bf16[2048,128]{1,0:T(8,128)(2,1)S(1)}, u32[]{:S(2)}, u32[]{:S(2)}) collective-permute-start(bf16[2048,128]{1,0:T(8,128)(2,1)S(1)} %get-tuple-element.46), channel_id=1, source_target_pairs={{0,16},{16,0},{32,48},{48,32},{64,80},{80,64},{96,112},{112,96},{1... | collective-permute-start | bytes 1572872 | tf_op jit(solution)/shard_map/ppermute | solution.py:613
  62.5 1.5 %collective-permute-done.4.other_ref = bf16[2048,128]{1,0:T(8,128)(2,1)S(1)} collective-permute-done((bf16[2048,128]{1,0:T(8,128)(2,1)S(1)}, bf16[2048,128]{1,0:T(8,128)(2,1)S(1)}, u32[]{:S(2)}, u32[]{:S(2)}) %collective-permute-start.4) | collective-permute-done | bytes 524320 | tf_op jit(solution)/shard_map/ppermute | solution.py:613
  64.0 0.9 pair.1
  64.9 0.0 copy-done.2
  64.9 6.6 %all-to-all-start.1 = ((bf16[64,32,128]{2,1,0:T(8,128)(2,1)}), bf16[64,32,128]{2,1,0:T(8,128)(2,1)S(1)}, u32[]{:S(2)}, u32[]{:S(2)}) async-start(bf16[64,32,128]{2,1,0:T(8,128)(2,1)} %bitcast.10), calls=%async_computation.1 | async-start | bytes 1048576 | tf_op jit(solution)/shard_map/all_to_all | solution.py:617
  71.5 0.0 copy-start.3
  71.5 1.1 copy-done.3
  72.6 0.0 copy-start.9
  72.6 1.5 %copy-done.9 = bf16[3456,256]{1,0:T(8,128)(2,1)S(1)} copy-done((bf16[3456,256]{1,0:T(8,128)(2,1)S(1)}, bf16[3456,256]{1,0:T(8,128)(2,1)}, u32[]{:S(2)}) %copy-start.9) | copy-done | bytes 1769496
  74.1 4.5 %input_grad.1.back_ref = bf16[1024,384]{1,0:T(8,128)(2,1)S(1)} custom-call(bf16[1440,256]{1,0:T(8,128)(2,1)S(1)} %copy-done.3, bf16[3456,256]{1,0:T(8,128)(2,1)S(1)} %copy-done.9, bf16[1024,512]{1,0:T(8,128)(2,1)S(1)} %bitcast.19), custom_call_target="tpu_custom_call" | custom-call | flops 3959422976 | bytes 8000000 | tf_op jit(solution)/shard_map/input_grad/pallas_call | solution.py:45
  78.6 5.1 %all-to-all-done.1.terms_ref = bf16[64,32,128]{2,1,0:T(8,128)(2,1)S(1)} async-done(((bf16[64,32,128]{2,1,0:T(8,128)(2,1)}), bf16[64,32,128]{2,1,0:T(8,128)(2,1)S(1)}, u32[]{:S(2)}, u32[]{:S(2)}) %all-to-all-start.1) | async-done | bytes 524320 | tf_op jit(solution)/shard_map/all_to_all | solution.py:617
  83.8 0.2 join.1
  84.0 0.0 copy-start.10
  84.0 26.3 %all_to_all.15 = bf16[128,8,640]{2,1,0:T(8,128)(2,1)S(1)} all-to-all(bf16[128,8,640]{2,1,0:T(8,128)(2,1)S(1)} %bitcast.17), channel_id=1, replica_groups=mesh['gx'=8,'gy'=16] {'gx','gy'}, dimensions={0} | all-to-all | bytes 2621440 | tf_op jit(solution)/shard_map/all_to_all | solution.py:617
  110.3 1.6 %collective-permute-start.5 = (bf16[1024,256]{1,0:T(8,128)(2,1)S(1)}, bf16[1024,256]{1,0:T(8,128)(2,1)S(1)}, u32[]{:S(2)}, u32[]{:S(2)}) collective-permute-start(bf16[1024,256]{1,0:T(8,128)(2,1)S(1)} %slice.4), channel_id=1, source_target_pairs={{0,16},{16,0},{32,48},{48,32},{64,80},{80,64},{96,112},{112,96},{1... | collective-permute-start | bytes 1572872 | tf_op jit(solution)/shard_map/ppermute | solution.py:613
  111.9 0.0 copy-done.10
  111.9 2.7 %collect.1 = bf16[96,2048]{1,0:T(8,128)(2,1)} custom-call(bf16[1024,640]{1,0:T(8,128)(2,1)S(1)} %bitcast.15, s32[2,2048]{1,0:T(2,128)S(1)} %copy-done.10), custom_call_target="tpu_custom_call" | custom-call | flops 2147483648 | bytes 4000000 | tf_op jit(solution)/shard_map/collect/pallas_call | solution.py:45
  114.6 0.0 collective-permute-done.5.theirs_ref
  114.6 2.1 %unpack.1 = (f32[27,96,96]{2,1,0:T(8,128)}, f32[8,96,192]{2,1,0:T(8,128)}) custom-call(s32[2]{0:T(128)S(1)} %pad_add_fusion.place_ref, bf16[1024,640]{1,0:T(8,128)(2,1)S(1)} %bitcast.16, bf16[1024,256]{1,0:T(8,128)(2,1)S(1)} %collective-permute-done.5.theirs_ref), custom_call_target="tpu_custom_call" | custom-call | bytes 4000000 | tf_op jit(solution)/shard_map/unpack/pallas_call | solution.py:45
  (1 shorter events, 0.0 us)
Async XLA Ops:
  5.5 11.5 %copy-start.7 = (s32[8,16,16]{2,1,0:T(8,128)S(1)}, s32[8,16,16]{2,1,0:T(8,128)}, u32[]{:S(2)}) copy-start(s32[8,16,16]{2,1,0:T(8,128)} %param.10) | copy-start | bytes 24580
  5.5 30.1 %all-to-all-start = ((bf16[128,8,512]{2,1,0:T(8,128)(2,1)}), bf16[128,8,512]{2,1,0:T(8,128)(2,1)S(1)}, u32[]{:S(2)}, u32[]{:S(2)}) async-start(bf16[128,8,512]{2,1,0:T(8,128)(2,1)} %bitcast.22), calls=%async_computation | async-start | bytes 2097152 | tf_op jit(solution)/shard_map/all_to_all | solution.py:617
  17.0 1.1 copy-start.4
  18.1 1.0 copy-start.5
  19.1 0.9 copy-start.6
  21.0 0.7 copy-start
  21.7 1.3 %copy-start.8 = (bf16[3456,256]{1,0:T(8,128)(2,1)}, bf16[3456,256]{1,0:T(8,128)(2,1)S(1)}, u32[]{:S(2)}) copy-start(bf16[3456,256]{1,0:T(8,128)(2,1)S(1)} %get-tuple-element.48.conv_ref) | copy-start | bytes 5308420
  35.6 12.5 %copy-start.1 = (bf16[192,1024]{1,0:T(8,128)(2,1)S(1)}, bf16[192,1024]{1,0:T(8,128)(2,1)}, u32[]{:S(2)}) copy-start(bf16[192,1024]{1,0:T(8,128)(2,1)} %copy-done) | copy-start | bytes 1179652
  39.0 2.6 %collective-permute-start = (bf16[352,256]{1,0:T(8,128)(2,1)S(1)}, bf16[352,256]{1,0:T(8,128)(2,1)S(1)}, u32[]{:S(2)}, u32[]{:S(2)}) collective-permute-start(bf16[352,256]{1,0:T(8,128)(2,1)S(1)} %get-tuple-element.31), channel_id=1, source_target_pairs={{0,16},{32,48},{64,80},{96,112},{16,0},{48,32},{80,64},{112,96},{1... | collective-permute-start | bytes 540680 | tf_op jit(solution)/shard_map/ppermute | solution.py:609
  40.5 5.2 %collective-permute-start.1 = (bf16[352,256]{1,0:T(8,128)(2,1)S(1)}, bf16[352,256]{1,0:T(8,128)(2,1)S(1)}, u32[]{:S(2)}, u32[]{:S(2)}) collective-permute-start(bf16[352,256]{1,0:T(8,128)(2,1)S(1)} %get-tuple-element.32), channel_id=1, source_target_pairs={{16,32},{48,64},{80,96},{112,0},{32,16},{64,48},{96,80},{0,112},{1... | collective-permute-start | bytes 540680 | tf_op jit(solution)/shard_map/ppermute | solution.py:608
  46.5 9.5 %collective-permute-start.2 = (bf16[304,256]{1,0:T(8,128)(2,1)S(1)}, bf16[304,256]{1,0:T(8,128)(2,1)S(1)}, u32[]{:S(2)}, u32[]{:S(2)}) collective-permute-start(bf16[304,256]{1,0:T(8,128)(2,1)S(1)} %get-tuple-element.33), channel_id=1, source_target_pairs={{0,1},{2,3},{4,5},{6,7},{8,9},{10,11},{12,13},{14,15},{1,0},{3,2},... | collective-permute-start | bytes 466952 | tf_op jit(solution)/shard_map/ppermute | solution.py:609
  47.2 8.8 %collective-permute-start.3 = (bf16[304,256]{1,0:T(8,128)(2,1)S(1)}, bf16[304,256]{1,0:T(8,128)(2,1)S(1)}, u32[]{:S(2)}, u32[]{:S(2)}) collective-permute-start(bf16[304,256]{1,0:T(8,128)(2,1)S(1)} %get-tuple-element.34), channel_id=1, source_target_pairs={{1,2},{3,4},{5,6},{7,8},{9,10},{11,12},{13,14},{15,0},{2,1},{4,3},... | collective-permute-start | bytes 466952 | tf_op jit(solution)/shard_map/ppermute | solution.py:608
  60.9 4.0 %copy-start.2 = (bf16[1440,256]{1,0:T(8,128)(2,1)}, bf16[1440,256]{1,0:T(8,128)(2,1)S(1)}, u32[]{:S(2)}) copy-start(bf16[1440,256]{1,0:T(8,128)(2,1)S(1)} %get-tuple-element.47.delta_ref) | copy-start | bytes 2211844
  60.9 3.1 %collective-permute-start.4 = (bf16[2048,128]{1,0:T(8,128)(2,1)S(1)}, bf16[2048,128]{1,0:T(8,128)(2,1)S(1)}, u32[]{:S(2)}, u32[]{:S(2)}) collective-permute-start(bf16[2048,128]{1,0:T(8,128)(2,1)S(1)} %get-tuple-element.46), channel_id=1, source_target_pairs={{0,16},{16,0},{32,48},{48,32},{64,80},{80,64},{96,112},{112,96},{1... | collective-permute-start | bytes 1572872 | tf_op jit(solution)/shard_map/ppermute | solution.py:613
  64.9 18.9 %all-to-all-start.1 = ((bf16[64,32,128]{2,1,0:T(8,128)(2,1)}), bf16[64,32,128]{2,1,0:T(8,128)(2,1)S(1)}, u32[]{:S(2)}, u32[]{:S(2)}) async-start(bf16[64,32,128]{2,1,0:T(8,128)(2,1)} %bitcast.10), calls=%async_computation.1 | async-start | bytes 1048576 | tf_op jit(solution)/shard_map/all_to_all | solution.py:617
  71.5 1.1 copy-start.3
  72.6 1.5 %copy-start.9 = (bf16[3456,256]{1,0:T(8,128)(2,1)S(1)}, bf16[3456,256]{1,0:T(8,128)(2,1)}, u32[]{:S(2)}) copy-start(bf16[3456,256]{1,0:T(8,128)(2,1)} %copy-done.8) | copy-start | bytes 5308420
  84.0 27.9 %copy-start.10 = (s32[2,2048]{1,0:T(2,128)S(1)}, s32[2,2048]{1,0:T(2,128)}, u32[]{:S(2)}) copy-start(s32[2,2048]{1,0:T(2,128)} %get-tuple-element.49.slot_ref) | copy-start | bytes 49156
  110.3 4.3 %collective-permute-start.5 = (bf16[1024,256]{1,0:T(8,128)(2,1)S(1)}, bf16[1024,256]{1,0:T(8,128)(2,1)S(1)}, u32[]{:S(2)}, u32[]{:S(2)}) collective-permute-start(bf16[1024,256]{1,0:T(8,128)(2,1)S(1)} %slice.4), channel_id=1, source_target_pairs={{0,16},{16,0},{32,48},{48,32},{64,80},{80,64},{96,112},{112,96},{1... | collective-permute-start | bytes 1572872 | tf_op jit(solution)/shard_map/ppermute | solution.py:613

commit v10 on v9

--- a/solution.py
+++ b/solution.py
@@ -373,7 +373,7 @@
     coarse_s[:1], coarse_s[coarse_x - 1 :] = low, high
     coarse_s[1 : coarse_x - 1] = as_field(coarse_ref[...], coarse_x - 2, coarse_y, half)
     coarse_mask = child_masks(coarse_s, mask_s, coarse)
-    count, inside_y = 4, ext_y - 2
+    count, inside_y = 2, ext_y - 2
     for first in range(0, ext_x - 2, count):
         (pre,) = convolve(four_ref, conv_ref, [(first, count, 0, inside_y)])
         silu, slope = silu_and_slope(pre)
@@ -399,8 +399,10 @@
     delta_ref[...] = rows_of(delta[1 : 2 * coarse_x - 1]).astype(BF16)
     turned = rows_of(delta[2 : 2 * coarse_x - 2]).T.astype(BF16)
     box = (rim - 1, 2 * (coarse_x - 2), 1, 2 * middle)
-    for j, part in enumerate(windows(four_ref, *box)):
-        conv_grad_ref[j * LANE : (j + 1) * LANE, :] = fold(mm(turned, part), channels)
+    grads = mm(turned, jnp.concatenate(windows(four_ref, *box), axis=1))
+    for j in range(9):
+        part = grads[:, 4 * j * channels : 4 * (j + 1) * channels]
+        conv_grad_ref[j * LANE : (j + 1) * LANE, :] = fold(part, channels)
     ours = rows_of(delta_coarse[1 : coarse_x - 1]).astype(BF16)
     for j in range(4):
         piece = fine_s[1 : coarse_x - 1, j // 2, 1 : 1 + middle, j % 2]

time: 117 us -> 116 us (level)
  Pallas kernels: 33 us -> 31.3 us
    pallas_call x11, Pallas kernels: 33 us -> 31.3 us  [call(): pl.pallas_call(kernel, out_shape=outs, in_specs=[spec(i, arg, far) for i,...]
  transfers between devices with their start and end apart: 8 -> 8, of which waited for: 5 -> 6; matrix products, arithmetic and copies ran while one was open for 0% -> 0% of each run, Pallas kernels for 14% -> 12%
where the time goes in v10:
time: 116 us; the launch traced here: 115 us
  Pallas kernels  31.3 us (27%)
  blocking collectives  26.3 us (23%)
  starting transfers between devices  24.6 us (21%)
  waiting for transfers between devices  24.4 us (21%)
  local copies, waits for them, and re-layouts  7.61 us (7%)
    pallas_call x11, Pallas kernels, call(): pl.pallas_call(kernel, out_shape=outs, in_specs=[spec(i, arg, far) for i,...  31.3 us
    all_to_all x1, blocking collectives, exchange(): lax.all_to_all(blocks, AXES, split_axis=0, concat_axis=0, tiled=True, **g...  26.3 us
    all_to_all x2, waiting for transfers between devices, exchange(): lax.all_to_all(blocks, AXES, split_axis=0, concat_axis=0, tiled=True, **g...  17.7 us
    all_to_all x2, starting transfers between devices, exchange(): lax.all_to_all(blocks, AXES, split_axis=0, concat_axis=0, tiled=True, **g...  17 us
    unnamed x22, local copies, waits for them, and re-layouts  7.58 us
    ppermute x2, waiting for transfers between devices, swap_faces(): odd = lax.ppermute(odd, axis, pairs[1])  4.4 us
    ppermute x2, starting transfers between devices, to_other_core(): lax.ppermute(block, 'gx', [(i, i ^ 1) for i in range(lax.axis_size('gx'))])  4 us
  transfers between devices with their start and end apart: 8, of which 6 were waited for; matrix products, arithmetic and copies ran while one was open for 0% of the time, Pallas kernels for 12%

profile of v10, /device:TPU:1, one launch (start us, length us, event | category | flops | bytes accessed | tf_op | source)
XLA Modules:
  0.0 115.0 jit_solution(8163288030338344007)
XLA Ops:
  0.6 4.8 %dispatch.1 = (bf16[1024,512]{1,0:T(8,128)(2,1)}, s32[2,2048]{1,0:T(2,128)}) custom-call(bf16[96,2048]{1,0:T(8,128)(2,1)} %bitcast.23, s32[1,2048]{1,0:T(1,128)} %bitcast.25, s32[1,2048]{1,0:T(1,128)} %bitcast.26), custom_call_target="tpu_custom_call" | custom-call | flops 2147483648 | bytes 4000000 | tf_op jit(solution)/shard_map/dispatch/pallas_call | solution.py:45
  5.5 0.0 copy-start.7
  5.5 11.5 %all-to-all-start = ((bf16[128,8,512]{2,1,0:T(8,128)(2,1)}), bf16[128,8,512]{2,1,0:T(8,128)(2,1)S(1)}, u32[]{:S(2)}, u32[]{:S(2)}) async-start(bf16[128,8,512]{2,1,0:T(8,128)(2,1)} %bitcast.22), calls=%async_computation | async-start | bytes 2097152 | tf_op jit(solution)/shard_map/all_to_all | solution.py:619
  17.0 0.0 copy-done.7
  17.0 0.0 copy-start.4
  17.0 1.1 copy-done.4
  18.1 0.0 copy-start.5
  18.1 1.0 copy-done.5
  19.1 0.0 copy-start.6
  19.1 0.9 copy-done.6
  20.0 1.0 prepare.1
  21.0 0.0 copy-start
  21.0 0.7 copy-done
  21.7 0.0 copy-start.8
  21.7 1.2 %copy-done.8 = bf16[3456,256]{1,0:T(8,128)(2,1)} copy-done((bf16[3456,256]{1,0:T(8,128)(2,1)}, bf16[3456,256]{1,0:T(8,128)(2,1)S(1)}, u32[]{:S(2)}) %copy-start.8) | copy-done | bytes 1769496
  23.0 0.1 pad_add_fusion.place_ref
  23.1 12.6 %all-to-all-done = bf16[128,8,512]{2,1,0:T(8,128)(2,1)S(1)} async-done(((bf16[128,8,512]{2,1,0:T(8,128)(2,1)}), bf16[128,8,512]{2,1,0:T(8,128)(2,1)S(1)}, u32[]{:S(2)}, u32[]{:S(2)}) %all-to-all-start) | async-done | bytes 1048608 | tf_op jit(solution)/shard_map/all_to_all | solution.py:619
  35.6 0.0 copy-start.1
  35.6 3.3 %pool.1 = (bf16[1024,256]{1,0:T(8,128)(2,1)S(1)}, bf16[352,256]{1,0:T(8,128)(2,1)S(1)}, bf16[352,256]{1,0:T(8,128)(2,1)S(1)}) custom-call(s32[2]{0:T(128)S(1)} %pad_add_fusion.place_ref, bf16[1024,512]{1,0:T(8,128)(2,1)S(1)} %bitcast.18, bf16[256,256]{1,0:T(8,128)(2,1)S(1)} %get-tuple-element.29.coarse_ref), custom_call_target="tpu_custom_call" | custom-call | flops 2147483648 | bytes 4000000 | tf_op jit(solution)/shard_map/pool/pallas_call | solution.py:45
  39.0 1.6 %collective-permute-start = (bf16[352,256]{1,0:T(8,128)(2,1)S(1)}, bf16[352,256]{1,0:T(8,128)(2,1)S(1)}, u32[]{:S(2)}, u32[]{:S(2)}) collective-permute-start(bf16[352,256]{1,0:T(8,128)(2,1)S(1)} %get-tuple-element.31), channel_id=1, source_target_pairs={{0,16},{32,48},{64,80},{96,112},{16,0},{48,32},{80,64},{112,96},{1... | collective-permute-start | bytes 540680 | tf_op jit(solution)/shard_map/ppermute | solution.py:611
  40.5 0.3 collective-permute-start.1
  40.9 0.7 collective-permute-done.x_even
  41.6 4.2 %collective-permute-done.1.x_odd = bf16[352,256]{1,0:T(8,128)(2,1)S(1)} collective-permute-done((bf16[352,256]{1,0:T(8,128)(2,1)S(1)}, bf16[352,256]{1,0:T(8,128)(2,1)S(1)}, u32[]{:S(2)}, u32[]{:S(2)}) %collective-permute-start.1) | collective-permute-done | bytes 180256 | tf_op jit(solution)/shard_map/ppermute | solution.py:610
  45.7 0.7 edge.1
  46.5 0.7 collective-permute-start.2
  47.2 1.0 collective-permute-start.3
  48.2 0.0 copy-done.1
  48.2 6.2 %middle.1 = (bf16[192,256]{1,0:T(8,128)(2,1)S(1)}, f32[192,256]{1,0:T(8,128)S(1)}, bf16[192,192]{1,0:T(8,128)(2,1)S(1)}, bf16[960,256]{1,0:T(8,128)(2,1)S(1)}, f...) custom-call(s32[2]{0:T(128)S(1)} %pad_add_fusion.place_ref, bf16[1024,256]{1,0:T(8,128)(2,1)S(1)} %get-tuple-element.30.grid_ref, ...), custom_call_target="tpu_custom_call" | custom-call | flops 5435817984 | bytes 4000000 | tf_op jit(solution)/shard_map/middle/pallas_call | solution.py:45
  54.3 0.0 collective-permute-done.2.y_even
  54.4 0.2 collective-permute-done.3.y_odd
  54.6 4.8 %strip.1 = (bf16[256,192]{1,0:T(8,128)(2,1)}, bf16[1440,256]{1,0:T(8,128)(2,1)S(1)}, bf16[2048,128]{1,0:T(8,128)(2,1)S(1)}, bf16[2048,128]{1,0:T(8,128)(2,1)S(1)}) custom-call(s32[2]{0:T(128)S(1)} %pad_add_fusion.place_ref, bf16[1024,256]{1,0:T(8,128)(2,1)S(1)} %get-tuple-element.30.grid_ref, bf16[256,256]{1,0:T(8,128)(2,1)S(1)} %get-tuple-element.29.coarse_ref, ...), custom_call_target="tpu_custom_call" | custom-call | flops 1811939328 | bytes 8000000 | tf_op jit(solution)/shard_map/strip/pallas_call | solution.py:45
  59.4 0.0 copy-start.2
  59.4 2.4 %collective-permute-start.4 = (bf16[2048,128]{1,0:T(8,128)(2,1)S(1)}, bf16[2048,128]{1,0:T(8,128)(2,1)S(1)}, u32[]{:S(2)}, u32[]{:S(2)}) collective-permute-start(bf16[2048,128]{1,0:T(8,128)(2,1)S(1)} %get-tuple-element.46), channel_id=1, source_target_pairs={{0,16},{16,0},{32,48},{48,32},{64,80},{80,64},{96,112},{112,96},{1... | collective-permute-start | bytes 1572872 | tf_op jit(solution)/shard_map/ppermute | solution.py:615
  61.9 1.5 %collective-permute-done.4.other_ref = bf16[2048,128]{1,0:T(8,128)(2,1)S(1)} collective-permute-done((bf16[2048,128]{1,0:T(8,128)(2,1)S(1)}, bf16[2048,128]{1,0:T(8,128)(2,1)S(1)}, u32[]{:S(2)}, u32[]{:S(2)}) %collective-permute-start.4) | collective-permute-done | bytes 524320 | tf_op jit(solution)/shard_map/ppermute | solution.py:615
  63.4 0.9 pair.1
  64.3 0.0 copy-done.2
  64.3 5.5 %all-to-all-start.1 = ((bf16[64,32,128]{2,1,0:T(8,128)(2,1)}), bf16[64,32,128]{2,1,0:T(8,128)(2,1)S(1)}, u32[]{:S(2)}, u32[]{:S(2)}) async-start(bf16[64,32,128]{2,1,0:T(8,128)(2,1)} %bitcast.10), calls=%async_computation.1 | async-start | bytes 1048576 | tf_op jit(solution)/shard_map/all_to_all | solution.py:619
  69.8 0.0 copy-start.3
  69.8 1.1 copy-done.3
  71.0 0.0 copy-start.9
  71.0 1.5 %copy-done.9 = bf16[3456,256]{1,0:T(8,128)(2,1)S(1)} copy-done((bf16[3456,256]{1,0:T(8,128)(2,1)S(1)}, bf16[3456,256]{1,0:T(8,128)(2,1)}, u32[]{:S(2)}) %copy-start.9) | copy-done | bytes 1769496
  72.4 4.5 %input_grad.1.back_ref = bf16[1024,384]{1,0:T(8,128)(2,1)S(1)} custom-call(bf16[1440,256]{1,0:T(8,128)(2,1)S(1)} %copy-done.3, bf16[3456,256]{1,0:T(8,128)(2,1)S(1)} %copy-done.9, bf16[1024,512]{1,0:T(8,128)(2,1)S(1)} %bitcast.19), custom_call_target="tpu_custom_call" | custom-call | flops 3959422976 | bytes 8000000 | tf_op jit(solution)/shard_map/input_grad/pallas_call | solution.py:45
  77.0 5.1 %all-to-all-done.1.terms_ref = bf16[64,32,128]{2,1,0:T(8,128)(2,1)S(1)} async-done(((bf16[64,32,128]{2,1,0:T(8,128)(2,1)}), bf16[64,32,128]{2,1,0:T(8,128)(2,1)S(1)}, u32[]{:S(2)}, u32[]{:S(2)}) %all-to-all-start.1) | async-done | bytes 524320 | tf_op jit(solution)/shard_map/all_to_all | solution.py:619
  82.1 0.2 join.1
  82.3 0.0 copy-start.10
  82.3 26.3 %all_to_all.15 = bf16[128,8,640]{2,1,0:T(8,128)(2,1)S(1)} all-to-all(bf16[128,8,640]{2,1,0:T(8,128)(2,1)S(1)} %bitcast.17), channel_id=1, replica_groups=mesh['gx'=8,'gy'=16] {'gx','gy'}, dimensions={0} | all-to-all | bytes 2621440 | tf_op jit(solution)/shard_map/all_to_all | solution.py:619
  108.6 1.6 %collective-permute-start.5 = (bf16[1024,256]{1,0:T(8,128)(2,1)S(1)}, bf16[1024,256]{1,0:T(8,128)(2,1)S(1)}, u32[]{:S(2)}, u32[]{:S(2)}) collective-permute-start(bf16[1024,256]{1,0:T(8,128)(2,1)S(1)} %slice.4), channel_id=1, source_target_pairs={{0,16},{16,0},{32,48},{48,32},{64,80},{80,64},{96,112},{112,96},{1... | collective-permute-start | bytes 1572872 | tf_op jit(solution)/shard_map/ppermute | solution.py:615
  110.2 0.0 copy-done.10
  110.2 2.7 %collect.1 = bf16[96,2048]{1,0:T(8,128)(2,1)} custom-call(bf16[1024,640]{1,0:T(8,128)(2,1)S(1)} %bitcast.15, s32[2,2048]{1,0:T(2,128)S(1)} %copy-done.10), custom_call_target="tpu_custom_call" | custom-call | flops 2147483648 | bytes 4000000 | tf_op jit(solution)/shard_map/collect/pallas_call | solution.py:45
  112.9 0.0 collective-permute-done.5.theirs_ref
  112.9 2.1 %unpack.1 = (f32[27,96,96]{2,1,0:T(8,128)}, f32[8,96,192]{2,1,0:T(8,128)}) custom-call(s32[2]{0:T(128)S(1)} %pad_add_fusion.place_ref, bf16[1024,640]{1,0:T(8,128)(2,1)S(1)} %bitcast.16, bf16[1024,256]{1,0:T(8,128)(2,1)S(1)} %collective-permute-done.5.theirs_ref), custom_call_target="tpu_custom_call" | custom-call | bytes 4000000 | tf_op jit(solution)/shard_map/unpack/pallas_call | solution.py:45
  (1 shorter events, 0.0 us)
Async XLA Ops:
  5.5 11.5 %copy-start.7 = (s32[8,16,16]{2,1,0:T(8,128)S(1)}, s32[8,16,16]{2,1,0:T(8,128)}, u32[]{:S(2)}) copy-start(s32[8,16,16]{2,1,0:T(8,128)} %param.10) | copy-start | bytes 24580
  5.5 30.1 %all-to-all-start = ((bf16[128,8,512]{2,1,0:T(8,128)(2,1)}), bf16[128,8,512]{2,1,0:T(8,128)(2,1)S(1)}, u32[]{:S(2)}, u32[]{:S(2)}) async-start(bf16[128,8,512]{2,1,0:T(8,128)(2,1)} %bitcast.22), calls=%async_computation | async-start | bytes 2097152 | tf_op jit(solution)/shard_map/all_to_all | solution.py:619
  17.0 1.1 copy-start.4
  18.1 1.0 copy-start.5
  19.1 0.9 copy-start.6
  21.0 0.7 copy-start
  21.7 1.3 %copy-start.8 = (bf16[3456,256]{1,0:T(8,128)(2,1)}, bf16[3456,256]{1,0:T(8,128)(2,1)S(1)}, u32[]{:S(2)}) copy-start(bf16[3456,256]{1,0:T(8,128)(2,1)S(1)} %get-tuple-element.48.conv_ref) | copy-start | bytes 5308420
  35.6 12.5 %copy-start.1 = (bf16[192,1024]{1,0:T(8,128)(2,1)S(1)}, bf16[192,1024]{1,0:T(8,128)(2,1)}, u32[]{:S(2)}) copy-start(bf16[192,1024]{1,0:T(8,128)(2,1)} %copy-done) | copy-start | bytes 1179652
  39.0 2.6 %collective-permute-start = (bf16[352,256]{1,0:T(8,128)(2,1)S(1)}, bf16[352,256]{1,0:T(8,128)(2,1)S(1)}, u32[]{:S(2)}, u32[]{:S(2)}) collective-permute-start(bf16[352,256]{1,0:T(8,128)(2,1)S(1)} %get-tuple-element.31), channel_id=1, source_target_pairs={{0,16},{32,48},{64,80},{96,112},{16,0},{48,32},{80,64},{112,96},{1... | collective-permute-start | bytes 540680 | tf_op jit(solution)/shard_map/ppermute | solution.py:611
  40.5 5.2 %collective-permute-start.1 = (bf16[352,256]{1,0:T(8,128)(2,1)S(1)}, bf16[352,256]{1,0:T(8,128)(2,1)S(1)}, u32[]{:S(2)}, u32[]{:S(2)}) collective-permute-start(bf16[352,256]{1,0:T(8,128)(2,1)S(1)} %get-tuple-element.32), channel_id=1, source_target_pairs={{16,32},{48,64},{80,96},{112,0},{32,16},{64,48},{96,80},{0,112},{1... | collective-permute-start | bytes 540680 | tf_op jit(solution)/shard_map/ppermute | solution.py:610
  46.5 7.9 %collective-permute-start.2 = (bf16[304,256]{1,0:T(8,128)(2,1)S(1)}, bf16[304,256]{1,0:T(8,128)(2,1)S(1)}, u32[]{:S(2)}, u32[]{:S(2)}) collective-permute-start(bf16[304,256]{1,0:T(8,128)(2,1)S(1)} %get-tuple-element.33), channel_id=1, source_target_pairs={{0,1},{2,3},{4,5},{6,7},{8,9},{10,11},{12,13},{14,15},{1,0},{3,2},... | collective-permute-start | bytes 466952 | tf_op jit(solution)/shard_map/ppermute | solution.py:611
  47.2 7.4 %collective-permute-start.3 = (bf16[304,256]{1,0:T(8,128)(2,1)S(1)}, bf16[304,256]{1,0:T(8,128)(2,1)S(1)}, u32[]{:S(2)}, u32[]{:S(2)}) collective-permute-start(bf16[304,256]{1,0:T(8,128)(2,1)S(1)} %get-tuple-element.34), channel_id=1, source_target_pairs={{1,2},{3,4},{5,6},{7,8},{9,10},{11,12},{13,14},{15,0},{2,1},{4,3},... | collective-permute-start | bytes 466952 | tf_op jit(solution)/shard_map/ppermute | solution.py:610
  59.4 4.9 %copy-start.2 = (bf16[1440,256]{1,0:T(8,128)(2,1)}, bf16[1440,256]{1,0:T(8,128)(2,1)S(1)}, u32[]{:S(2)}) copy-start(bf16[1440,256]{1,0:T(8,128)(2,1)S(1)} %get-tuple-element.47.delta_ref) | copy-start | bytes 2211844
  59.4 4.0 %collective-permute-start.4 = (bf16[2048,128]{1,0:T(8,128)(2,1)S(1)}, bf16[2048,128]{1,0:T(8,128)(2,1)S(1)}, u32[]{:S(2)}, u32[]{:S(2)}) collective-permute-start(bf16[2048,128]{1,0:T(8,128)(2,1)S(1)} %get-tuple-element.46), channel_id=1, source_target_pairs={{0,16},{16,0},{32,48},{48,32},{64,80},{80,64},{96,112},{112,96},{1... | collective-permute-start | bytes 1572872 | tf_op jit(solution)/shard_map/ppermute | solution.py:615
  64.3 17.8 %all-to-all-start.1 = ((bf16[64,32,128]{2,1,0:T(8,128)(2,1)}), bf16[64,32,128]{2,1,0:T(8,128)(2,1)S(1)}, u32[]{:S(2)}, u32[]{:S(2)}) async-start(bf16[64,32,128]{2,1,0:T(8,128)(2,1)} %bitcast.10), calls=%async_computation.1 | async-start | bytes 1048576 | tf_op jit(solution)/shard_map/all_to_all | solution.py:619
  69.8 1.1 copy-start.3
  71.0 1.5 %copy-start.9 = (bf16[3456,256]{1,0:T(8,128)(2,1)S(1)}, bf16[3456,256]{1,0:T(8,128)(2,1)}, u32[]{:S(2)}) copy-start(bf16[3456,256]{1,0:T(8,128)(2,1)} %copy-done.8) | copy-start | bytes 5308420
  82.3 27.9 %copy-start.10 = (s32[2,2048]{1,0:T(2,128)S(1)}, s32[2,2048]{1,0:T(2,128)}, u32[]{:S(2)}) copy-start(s32[2,2048]{1,0:T(2,128)} %get-tuple-element.49.slot_ref) | copy-start | bytes 49156
  108.6 4.3 %collective-permute-start.5 = (bf16[1024,256]{1,0:T(8,128)(2,1)S(1)}, bf16[1024,256]{1,0:T(8,128)(2,1)S(1)}, u32[]{:S(2)}, u32[]{:S(2)}) collective-permute-start(bf16[1024,256]{1,0:T(8,128)(2,1)S(1)} %slice.4), channel_id=1, source_target_pairs={{0,16},{16,0},{32,48},{48,32},{64,80},{80,64},{96,112},{112,96},{1... | collective-permute-start | bytes 1572872 | tf_op jit(solution)/shard_map/ppermute | solution.py:615
